TPU v7x, 256 devices: a whole 4x4x8 slice. The times are simulated.
256 devices in a mesh: seq: 64 (over y, z, x_hi), rep: 4 (over x_lo, core).
Axes of the slice: x: 4 (x_hi: 2, x_lo: 2; x = x_hi * 2 + x_lo), y: 4, z: 8, core: 2. Of those that a mesh axis runs over, the one named last changes fastest.
Arguments:
- queries: bfloat16 [4, 8192, 1024], P('rep', 'seq'), may hold values from -24 to 24
- keys: bfloat16 [4, 8192, 1024], P('rep', 'seq'), may hold values from -24 to 24
- values: bfloat16 [4, 8192, 1024], P('rep', 'seq'), may hold values from -6 to 6
- w_out: bfloat16 [1024, 2048], P('rep'), may hold values from -0.1875 to 0.1875
- d_out: bfloat16 [4, 8192, 2048], P('rep', 'seq'), may hold values from -6 to 6
- rand_slot: int32 [4, 64, 6], P('rep', 'seq'), may hold values from 0 to 1
- global_ids: int32 [4, 2], P('rep'), may hold values from 0 to 127
Outputs:
- layer_out: bfloat16 [4, 8192, 2048], P('rep', 'seq')
- query_grad: bfloat16 [4, 8192, 1024], P('rep', 'seq')
- key_grad: bfloat16 [4, 8192, 1024], P('rep', 'seq')
- value_grad: bfloat16 [4, 8192, 1024], P('rep', 'seq')
- weight_grad: float32 [1024, 2048], P(('seq', 'rep'))
Inputs may be any that keep to these rules, and one draw needn't show every extreme that they name: `rand_slot`: entries name a block by its position 0 to 1 within its stretch.
All inputs are finite; a program needn't handle non-finite values.
Results may differ from a plain program's by a relative error of at most 0.014.
Values may be sent and summed in bfloat16 or wider, within the bound.
No kernel may reach another device: no remote copies, remote signals or barrier semaphores. Data moves between devices by JAX's collectives and lax.ppermute only.
A program may use at most 128 MiB of HBM per device.

v0:
```python
import jax
import jax.numpy as jnp
from jax import lax
from jax.sharding import PartitionSpec as P

HEADS = 8
HEAD_DIM = 128
BLK = 64
GLOB = 2


def shifted(value, axis, steps):
    count = lax.axis_size(axis)
    pairs = [(source, (source + steps) % count) for source in range(count)]
    return lax.ppermute(value, axis, pairs)


def padded_2(block, sides, width):
    for axis, dim in sides:
        count = lax.axis_size(axis)
        forward = [(i, i + 1) for i in range(count - 1)]
        forward.append((count - 1, 0))
        backward = [(target, source) for source, target in forward]
        low = lax.ppermute(
            lax.slice_in_dim(block, block.shape[dim] - width, None, axis=dim), axis, forward
        )
        high = lax.ppermute(lax.slice_in_dim(block, 0, width, axis=dim), axis, backward)
        block = jnp.concatenate([low, block, high], axis=dim)
    return block


def swapped(block, axis, stride):
    count = lax.axis_size(axis)
    route = []
    for low in range(count):
        high = low | 1 << stride
        if high != low and high < count:
            route += [(low, high), (high, low)]
    return lax.ppermute(block, axis, route)


def mult(form, left, right):
    return jnp.einsum(form, left, right, preferred_element_type=jnp.float32)


def local_attention(q_dev, padded, global_kv, partner_kv, my_slots, d_attn):
    nblock = q_dev.shape[0] // BLK
    width = HEADS * HEAD_DIM
    scale = HEAD_DIM ** (-0.5)
    queries = q_dev.reshape(nblock, BLK, HEADS, HEAD_DIM)
    grads_in = d_attn.reshape(nblock, BLK, HEADS, HEAD_DIM)
    blocks = padded.reshape(2, nblock + 2, BLK, HEADS, HEAD_DIM)
    window = jnp.concatenate(
        [blocks[:, 0:nblock], blocks[:, 1 : nblock + 1], blocks[:, 2 : nblock + 2]], axis=2
    )
    glob_heads = global_kv.reshape(2, -1, HEADS, HEAD_DIM)
    rand_heads = partner_kv.reshape(2, -1, HEADS, HEAD_DIM)
    wide = 3 * BLK
    gwide = glob_heads.shape[1]
    owned = my_slots[None, :] == jnp.arange(nblock, dtype=jnp.int32)[:, None]
    keep_rand = jnp.repeat(owned, BLK, axis=1)
    s_win = mult("nqhd,nkhd->nhqk", queries, window[0]) * scale
    s_glob = mult("nqhd,khd->nhqk", queries, glob_heads[0]) * scale
    s_rand = mult("nqhd,khd->nhqk", queries, rand_heads[0]) * scale
    s_rand = jnp.where(keep_rand[:, None, None, :], s_rand, jnp.float32(-1e30))
    scores = jnp.concatenate([s_win, s_glob, s_rand], axis=-1)
    top_score = jnp.max(scores, axis=-1, keepdims=True)
    expd = jnp.exp(scores - top_score)
    probs = expd / jnp.sum(expd, axis=-1, keepdims=True)
    probs_b = probs.astype(jnp.bfloat16)
    p_win = probs_b[..., :wide]
    p_glob = probs_b[..., wide : wide + gwide]
    p_rand = probs_b[..., wide + gwide :]
    output = (
        mult("nhqk,nkhd->nqhd", p_win, window[1])
        + mult("nhqk,khd->nqhd", p_glob, glob_heads[1])
        + mult("nhqk,khd->nqhd", p_rand, rand_heads[1])
    )
    attn = output.astype(jnp.bfloat16).reshape(nblock * BLK, width)
    dprob = jnp.concatenate(
        [
            mult("nqhd,nkhd->nhqk", grads_in, window[1]),
            mult("nqhd,khd->nhqk", grads_in, glob_heads[1]),
            mult("nqhd,khd->nhqk", grads_in, rand_heads[1]),
        ],
        axis=-1,
    )
    delta = jnp.sum(dprob * probs, axis=-1, keepdims=True)
    dscore = (probs * (dprob - delta) * scale).astype(jnp.bfloat16)
    d_win = dscore[..., :wide]
    d_glob = dscore[..., wide : wide + gwide]
    d_rand = dscore[..., wide + gwide :]
    query_grad = (
        mult("nhqk,nkhd->nqhd", d_win, window[0])
        + mult("nhqk,khd->nqhd", d_glob, glob_heads[0])
        + mult("nhqk,khd->nqhd", d_rand, rand_heads[0])
    )
    query_grad = query_grad.reshape(nblock * BLK, width)
    dk_win = mult("nhqk,nqhd->nkhd", d_win, queries)
    dv_win = mult("nhqk,nqhd->nkhd", p_win, grads_in)
    dkv_win = jnp.stack([dk_win, dv_win]).reshape(2, nblock, 3, BLK, width)
    zeros_one = jnp.zeros((2, 1, BLK, width), jnp.float32)
    dpad = jnp.concatenate([dkv_win[:, :, 0], zeros_one, zeros_one], axis=1)
    dpad = dpad + jnp.concatenate([zeros_one, dkv_win[:, :, 1], zeros_one], axis=1)
    dpad = dpad + jnp.concatenate([zeros_one, zeros_one, dkv_win[:, :, 2]], axis=1)
    dglob = jnp.stack(
        [mult("nhqk,nqhd->khd", d_glob, queries), mult("nhqk,nqhd->khd", p_glob, grads_in)]
    ).reshape(2, gwide, width)
    drand = jnp.stack(
        [mult("nhqk,nqhd->khd", d_rand, queries), mult("nhqk,nqhd->khd", p_rand, grads_in)]
    ).reshape(2, -1, width)
    return (attn, query_grad, dpad, dglob, drand)


def edge_send(edge_block, offset):
    return shifted(edge_block, "seq", offset)


def per_device(queries, keys, values, w_out, d_out, rand_slot, global_ids):
    q_dev = queries[0]
    tok_rows = q_dev.shape[0]
    width = q_dev.shape[1]
    nblock = tok_rows // BLK
    key_vals = jnp.stack([keys[0], values[0]])
    my_slots = rand_slot[0, 0]
    gids = global_ids[0]
    grad_out = d_out[0]
    my_index = lax.axis_index("seq")
    nbits = lax.axis_size("seq").bit_length() - 1
    block_ids = jnp.arange(nblock, dtype=jnp.int32)
    d_attn = lax.dot_general(
        grad_out,
        lax.all_gather(w_out, "rep", axis=0, tiled=True),
        (((1,), (1,)), ((), ())),
        preferred_element_type=jnp.float32,
    ).astype(jnp.bfloat16)
    padded = padded_2(key_vals, (("seq", 1),), BLK)
    received = []
    for bit_num in range(nbits):
        chosen = lax.dynamic_slice_in_dim(key_vals, my_slots[bit_num] * BLK, BLK, 1)
        received.append(swapped(chosen, "seq", bit_num))
    partner_kv = jnp.concatenate(received, axis=1)
    owner = gids // nblock
    position = gids % nblock
    pick_hot = ((position[:, None] == block_ids[None, :]) & (owner[:, None] == my_index)).astype(
        jnp.bfloat16
    )
    picked = jnp.einsum(
        "gn,cnbx->cgbx",
        pick_hot,
        key_vals.reshape(2, nblock, BLK, width),
        preferred_element_type=jnp.float32,
    )
    global_kv = lax.psum(picked, "seq").astype(jnp.bfloat16).reshape(2, GLOB * BLK, width)
    attn, query_grad, dpad, dglob, drand = local_attention(
        q_dev, padded, global_kv, partner_kv, my_slots, d_attn
    )
    own = dpad[:, 1 : nblock + 1]
    from_right = edge_send(dpad[:, 0], -1)
    from_left = edge_send(dpad[:, nblock + 1], 1)
    own = own.at[:, nblock - 1].add(from_right)
    own = own.at[:, 0].add(from_left)
    for bit_num in range(nbits):
        sent_back = swapped(drand[:, bit_num * BLK : (bit_num + 1) * BLK], "seq", bit_num)
        slot_mask = (block_ids == my_slots[bit_num]).astype(jnp.float32)
        own = own + slot_mask[None, :, None, None] * sent_back[:, None]
    glob_total = lax.psum(dglob, "seq").reshape(2, GLOB, BLK, width)
    place_hot = ((position[:, None] == block_ids[None, :]) & (owner[:, None] == my_index)).astype(
        jnp.float32
    )
    own = own + jnp.einsum("gn,cgbx->cnbx", place_hot, glob_total, precision=lax.Precision.HIGHEST)
    part_cols = attn
    layer_out = jnp.dot(
        part_cols,
        lax.all_gather(w_out, "rep", axis=0, tiled=True),
        preferred_element_type=jnp.float32,
    )
    part_cols = attn
    weight_grad = lax.psum_scatter(
        lax.dot_general(
            part_cols, grad_out, (((0,), (0,)), ((), ())), preferred_element_type=jnp.float32
        ),
        ("seq", "rep"),
        scatter_dimension=0,
        tiled=True,
    )
    return (
        layer_out.astype(jnp.bfloat16)[None],
        query_grad.astype(jnp.bfloat16)[None],
        own[0].reshape(tok_rows, width).astype(jnp.bfloat16)[None],
        own[1].reshape(tok_rows, width).astype(jnp.bfloat16)[None],
        weight_grad,
    )


def solution(mesh):
    return jax.shard_map(
        per_device,
        mesh=mesh,
        in_specs=(
            P("rep", "seq", None),
            P("rep", "seq", None),
            P("rep", "seq", None),
            P("rep", None),
            P("rep", "seq", None),
            P("rep", "seq", None),
            P("rep", None),
        ),
        out_specs=(
            P("rep", "seq", None),
            P("rep", "seq", None),
            P("rep", "seq", None),
            P("rep", "seq", None),
            P(("seq", "rep"), None),
        ),
        check_vma=False,
    )
```

profile of v0, /device:TPU:8, one launch (start us, length us, event | category | flops | bytes accessed | tf_op | source)
XLA Modules:
  0.0 1487.2 jit_solution(12116423025747049156)
XLA Ops:
  8.1 1.6 fusion.77
  13.5 1.0 constant_dynamic-update-slice_fusion.1
  14.5 1.0 constant_dynamic-update-slice_fusion
  15.5 1.2 fusion.76
  16.8 3.0 collective-permute-start.2
  19.8 1.9 collective-permute-start.3
  21.7 3.3 collective-permute-start.4
  25.0 4.5 collective-permute-start.5
  30.8 341.3 %all-reduce.10 = bf16[2,2,64,1024]{3,1,2,0:T(2,128)(2,1)S(1)} all-reduce(f32[2,2,64,1024]{3,1,2,0:T(2,128)S(1)} %convolution_bitcast_fusion.3), channel_id=1, replica_groups=mesh['seq'=64,'rep'=4] {'seq'}, use_global_device_ids=true, to_apply=%region_0.1 | all-reduce | flops 262144 | bytes 1572864 | tf_op jit(solution)/shard_map/psum | solution.py:154
  372.9 0.8 multiply_bitcast_fusion
  374.3 0.8 copy.240
  375.0 4.0 collective-permute-start.7
  379.0 1.0 constant_dynamic-update-slice_fusion.7
  380.4 1.0 constant_dynamic-update-slice_fusion.6
  381.4 3.5 collective-permute-start
  384.9 1.0 constant_dynamic-update-slice_fusion.5
  385.9 1.0 constant_dynamic-update-slice_fusion.4
  386.9 1.0 constant_dynamic-update-slice_fusion.3
  388.0 1.2 copy.176
  390.0 2.7 collective-permute-done
  392.8 1.1 pad_maximum_fusion.2
  396.7 1.4 fusion.8
  398.1 1.8 fusion.69
  402.7 4.5 fusion.27
  408.4 1.3 compare_convert_fusion
  409.7 1.3 compare_convert_fusion.2
  411.0 1.3 compare_convert_fusion.4
  412.3 310.8 %all-reduce.9.cloned.1.call-done = f32[1024,2048]{1,0:T(8,128)} async-done(((f32[1024,2048]{1,0:T(8,128)}), f32[1024,2048]{1,0:T(8,128)}) %all-reduce.9.cloned.1.call-update) | async-done | bytes 8388624
  723.1 1.5 constant_dynamic-slice_fusion.6
  724.6 3.8 fusion.16
  729.8 1.6 convolution_bitcast_fusion
  732.8 14.1 multiply_convert_fusion
  747.3 1.7 fusion.60
  749.0 1.8 fusion.63
  751.5 0.9 copy.194
  752.4 1.4 stack.31
  753.8 2.9 constant_dynamic-update-slice_fusion.9
  756.7 2.1 copy.197
  758.8 1.5 stack.32
  760.3 1.3 constant_dynamic-update-slice_fusion.8
  761.6 2.1 fusion.71
  764.4 1.1 slice_bitcast_fusion.4
  765.6 2.7 collective-permute-start.8
  768.3 1.0 collective-permute-start.9
  769.2 3.1 copy.204
  772.3 3.0 copy.205
  775.3 3.6 fusion.22
  778.9 2.1 collective-permute-start.15
  781.0 1.5 collective-permute-start.14
  782.5 4.7 collective-permute-start.13
  787.2 1.0 copy.209
  788.4 1.1 pad_maximum_fusion.3
  789.5 1.8 copy.210
  791.4 3.9 fusion.5
  796.7 5.1 collective-permute-start.10
  802.2 1.1 slice.249
  803.4 0.8 convert_element_type.104
  804.2 1.9 fusion.26
  806.1 2.1 copy.201
  808.3 1.7 copy_add_fusion
  810.0 3.8 scatter-add.9
  813.9 19.5 %collective-permute-done.12 = f32[2,64,1024]{2,1,0:T(8,128)} collective-permute-done((f32[2,64,1024]{2,1,0:T(8,128)}, f32[2,64,1024]{2,1,0:T(8,128)}, u32[]{:S(2)}, u32[]{:S(2)}) %collective-permute-start.12) | collective-permute-done | bytes 524320 | tf_op jit(solution)/shard_map/ppermute | solution.py:39
  833.4 638.5 %all-reduce.7.cloned.1.call-done = f32[2,2,64,1024]{3,1,2,0:T(2,128)} async-done(((f32[2,2,64,1024]{3,1,2,0:T(2,128)}), f32[2,2,64,1024]{3,1,2,0:T(2,128)}) %all-reduce.7.cloned.1.call-update) | async-done | bytes 1048592 | tf_op jit(solution)/shard_map/psum | solution.py:167
  1471.9 5.7 add_convert_fusion
  (133 shorter events, 19.2 us)
Async XLA Ops:
  8.0 394.7 %copy-start = (bf16[1,128,2048]{2,1,0:T(8,128)(2,1)S(1)}, bf16[1,128,2048]{2,1,0:T(8,128)(2,1)}, u32[]{:S(2)}) copy-start(bf16[1,128,2048]{2,1,0:T(8,128)(2,1)} %param.15) | copy-start | bytes 1572868
  8.0 715.1 %all-reduce.9.cloned.1.call-start = ((), (), s32[]{:S(2)}) async-start(), calls=%async_computation.2 | async-start | bytes 16777216
  15.5 14.4 copy-start.25
  15.5 14.5 copy-start.27
  16.8 358.3 %collective-permute-start.2 = (bf16[2,64,1024]{2,1,0:T(8,128)(2,1)}, bf16[2,64,1024]{2,1,0:T(8,128)(2,1)}, u32[]{:S(2)}, u32[]{:S(2)}) collective-permute-start(bf16[2,64,1024]{2,1,0:T(8,128)(2,1)} %get-tuple-element.57), channel_id=1, source_target_pairs={{0,4},{4,0},{8,12},{12,8},{16,20},{20,16},{24,28},{28,24},{32,36},... | collective-permute-start | bytes 786440 | tf_op jit(solution)/shard_map/ppermute | solution.py:39
  19.8 360.2 %collective-permute-start.3 = (bf16[2,64,1024]{2,1,0:T(8,128)(2,1)}, bf16[2,64,1024]{2,1,0:T(8,128)(2,1)}, u32[]{:S(2)}, u32[]{:S(2)}) collective-permute-start(bf16[2,64,1024]{2,1,0:T(8,128)(2,1)} %get-tuple-element.56), channel_id=1, source_target_pairs={{0,8},{8,0},{4,12},{12,4},{16,24},{24,16},{20,28},{28,20},{32,40},... | collective-permute-start | bytes 786440 | tf_op jit(solution)/shard_map/ppermute | solution.py:39
  21.7 359.7 %collective-permute-start.4 = (bf16[2,64,1024]{2,1,0:T(8,128)(2,1)}, bf16[2,64,1024]{2,1,0:T(8,128)(2,1)}, u32[]{:S(2)}, u32[]{:S(2)}) collective-permute-start(bf16[2,64,1024]{2,1,0:T(8,128)(2,1)} %get-tuple-element.55), channel_id=1, source_target_pairs={{0,16},{16,0},{4,20},{20,4},{8,24},{24,8},{12,28},{28,12},{32,48},... | collective-permute-start | bytes 786440 | tf_op jit(solution)/shard_map/ppermute | solution.py:39
  25.0 360.9 %collective-permute-start.5 = (bf16[2,64,1024]{2,1,0:T(8,128)(2,1)}, bf16[2,64,1024]{2,1,0:T(8,128)(2,1)}, u32[]{:S(2)}, u32[]{:S(2)}) collective-permute-start(bf16[2,64,1024]{2,1,0:T(8,128)(2,1)} %get-tuple-element.54), channel_id=1, source_target_pairs={{0,32},{32,0},{4,36},{36,4},{8,40},{40,8},{12,44},{44,12},{16,48},... | collective-permute-start | bytes 786440 | tf_op jit(solution)/shard_map/ppermute | solution.py:39
  29.5 357.4 %collective-permute-start.6 = (bf16[2,64,1024]{2,1,0:T(8,128)(2,1)}, bf16[2,64,1024]{2,1,0:T(8,128)(2,1)}, u32[]{:S(2)}, u32[]{:S(2)}) collective-permute-start(bf16[2,64,1024]{2,1,0:T(8,128)(2,1)} %get-tuple-element.53), channel_id=1, source_target_pairs={{0,64},{64,0},{4,68},{68,4},{8,72},{72,8},{12,76},{76,12},{16,80},... | collective-permute-start | bytes 786440 | tf_op jit(solution)/shard_map/ppermute | solution.py:39
  372.5 1.3 copy-start.26
  372.6 1.6 copy-start.19
  372.9 2.1 copy-start.24
  375.0 12.8 collective-permute-start.7
  380.0 10.0 collective-permute-start.1
  381.4 11.4 collective-permute-start
  389.6 4.2 copy-start.15
  394.9 6.4 copy-start.4
  395.6 1.0 copy-start.9
  398.1 1.9 copy-start.17
  399.9 1.4 copy-start.2
  399.9 1.1 copy-start.21
  402.0 0.7 copy-start.13
  407.2 317.4 %all-gather.2.cloned.1.call-start = ((), (), s32[]{:S(2)}) async-start(), calls=%async_computation | async-start | bytes 5242880 | tf_op jit(solution)/shard_map/all_gather | solution.py:175
  407.8 1064.1 %all-reduce.7.cloned.1.call-start = ((), (), s32[]{:S(2)}) async-start(), calls=%async_computation.1 | async-start | bytes 2097152 | tf_op jit(solution)/shard_map/psum | solution.py:167
  724.6 3.9 copy-start.5
  728.4 1.4 copy-start.3
  729.8 1.6 copy-start.22
  729.8 1.9 copy-start.18
  731.7 1.0 copy-start.10
  746.9 4.3 copy-start.11
  753.8 2.9 copy-start.8
  765.6 30.9 %collective-permute-start.8 = (f32[2,64,1024]{2,1,0:T(8,128)}, f32[2,64,1024]{2,1,0:T(8,128)}, u32[]{:S(2)}, u32[]{:S(2)}) collective-permute-start(f32[2,64,1024]{2,1,0:T(8,128)} %get-tuple-element.41), channel_id=1, source_target_pairs={{0,252},{4,0},{8,4},{12,8},{16,12},{20,16},{24,20},{28,24},{32,28}... | collective-permute-start | bytes 1572872 | tf_op jit(solution)/shard_map/ppermute | solution.py:15
  768.3 28.3 %collective-permute-start.9 = (f32[2,64,1024]{2,1,0:T(8,128)}, f32[2,64,1024]{2,1,0:T(8,128)}, u32[]{:S(2)}, u32[]{:S(2)}) collective-permute-start(f32[2,64,1024]{2,1,0:T(8,128)} %get-tuple-element.40), channel_id=1, source_target_pairs={{0,4},{4,8},{8,12},{12,16},{16,20},{20,24},{24,28},{28,32},{32,36}... | collective-permute-start | bytes 1572872 | tf_op jit(solution)/shard_map/ppermute | solution.py:15
  778.9 17.8 %collective-permute-start.15 = (f32[2,64,1024]{2,1,0:T(8,128)}, f32[2,64,1024]{2,1,0:T(8,128)}, u32[]{:S(2)}, u32[]{:S(2)}) collective-permute-start(f32[2,64,1024]{2,1,0:T(8,128)} %get-tuple-element.35), channel_id=1, source_target_pairs={{0,128},{128,0},{4,132},{132,4},{8,136},{136,8},{12,140},{140,12},... | collective-permute-start | bytes 1572872 | tf_op jit(solution)/shard_map/ppermute | solution.py:39
  781.0 32.8 %collective-permute-start.14 = (f32[2,64,1024]{2,1,0:T(8,128)}, f32[2,64,1024]{2,1,0:T(8,128)}, u32[]{:S(2)}, u32[]{:S(2)}) collective-permute-start(f32[2,64,1024]{2,1,0:T(8,128)} %get-tuple-element.36), channel_id=1, source_target_pairs={{0,64},{64,0},{4,68},{68,4},{8,72},{72,8},{12,76},{76,12},{16,80},... | collective-permute-start | bytes 1572872 | tf_op jit(solution)/shard_map/ppermute | solution.py:39
  782.5 31.4 %collective-permute-start.13 = (f32[2,64,1024]{2,1,0:T(8,128)}, f32[2,64,1024]{2,1,0:T(8,128)}, u32[]{:S(2)}, u32[]{:S(2)}) collective-permute-start(f32[2,64,1024]{2,1,0:T(8,128)} %get-tuple-element.34), channel_id=1, source_target_pairs={{0,32},{32,0},{4,36},{36,4},{8,40},{40,8},{12,44},{44,12},{16,48},... | collective-permute-start | bytes 1572872 | tf_op jit(solution)/shard_map/ppermute | solution.py:39
  789.5 1.8 copy-start.14
  791.3 3.9 copy-start.12
  791.3 3.9 copy-start.16
  795.2 0.9 copy-start.20
  795.2 1.5 copy-start.23
  795.2 6.5 copy-start.6
  796.4 36.9 %collective-permute-start.12 = (f32[2,64,1024]{2,1,0:T(8,128)}, f32[2,64,1024]{2,1,0:T(8,128)}, u32[]{:S(2)}, u32[]{:S(2)}) collective-permute-start(f32[2,64,1024]{2,1,0:T(8,128)} %get-tuple-element.33), channel_id=1, source_target_pairs={{0,16},{16,0},{4,20},{20,4},{8,24},{24,8},{12,28},{28,12},{32,48},... | collective-permute-start | bytes 1572872 | tf_op jit(solution)/shard_map/ppermute | solution.py:39
  796.6 36.8 %collective-permute-start.11 = (f32[2,64,1024]{2,1,0:T(8,128)}, f32[2,64,1024]{2,1,0:T(8,128)}, u32[]{:S(2)}, u32[]{:S(2)}) collective-permute-start(f32[2,64,1024]{2,1,0:T(8,128)} %get-tuple-element.32), channel_id=1, source_target_pairs={{0,8},{8,0},{4,12},{12,4},{16,24},{24,16},{20,28},{28,20},{32,40},... | collective-permute-start | bytes 1572872 | tf_op jit(solution)/shard_map/ppermute | solution.py:39
  796.7 36.7 %collective-permute-start.10 = (f32[2,64,1024]{2,1,0:T(8,128)S(1)}, f32[2,64,1024]{2,1,0:T(8,128)}, u32[]{:S(2)}, u32[]{:S(2)}) collective-permute-start(f32[2,64,1024]{2,1,0:T(8,128)S(1)} %copy-done.23), channel_id=1, source_target_pairs={{0,4},{4,0},{8,12},{12,8},{16,20},{20,16},{24,28},{28,24},{32,36},... | collective-permute-start | bytes 1572872 | tf_op jit(solution)/shard_map/ppermute | solution.py:39
  806.1 2.1 copy-start.7
  1471.9 7.6 copy-start.1
Sparse Core Ops, SparseCore 0:
  407.3 315.7 all-reduce.8
Sparse Core Ops, SparseCore 1:
  409.5 68.2 all-gather.1
  791.4 680.4 all-reduce.6
where the time goes:
time: 1510 us; the launch traced here: 1490 us
  waiting for transfers between devices  972 us (64%)
  blocking collectives  341 us (23%)
  local copies, waits for them, and re-layouts  52.1 us (3%)
  starting transfers between devices  38.9 us (3%)
  other arithmetic  32.3 us (2%)
  matrix products  30 us (2%)
  between operations  20.4 us (1%)
    psum x1, waiting for transfers between devices, per_device(): glob_total = lax.psum(dglob, 'seq').reshape(2, GLOB, BLK, width)  639 us
    psum x1, blocking collectives, per_device(): lax.psum(picked, 'seq').astype(jnp.bfloat16).reshape(2, GLOB * BLK, width)  341 us
    unnamed x4, waiting for transfers between devices  311 us
    ppermute x12, starting transfers between devices, swapped(): return lax.ppermute(block, axis, route)  30.6 us
  transfers between devices with their start and end apart: 19, of which 4 were waited for; matrix products, arithmetic and copies ran while one was open for 3% of the time, Pallas kernels for 0%

commit v1 on v0

--- a/solution.py
+++ b/solution.py
@@ -112,8 +112,51 @@
     return (attn, query_grad, dpad, dglob, drand)
 
 
-def edge_send(edge_block, offset):
-    return shifted(edge_block, "seq", offset)
+def stretch_id(y, z, x):
+    return y * 16 + z * 2 + x
+
+
+Z_GROUPS = [[stretch_id(y, z, x) for z in range(8)] for y in range(4) for x in range(2)]
+YX_GROUPS = [[stretch_id(y, z, x) for y in range(4) for x in range(2)] for z in range(8)]
+
+
+def trade(value, groups):
+    return lax.all_to_all(value, "seq", 0, 0, axis_index_groups=groups, tiled=True)
+
+
+def summed(value):
+    return jnp.sum(value.astype(jnp.float32), axis=0)
+
+
+def spread_global(picked):
+    chunks = picked.reshape(8, 32, 1024)
+    mine = summed(trade(chunks, Z_GROUPS)).astype(jnp.bfloat16)
+    mine = summed(trade(jnp.broadcast_to(mine, (8, 32, 1024)), YX_GROUPS)).astype(jnp.bfloat16)
+    return trade(jnp.broadcast_to(mine, (8, 32, 1024)), Z_GROUPS).reshape(2, GLOB * BLK, 1024)
+
+
+def reduce_global(dglob, weight_part, owner, my_index):
+    slots = jnp.arange(8, dtype=jnp.int32)
+    owner_z = (owner // 2) % 8
+    owner_m = (owner // 16) * 2 + owner % 2
+    my_m = (my_index // 16) * 2 + my_index % 2
+    which = (my_m // 2) % 2
+    chunks = dglob.reshape(8, 32, 1024).astype(jnp.bfloat16)
+    mine = summed(trade(chunks, YX_GROUPS)).astype(jnp.bfloat16)
+    routed = jnp.where((slots == owner_z[which])[:, None, None], mine[None], jnp.bfloat16(0))
+    mine = summed(trade(routed, Z_GROUPS)).astype(jnp.bfloat16)
+    routed = jnp.where((slots == owner_m[which])[:, None, None], mine[None], jnp.bfloat16(0))
+    weight_rows = weight_part.astype(jnp.bfloat16).reshape(8, 8, 1024)
+    both = trade(jnp.concatenate([routed, weight_rows], axis=1), YX_GROUPS)
+    total = both[:, :32].astype(jnp.float32).reshape(2, GLOB, BLK, 1024)
+    return total, summed(both[:, 32:]).reshape(4, 2048)
+
+
+def feature_order():
+    new = jnp.arange(1024, dtype=jnp.int32)
+    r, z, y, x, j = new // 256, (new // 32) % 8, (new // 8) % 4, (new // 4) % 2, new % 4
+    old = y * 256 + z * 32 + x * 16 + r * 4 + j
+    return (jnp.arange(1024, dtype=jnp.int32)[:, None] == old[None, :]).astype(jnp.bfloat16)
 
 
 def per_device(queries, keys, values, w_out, d_out, rand_slot, global_ids):
@@ -128,11 +171,10 @@
     my_index = lax.axis_index("seq")
     nbits = lax.axis_size("seq").bit_length() - 1
     block_ids = jnp.arange(nblock, dtype=jnp.int32)
+    all_grads = lax.all_gather(grad_out, "rep", axis=0, tiled=False)
+    all_w = lax.all_gather(w_out, "rep", axis=0, tiled=True)
     d_attn = lax.dot_general(
-        grad_out,
-        lax.all_gather(w_out, "rep", axis=0, tiled=True),
-        (((1,), (1,)), ((), ())),
-        preferred_element_type=jnp.float32,
+        grad_out, all_w, (((1,), (1,)), ((), ())), preferred_element_type=jnp.float32
     ).astype(jnp.bfloat16)
     padded = padded_2(key_vals, (("seq", 1),), BLK)
     received = []
@@ -142,48 +184,52 @@
     partner_kv = jnp.concatenate(received, axis=1)
     owner = gids // nblock
     position = gids % nblock
-    pick_hot = ((position[:, None] == block_ids[None, :]) & (owner[:, None] == my_index)).astype(
-        jnp.bfloat16
-    )
-    picked = jnp.einsum(
-        "gn,cnbx->cgbx",
-        pick_hot,
-        key_vals.reshape(2, nblock, BLK, width),
-        preferred_element_type=jnp.float32,
-    )
-    global_kv = lax.psum(picked, "seq").astype(jnp.bfloat16).reshape(2, GLOB * BLK, width)
+    place = (position[:, None] == block_ids[None, :]) & (owner[:, None] == my_index)
+    blocks = key_vals.reshape(2, nblock, BLK, width)
+    picked = jnp.stack(
+        [
+            jnp.where(
+                owner[g] == my_index,
+                jnp.where(position[g] == 0, blocks[:, 0], blocks[:, 1]),
+                jnp.bfloat16(0),
+            )
+            for g in range(GLOB)
+        ],
+        axis=1,
+    )
+    global_kv = spread_global(picked)
     attn, query_grad, dpad, dglob, drand = local_attention(
         q_dev, padded, global_kv, partner_kv, my_slots, d_attn
     )
+    ordered = jnp.dot(attn, feature_order(), preferred_element_type=jnp.float32)
+    ordered = ordered.astype(jnp.bfloat16).reshape(tok_rows, 4, 256).transpose(1, 0, 2)
+    columns = lax.all_to_all(ordered, "rep", 0, 0, tiled=True)
+    weight_part = lax.psum_scatter(
+        lax.dot_general(
+            columns.reshape(4 * tok_rows, 256),
+            all_grads.reshape(4 * tok_rows, 2048),
+            (((0,), (0,)), ((), ())),
+            preferred_element_type=jnp.float32,
+        ),
+        "seq",
+        scatter_dimension=0,
+        axis_index_groups=Z_GROUPS,
+        tiled=True,
+    )
     own = dpad[:, 1 : nblock + 1]
-    from_right = edge_send(dpad[:, 0], -1)
-    from_left = edge_send(dpad[:, nblock + 1], 1)
+    from_right = shifted(dpad[:, 0].astype(jnp.bfloat16), "seq", -1).astype(jnp.float32)
+    from_left = shifted(dpad[:, nblock + 1].astype(jnp.bfloat16), "seq", 1).astype(jnp.float32)
     own = own.at[:, nblock - 1].add(from_right)
     own = own.at[:, 0].add(from_left)
     for bit_num in range(nbits):
-        sent_back = swapped(drand[:, bit_num * BLK : (bit_num + 1) * BLK], "seq", bit_num)
+        back = drand[:, bit_num * BLK : (bit_num + 1) * BLK].astype(jnp.bfloat16)
+        sent_back = swapped(back, "seq", bit_num).astype(jnp.float32)
         slot_mask = (block_ids == my_slots[bit_num]).astype(jnp.float32)
         own = own + slot_mask[None, :, None, None] * sent_back[:, None]
-    glob_total = lax.psum(dglob, "seq").reshape(2, GLOB, BLK, width)
-    place_hot = ((position[:, None] == block_ids[None, :]) & (owner[:, None] == my_index)).astype(
-        jnp.float32
-    )
-    own = own + jnp.einsum("gn,cgbx->cnbx", place_hot, glob_total, precision=lax.Precision.HIGHEST)
-    part_cols = attn
-    layer_out = jnp.dot(
-        part_cols,
-        lax.all_gather(w_out, "rep", axis=0, tiled=True),
-        preferred_element_type=jnp.float32,
-    )
-    part_cols = attn
-    weight_grad = lax.psum_scatter(
-        lax.dot_general(
-            part_cols, grad_out, (((0,), (0,)), ((), ())), preferred_element_type=jnp.float32
-        ),
-        ("seq", "rep"),
-        scatter_dimension=0,
-        tiled=True,
-    )
+    glob_total, weight_grad = reduce_global(dglob, weight_part, owner, my_index)
+    for g in range(GLOB):
+        own = own + place[g].astype(jnp.float32)[None, :, None, None] * glob_total[:, g][:, None]
+    layer_out = jnp.dot(attn, all_w, preferred_element_type=jnp.float32)
     return (
         layer_out.astype(jnp.bfloat16)[None],
         query_grad.astype(jnp.bfloat16)[None],

time: 1510 us -> 275 us (0.18); the launches traced: 1490 us -> 270 us
  waiting for transfers between devices: 972 us -> 33.6 us
  blocking collectives: 341 us -> 0 us
  starting transfers between devices: 38.9 us -> 81.3 us
  other arithmetic: 32.3 us -> 51.2 us
    psum x1 -> x0, waiting for transfers between devices: 639 us -> none  [per_device(): glob_total = lax.psum(dglob, 'seq').reshape(2, GLOB, BLK, width)]
    psum x1 -> x0, blocking collectives: 341 us -> none  [per_device(): lax.psum(picked, 'seq').astype(jnp.bfloat16).reshape(2, GLOB * BLK, width)]
    unnamed x4 -> x3, waiting for transfers between devices: 311 us -> 0.71 us
    all_to_all x0 -> x7, starting transfers between devices: none -> 40 us  [the longest x6 36 us: trade(): lax.all_to_all(value, 'seq', 0, 0, axis_index_groups=groups, tiled=True)]
    all_to_all x0 -> x7, waiting for transfers between devices: none -> 23.3 us  [the longest x6 18 us: trade(): lax.all_to_all(value, 'seq', 0, 0, axis_index_groups=groups, tiled=True)]
    ppermute x12, waiting for transfers between devices: 19.5 us -> 0.03 us  [swapped(): return lax.ppermute(block, axis, route)]
  transfers between devices with their start and end apart: 19 -> 26, of which waited for: 4 -> 5; matrix products, arithmetic and copies ran while one was open for 3% -> 46% of each run, Pallas kernels for 0% -> 0%
where the time goes in v1:
time: 275 us; the launch traced here: 270 us
  starting transfers between devices  81.3 us (30%)
  local copies, waits for them, and re-layouts  57.8 us (21%)
  other arithmetic  51.2 us (19%)
  waiting for transfers between devices  33.6 us (12%)
  matrix products  24.6 us (9%)
  between operations  21.2 us (8%)
    all_to_all x6, starting transfers between devices, trade(): lax.all_to_all(value, 'seq', 0, 0, axis_index_groups=groups, tiled=True)  36 us
    ppermute x12, starting transfers between devices, swapped(): return lax.ppermute(block, axis, route)  33.9 us
    all_to_all x6, waiting for transfers between devices, trade(): lax.all_to_all(value, 'seq', 0, 0, axis_index_groups=groups, tiled=True)  18 us
    unnamed x85, local copies, waits for them, and re-layouts  15.8 us
    sub x1, other arithmetic, local_attention(): dscore = (probs * (dprob - delta) * scale).astype(jnp.bfloat16)  14.1 us
    dot_general x14, matrix products, mult(): return jnp.einsum(form, left, right, preferred_element_type=jnp.float32)  12.4 us
    ppermute x1, waiting for transfers between devices, padded_2(): lax.ppermute(lax.slice_in_dim(block, 0, width, axis=dim), axis, backward)  9.55 us
    convert_element_type x6, other arithmetic, per_device(): sent_back = swapped(back, 'seq', bit_num).astype(jnp.float32)  7.59 us
  transfers between devices with their start and end apart: 26, of which 5 were waited for; matrix products, arithmetic and copies ran while one was open for 46% of the time, Pallas kernels for 0%

profile of v1, /device:TPU:8, one launch (start us, length us, event | category | flops | bytes accessed | tf_op | source)
XLA Modules:
  0.0 269.6 jit_solution(3688722700730828127)
XLA Ops:
  7.9 1.5 fusion.107
  16.4 3.0 %collective-permute-start.2 = (bf16[2,64,1024]{2,1,0:T(8,128)(2,1)}, bf16[2,64,1024]{2,1,0:T(8,128)(2,1)}, u32[]{:S(2)}, u32[]{:S(2)}) collective-permute-start(bf16[2,64,1024]{2,1,0:T(8,128)(2,1)} %get-tuple-element.63), channel_id=1, source_target_pairs={{0,4},{4,0},{8,12},{12,8},{16,20},{20,16},{24,28},{28,24},{32,36},... | collective-permute-start | bytes 786440 | tf_op jit(solution)/shard_map/ppermute | solution.py:39
  19.5 1.9 collective-permute-start.3
  21.4 3.3 %collective-permute-start.4 = (bf16[2,64,1024]{2,1,0:T(8,128)(2,1)}, bf16[2,64,1024]{2,1,0:T(8,128)(2,1)}, u32[]{:S(2)}, u32[]{:S(2)}) collective-permute-start(bf16[2,64,1024]{2,1,0:T(8,128)(2,1)} %get-tuple-element.61), channel_id=1, source_target_pairs={{0,16},{16,0},{4,20},{20,4},{8,24},{24,8},{12,28},{28,12},{32,48},... | collective-permute-start | bytes 786440 | tf_op jit(solution)/shard_map/ppermute | solution.py:39
  29.5 5.8 %all-to-all-start = ((bf16[8,32,1024]{2,1,0:T(8,128)(2,1)}), bf16[8,32,1024]{2,1,0:T(8,128)(2,1)}, u32[]{:S(2)}, u32[]{:S(2)}) async-start(bf16[8,32,1024]{2,1,0:T(8,128)(2,1)} %bitcast.9), calls=%async_computation | async-start | bytes 1048576 | tf_op jit(solution)/shard_map/all_to_all | solution.py:124
  35.3 3.0 %collective-permute-start.1 = (bf16[2,64,1024]{2,1,0:T(8,128)(2,1)S(1)}, bf16[2,64,1024]{2,1,0:T(8,128)(2,1)S(1)}, u32[]{:S(2)}, u32[]{:S(2)}) collective-permute-start(bf16[2,64,1024]{2,1,0:T(8,128)(2,1)S(1)} %get-tuple-element.64), channel_id=1, source_target_pairs={{4,0},{8,4},{12,8},{16,12},{20,16},{24,20},{28,24},{32,28},{36,32}... | collective-permute-start | bytes 786440 | tf_op jit(solution)/shard_map/ppermute | solution.py:27
  39.0 1.3 compare_convert_fusion
  40.3 1.3 compare_convert_fusion.2
  41.6 1.9 compare_convert_fusion.4
  44.1 1.2 iota_compare_fusion.6
  46.9 9.6 %collective-permute-done.1 = bf16[2,64,1024]{2,1,0:T(8,128)(2,1)S(1)} collective-permute-done((bf16[2,64,1024]{2,1,0:T(8,128)(2,1)S(1)}, bf16[2,64,1024]{2,1,0:T(8,128)(2,1)S(1)}, u32[]{:S(2)}, u32[]{:S(2)}) %collective-permute-start.1) | collective-permute-done | bytes 262176 | tf_op jit(solution)/shard_map/ppermute | solution.py:27
  56.5 5.7 %collective-permute-start.5 = (bf16[2,64,1024]{2,1,0:T(8,128)(2,1)}, bf16[2,64,1024]{2,1,0:T(8,128)(2,1)S(1)}, u32[]{:S(2)}, u32[]{:S(2)}) collective-permute-start(bf16[2,64,1024]{2,1,0:T(8,128)(2,1)} %get-tuple-element.60), channel_id=1, source_target_pairs={{0,32},{32,0},{4,36},{36,4},{8,40},{40,8},{12,44},{44,12},{16,48},... | collective-permute-start | bytes 786440 | tf_op jit(solution)/shard_map/ppermute | solution.py:39
  64.3 2.7 collective-permute-start.7
  67.0 1.7 constant_dynamic-update-slice_fusion.7
  68.6 1.7 constant_dynamic-update-slice_fusion.6
  70.3 1.7 constant_dynamic-update-slice_fusion.5
  74.8 5.9 %all-to-all-start.1 = ((bf16[8,32,1024]{2,1,0:T(8,128)(2,1)}), bf16[8,32,1024]{2,1,0:T(8,128)(2,1)}, u32[]{:S(2)}, u32[]{:S(2)}) async-start(bf16[8,32,1024]{2,1,0:T(8,128)(2,1)} %broadcast_in_dim.96), calls=%async_computation.1 | async-start | bytes 1048576 | tf_op jit(solution)/shard_map/all_to_all | solution.py:124
  80.7 1.7 constant_dynamic-update-slice_fusion.3
  83.1 2.4 fusion.100
  85.5 9.8 %all-to-all-done.1 = bf16[8,32,1024]{2,1,0:T(8,128)(2,1)} async-done(((bf16[8,32,1024]{2,1,0:T(8,128)(2,1)}), bf16[8,32,1024]{2,1,0:T(8,128)(2,1)}, u32[]{:S(2)}, u32[]{:S(2)}) %all-to-all-start.1) | async-done | bytes 524320 | tf_op jit(solution)/shard_map/all_to_all | solution.py:124
  97.2 5.7 %all-to-all-start.2 = ((bf16[8,32,1024]{2,1,0:T(8,128)(2,1)}), bf16[8,32,1024]{2,1,0:T(8,128)(2,1)}, u32[]{:S(2)}, u32[]{:S(2)}) async-start(bf16[8,32,1024]{2,1,0:T(8,128)(2,1)} %broadcast_in_dim.97), calls=%async_computation.2 | async-start | bytes 1048576 | tf_op jit(solution)/shard_map/all_to_all | solution.py:124
  102.9 1.2 copy_dynamic-update-slice_fusion
  104.2 2.9 %copy.333 = bf16[1,384,1024]{1,2,0:T(8,128)(2,1)} copy(bf16[1,384,1024]{2,1,0:T(8,128)(2,1)} %get-tuple-element.45) | data formatting | bytes 1572864 | tf_op jit(solution)/shard_map/slice | solution.py:77
  107.0 1.2 copy.323
  110.0 8.0 %all-to-all-done.2 = bf16[8,32,1024]{2,1,0:T(8,128)(2,1)} async-done(((bf16[8,32,1024]{2,1,0:T(8,128)(2,1)}), bf16[8,32,1024]{2,1,0:T(8,128)(2,1)}, u32[]{:S(2)}, u32[]{:S(2)}) %all-to-all-start.2) | async-done | bytes 524320 | tf_op jit(solution)/shard_map/all_to_all | solution.py:124
  119.9 1.4 fusion.10
  121.3 3.0 %fusion.95 = bf16[2,8,64,704]{3,2,0,1:T(8,128)(2,1)S(1)} fusion(f32[2,8,64]{2,0,1:T(2,128)S(1)} %fusion.10, f32[2,8,64]{2,0,1:T(2,128)S(1)} %copy.329, f32[2,8,64,384]{3,2,0,1:T(8,128)S(1)} %get-tuple-element.34, f32[2,8,64,128]{3,2,0,1:T(8,128)S(1)} %multiply_bitcast_fusion, f32[2,8,64,192]{3,2,1,0:T(8,128)} %copy-done.1), kind=kLoop, calls=%fused_computation.210 | loop fusion | flops 3604480 | bytes 4333568 | tf_op jit(solution)/shard_map/convert_element_type | solution.py:70
  127.0 1.6 fusion.20
  128.7 1.8 copy.386
  130.4 4.0 %all-to-all-start.5 = ((bf16[4,128,256]{1,2,0:T(8,128)(2,1)}), bf16[4,128,256]{1,2,0:T(8,128)(2,1)}, u32[]{:S(2)}, u32[]{:S(2)}) async-start(bf16[4,128,256]{1,2,0:T(8,128)(2,1)} %bitcast.271), calls=%async_computation.5 | async-start | bytes 524288 | tf_op jit(solution)/shard_map/all_to_all | solution.py:206
  135.3 5.2 %all-to-all-done.5 = bf16[4,128,256]{1,2,0:T(8,128)(2,1)} async-done(((bf16[4,128,256]{1,2,0:T(8,128)(2,1)}), bf16[4,128,256]{1,2,0:T(8,128)(2,1)}, u32[]{:S(2)}, u32[]{:S(2)}) %all-to-all-start.5) | async-done | bytes 262176 | tf_op jit(solution)/shard_map/all_to_all | solution.py:206
  140.6 3.8 %convolution_bitcast_fusion = f32[256,2048]{1,0:T(8,128)} fusion(bf16[4,128,256]{1,2,0:T(8,128)(2,1)} %all-to-all-done.5, bf16[4,128,2048]{2,1,0:T(8,128)(2,1)} %all-gather.5.cloned.1.call-done), kind=kOutput, calls=%fused_computation.10 | convolution fusion | flops 536870912 | bytes 4456448 | tf_op jit(solution)/shard_map/dot_general | solution.py:208
  144.4 4.0 %fusion.21 = bf16[16,8,8,128]{3,1,2,0:T(8,128)(2,1)S(1)} fusion(bf16[1024,2048]{1,0:T(8,128)(2,1)} %all-gather.3.cloned.1.call-done, bf16[1,128,2048]{2,1,0:T(8,128)(2,1)} %param.15), kind=kOutput, calls=%fused_computation.41 | convolution fusion | flops 537001984 | bytes 4980736 | tf_op jit(solution)/shard_map/dot_general | solution.py:176
  151.1 14.1 %multiply_convert_fusion = bf16[2,8,64,704]{3,2,0,1:T(8,128)(2,1)S(1)} fusion(f32[2,8,64,384]{3,2,0,1:T(8,128)S(1)} %bitcast.268, f32[2,8,64,128]{3,2,0,1:T(8,128)S(1)} %bitcast.274, f32[2,8,64,192]{3,2,0,1:T(8,128)S(1)} %fusion.24, f32[2,8,64]{2,0,1:T(2,128)S(1)} %fusion.10, f32[2,8,64]{2,0,1:T(2,128)S(1)} %copy.329, ...), kind=kOutput, calls=%fused_computation.7 | output fusion | flops 12256959 | bytes 7217152 | tf_op jit(solution)/shard_map/sub | solution.py:89
  166.3 2.1 copy.351
  168.4 2.6 stack.40
  171.5 2.1 copy.354
  173.6 2.6 stack.41
  176.5 1.4 fusion.23
  179.4 6.4 %all-to-all-start.3 = ((bf16[8,32,1024]{2,1,0:T(8,128)(2,1)}), bf16[8,32,1024]{2,1,0:T(8,128)(2,1)}, u32[]{:S(2)}, u32[]{:S(2)}) async-start(bf16[8,32,1024]{2,1,0:T(8,128)(2,1)} %convert_element_type.192), calls=%async_computation.3 | async-start | bytes 1048576 | tf_op jit(solution)/shard_map/all_to_all | solution.py:124
  185.8 1.6 constant_dynamic-update-slice_fusion.9
  188.0 1.9 fusion.96
  190.0 1.5 fusion.89
  192.3 1.5 collective-permute-start.8
  193.8 2.0 collective-permute-start.9
  195.8 2.3 copy.384
  199.8 1.5 maximum_convert_fusion
  203.4 4.1 %all-to-all-start.4 = ((bf16[8,32,1024]{2,1,0:T(8,128)(2,1)}), bf16[8,32,1024]{2,1,0:T(8,128)(2,1)}, u32[]{:S(2)}, u32[]{:S(2)}) async-start(bf16[8,32,1024]{2,1,0:T(8,128)(2,1)} %broadcast_select_fusion), calls=%async_computation.4 | async-start | bytes 1048576 | tf_op jit(solution)/shard_map/all_to_all | solution.py:124
  207.6 1.2 fusion.99
  208.8 2.1 collective-permute-start.15
  210.8 1.5 collective-permute-start.14
  212.3 5.8 %collective-permute-start.13 = (bf16[2,64,1024]{2,1,0:T(8,128)(2,1)}, bf16[2,64,1024]{2,1,0:T(8,128)(2,1)}, u32[]{:S(2)}, u32[]{:S(2)}) collective-permute-start(bf16[2,64,1024]{2,1,0:T(8,128)(2,1)} %get-tuple-element.41), channel_id=1, source_target_pairs={{0,32},{32,0},{4,36},{36,4},{8,40},{40,8},{12,44},{44,12},{16,48},... | collective-permute-start | bytes 786440 | tf_op jit(solution)/shard_map/ppermute | solution.py:39
  219.2 2.5 convolution_bitcast_fusion.7
  221.7 1.5 fusion.6
  224.4 1.8 reduce_sum.80
  228.2 8.1 %all-to-all-start.6 = ((bf16[8,40,1024]{2,1,0:T(8,128)(2,1)}), bf16[8,40,1024]{2,1,0:T(8,128)(2,1)}, u32[]{:S(2)}, u32[]{:S(2)}) async-start(bf16[8,40,1024]{2,1,0:T(8,128)(2,1)} %pad_maximum_fusion.3), calls=%async_computation.7 | async-start | bytes 1310720 | tf_op jit(solution)/shard_map/all_to_all | solution.py:124
  236.3 3.1 %collective-permute-start.12 = (bf16[2,64,1024]{2,1,0:T(8,128)(2,1)}, bf16[2,64,1024]{2,1,0:T(8,128)(2,1)}, u32[]{:S(2)}, u32[]{:S(2)}) collective-permute-start(bf16[2,64,1024]{2,1,0:T(8,128)(2,1)} %get-tuple-element.42), channel_id=1, source_target_pairs={{0,16},{16,0},{4,20},{20,4},{8,24},{24,8},{12,28},{28,12},{32,48},... | collective-permute-start | bytes 786440 | tf_op jit(solution)/shard_map/ppermute | solution.py:39
  239.4 1.4 collective-permute-start.11
  240.8 3.0 %collective-permute-start.10 = (bf16[2,64,1024]{2,1,0:T(8,128)(2,1)S(1)}, bf16[2,64,1024]{2,1,0:T(8,128)(2,1)}, u32[]{:S(2)}, u32[]{:S(2)}) collective-permute-start(bf16[2,64,1024]{2,1,0:T(8,128)(2,1)S(1)} %copy-done.27), channel_id=1, source_target_pairs={{0,4},{4,0},{8,12},{12,8},{16,20},{20,16},{24,28},{28,24},{32,36},... | collective-permute-start | bytes 786440 | tf_op jit(solution)/shard_map/ppermute | solution.py:39
  243.7 1.6 fusion.19
  246.3 1.3 slice.309
  251.8 1.8 convert_element_type.181
  253.6 1.8 convert_element_type.179
  255.4 1.2 fusion.30
  (185 shorter events, 50.3 us)
Async XLA Ops:
  7.2 133.4 %all-gather.5.cloned.1.call-start = ((), (), s32[]{:S(2)}) async-start(), calls=%async_computation.9 | async-start | bytes 2621440 | tf_op jit(solution)/shard_map/all_gather | solution.py:174
  15.3 9.3 %copy-start.34 = (s32[1,2]{1,0:T(1,128)S(1)}, s32[1,2]{1,0:T(1,128)}, u32[]{:S(2)}) copy-start(s32[1,2]{1,0:T(1,128)} %param.17) | copy-start | bytes 28
  16.4 47.9 %collective-permute-start.2 = (bf16[2,64,1024]{2,1,0:T(8,128)(2,1)}, bf16[2,64,1024]{2,1,0:T(8,128)(2,1)}, u32[]{:S(2)}, u32[]{:S(2)}) collective-permute-start(bf16[2,64,1024]{2,1,0:T(8,128)(2,1)} %get-tuple-element.63), channel_id=1, source_target_pairs={{0,4},{4,0},{8,12},{12,8},{16,20},{20,16},{24,28},{28,24},{32,36},... | collective-permute-start | bytes 786440 | tf_op jit(solution)/shard_map/ppermute | solution.py:39
  19.5 49.2 %collective-permute-start.3 = (bf16[2,64,1024]{2,1,0:T(8,128)(2,1)}, bf16[2,64,1024]{2,1,0:T(8,128)(2,1)}, u32[]{:S(2)}, u32[]{:S(2)}) collective-permute-start(bf16[2,64,1024]{2,1,0:T(8,128)(2,1)} %get-tuple-element.62), channel_id=1, source_target_pairs={{0,8},{8,0},{4,12},{12,4},{16,24},{24,16},{20,28},{28,20},{32,40},... | collective-permute-start | bytes 786440 | tf_op jit(solution)/shard_map/ppermute | solution.py:39
  21.4 49.0 %collective-permute-start.4 = (bf16[2,64,1024]{2,1,0:T(8,128)(2,1)}, bf16[2,64,1024]{2,1,0:T(8,128)(2,1)}, u32[]{:S(2)}, u32[]{:S(2)}) collective-permute-start(bf16[2,64,1024]{2,1,0:T(8,128)(2,1)} %get-tuple-element.61), channel_id=1, source_target_pairs={{0,16},{16,0},{4,20},{20,4},{8,24},{24,8},{12,28},{28,12},{32,48},... | collective-permute-start | bytes 786440 | tf_op jit(solution)/shard_map/ppermute | solution.py:39
  28.6 14.9 %copy-start.29 = (s32[1,1,6]{2,1,0:T(1,128)S(1)}, s32[1,1,6]{2,1,0:T(1,128)}, u32[]{:S(2)}) copy-start(s32[1,1,6]{2,1,0:T(1,128)} %param.16) | copy-start | bytes 76
  28.6 18.0 %copy-start.28 = (bf16[1,128,1024]{2,1,0:T(8,128)(2,1)S(1)}, bf16[1,128,1024]{2,1,0:T(8,128)(2,1)}, u32[]{:S(2)}) copy-start(bf16[1,128,1024]{2,1,0:T(8,128)(2,1)} %param.11) | copy-start | bytes 786436
  29.5 43.3 %all-to-all-start = ((bf16[8,32,1024]{2,1,0:T(8,128)(2,1)}), bf16[8,32,1024]{2,1,0:T(8,128)(2,1)}, u32[]{:S(2)}, u32[]{:S(2)}) async-start(bf16[8,32,1024]{2,1,0:T(8,128)(2,1)} %bitcast.9), calls=%async_computation | async-start | bytes 1048576 | tf_op jit(solution)/shard_map/all_to_all | solution.py:124
  35.2 109.2 %all-gather.3.cloned.1.call-start = ((), (), s32[]{:S(2)}) async-start(), calls=%async_computation.8 | async-start | bytes 5242880 | tf_op jit(solution)/shard_map/all_gather | solution.py:175
  35.3 21.2 %collective-permute-start.1 = (bf16[2,64,1024]{2,1,0:T(8,128)(2,1)S(1)}, bf16[2,64,1024]{2,1,0:T(8,128)(2,1)S(1)}, u32[]{:S(2)}, u32[]{:S(2)}) collective-permute-start(bf16[2,64,1024]{2,1,0:T(8,128)(2,1)S(1)} %get-tuple-element.64), channel_id=1, source_target_pairs={{4,0},{8,4},{12,8},{16,12},{20,16},{24,20},{28,24},{32,28},{36,32}... | collective-permute-start | bytes 786440 | tf_op jit(solution)/shard_map/ppermute | solution.py:27
  38.3 23.9 %collective-permute-start = (bf16[2,64,1024]{2,1,0:T(8,128)(2,1)S(1)}, bf16[2,64,1024]{2,1,0:T(8,128)(2,1)S(1)}, u32[]{:S(2)}, u32[]{:S(2)}) collective-permute-start(bf16[2,64,1024]{2,1,0:T(8,128)(2,1)S(1)} %get-tuple-element.57), channel_id=1, source_target_pairs={{0,4},{4,8},{8,12},{12,16},{16,20},{20,24},{24,28},{28,32},{32,36}... | collective-permute-start | bytes 786440 | tf_op jit(solution)/shard_map/ppermute | solution.py:24
  46.7 62.2 %copy-start.17 = (bf16[2,64,8,128]{3,1,0,2:T(8,128)(2,1)}, bf16[2,64,8,128]{3,1,0,2:T(8,128)(2,1)S(1)}, u32[]{:S(2)}) copy-start(bf16[2,64,8,128]{3,1,0,2:T(8,128)(2,1)S(1)} %copy.322) | copy-start | bytes 786436
  56.5 15.6 %collective-permute-start.5 = (bf16[2,64,1024]{2,1,0:T(8,128)(2,1)}, bf16[2,64,1024]{2,1,0:T(8,128)(2,1)S(1)}, u32[]{:S(2)}, u32[]{:S(2)}) collective-permute-start(bf16[2,64,1024]{2,1,0:T(8,128)(2,1)} %get-tuple-element.60), channel_id=1, source_target_pairs={{0,32},{32,0},{4,36},{36,4},{8,40},{40,8},{12,44},{44,12},{16,48},... | collective-permute-start | bytes 786440 | tf_op jit(solution)/shard_map/ppermute | solution.py:39
  62.2 18.4 %collective-permute-start.6 = (bf16[2,64,1024]{2,1,0:T(8,128)(2,1)}, bf16[2,64,1024]{2,1,0:T(8,128)(2,1)}, u32[]{:S(2)}, u32[]{:S(2)}) collective-permute-start(bf16[2,64,1024]{2,1,0:T(8,128)(2,1)} %get-tuple-element.59), channel_id=1, source_target_pairs={{0,64},{64,0},{4,68},{68,4},{8,72},{72,8},{12,76},{76,12},{16,80},... | collective-permute-start | bytes 786440 | tf_op jit(solution)/shard_map/ppermute | solution.py:39
  64.3 18.0 %collective-permute-start.7 = (bf16[2,64,1024]{2,1,0:T(8,128)(2,1)S(1)}, bf16[2,64,1024]{2,1,0:T(8,128)(2,1)S(1)}, u32[]{:S(2)}, u32[]{:S(2)}) collective-permute-start(bf16[2,64,1024]{2,1,0:T(8,128)(2,1)S(1)} %get-tuple-element.58), channel_id=1, source_target_pairs={{0,128},{128,0},{4,132},{132,4},{8,136},{136,8},{12,140},{140,12},... | collective-permute-start | bytes 786440 | tf_op jit(solution)/shard_map/ppermute | solution.py:39
  74.8 20.5 %all-to-all-start.1 = ((bf16[8,32,1024]{2,1,0:T(8,128)(2,1)}), bf16[8,32,1024]{2,1,0:T(8,128)(2,1)}, u32[]{:S(2)}, u32[]{:S(2)}) async-start(bf16[8,32,1024]{2,1,0:T(8,128)(2,1)} %broadcast_in_dim.96), calls=%async_computation.1 | async-start | bytes 1048576 | tf_op jit(solution)/shard_map/all_to_all | solution.py:124
  97.2 20.8 %all-to-all-start.2 = ((bf16[8,32,1024]{2,1,0:T(8,128)(2,1)}), bf16[8,32,1024]{2,1,0:T(8,128)(2,1)}, u32[]{:S(2)}, u32[]{:S(2)}) async-start(bf16[8,32,1024]{2,1,0:T(8,128)(2,1)} %broadcast_in_dim.97), calls=%async_computation.2 | async-start | bytes 1048576 | tf_op jit(solution)/shard_map/all_to_all | solution.py:124
  104.2 4.1 %copy-start.5 = (bf16[2,2,192,8,128]{4,2,3,1,0:T(8,128)(2,1)}, bf16[2,2,192,8,128]{4,2,3,1,0:T(8,128)(2,1)S(1)}, u32[]{:S(2)}) copy-start(bf16[2,2,192,8,128]{4,2,3,1,0:T(8,128)(2,1)S(1)} %copy_dynamic-update-slice_fusion) | copy-start | bytes 4718596
  108.2 1.1 copy-start.14
  108.9 11.0 %copy-start.1 = (f32[2,8,64,192]{3,2,1,0:T(8,128)}, f32[2,8,64,192]{3,2,1,0:T(8,128)S(1)}, u32[]{:S(2)}) copy-start(f32[2,8,64,192]{3,2,1,0:T(8,128)S(1)} %get-tuple-element.82) | copy-start | bytes 2359300
  118.0 1.2 copy-start.18
  119.2 0.7 copy-start.19
  119.8 4.5 %copy-start.21 = (bf16[16,8,8,128]{3,2,1,0:T(8,128)(2,1)}, bf16[16,8,8,128]{3,2,1,0:T(8,128)(2,1)S(1)}, u32[]{:S(2)}) copy-start(bf16[16,8,8,128]{3,2,1,0:T(8,128)(2,1)S(1)} %copy.398) | copy-start | bytes 786436
  119.9 1.4 copy-start.10
  121.3 3.3 %copy-start.15 = (bf16[1,384,1024]{1,2,0:T(8,128)(2,1)S(1)}, bf16[1,384,1024]{1,2,0:T(8,128)(2,1)}, u32[]{:S(2)}) copy-start(bf16[1,384,1024]{1,2,0:T(8,128)(2,1)} %copy.333) | copy-start | bytes 2359300
  124.3 1.4 copy-start.6
  126.3 0.7 copy-start.25
  130.4 10.1 %all-to-all-start.5 = ((bf16[4,128,256]{1,2,0:T(8,128)(2,1)}), bf16[4,128,256]{1,2,0:T(8,128)(2,1)}, u32[]{:S(2)}, u32[]{:S(2)}) async-start(bf16[4,128,256]{1,2,0:T(8,128)(2,1)} %bitcast.271), calls=%async_computation.5 | async-start | bytes 524288 | tf_op jit(solution)/shard_map/all_to_all | solution.py:206
  134.5 88.7 %reduce-scatter.2.cloned.1.call-start = ((), (), s32[]{:S(2)}) async-start(), calls=%async_computation.10 | async-start | bytes 2359296 | tf_op jit(solution)/shard_map/reduce_scatter | solution.py:207
  144.4 4.1 %copy-start.7 = (bf16[2,2,192,8,128]{4,2,3,1,0:T(8,128)(2,1)S(1)}, bf16[2,2,192,8,128]{4,2,3,1,0:T(8,128)(2,1)}, u32[]{:S(2)}) copy-start(bf16[2,2,192,8,128]{4,2,3,1,0:T(8,128)(2,1)} %copy-done.5) | copy-start | bytes 4718596
  148.4 1.0 copy-start.22
  148.5 1.2 copy-start.3
  148.6 1.2 copy-start.16
  149.7 1.3 copy-start.2
  149.7 1.4 copy-start.11
  165.2 1.1 copy-start.12
  168.4 2.7 copy-start.4
  179.4 21.9 %all-to-all-start.3 = ((bf16[8,32,1024]{2,1,0:T(8,128)(2,1)}), bf16[8,32,1024]{2,1,0:T(8,128)(2,1)}, u32[]{:S(2)}, u32[]{:S(2)}) async-start(bf16[8,32,1024]{2,1,0:T(8,128)(2,1)} %convert_element_type.192), calls=%async_computation.3 | async-start | bytes 1048576 | tf_op jit(solution)/shard_map/all_to_all | solution.py:124
  185.8 1.9 copy-start.9
  191.4 6.6 %copy-start.13 = (bf16[2,8,64,704]{3,2,0,1:T(8,128)(2,1)S(1)}, bf16[2,8,64,704]{3,2,0,1:T(8,128)(2,1)}, u32[]{:S(2)}) copy-start(bf16[2,8,64,704]{3,2,0,1:T(8,128)(2,1)} %copy-done.12) | copy-start | bytes 4325380
  192.3 63.1 %collective-permute-start.8 = (bf16[2,64,1024]{2,1,0:T(8,128)(2,1)}, bf16[2,64,1024]{2,1,0:T(8,128)(2,1)}, u32[]{:S(2)}, u32[]{:S(2)}) collective-permute-start(bf16[2,64,1024]{2,1,0:T(8,128)(2,1)} %get-tuple-element.49), channel_id=1, source_target_pairs={{0,252},{4,0},{8,4},{12,8},{16,12},{20,16},{24,20},{28,24},{32,28}... | collective-permute-start | bytes 786440 | tf_op jit(solution)/shard_map/ppermute | solution.py:15
  193.8 62.8 %collective-permute-start.9 = (bf16[2,64,1024]{2,1,0:T(8,128)(2,1)}, bf16[2,64,1024]{2,1,0:T(8,128)(2,1)}, u32[]{:S(2)}, u32[]{:S(2)}) collective-permute-start(bf16[2,64,1024]{2,1,0:T(8,128)(2,1)} %get-tuple-element.48), channel_id=1, source_target_pairs={{0,4},{4,8},{8,12},{12,16},{16,20},{20,24},{24,28},{28,32},{32,36}... | collective-permute-start | bytes 786440 | tf_op jit(solution)/shard_map/ppermute | solution.py:15
  202.5 15.7 %copy-start.20 = (bf16[16,8,8,128]{3,2,1,0:T(8,128)(2,1)S(1)}, bf16[16,8,8,128]{3,2,1,0:T(8,128)(2,1)}, u32[]{:S(2)}) copy-start(bf16[16,8,8,128]{3,2,1,0:T(8,128)(2,1)} %copy-done.19) | copy-start | bytes 786436
  203.4 21.0 %all-to-all-start.4 = ((bf16[8,32,1024]{2,1,0:T(8,128)(2,1)}), bf16[8,32,1024]{2,1,0:T(8,128)(2,1)}, u32[]{:S(2)}, u32[]{:S(2)}) async-start(bf16[8,32,1024]{2,1,0:T(8,128)(2,1)} %broadcast_select_fusion), calls=%async_computation.4 | async-start | bytes 1048576 | tf_op jit(solution)/shard_map/all_to_all | solution.py:124
  207.6 14.1 %copy-start = (bf16[1024,2048]{1,0:T(8,128)(2,1)S(1)}, bf16[1024,2048]{1,0:T(8,128)(2,1)}, u32[]{:S(2)}) copy-start(bf16[1024,2048]{1,0:T(8,128)(2,1)} %all-gather.3.cloned.1.call-done) | copy-start | bytes 12582916
  208.8 27.5 %collective-permute-start.15 = (bf16[2,64,1024]{2,1,0:T(8,128)(2,1)}, bf16[2,64,1024]{2,1,0:T(8,128)(2,1)}, u32[]{:S(2)}, u32[]{:S(2)}) collective-permute-start(bf16[2,64,1024]{2,1,0:T(8,128)(2,1)} %get-tuple-element.39), channel_id=1, source_target_pairs={{0,128},{128,0},{4,132},{132,4},{8,136},{136,8},{12,140},{140,12},... | collective-permute-start | bytes 786440 | tf_op jit(solution)/shard_map/ppermute | solution.py:39
  210.8 28.5 %collective-permute-start.14 = (bf16[2,64,1024]{2,1,0:T(8,128)(2,1)}, bf16[2,64,1024]{2,1,0:T(8,128)(2,1)}, u32[]{:S(2)}, u32[]{:S(2)}) collective-permute-start(bf16[2,64,1024]{2,1,0:T(8,128)(2,1)} %get-tuple-element.40), channel_id=1, source_target_pairs={{0,64},{64,0},{4,68},{68,4},{8,72},{72,8},{12,76},{76,12},{16,80},... | collective-permute-start | bytes 786440 | tf_op jit(solution)/shard_map/ppermute | solution.py:39
  212.3 9.3 %copy-start.26 = (bf16[2,64,8,128]{3,2,1,0:T(8,128)(2,1)S(1)}, bf16[2,64,8,128]{3,2,1,0:T(8,128)(2,1)}, u32[]{:S(2)}) copy-start(bf16[2,64,8,128]{3,2,1,0:T(8,128)(2,1)} %copy-done.25) | copy-start | bytes 786436
  212.3 28.5 %collective-permute-start.13 = (bf16[2,64,1024]{2,1,0:T(8,128)(2,1)}, bf16[2,64,1024]{2,1,0:T(8,128)(2,1)}, u32[]{:S(2)}, u32[]{:S(2)}) collective-permute-start(bf16[2,64,1024]{2,1,0:T(8,128)(2,1)} %get-tuple-element.41), channel_id=1, source_target_pairs={{0,32},{32,0},{4,36},{36,4},{8,40},{40,8},{12,44},{44,12},{16,48},... | collective-permute-start | bytes 786440 | tf_op jit(solution)/shard_map/ppermute | solution.py:39
  226.2 14.6 %copy-start.27 = (bf16[2,64,1024]{2,1,0:T(8,128)(2,1)S(1)}, bf16[2,64,1024]{2,1,0:T(8,128)(2,1)}, u32[]{:S(2)}) copy-start(bf16[2,64,1024]{2,1,0:T(8,128)(2,1)} %get-tuple-element.38) | copy-start | bytes 786436
  226.2 17.6 %copy-start.8 = (bf16[2,2,192,8,128]{4,2,3,1,0:T(8,128)(2,1)S(1)}, bf16[2,2,192,8,128]{4,2,3,1,0:T(8,128)(2,1)}, u32[]{:S(2)}) copy-start(bf16[2,2,192,8,128]{4,2,3,1,0:T(8,128)(2,1)} %copy-done.5) | copy-start | bytes 4718596
  228.2 29.5 %all-to-all-start.6 = ((bf16[8,40,1024]{2,1,0:T(8,128)(2,1)}), bf16[8,40,1024]{2,1,0:T(8,128)(2,1)}, u32[]{:S(2)}, u32[]{:S(2)}) async-start(bf16[8,40,1024]{2,1,0:T(8,128)(2,1)} %pad_maximum_fusion.3), calls=%async_computation.7 | async-start | bytes 1310720 | tf_op jit(solution)/shard_map/all_to_all | solution.py:124
  236.3 14.5 %collective-permute-start.12 = (bf16[2,64,1024]{2,1,0:T(8,128)(2,1)}, bf16[2,64,1024]{2,1,0:T(8,128)(2,1)}, u32[]{:S(2)}, u32[]{:S(2)}) collective-permute-start(bf16[2,64,1024]{2,1,0:T(8,128)(2,1)} %get-tuple-element.42), channel_id=1, source_target_pairs={{0,16},{16,0},{4,20},{20,4},{8,24},{24,8},{12,28},{28,12},{32,48},... | collective-permute-start | bytes 786440 | tf_op jit(solution)/shard_map/ppermute | solution.py:39
  239.4 12.4 %collective-permute-start.11 = (bf16[2,64,1024]{2,1,0:T(8,128)(2,1)}, bf16[2,64,1024]{2,1,0:T(8,128)(2,1)}, u32[]{:S(2)}, u32[]{:S(2)}) collective-permute-start(bf16[2,64,1024]{2,1,0:T(8,128)(2,1)} %get-tuple-element.43), channel_id=1, source_target_pairs={{0,8},{8,0},{4,12},{12,4},{16,24},{24,16},{20,28},{28,20},{32,40},... | collective-permute-start | bytes 786440 | tf_op jit(solution)/shard_map/ppermute | solution.py:39
  240.8 12.8 %collective-permute-start.10 = (bf16[2,64,1024]{2,1,0:T(8,128)(2,1)S(1)}, bf16[2,64,1024]{2,1,0:T(8,128)(2,1)}, u32[]{:S(2)}, u32[]{:S(2)}) collective-permute-start(bf16[2,64,1024]{2,1,0:T(8,128)(2,1)S(1)} %copy-done.27), channel_id=1, source_target_pairs={{0,4},{4,0},{8,12},{12,8},{16,20},{20,16},{24,28},{28,24},{32,36},... | collective-permute-start | bytes 786440 | tf_op jit(solution)/shard_map/ppermute | solution.py:39
  258.8 1.0 copy-start.23
  258.8 1.2 copy-start.24
  258.8 1.2 copy-start.30
  258.8 1.2 copy-start.31
  258.8 1.2 copy-start.32
  258.8 1.2 copy-start.33
Sparse Core Ops, SparseCore 0:
  9.8 44.2 all-gather.4
  55.9 56.7 all-gather.2
  144.5 35.6 reduce-scatter.1

commit v2 on v0

v2 whole, which is shorter than its diff:
```python
import jax
import jax.numpy as jnp
from jax import lax
from jax.experimental import pallas as pl
from jax.experimental.pallas import tpu as pltpu
from jax.sharding import PartitionSpec as P

HEADS = 8
HEAD_DIM = 128
BLK = 64
GLOB = 2
BITS = 6
TOK = 128
WIDTH = HEADS * HEAD_DIM
D = 2048
KEYS = 768
SCALE = HEAD_DIM ** (-0.5)
BF = jnp.bfloat16
F32 = jnp.float32
ROWS = (((1,), (1,)), ((), ()))
COLS = (((0,), (0,)), ((), ()))
PLAIN = (((1,), (0,)), ((), ()))
VMEM_LIMIT = 48 * 1024 * 1024


def stretch_id(y, z, x):
    return y * 16 + z * 2 + x


Z_GROUPS = [[stretch_id(y, z, x) for z in range(8)] for y in range(4) for x in range(2)]
YX_GROUPS = [[stretch_id(y, z, x) for y in range(4) for x in range(2)] for z in range(8)]


def mm(left, right, dims):
    return lax.dot_general(left, right, dims, preferred_element_type=F32)


def trade(value, groups):
    return lax.all_to_all(value, "seq", 0, 0, axis_index_groups=groups, tiled=True)


def shifted(value, steps):
    return lax.ppermute(value, "seq", [(s, (s + steps) % 64) for s in range(64)])


def swapped(value, bit):
    return lax.ppermute(value, "seq", [(s, s ^ (1 << bit)) for s in range(64)])


def smem():
    return pl.BlockSpec(memory_space=pltpu.SMEM)


def params(**kw):
    return pltpu.CompilerParams(vmem_limit_bytes=VMEM_LIMIT, **kw)


def where_of(rand_slot, global_ids):
    me = lax.axis_index("seq")
    owner = global_ids // 2
    here = jnp.where(owner == me, global_ids % 2, -1)
    my_m = (me // 16) * 2 + me % 2
    which = jnp.full((1,), (my_m // 2) % 2, jnp.int32)
    return jnp.concatenate(
        [rand_slot, here, (owner // 2) % 8, (owner // 16) * 2 + owner % 2, which]
    ).astype(jnp.int32)


def pick_kernel(where, k_ref, v_ref, *outs):
    for b in range(BITS):
        rows = pl.ds(pl.multiple_of(where[b] * BLK, BLK), BLK)
        outs[b][0] = k_ref[rows, :]
        outs[b][1] = v_ref[rows, :]
    first, last, picked = outs[BITS:]
    first[0] = k_ref[0:BLK, :]
    first[1] = v_ref[0:BLK, :]
    last[0] = k_ref[BLK : 2 * BLK, :]
    last[1] = v_ref[BLK : 2 * BLK, :]
    for g in range(GLOB):
        here = where[6 + g]

        @pl.when(here < 0)
        def _():
            picked[0, g] = jnp.zeros((BLK, WIDTH), BF)
            picked[1, g] = jnp.zeros((BLK, WIDTH), BF)

        @pl.when(here >= 0)
        def _():
            rows = pl.ds(pl.multiple_of(jnp.maximum(here, 0) * BLK, BLK), BLK)
            picked[0, g] = k_ref[rows, :]
            picked[1, g] = v_ref[rows, :]


def pick(where, keys, values):
    block = jax.ShapeDtypeStruct((2, BLK, WIDTH), BF)
    outs = [block] * (BITS + 2) + [jax.ShapeDtypeStruct((2, GLOB, BLK, WIDTH), BF)]
    vm = pl.BlockSpec(memory_space=pltpu.VMEM)
    return pl.pallas_call(
        pick_kernel,
        out_shape=outs,
        in_specs=[smem(), vm, vm],
        out_specs=[vm] * len(outs),
        compiler_params=params(),
        name="pick",
    )(where, keys, values)


def relay_kernel(x_ref, o_ref):
    total = jnp.sum(x_ref[...].astype(F32), axis=0).astype(BF)
    for j in range(8):
        o_ref[j] = total


def relay(x):
    return pl.pallas_call(
        relay_kernel,
        out_shape=jax.ShapeDtypeStruct(x.shape, BF),
        compiler_params=params(),
        name="relay",
    )(x)


def gather_heads(dst, c, own, lo, hi, rand, glob):
    dst[0:64, :] = lo[c]
    dst[64:192, :] = own[...]
    dst[192:256, :] = hi[c]
    dst[256:384, :] = glob[c]
    for b in range(BITS):
        dst[384 + 64 * b : 448 + 64 * b, :] = rand[b][c]


def fill_bias(where, bias):
    lane = lax.broadcasted_iota(jnp.int32, (BLK, TOK), 1) // BLK
    for kb in range(12):
        if kb < 4:
            keep = jnp.logical_and(lane <= kb, lane >= kb - 2)
        elif kb < 6:
            keep = lane >= 0
        else:
            keep = lane == where[kb - 6]
        bias[kb * BLK : (kb + 1) * BLK, :] = jnp.where(keep, 0.0, -1e30).astype(F32)


def forward_kernel(where, q, k, v, lo, hi, *rest):
    rand, (glob, perm, attn, stats, ordered, ks, vs, bias, acc) = rest[:BITS], rest[BITS:]
    head = pl.program_id(0)

    @pl.when(head == 0)
    def _():
        fill_bias(where, bias)
        acc[...] = jnp.zeros_like(acc)

    gather_heads(ks, 0, k, lo, hi, rand, glob)
    gather_heads(vs, 1, v, lo, hi, rand, glob)
    scores = mm(ks[...], q[...], ROWS) * SCALE + bias[...]
    top = jnp.max(scores, axis=0, keepdims=True)
    expd = jnp.exp(scores - top)
    inv = 1.0 / jnp.sum(expd, axis=0, keepdims=True)
    probs = (expd * inv).astype(BF)
    out = mm(probs, vs[...], COLS).astype(BF)
    attn[...] = out
    stats[0, 0:1, :] = top
    stats[0, 1:2, :] = inv
    acc[...] += mm(out, perm[...], PLAIN)

    @pl.when(head == HEADS - 1)
    def _():
        for r in range(4):
            ordered[r] = acc[:, r * 256 : (r + 1) * 256].astype(BF)


def head_specs():
    flat = pl.BlockSpec((TOK, HEAD_DIM), lambda h: (0, h))
    pair = pl.BlockSpec((2, BLK, HEAD_DIM), lambda h: (0, 0, h))
    both = pl.BlockSpec((2, TOK, HEAD_DIM), lambda h: (0, 0, h))
    return flat, pair, both


def forward(where, q, k, v, lo, hi, rand, glob, perm):
    flat, pair, both = head_specs()
    return pl.pallas_call(
        forward_kernel,
        grid=(HEADS,),
        in_specs=[smem(), flat, flat, flat, pair, pair]
        + [pair] * BITS
        + [both, pl.BlockSpec((HEAD_DIM, WIDTH), lambda h: (h, 0))],
        out_specs=[
            flat,
            pl.BlockSpec((1, 8, TOK), lambda h: (h, 0, 0)),
            pl.BlockSpec((4, TOK, 256), lambda h: (0, 0, 0)),
        ],
        out_shape=[
            jax.ShapeDtypeStruct((TOK, WIDTH), BF),
            jax.ShapeDtypeStruct((HEADS, 8, TOK), F32),
            jax.ShapeDtypeStruct((4, TOK, 256), BF),
        ],
        scratch_shapes=[
            pltpu.VMEM((KEYS, HEAD_DIM), BF),
            pltpu.VMEM((KEYS, HEAD_DIM), BF),
            pltpu.VMEM((KEYS, TOK), F32),
            pltpu.VMEM((TOK, WIDTH), F32),
        ],
        compiler_params=params(dimension_semantics=("arbitrary",)),
        name="forward",
    )(where, q, k, v, lo, hi, *rand, glob, perm)


def backward_kernel(where, q, k, v, lo, hi, *rest):
    rand, rest = rest[:BITS], rest[BITS:]
    glob, attn, stats, w, d_out = rest[:5]
    dq, down, dlo, dhi = rest[5:9]
    drand, rest = rest[9 : 9 + BITS], rest[9 + BITS :]
    dglob, layer, ks, vs, bias, acc = rest
    head = pl.program_id(0)

    @pl.when(head == 0)
    def _():
        fill_bias(where, bias)
        acc[...] = jnp.zeros_like(acc)

    gather_heads(ks, 0, k, lo, hi, rand, glob)
    gather_heads(vs, 1, v, lo, hi, rand, glob)
    d_attn = mm(d_out[...], w[...], ROWS).astype(BF)
    acc[...] += mm(attn[...], w[...], PLAIN)
    scores = mm(ks[...], q[...], ROWS) * SCALE + bias[...]
    probs = jnp.exp(scores - stats[0, 0:1, :]) * stats[0, 1:2, :]
    probs_b = probs.astype(BF)
    dprob = mm(vs[...], d_attn, ROWS)
    delta = jnp.sum(dprob * probs, axis=0, keepdims=True)
    dscore = (probs * (dprob - delta) * SCALE).astype(BF)
    dq[...] = mm(dscore, ks[...], COLS).astype(BF)
    for c, grad in ((0, mm(dscore, q[...], PLAIN)), (1, mm(probs_b, d_attn, PLAIN))):
        dlo[c] = grad[0:64].astype(BF)
        down[c] = grad[64:192]
        dhi[c] = grad[192:256].astype(BF)
        dglob[c] = grad[256:384].astype(BF)
        for b in range(BITS):
            drand[b][c] = grad[384 + 64 * b : 448 + 64 * b].astype(BF)

    @pl.when(head == HEADS - 1)
    def _():
        layer[...] = acc[...].astype(BF)


def backward(where, q, k, v, lo, hi, rand, glob, attn, stats, w, d_out):
    flat, pair, both = head_specs()
    whole = pl.BlockSpec((TOK, D), lambda h: (0, 0))
    block = jax.ShapeDtypeStruct((2, BLK, WIDTH), BF)
    outs = pl.pallas_call(
        backward_kernel,
        grid=(HEADS,),
        in_specs=[smem(), flat, flat, flat, pair, pair]
        + [pair] * BITS
        + [
            both,
            flat,
            pl.BlockSpec((1, 8, TOK), lambda h: (h, 0, 0)),
            pl.BlockSpec((HEAD_DIM, D), lambda h: (h, 0)),
            whole,
        ],
        out_specs=[flat, both, pair, pair] + [pair] * BITS + [both, whole],
        out_shape=[
            jax.ShapeDtypeStruct((TOK, WIDTH), BF),
            jax.ShapeDtypeStruct((2, TOK, WIDTH), F32),
            block,
            block,
        ]
        + [block] * BITS
        + [
            jax.ShapeDtypeStruct((2, TOK, WIDTH), BF),
            jax.ShapeDtypeStruct((TOK, D), BF),
        ],
        scratch_shapes=[
            pltpu.VMEM((KEYS, HEAD_DIM), BF),
            pltpu.VMEM((KEYS, HEAD_DIM), BF),
            pltpu.VMEM((KEYS, TOK), F32),
            pltpu.VMEM((TOK, D), F32),
        ],
        compiler_params=params(dimension_semantics=("arbitrary",)),
        name="backward",
    )(where, q, k, v, lo, hi, *rand, glob, attn, stats, w, d_out)
    return outs[:4], outs[4 : 4 + BITS], outs[4 + BITS], outs[5 + BITS]


def weight_kernel(cols, grads, dglob, out):
    step = pl.program_id(0)

    @pl.when(step == 0)
    def _():
        out[...] = dglob[...]

    @pl.when(step > 0)
    def _():
        out[...] = mm(cols[...], grads[...], COLS).astype(BF).reshape(8, 32, 1024)


def weight_payload(cols, grads, dglob):
    return pl.pallas_call(
        weight_kernel,
        grid=(3,),
        in_specs=[
            pl.BlockSpec((4 * TOK, 256), lambda i: (0, 0)),
            pl.BlockSpec((4 * TOK, 1024), lambda i: (0, jnp.maximum(i - 1, 0))),
            pl.BlockSpec((8, 32, 1024), lambda i: (0, 0, 0)),
        ],
        out_specs=pl.BlockSpec((8, 32, 1024), lambda i: (0, i, 0)),
        out_shape=jax.ShapeDtypeStruct((8, 96, 1024), BF),
        compiler_params=params(dimension_semantics=("arbitrary",)),
        name="weight",
    )(cols, grads, dglob)


def route_z_kernel(where, x, out, total, small):
    total[...] = jnp.sum(x[...].astype(F32), axis=0)
    which = where[12]
    target = jnp.where(which == 0, where[8], where[9])
    chunk = total[0:32, :]
    small[8:16, :] = jnp.zeros((8, 1024), F32)
    for j in range(8):
        out[j, 0:32] = jnp.where(target == j, chunk, 0.0).astype(BF)
        small[0:4, :] = total[32 + 4 * j : 36 + 4 * j, :]
        small[4:8, :] = total[64 + 4 * j : 68 + 4 * j, :]
        out[j, 32:48] = small[...].astype(BF)


def route_z(where, x):
    vm = pl.BlockSpec(memory_space=pltpu.VMEM)
    return pl.pallas_call(
        route_z_kernel,
        out_shape=jax.ShapeDtypeStruct((8, 48, 1024), BF),
        in_specs=[smem(), vm],
        out_specs=vm,
        scratch_shapes=[pltpu.VMEM((96, 1024), F32), pltpu.VMEM((16, 1024), F32)],
        compiler_params=params(),
        name="route_z",
    )(where, x)


def route_yx_kernel(where, x, out, weight, total):
    total[...] = jnp.sum(x[...].astype(F32), axis=0)
    which = where[12]
    target = jnp.where(which == 0, where[10], where[11])
    chunk = total[0:32, :]
    for j in range(8):
        out[j] = jnp.where(target == j, chunk, 0.0).astype(BF)
    weight[:, 0:1024] = total[32:36, :]
    weight[:, 1024:2048] = total[36:40, :]


def route_yx(where, x):
    vm = pl.BlockSpec(memory_space=pltpu.VMEM)
    return pl.pallas_call(
        route_yx_kernel,
        out_shape=[
            jax.ShapeDtypeStruct((8, 32, 1024), BF),
            jax.ShapeDtypeStruct((4, D), F32),
        ],
        in_specs=[smem(), vm],
        out_specs=[vm, vm],
        scratch_shapes=[pltpu.VMEM((48, 1024), F32)],
        compiler_params=params(),
        name="route_yx",
    )(where, x)


def finish_kernel(where, own, left, right, *rest):
    rand, (glob, dk, dv, acc) = rest[:BITS], rest[BITS:]
    acc[...] = own[...]
    acc[:, 0:BLK, :] += left[...].astype(F32)
    acc[:, BLK : 2 * BLK, :] += right[...].astype(F32)
    for b in range(BITS):
        rows = pl.ds(pl.multiple_of(where[b] * BLK, BLK), BLK)
        acc[:, rows, :] += rand[b][...].astype(F32)
    for g in range(GLOB):
        here = where[6 + g]

        @pl.when(here >= 0)
        def _():
            rows = pl.ds(pl.multiple_of(jnp.maximum(here, 0) * BLK, BLK), BLK)
            acc[:, rows, :] += glob[:, g].astype(F32)

    dk[...] = acc[0].astype(BF)
    dv[...] = acc[1].astype(BF)


def finish(where, own, left, right, rand, glob):
    wide = 256
    pair = pl.BlockSpec((2, BLK, wide), lambda i: (0, 0, i))
    flat = pl.BlockSpec((TOK, wide), lambda i: (0, i))
    return pl.pallas_call(
        finish_kernel,
        grid=(WIDTH // wide,),
        in_specs=[smem(), pl.BlockSpec((2, TOK, wide), lambda i: (0, 0, i)), pair, pair]
        + [pair] * BITS
        + [pl.BlockSpec((2, GLOB, BLK, wide), lambda i: (0, 0, 0, i))],
        out_specs=[flat, flat],
        out_shape=[jax.ShapeDtypeStruct((TOK, WIDTH), BF)] * 2,
        scratch_shapes=[pltpu.VMEM((2, TOK, wide), F32)],
        compiler_params=params(dimension_semantics=("arbitrary",)),
        name="finish",
    )(where, own, left, right, *rand, glob)


def feature_order():
    new = jnp.arange(WIDTH, dtype=jnp.int32)
    r, y, x, z, j = new // 256, (new // 64) % 4, (new // 32) % 2, (new // 4) % 8, new % 4
    old = y * 256 + z * 32 + x * 16 + r * 4 + j
    return (jnp.arange(WIDTH, dtype=jnp.int32)[:, None] == old[None, :]).astype(BF)


def per_device(queries, keys, values, w_out, d_out, rand_slot, global_ids):
    q, k, v, grad_out = queries[0], keys[0], values[0], d_out[0]
    where = where_of(rand_slot[0, 0], global_ids[0])
    all_grads = lax.all_gather(grad_out, "rep", axis=0, tiled=True)
    all_w = lax.all_gather(w_out, "rep", axis=0, tiled=True)
    *chosen, first, last, picked = pick(where, k, v)
    spread = trade(picked.reshape(8, 32, WIDTH), Z_GROUPS)
    lo = shifted(last, 1)
    hi = shifted(first, -1)
    rand = [swapped(chosen[b], b) for b in range(BITS)]
    spread = trade(relay(spread), YX_GROUPS)
    glob = trade(relay(spread), Z_GROUPS).reshape(2, GLOB * BLK, WIDTH)
    attn, stats, ordered = forward(where, q, k, v, lo, hi, rand, glob, feature_order())
    cols = lax.all_to_all(ordered, "rep", 0, 0, tiled=True).reshape(4 * TOK, 256)
    (dq, down, dlo, dhi), drand, dglob, layer = backward(
        where, q, k, v, lo, hi, rand, glob, attn, stats, all_w, grad_out
    )
    payload = weight_payload(cols, all_grads, dglob.reshape(8, 32, WIDTH))
    payload = route_z(where, trade(payload, YX_GROUPS))
    payload, weight_grad = route_yx(where, trade(payload, Z_GROUPS))
    glob_total = trade(payload, YX_GROUPS).reshape(2, GLOB, BLK, WIDTH)
    right = shifted(dlo, -1)
    left = shifted(dhi, 1)
    back = [swapped(drand[b], b) for b in range(BITS)]
    dk, dv = finish(where, down, left, right, back, glob_total)
    return (layer[None], dq[None], dk[None], dv[None], weight_grad)


def solution(mesh):
    return jax.shard_map(
        per_device,
        mesh=mesh,
        in_specs=(
            P("rep", "seq", None),
            P("rep", "seq", None),
            P("rep", "seq", None),
            P("rep", None),
            P("rep", "seq", None),
            P("rep", "seq", None),
            P("rep", None),
        ),
        out_specs=(
            P("rep", "seq", None),
            P("rep", "seq", None),
            P("rep", "seq", None),
            P("rep", "seq", None),
            P(("seq", "rep"), None),
        ),
        check_vma=False,
    )
```

time: 1510 us -> 261 us (0.17); the launches traced: 1490 us -> 257 us
  waiting for transfers between devices: 972 us -> 48.5 us
  blocking collectives: 341 us -> 80 us
  Pallas kernels: 0 us -> 31.9 us
  other arithmetic: 32.3 us -> 2.24 us
  matrix products: 30 us -> 0 us
  local copies, waits for them, and re-layouts: 52.1 us -> 31.1 us
    psum x1 -> x0, waiting for transfers between devices: 639 us -> none  [per_device(): glob_total = lax.psum(dglob, 'seq').reshape(2, GLOB, BLK, width)]
    psum x1 -> x0, blocking collectives: 341 us -> none  [per_device(): lax.psum(picked, 'seq').astype(jnp.bfloat16).reshape(2, GLOB * BLK, width)]
    unnamed x4 -> x2, waiting for transfers between devices: 311 us -> 1.38 us
    all_to_all x0 -> x3, blocking collectives: none -> 80 us  [trade(): lax.all_to_all(value, 'seq', 0, 0, axis_index_groups=groups, tiled=True)]
    pallas_call x0 -> x9, Pallas kernels: none -> 31.9 us  [the longest x1 13 us: backward(): pl.pallas_call(backward_kernel, grid=(HEADS,), in_specs=[smem(), flat, fl...]
    dot_general x19 -> x0, matrix products: 28.7 us -> none  [the longest x14 10 us: mult(): return jnp.einsum(form, left, right, preferred_element_type=jnp.float32)]
    all_to_all x0 -> x4, waiting for transfers between devices: none -> 16.1 us  [the longest x3 16.1 us: trade(): lax.all_to_all(value, 'seq', 0, 0, axis_index_groups=groups, tiled=True)]
    all_to_all x0 -> x4, starting transfers between devices: none -> 15.5 us  [the longest x3 12.1 us: trade(): lax.all_to_all(value, 'seq', 0, 0, axis_index_groups=groups, tiled=True)]
  transfers between devices with their start and end apart: 19 -> 22, of which waited for: 4 -> 8; matrix products, arithmetic and copies ran while one was open for 3% -> 1% of each run, Pallas kernels for 0% -> 10%
where the time goes in v2:
time: 261 us; the launch traced here: 257 us
  blocking collectives  80 us (31%)
  starting transfers between devices  48.6 us (19%)
  waiting for transfers between devices  48.5 us (19%)
  Pallas kernels  31.9 us (12%)
  local copies, waits for them, and re-layouts  31.1 us (12%)
  between operations  14.3 us (5%)
    all_to_all x3, blocking collectives, trade(): lax.all_to_all(value, 'seq', 0, 0, axis_index_groups=groups, tiled=True)  80 us
    unnamed x90, local copies, waits for them, and re-layouts  30.4 us
    ppermute x12, starting transfers between devices, swapped(): return lax.ppermute(value, 'seq', [(s, s ^ 1 << bit) for s in range(64)])  19.2 us
    ppermute x12, waiting for transfers between devices, swapped(): return lax.ppermute(value, 'seq', [(s, s ^ 1 << bit) for s in range(64)])  16.1 us
    all_to_all x3, waiting for transfers between devices, trade(): lax.all_to_all(value, 'seq', 0, 0, axis_index_groups=groups, tiled=True)  16.1 us
    ppermute x4, waiting for transfers between devices, shifted(): lax.ppermute(value, 'seq', [(s, (s + steps) % 64) for s in range(64)])  14.9 us
    ppermute x4, starting transfers between devices, shifted(): lax.ppermute(value, 'seq', [(s, (s + steps) % 64) for s in range(64)])  13.9 us
    pallas_call x1, Pallas kernels, backward(): pl.pallas_call(backward_kernel, grid=(HEADS,), in_specs=[smem(), flat, fl...  13 us
  transfers between devices with their start and end apart: 22, of which 8 were waited for; matrix products, arithmetic and copies ran while one was open for 1% of the time, Pallas kernels for 10%

profile of v2, /device:TPU:8, one launch (start us, length us, event | category | flops | bytes accessed | tf_op | source)
XLA Modules:
  0.0 256.7 jit_solution(8636115652703371624)
XLA Ops:
  10.1 0.7 concatenate.3.where
  10.8 0.9 copy-done.1
  11.7 0.9 copy-done.3
  12.7 1.8 pick.1
  14.5 25.7 %all_to_all.35.x_ref = bf16[8,32,1024]{2,1,0:T(8,128)(2,1)S(1)} all-to-all(bf16[8,32,1024]{2,1,0:T(8,128)(2,1)S(1)} %bitcast.46), channel_id=1, replica_groups={{0,8,16,24,32,40,48,56},{4,12,20,28,36,44,52,60},{64,72,80,88,96,104,11..., dimensions={0} | all-to-all | bytes 1048576 | tf_op jit(solution)/shard_map/all_to_all | solution.py:39
  40.3 22.0 %all_to_all.36.x_ref = bf16[8,32,1024]{2,1,0:T(8,128)(2,1)S(1)} all-to-all(bf16[8,32,1024]{2,1,0:T(8,128)(2,1)S(1)} %relay.2), channel_id=1, replica_groups={{0,4,64,68,128,132,192,196},{8,12,72,76,136,140,200,204},{16,20,80,84,1..., dimensions={0} | all-to-all | bytes 1048576 | tf_op jit(solution)/shard_map/all_to_all | solution.py:39
  62.3 0.9 relay.3
  63.2 3.5 %all-to-all-start.2 = ((bf16[8,32,1024]{2,1,0:T(8,128)(2,1)}), bf16[8,32,1024]{2,1,0:T(8,128)(2,1)S(1)}, u32[]{:S(2)}, u32[]{:S(2)}) async-start(bf16[8,32,1024]{2,1,0:T(8,128)(2,1)} %relay.3), calls=%async_computation.2 | async-start | bytes 1048576 | tf_op jit(solution)/shard_map/all_to_all | solution.py:39
  66.7 1.1 collective-permute-start
  67.8 5.5 %collective-permute-start.1 = (bf16[2,64,1024]{2,1,0:T(8,128)(2,1)S(1)}, bf16[2,64,1024]{2,1,0:T(8,128)(2,1)S(1)}, u32[]{:S(2)}, u32[]{:S(2)}) collective-permute-start(bf16[2,64,1024]{2,1,0:T(8,128)(2,1)S(1)} %get-tuple-element.34), channel_id=1, source_target_pairs={{0,252},{4,0},{8,4},{12,8},{16,12},{20,16},{24,20},{28,24},{32,28}... | collective-permute-start | bytes 786440 | tf_op jit(solution)/shard_map/ppermute | solution.py:43
  73.3 3.3 %collective-permute-start.4 = (bf16[2,64,1024]{2,1,0:T(8,128)(2,1)}, bf16[2,64,1024]{2,1,0:T(8,128)(2,1)S(1)}, u32[]{:S(2)}, u32[]{:S(2)}) collective-permute-start(bf16[2,64,1024]{2,1,0:T(8,128)(2,1)} %get-tuple-element.37), channel_id=1, source_target_pairs={{0,16},{4,20},{8,24},{12,28},{16,0},{20,4},{24,8},{28,12},{32,48},... | collective-permute-start | bytes 786440 | tf_op jit(solution)/shard_map/ppermute | solution.py:47
  76.6 8.5 %collective-permute-done.lo = bf16[2,64,1024]{2,1,0:T(8,128)(2,1)S(1)} collective-permute-done((bf16[2,64,1024]{2,1,0:T(8,128)(2,1)S(1)}, bf16[2,64,1024]{2,1,0:T(8,128)(2,1)S(1)}, u32[]{:S(2)}, u32[]{:S(2)}) %collective-permute-start) | collective-permute-done | bytes 262176 | tf_op jit(solution)/shard_map/ppermute | solution.py:43
  85.8 2.6 %collective-permute-start.5 = (bf16[2,64,1024]{2,1,0:T(8,128)(2,1)}, bf16[2,64,1024]{2,1,0:T(8,128)(2,1)S(1)}, u32[]{:S(2)}, u32[]{:S(2)}) collective-permute-start(bf16[2,64,1024]{2,1,0:T(8,128)(2,1)} %get-tuple-element.38), channel_id=1, source_target_pairs={{0,32},{4,36},{8,40},{12,44},{16,48},{20,52},{24,56},{28,60},{32,0... | collective-permute-start | bytes 786440 | tf_op jit(solution)/shard_map/ppermute | solution.py:47
  89.1 1.3 collective-permute-start.6
  90.4 0.7 copy-done.13
  91.1 1.7 collective-permute-start.7
  92.8 0.9 fusion.rest_7_
  93.7 5.4 %collective-permute-done.3.rest_1_ = bf16[2,64,1024]{2,1,0:T(8,128)(2,1)S(1)} collective-permute-done((bf16[2,64,1024]{2,1,0:T(8,128)(2,1)}, bf16[2,64,1024]{2,1,0:T(8,128)(2,1)S(1)}, u32[]{:S(2)}, u32[]{:S(2)}) %collective-permute-start.3) | collective-permute-done | bytes 262176 | tf_op jit(solution)/shard_map/ppermute | solution.py:47
  99.8 0.7 copy-done.19
  100.5 3.1 %collective-permute-done.5.rest_3_ = bf16[2,64,1024]{2,1,0:T(8,128)(2,1)S(1)} collective-permute-done((bf16[2,64,1024]{2,1,0:T(8,128)(2,1)}, bf16[2,64,1024]{2,1,0:T(8,128)(2,1)S(1)}, u32[]{:S(2)}, u32[]{:S(2)}) %collective-permute-start.5) | collective-permute-done | bytes 262176 | tf_op jit(solution)/shard_map/ppermute | solution.py:47
  104.3 0.7 copy-done.25
  105.1 0.7 copy-done.28
  105.8 1.1 copy-done.8
  106.9 0.9 copy-done.11
  107.9 0.9 copy-done.14
  108.8 0.9 copy-done.17
  109.8 0.9 copy-done.20
  110.7 0.9 copy-done.23
  111.7 0.9 copy-done.26
  112.6 0.9 copy-done.29
  113.6 8.9 %forward.1 = (bf16[128,1024]{1,0:T(8,128)(2,1)S(1)}, f32[8,8,128]{2,1,0:T(8,128)S(1)}, bf16[4,128,256]{2,1,0:T(8,128)(2,1)S(1)}) custom-call(s32[13]{0:T(128)S(1)} %concatenate.3.where, bf16[128,1024]{1,0:T(8,128)(2,1)S(1)} %bitcast.42, bf16[128,1024]{1,0:T(8,128)(2,1)S(1)} %bitcast.35, bf16[128,1024]{1,0:T(8,128)(2,1)S(1)} %bitcast.38, ...), custom_call_target="tpu_custom_call" | custom-call | tf_op jit(solution)/shard_map/forward/pallas_call | solution.py:181
  123.2 0.7 copy-done.34
  123.9 3.4 %all-to-all-start.3 = ((bf16[4,128,256]{2,1,0:T(8,128)(2,1)}), bf16[4,128,256]{2,1,0:T(8,128)(2,1)S(1)}, u32[]{:S(2)}, u32[]{:S(2)}) async-start(bf16[4,128,256]{2,1,0:T(8,128)(2,1)} %copy-done.34), calls=%async_computation.3 | async-start | bytes 524288 | tf_op jit(solution)/shard_map/all_to_all | solution.py:424
  127.4 0.9 copy-done.9
  128.3 0.9 copy-done.12
  129.3 0.9 copy-done.15
  130.2 0.9 copy-done.18
  131.2 0.9 copy-done.21
  132.1 0.9 copy-done.24
  133.1 0.9 copy-done.27
  134.0 0.9 copy-done.30
  135.0 0.9 copy-done.33
  135.9 13.0 %backward.1 = (bf16[128,1024]{1,0:T(8,128)(2,1)}, f32[2,128,1024]{2,1,0:T(8,128)}, bf16[2,64,1024]{2,1,0:T(8,128)(2,1)S(1)}, bf16[2,64,1024]{2,1,0:T(8,128)(2,1)...) custom-call(s32[13]{0:T(128)S(1)} %concatenate.3.where, ...), custom_call_target="tpu_custom_call" | custom-call | tf_op jit(solution)/shard_map/backward/pallas_call | solution.py:249
  149.0 0.7 copy-done.37
  150.4 2.0 copy-done.5
  152.5 1.3 weight.1
  153.8 32.2 %all_to_all.37.x = bf16[8,96,1024]{2,1,0:T(8,128)(2,1)S(1)} all-to-all(bf16[8,96,1024]{2,1,0:T(8,128)(2,1)S(1)} %weight.1), channel_id=1, replica_groups={{0,4,64,68,128,132,192,196},{8,12,72,76,136,140,200,204},{16,20,80,84,1..., dimensions={0} | all-to-all | bytes 3145728 | tf_op jit(solution)/shard_map/all_to_all | solution.py:39
  186.0 1.9 route_z.1
  187.9 3.7 %all-to-all-start.5 = ((bf16[8,48,1024]{2,1,0:T(8,128)(2,1)}), bf16[8,48,1024]{2,1,0:T(8,128)(2,1)S(1)}, u32[]{:S(2)}, u32[]{:S(2)}) async-start(bf16[8,48,1024]{2,1,0:T(8,128)(2,1)} %route_z.1), calls=%async_computation.5 | async-start | bytes 1572864 | tf_op jit(solution)/shard_map/all_to_all | solution.py:39
  191.6 1.3 collective-permute-start.10
  192.8 1.8 collective-permute-start.11
  194.7 2.4 collective-permute-start.12
  197.0 16.1 %all-to-all-done.5.x = bf16[8,48,1024]{2,1,0:T(8,128)(2,1)S(1)} async-done(((bf16[8,48,1024]{2,1,0:T(8,128)(2,1)}), bf16[8,48,1024]{2,1,0:T(8,128)(2,1)S(1)}, u32[]{:S(2)}, u32[]{:S(2)}) %all-to-all-start.5) | async-done | bytes 786464 | tf_op jit(solution)/shard_map/all_to_all | solution.py:39
  213.1 1.5 route_yx.1
  214.7 4.9 %all-to-all-start.6 = ((bf16[8,32,1024]{2,1,0:T(8,128)(2,1)}), bf16[8,32,1024]{2,1,0:T(8,128)(2,1)S(1)}, u32[]{:S(2)}, u32[]{:S(2)}) async-start(bf16[8,32,1024]{2,1,0:T(8,128)(2,1)} %get-tuple-element.57), calls=%async_computation.6 | async-start | bytes 1048576 | tf_op jit(solution)/shard_map/all_to_all | solution.py:39
  219.6 1.9 collective-permute-start.13
  221.7 2.8 %collective-permute-start.15 = (bf16[2,64,1024]{2,1,0:T(8,128)(2,1)}, bf16[2,64,1024]{2,1,0:T(8,128)(2,1)S(1)}, u32[]{:S(2)}, u32[]{:S(2)}) collective-permute-start(bf16[2,64,1024]{2,1,0:T(8,128)(2,1)} %copy-done.39), channel_id=1, source_target_pairs={{0,128},{4,132},{8,136},{12,140},{16,144},{20,148},{24,152},{28,15... | collective-permute-start | bytes 786440 | tf_op jit(solution)/shard_map/ppermute | solution.py:47
  224.4 3.0 %collective-permute-start.8 = (bf16[2,64,1024]{2,1,0:T(8,128)(2,1)}, bf16[2,64,1024]{2,1,0:T(8,128)(2,1)S(1)}, u32[]{:S(2)}, u32[]{:S(2)}) collective-permute-start(bf16[2,64,1024]{2,1,0:T(8,128)(2,1)} %copy-done.38), channel_id=1, source_target_pairs={{0,4},{4,8},{8,12},{12,16},{16,20},{20,24},{24,28},{28,32},{32,36}... | collective-permute-start | bytes 786440 | tf_op jit(solution)/shard_map/ppermute | solution.py:43
  227.4 4.3 %collective-permute-start.9 = (bf16[2,64,1024]{2,1,0:T(8,128)(2,1)}, bf16[2,64,1024]{2,1,0:T(8,128)(2,1)S(1)}, u32[]{:S(2)}, u32[]{:S(2)}) collective-permute-start(bf16[2,64,1024]{2,1,0:T(8,128)(2,1)} %copy-done.37), channel_id=1, source_target_pairs={{0,252},{4,0},{8,4},{12,8},{16,12},{20,16},{24,20},{28,24},{32,28}... | collective-permute-start | bytes 786440 | tf_op jit(solution)/shard_map/ppermute | solution.py:43
  231.7 2.8 %collective-permute-done.13.rest_3_ = bf16[2,64,1024]{2,1,0:T(8,128)(2,1)S(1)} collective-permute-done((bf16[2,64,1024]{2,1,0:T(8,128)(2,1)}, bf16[2,64,1024]{2,1,0:T(8,128)(2,1)S(1)}, u32[]{:S(2)}, u32[]{:S(2)}) %collective-permute-start.13) | collective-permute-done | bytes 262176 | tf_op jit(solution)/shard_map/ppermute | solution.py:47
  234.5 4.7 %collective-permute-done.15.rest_5_ = bf16[2,64,1024]{2,1,0:T(8,128)(2,1)S(1)} collective-permute-done((bf16[2,64,1024]{2,1,0:T(8,128)(2,1)}, bf16[2,64,1024]{2,1,0:T(8,128)(2,1)S(1)}, u32[]{:S(2)}, u32[]{:S(2)}) %collective-permute-start.15) | collective-permute-done | bytes 262176 | tf_op jit(solution)/shard_map/ppermute | solution.py:47
  239.2 6.1 %collective-permute-done.8.left = bf16[2,64,1024]{2,1,0:T(8,128)(2,1)S(1)} collective-permute-done((bf16[2,64,1024]{2,1,0:T(8,128)(2,1)}, bf16[2,64,1024]{2,1,0:T(8,128)(2,1)S(1)}, u32[]{:S(2)}, u32[]{:S(2)}) %collective-permute-start.8) | collective-permute-done | bytes 262176 | tf_op jit(solution)/shard_map/ppermute | solution.py:43
  246.4 0.9 copy-done.36
  247.3 2.5 finish.1
  (89 shorter events, 8.5 us)
Async XLA Ops:
  7.2 120.2 %all-gather.4.cloned.1.call-start = ((), (), s32[]{:S(2)}) async-start(), calls=%async_computation.7 | async-start | bytes 5242880 | tf_op jit(solution)/shard_map/all_gather | solution.py:415
  7.9 142.5 %all-gather.6.cloned.1.call-start = ((), (), s32[]{:S(2)}) async-start(), calls=%async_computation.8 | async-start | bytes 2621440 | tf_op jit(solution)/shard_map/all_gather | solution.py:414
  10.8 1.0 copy-start.1
  11.7 0.9 copy-start.3
  62.3 43.5 %copy-start.2 = (bf16[1,128,1024]{2,1,0:T(8,128)(2,1)S(1)}, bf16[1,128,1024]{2,1,0:T(8,128)(2,1)}, u32[]{:S(2)}) copy-start(bf16[1,128,1024]{2,1,0:T(8,128)(2,1)} %param.8) | copy-start | bytes 786436
  62.3 43.5 %copy-start.4 = (bf16[1,128,1024]{2,1,0:T(8,128)(2,1)S(1)}, bf16[1,128,1024]{2,1,0:T(8,128)(2,1)}, u32[]{:S(2)}) copy-start(bf16[1,128,1024]{2,1,0:T(8,128)(2,1)} %param.9) | copy-start | bytes 786436
  62.3 43.5 %copy-start.6 = (bf16[1,128,1024]{2,1,0:T(8,128)(2,1)S(1)}, bf16[1,128,1024]{2,1,0:T(8,128)(2,1)}, u32[]{:S(2)}) copy-start(bf16[1,128,1024]{2,1,0:T(8,128)(2,1)} %param.7) | copy-start | bytes 786436
  63.2 42.6 %all-to-all-start.2 = ((bf16[8,32,1024]{2,1,0:T(8,128)(2,1)}), bf16[8,32,1024]{2,1,0:T(8,128)(2,1)S(1)}, u32[]{:S(2)}, u32[]{:S(2)}) async-start(bf16[8,32,1024]{2,1,0:T(8,128)(2,1)} %relay.3), calls=%async_computation.2 | async-start | bytes 1048576 | tf_op jit(solution)/shard_map/all_to_all | solution.py:39
  66.7 18.4 %collective-permute-start = (bf16[2,64,1024]{2,1,0:T(8,128)(2,1)S(1)}, bf16[2,64,1024]{2,1,0:T(8,128)(2,1)S(1)}, u32[]{:S(2)}, u32[]{:S(2)}) collective-permute-start(bf16[2,64,1024]{2,1,0:T(8,128)(2,1)S(1)} %get-tuple-element.33), channel_id=1, source_target_pairs={{0,4},{4,8},{8,12},{12,16},{16,20},{20,24},{24,28},{28,32},{32,36}... | collective-permute-start | bytes 786440 | tf_op jit(solution)/shard_map/ppermute | solution.py:43
  67.8 20.7 %collective-permute-start.1 = (bf16[2,64,1024]{2,1,0:T(8,128)(2,1)S(1)}, bf16[2,64,1024]{2,1,0:T(8,128)(2,1)S(1)}, u32[]{:S(2)}, u32[]{:S(2)}) collective-permute-start(bf16[2,64,1024]{2,1,0:T(8,128)(2,1)S(1)} %get-tuple-element.34), channel_id=1, source_target_pairs={{0,252},{4,0},{8,4},{12,8},{16,12},{20,16},{24,20},{28,24},{32,28}... | collective-permute-start | bytes 786440 | tf_op jit(solution)/shard_map/ppermute | solution.py:43
  73.3 17.1 %collective-permute-start.2 = (bf16[2,64,1024]{2,1,0:T(8,128)(2,1)S(1)}, bf16[2,64,1024]{2,1,0:T(8,128)(2,1)S(1)}, u32[]{:S(2)}, u32[]{:S(2)}) collective-permute-start(bf16[2,64,1024]{2,1,0:T(8,128)(2,1)S(1)} %get-tuple-element.35), channel_id=1, source_target_pairs={{0,4},{4,0},{8,12},{12,8},{16,20},{20,16},{24,28},{28,24},{32,36},... | collective-permute-start | bytes 786440 | tf_op jit(solution)/shard_map/ppermute | solution.py:47
  73.3 25.8 %collective-permute-start.3 = (bf16[2,64,1024]{2,1,0:T(8,128)(2,1)}, bf16[2,64,1024]{2,1,0:T(8,128)(2,1)S(1)}, u32[]{:S(2)}, u32[]{:S(2)}) collective-permute-start(bf16[2,64,1024]{2,1,0:T(8,128)(2,1)} %get-tuple-element.36), channel_id=1, source_target_pairs={{0,8},{4,12},{8,0},{12,4},{16,24},{20,28},{24,16},{28,20},{32,40},... | collective-permute-start | bytes 786440 | tf_op jit(solution)/shard_map/ppermute | solution.py:47
  73.3 26.5 %collective-permute-start.4 = (bf16[2,64,1024]{2,1,0:T(8,128)(2,1)}, bf16[2,64,1024]{2,1,0:T(8,128)(2,1)S(1)}, u32[]{:S(2)}, u32[]{:S(2)}) collective-permute-start(bf16[2,64,1024]{2,1,0:T(8,128)(2,1)} %get-tuple-element.37), channel_id=1, source_target_pairs={{0,16},{4,20},{8,24},{12,28},{16,0},{20,4},{24,8},{28,12},{32,48},... | collective-permute-start | bytes 786440 | tf_op jit(solution)/shard_map/ppermute | solution.py:47
  85.8 17.8 %collective-permute-start.5 = (bf16[2,64,1024]{2,1,0:T(8,128)(2,1)}, bf16[2,64,1024]{2,1,0:T(8,128)(2,1)S(1)}, u32[]{:S(2)}, u32[]{:S(2)}) collective-permute-start(bf16[2,64,1024]{2,1,0:T(8,128)(2,1)} %get-tuple-element.38), channel_id=1, source_target_pairs={{0,32},{4,36},{8,40},{12,44},{16,48},{20,52},{24,56},{28,60},{32,0... | collective-permute-start | bytes 786440 | tf_op jit(solution)/shard_map/ppermute | solution.py:47
  89.1 15.2 %collective-permute-start.6 = (bf16[2,64,1024]{2,1,0:T(8,128)(2,1)}, bf16[2,64,1024]{2,1,0:T(8,128)(2,1)S(1)}, u32[]{:S(2)}, u32[]{:S(2)}) collective-permute-start(bf16[2,64,1024]{2,1,0:T(8,128)(2,1)} %get-tuple-element.39), channel_id=1, source_target_pairs={{0,64},{4,68},{8,72},{12,76},{16,80},{20,84},{24,88},{28,92},{32,9... | collective-permute-start | bytes 786440 | tf_op jit(solution)/shard_map/ppermute | solution.py:47
  90.4 0.7 copy-start.13
  91.1 13.9 %collective-permute-start.7 = (bf16[2,64,1024]{2,1,0:T(8,128)(2,1)}, bf16[2,64,1024]{2,1,0:T(8,128)(2,1)S(1)}, u32[]{:S(2)}, u32[]{:S(2)}) collective-permute-start(bf16[2,64,1024]{2,1,0:T(8,128)(2,1)} %get-tuple-element.40), channel_id=1, source_target_pairs={{0,128},{4,132},{8,136},{12,140},{16,144},{20,148},{24,152},{28,15... | collective-permute-start | bytes 786440 | tf_op jit(solution)/shard_map/ppermute | solution.py:47
  99.1 0.7 copy-start.16
  99.8 0.7 copy-start.19
  103.6 0.7 copy-start.22
  104.3 0.7 copy-start.25
  105.1 0.7 copy-start.28
  105.8 16.7 %copy-start = (bf16[8,32,1024]{2,1,0:T(8,128)(2,1)}, bf16[8,32,1024]{2,1,0:T(8,128)(2,1)S(1)}, u32[]{:S(2)}) copy-start(bf16[8,32,1024]{2,1,0:T(8,128)(2,1)S(1)} %all-to-all-done.2) | copy-start | bytes 1572868
  105.8 1.1 copy-start.8
  106.9 0.9 copy-start.11
  107.9 0.9 copy-start.14
  108.8 0.9 copy-start.17
  109.8 0.9 copy-start.20
  110.7 0.9 copy-start.23
  111.7 0.9 copy-start.26
  112.6 0.9 copy-start.29
  122.5 0.7 copy-start.32
  123.2 0.7 copy-start.34
  123.9 26.5 %all-to-all-start.3 = ((bf16[4,128,256]{2,1,0:T(8,128)(2,1)}), bf16[4,128,256]{2,1,0:T(8,128)(2,1)S(1)}, u32[]{:S(2)}, u32[]{:S(2)}) async-start(bf16[4,128,256]{2,1,0:T(8,128)(2,1)} %copy-done.34), calls=%async_computation.3 | async-start | bytes 524288 | tf_op jit(solution)/shard_map/all_to_all | solution.py:424
  127.4 1.0 copy-start.9
  128.3 0.9 copy-start.12
  129.3 0.9 copy-start.15
  130.2 0.9 copy-start.18
  131.2 0.9 copy-start.21
  132.1 0.9 copy-start.24
  133.1 0.9 copy-start.27
  134.0 0.9 copy-start.30
  135.0 0.9 copy-start.33
  148.9 0.7 copy-start.37
  150.4 3.4 %copy-start.43 = (bf16[2,64,1024]{2,1,0:T(8,128)(2,1)}, bf16[2,64,1024]{2,1,0:T(8,128)(2,1)S(1)}, u32[]{:S(2)}) copy-start(bf16[2,64,1024]{2,1,0:T(8,128)(2,1)S(1)} %get-tuple-element.50) | copy-start | bytes 786436
  150.4 37.5 %copy-start.41 = (bf16[2,64,1024]{2,1,0:T(8,128)(2,1)}, bf16[2,64,1024]{2,1,0:T(8,128)(2,1)S(1)}, u32[]{:S(2)}) copy-start(bf16[2,64,1024]{2,1,0:T(8,128)(2,1)S(1)} %get-tuple-element.52) | copy-start | bytes 786436
  150.4 37.5 %copy-start.42 = (bf16[2,64,1024]{2,1,0:T(8,128)(2,1)}, bf16[2,64,1024]{2,1,0:T(8,128)(2,1)S(1)}, u32[]{:S(2)}) copy-start(bf16[2,64,1024]{2,1,0:T(8,128)(2,1)S(1)} %get-tuple-element.51) | copy-start | bytes 786436
  150.4 64.3 %copy-start.39 = (bf16[2,64,1024]{2,1,0:T(8,128)(2,1)}, bf16[2,64,1024]{2,1,0:T(8,128)(2,1)S(1)}, u32[]{:S(2)}) copy-start(bf16[2,64,1024]{2,1,0:T(8,128)(2,1)S(1)} %get-tuple-element.54) | copy-start | bytes 786436
  150.4 64.3 %copy-start.40 = (bf16[2,64,1024]{2,1,0:T(8,128)(2,1)}, bf16[2,64,1024]{2,1,0:T(8,128)(2,1)S(1)}, u32[]{:S(2)}) copy-start(bf16[2,64,1024]{2,1,0:T(8,128)(2,1)S(1)} %get-tuple-element.53) | copy-start | bytes 786436
  150.4 2.0 copy-start.5
  186.0 6.8 %copy-start.44 = (bf16[2,64,1024]{2,1,0:T(8,128)(2,1)S(1)}, bf16[2,64,1024]{2,1,0:T(8,128)(2,1)}, u32[]{:S(2)}) copy-start(bf16[2,64,1024]{2,1,0:T(8,128)(2,1)} %copy-done.43) | copy-start | bytes 786436
  187.9 58.5 %copy-start.31 = (f32[2,128,1024]{2,1,0:T(8,128)S(1)}, f32[2,128,1024]{2,1,0:T(8,128)}, u32[]{:S(2)}) copy-start(f32[2,128,1024]{2,1,0:T(8,128)} %get-tuple-element.46.own) | copy-start | bytes 3145732
  187.9 25.3 %all-to-all-start.5 = ((bf16[8,48,1024]{2,1,0:T(8,128)(2,1)}), bf16[8,48,1024]{2,1,0:T(8,128)(2,1)S(1)}, u32[]{:S(2)}, u32[]{:S(2)}) async-start(bf16[8,48,1024]{2,1,0:T(8,128)(2,1)} %route_z.1), calls=%async_computation.5 | async-start | bytes 1572864 | tf_op jit(solution)/shard_map/all_to_all | solution.py:39
  191.6 30.1 %collective-permute-start.10 = (bf16[2,64,1024]{2,1,0:T(8,128)(2,1)}, bf16[2,64,1024]{2,1,0:T(8,128)(2,1)S(1)}, u32[]{:S(2)}, u32[]{:S(2)}) collective-permute-start(bf16[2,64,1024]{2,1,0:T(8,128)(2,1)} %get-tuple-element.49), channel_id=1, source_target_pairs={{0,4},{4,0},{8,12},{12,8},{16,20},{20,16},{24,28},{28,24},{32,36},... | collective-permute-start | bytes 786440 | tf_op jit(solution)/shard_map/ppermute | solution.py:47
  192.8 31.6 %collective-permute-start.11 = (bf16[2,64,1024]{2,1,0:T(8,128)(2,1)S(1)}, bf16[2,64,1024]{2,1,0:T(8,128)(2,1)S(1)}, u32[]{:S(2)}, u32[]{:S(2)}) collective-permute-start(bf16[2,64,1024]{2,1,0:T(8,128)(2,1)S(1)} %copy-done.44), channel_id=1, source_target_pairs={{0,8},{4,12},{8,0},{12,4},{16,24},{20,28},{24,16},{28,20},{32,40},... | collective-permute-start | bytes 786440 | tf_op jit(solution)/shard_map/ppermute | solution.py:47
  194.7 32.7 %collective-permute-start.12 = (bf16[2,64,1024]{2,1,0:T(8,128)(2,1)}, bf16[2,64,1024]{2,1,0:T(8,128)(2,1)S(1)}, u32[]{:S(2)}, u32[]{:S(2)}) collective-permute-start(bf16[2,64,1024]{2,1,0:T(8,128)(2,1)} %copy-done.42), channel_id=1, source_target_pairs={{0,16},{4,20},{8,24},{12,28},{16,0},{20,4},{24,8},{28,12},{32,48},... | collective-permute-start | bytes 786440 | tf_op jit(solution)/shard_map/ppermute | solution.py:47
  214.7 31.7 %all-to-all-start.6 = ((bf16[8,32,1024]{2,1,0:T(8,128)(2,1)}), bf16[8,32,1024]{2,1,0:T(8,128)(2,1)S(1)}, u32[]{:S(2)}, u32[]{:S(2)}) async-start(bf16[8,32,1024]{2,1,0:T(8,128)(2,1)} %get-tuple-element.57), calls=%async_computation.6 | async-start | bytes 1048576 | tf_op jit(solution)/shard_map/all_to_all | solution.py:39
  219.6 14.9 %collective-permute-start.13 = (bf16[2,64,1024]{2,1,0:T(8,128)(2,1)}, bf16[2,64,1024]{2,1,0:T(8,128)(2,1)S(1)}, u32[]{:S(2)}, u32[]{:S(2)}) collective-permute-start(bf16[2,64,1024]{2,1,0:T(8,128)(2,1)} %copy-done.41), channel_id=1, source_target_pairs={{0,32},{4,36},{8,40},{12,44},{16,48},{20,52},{24,56},{28,60},{32,0... | collective-permute-start | bytes 786440 | tf_op jit(solution)/shard_map/ppermute | solution.py:47
  221.5 13.0 %collective-permute-start.14 = (bf16[2,64,1024]{2,1,0:T(8,128)(2,1)}, bf16[2,64,1024]{2,1,0:T(8,128)(2,1)S(1)}, u32[]{:S(2)}, u32[]{:S(2)}) collective-permute-start(bf16[2,64,1024]{2,1,0:T(8,128)(2,1)} %copy-done.40), channel_id=1, source_target_pairs={{0,64},{4,68},{8,72},{12,76},{16,80},{20,84},{24,88},{28,92},{32,9... | collective-permute-start | bytes 786440 | tf_op jit(solution)/shard_map/ppermute | solution.py:47
  221.7 17.5 %collective-permute-start.15 = (bf16[2,64,1024]{2,1,0:T(8,128)(2,1)}, bf16[2,64,1024]{2,1,0:T(8,128)(2,1)S(1)}, u32[]{:S(2)}, u32[]{:S(2)}) collective-permute-start(bf16[2,64,1024]{2,1,0:T(8,128)(2,1)} %copy-done.39), channel_id=1, source_target_pairs={{0,128},{4,132},{8,136},{12,140},{16,144},{20,148},{24,152},{28,15... | collective-permute-start | bytes 786440 | tf_op jit(solution)/shard_map/ppermute | solution.py:47
  224.4 20.8 %collective-permute-start.8 = (bf16[2,64,1024]{2,1,0:T(8,128)(2,1)}, bf16[2,64,1024]{2,1,0:T(8,128)(2,1)S(1)}, u32[]{:S(2)}, u32[]{:S(2)}) collective-permute-start(bf16[2,64,1024]{2,1,0:T(8,128)(2,1)} %copy-done.38), channel_id=1, source_target_pairs={{0,4},{4,8},{8,12},{12,16},{16,20},{20,24},{24,28},{28,32},{32,36}... | collective-permute-start | bytes 786440 | tf_op jit(solution)/shard_map/ppermute | solution.py:43
  227.4 18.3 %collective-permute-start.9 = (bf16[2,64,1024]{2,1,0:T(8,128)(2,1)}, bf16[2,64,1024]{2,1,0:T(8,128)(2,1)S(1)}, u32[]{:S(2)}, u32[]{:S(2)}) collective-permute-start(bf16[2,64,1024]{2,1,0:T(8,128)(2,1)} %copy-done.37), channel_id=1, source_target_pairs={{0,252},{4,0},{8,4},{12,8},{16,12},{20,16},{24,20},{28,24},{32,28}... | collective-permute-start | bytes 786440 | tf_op jit(solution)/shard_map/ppermute | solution.py:43
  245.7 0.7 copy-start.35
  246.4 1.0 copy-start.36
  (3 other events, 2.1 us)
Sparse Core Ops, SparseCore 0:
  9.8 57.6 all-gather.3
  69.3 34.3 all-gather.5

commit v3 on v2

v3 whole, which is shorter than its diff:
```python
import jax
import jax.numpy as jnp
from jax import lax
from jax.experimental import pallas as pl
from jax.experimental.pallas import tpu as pltpu
from jax.sharding import PartitionSpec as P

HEADS = 8
HEAD_DIM = 128
BLK = 64
GLOB = 2
BITS = 6
TOK = 128
WIDTH = HEADS * HEAD_DIM
D = 2048
KEYS = 768
SCALE = HEAD_DIM ** (-0.5)
BF = jnp.bfloat16
F32 = jnp.float32
STEP = 4
WIDE = STEP * HEAD_DIM
ROWS = (((1,), (1,)), ((), ()))
COLS = (((0,), (0,)), ((), ()))
PLAIN = (((1,), (0,)), ((), ()))
VMEM_LIMIT = 20 * 1024 * 1024


def stretch_id(y, z, x):
    return y * 16 + z * 2 + x


Z_GROUPS = [[stretch_id(y, z, x) for z in range(8)] for y in range(4) for x in range(2)]
Y_GROUPS = [[stretch_id(y, z, x) for y in range(4)] for z in range(8) for x in range(2)]
YX_GROUPS = [[stretch_id(y, z, x) for y in range(4) for x in range(2)] for z in range(8)]


def mm(left, right, dims):
    return lax.dot_general(left, right, dims, preferred_element_type=F32)


def trade(value, groups):
    return lax.all_to_all(value, "seq", 0, 0, axis_index_groups=groups, tiled=True)


def shifted(value, steps):
    return lax.ppermute(value, "seq", [(s, (s + steps) % 64) for s in range(64)])


def swapped(value, bit):
    return lax.ppermute(value, "seq", [(s, s ^ (1 << bit)) for s in range(64)])


def across(value, flip):
    return lax.ppermute(value, "rep", [(r, r ^ flip) for r in range(4)])


def beside(value):
    pairs = [(s * 4 + r, (s ^ 1) * 4 + (r ^ 2)) for s in range(64) for r in range(4)]
    return lax.ppermute(value, ("seq", "rep"), pairs)


def far(shape, dtype=BF):
    return pltpu.HBM(shape, dtype)


def from_hbm(*values):
    return [pltpu.with_memory_space_constraint(x, pltpu.HBM) for x in values]


def smem():
    return pl.BlockSpec(memory_space=pltpu.SMEM)


def params(**kw):
    return pltpu.CompilerParams(vmem_limit_bytes=VMEM_LIMIT, **kw)


def where_of(rand_slot, global_ids):
    me = lax.axis_index("seq")
    owner = global_ids // 2
    here = jnp.where(owner == me, global_ids % 2, -1)
    my_m = (me // 16) * 2 + me % 2
    tail = jnp.stack([(my_m // 2) % 2, lax.axis_index("rep"), me % 2])
    return jnp.concatenate(
        [rand_slot, here, (owner // 2) % 8, (owner // 16) * 2 + owner % 2, tail]
    ).astype(jnp.int32)


def pick_kernel(where, k_ref, v_ref, *outs):
    for b in range(BITS):
        rows = pl.ds(pl.multiple_of(where[b] * BLK, BLK), BLK)
        outs[b][0] = k_ref[rows, :]
        outs[b][1] = v_ref[rows, :]
    first, last, picked = outs[BITS:]
    first[0] = k_ref[0:BLK, :]
    first[1] = v_ref[0:BLK, :]
    last[0] = k_ref[BLK : 2 * BLK, :]
    last[1] = v_ref[BLK : 2 * BLK, :]
    for g in range(GLOB):
        here = where[6 + g]

        @pl.when(here < 0)
        def _():
            picked[0, g] = jnp.zeros((BLK, WIDTH), BF)
            picked[1, g] = jnp.zeros((BLK, WIDTH), BF)

        @pl.when(here >= 0)
        def _():
            rows = pl.ds(pl.multiple_of(jnp.maximum(here, 0) * BLK, BLK), BLK)
            picked[0, g] = k_ref[rows, :]
            picked[1, g] = v_ref[rows, :]


def pick(where, keys, values):
    block = far((2, BLK, WIDTH))
    outs = [block] * (BITS + 2) + [far((2, GLOB, BLK, WIDTH))]
    vm = pl.BlockSpec(memory_space=pltpu.VMEM)
    return pl.pallas_call(
        pick_kernel,
        out_shape=outs,
        in_specs=[smem(), vm, vm],
        out_specs=[vm] * len(outs),
        compiler_params=params(),
        name="pick",
    )(where, keys, values)


def relay_kernel(x_ref, o_ref):
    total = jnp.sum(x_ref[...].astype(F32), axis=0).astype(BF)
    for j in range(8):
        o_ref[j] = total


def relay(x):
    return pl.pallas_call(
        relay_kernel,
        out_shape=far(x.shape),
        compiler_params=params(),
        name="relay",
    )(x)


def gather_heads(dst, c, cols, own, lo, hi, rand, glob):
    dst[0:64, :] = lo[c, :, cols]
    dst[64:192, :] = own[:, cols]
    dst[192:256, :] = hi[c, :, cols]
    dst[256:384, :] = glob[c, :, cols]
    for b in range(BITS):
        dst[384 + 64 * b : 448 + 64 * b, :] = rand[b][c, :, cols]


def fill_bias(where, bias):
    lane = lax.broadcasted_iota(jnp.int32, (BLK, TOK), 1) // BLK
    for kb in range(12):
        if kb < 4:
            keep = jnp.logical_and(lane <= kb, lane >= kb - 2)
        elif kb < 6:
            keep = lane >= 0
        else:
            keep = lane == where[kb - 6]
        bias[kb * BLK : (kb + 1) * BLK, :] = jnp.where(keep, 0.0, -1e30).astype(F32)


def forward_kernel(where, q, k, v, lo, hi, *rest):
    rand, rest = rest[:BITS], rest[BITS:]
    glob, perm, attn, stats, *ordered, ks, vs, bias, acc = rest
    step = pl.program_id(0)

    @pl.when(step == 0)
    def _():
        fill_bias(where, bias)

    for i in range(STEP):
        cols = slice(i * HEAD_DIM, (i + 1) * HEAD_DIM)
        gather_heads(ks.at[i], 0, cols, k, lo, hi, rand, glob)
        gather_heads(vs.at[i], 1, cols, v, lo, hi, rand, glob)
        scores = mm(ks[i], q[:, cols], ROWS) * SCALE + bias[...]
        top = jnp.max(scores, axis=0, keepdims=True)
        expd = jnp.exp(scores - top)
        inv = 1.0 / jnp.sum(expd, axis=0, keepdims=True)
        probs = (expd * inv).astype(BF)
        attn[:, cols] = mm(probs, vs[i], COLS).astype(BF)
        stats[i, 0:1, :] = top
        stats[i, 1:2, :] = inv

    part = mm(attn[...], perm[...], PLAIN)

    @pl.when(step == 0)
    def _():
        acc[...] = part

    @pl.when(step == HEADS // STEP - 1)
    def _():
        total = acc[...] + part
        for r in range(4):
            ordered[r][...] = total[:, r * 256 : (r + 1) * 256].astype(BF)


def head_specs():
    flat = pl.BlockSpec((TOK, WIDE), lambda h: (0, h))
    pair = pl.BlockSpec((2, BLK, WIDE), lambda h: (0, 0, h))
    both = pl.BlockSpec((2, TOK, WIDE), lambda h: (0, 0, h))
    return flat, pair, both


def forward(where, q, k, v, lo, hi, rand, glob, perm):
    flat, pair, both = head_specs()
    return pl.pallas_call(
        forward_kernel,
        grid=(HEADS // STEP,),
        in_specs=[smem(), flat, flat, flat, pair, pair]
        + [pair] * BITS
        + [both, pl.BlockSpec((WIDE, WIDTH), lambda h: (h, 0))],
        out_specs=[
            flat,
            pl.BlockSpec((STEP, 8, TOK), lambda h: (h, 0, 0)),
        ]
        + [pl.BlockSpec((TOK, 256), lambda h: (0, 0))] * 4,
        out_shape=[
            far((TOK, WIDTH)),
            far((HEADS, 8, TOK), F32),
        ]
        + [jax.ShapeDtypeStruct((TOK, 256), BF)] * 4,
        scratch_shapes=[
            pltpu.VMEM((STEP, KEYS, HEAD_DIM), BF),
            pltpu.VMEM((STEP, KEYS, HEAD_DIM), BF),
            pltpu.VMEM((KEYS, TOK), F32),
            pltpu.VMEM((TOK, WIDTH), F32),
        ],
        compiler_params=params(dimension_semantics=("arbitrary",)),
        name="forward",
    )(where, q, k, v, lo, hi, *rand, glob, perm)


def backward_kernel(where, q, k, v, lo, hi, *rest):
    rand, rest = rest[:BITS], rest[BITS:]
    glob, stats, d_attn_ref, dq, down, dlo, dhi = rest[:7]
    drand, rest = rest[7 : 7 + BITS], rest[7 + BITS :]
    dglob, ks, vs, bias = rest

    @pl.when(pl.program_id(0) == 0)
    def _():
        fill_bias(where, bias)

    for i in range(STEP):
        cols = slice(i * HEAD_DIM, (i + 1) * HEAD_DIM)
        gather_heads(ks.at[i], 0, cols, k, lo, hi, rand, glob)
        gather_heads(vs.at[i], 1, cols, v, lo, hi, rand, glob)
        d_attn = d_attn_ref[:, cols]
        scores = mm(ks[i], q[:, cols], ROWS) * SCALE + bias[...]
        probs = jnp.exp(scores - stats[i, 0:1, :]) * stats[i, 1:2, :]
        probs_b = probs.astype(BF)
        dprob = mm(vs[i], d_attn, ROWS)
        delta = jnp.sum(dprob * probs, axis=0, keepdims=True)
        dscore = (probs * (dprob - delta) * SCALE).astype(BF)
        dq[:, cols] = mm(dscore, ks[i], COLS).astype(BF)
        for c, grad in ((0, mm(dscore, q[:, cols], PLAIN)), (1, mm(probs_b, d_attn, PLAIN))):
            dlo[c, :, cols] = grad[0:64].astype(BF)
            down[c, :, cols] = grad[64:192]
            dhi[c, :, cols] = grad[192:256].astype(BF)
            dglob[c, :, cols] = grad[256:384].astype(BF)
            for b in range(BITS):
                drand[b][c, :, cols] = grad[384 + 64 * b : 448 + 64 * b].astype(BF)


def backward(where, q, k, v, lo, hi, rand, glob, stats, d_attn):
    flat, pair, both = head_specs()
    block = far((2, BLK, WIDTH))
    outs = pl.pallas_call(
        backward_kernel,
        grid=(HEADS // STEP,),
        in_specs=[smem(), flat, flat, flat, pair, pair]
        + [pair] * BITS
        + [both, pl.BlockSpec((STEP, 8, TOK), lambda h: (h, 0, 0)), flat],
        out_specs=[flat, both, pair, pair] + [pair] * BITS + [both],
        out_shape=[far((TOK, WIDTH)), far((2, TOK, WIDTH), F32), block, block]
        + [block] * BITS
        + [far((2, TOK, WIDTH))],
        scratch_shapes=[
            pltpu.VMEM((STEP, KEYS, HEAD_DIM), BF),
            pltpu.VMEM((STEP, KEYS, HEAD_DIM), BF),
            pltpu.VMEM((KEYS, TOK), F32),
        ],
        compiler_params=params(dimension_semantics=("arbitrary",)),
        name="backward",
    )(where, *from_hbm(q, k, v, lo, hi, *rand, glob, stats, d_attn))
    return outs[:4], outs[4 : 4 + BITS], outs[4 + BITS]


def head_of(i, where):
    return ((i // 2) ^ where[13]) * 2 + i % 2


def head_call(kernel, where, parts, extra, extra_spec, out_shape, out_spec, scratch, name):
    w_spec = pl.BlockSpec((HEAD_DIM, D), lambda i, at: (0, 0))
    return pl.pallas_call(
        kernel,
        grid_spec=pltpu.PrefetchScalarGridSpec(
            num_scalar_prefetch=1,
            grid=(HEADS,),
            in_specs=[w_spec] * HEADS + [extra_spec],
            out_specs=out_spec,
            scratch_shapes=scratch,
        ),
        out_shape=out_shape,
        compiler_params=params(dimension_semantics=("arbitrary",)),
        name=name,
    )(where, *parts, extra)


def project_kernel(where, *refs):
    w, (d_out, out) = refs[:HEADS], refs[HEADS:]
    for i in range(HEADS):

        @pl.when(pl.program_id(0) == i)
        def _():
            out[...] = mm(d_out[...], w[i][...], ROWS).astype(BF)


def project(where, parts, d_out):
    return head_call(
        project_kernel,
        where,
        parts,
        d_out,
        pl.BlockSpec((TOK, D), lambda i, at: (0, 0)),
        far((TOK, WIDTH)),
        pl.BlockSpec((TOK, HEAD_DIM), lambda i, at: (0, head_of(i, at))),
        [],
        "project",
    )


def layer_kernel(where, *refs):
    w, (attn, out, acc) = refs[:HEADS], refs[HEADS:]
    for i in range(HEADS):

        @pl.when(pl.program_id(0) == i)
        def _():
            part = mm(attn[...], w[i][...], PLAIN)
            if i == 0:
                acc[...] = part
            elif i < HEADS - 1:
                acc[...] += part
            else:
                out[...] = (acc[...] + part).astype(BF)


def layer_of(where, parts, attn):
    return head_call(
        layer_kernel,
        where,
        parts,
        attn,
        pl.BlockSpec((TOK, HEAD_DIM), lambda i, at: (0, head_of(i, at))),
        far((TOK, D)),
        pl.BlockSpec((TOK, D), lambda i, at: (0, 0)),
        [pltpu.VMEM((TOK, D), F32)],
        "layer",
    )


def weight_kernel(*refs):
    cols, grads, out = refs[:4], refs[4:8], refs[8]
    total = mm(cols[0][...], grads[0][...], COLS)
    for a in range(1, 4):
        total += mm(cols[a][...], grads[a][...], COLS)
    out[...] = total.astype(BF)


def weight_payload(cols, grads):
    return pl.pallas_call(
        weight_kernel,
        grid=(2,),
        in_specs=[pl.BlockSpec((TOK, 256), lambda i: (0, 0))] * 4
        + [pl.BlockSpec((TOK, 1024), lambda i: (0, i))]
        + [pl.BlockSpec((TOK, 1024), lambda i: (1, i))] * 3,
        out_specs=pl.BlockSpec((256, 1024), lambda i: (0, i)),
        out_shape=far((256, D)),
        compiler_params=params(dimension_semantics=("arbitrary",)),
        name="weight",
    )(*cols, *grads)


def route_z_kernel(where, x, w, out, rows, small):
    chunk = jnp.sum(x[...].astype(F32), axis=0)
    rows[...] = w[...].astype(F32)
    target = jnp.where(where[12] == 0, where[8], where[9])
    for j in range(8):
        out[j, 0:32] = jnp.where(target == j, chunk, 0.0).astype(BF)
        small[0:8, :] = rows[8 * j : 8 * j + 8, 0:1024]
        small[8:16, :] = rows[8 * j : 8 * j + 8, 1024:2048]
        out[j, 32:48] = small[...].astype(BF)


def route_z(where, x, w):
    vm = pl.BlockSpec(memory_space=pltpu.VMEM)
    return pl.pallas_call(
        route_z_kernel,
        out_shape=far((8, 48, 1024)),
        in_specs=[smem(), vm, vm],
        out_specs=vm,
        scratch_shapes=[pltpu.VMEM((64, D), F32), pltpu.VMEM((16, 1024), F32)],
        compiler_params=params(),
        name="route_z",
    )(where, x, w)


def route_yx_kernel(where, x, out, mine, other, total):
    total[...] = jnp.sum(x[...].astype(F32), axis=0)
    target = jnp.where(where[12] == 0, where[10], where[11])
    chunk = total[0:32, :]
    for j in range(8):
        out[j] = jnp.where(target == j, chunk, 0.0).astype(BF)
    left = where[14] == 0
    for half in range(2):
        cols = slice(half * 1024, (half + 1) * 1024)
        one = total[32 + 8 * half : 36 + 8 * half, :]
        two = total[36 + 8 * half : 40 + 8 * half, :]
        mine[:, cols] = jnp.where(left, one, two)
        other[:, cols] = jnp.where(left, two, one)


def route_yx(where, x):
    vm = pl.BlockSpec(memory_space=pltpu.VMEM)
    return pl.pallas_call(
        route_yx_kernel,
        out_shape=[far((8, 32, 1024)), far((4, D), F32), far((4, D), F32)],
        in_specs=[smem(), vm],
        out_specs=[vm] * 3,
        scratch_shapes=[pltpu.VMEM((48, 1024), F32)],
        compiler_params=params(),
        name="route_yx",
    )(where, x)


def finish_kernel(where, own, left, right, *rest):
    rand, (glob, mine, other, dk, dv, weight, acc) = rest[:BITS], rest[BITS:]
    weight[...] = mine[...] + other[...]
    acc[...] = own[...]
    acc[:, 0:BLK, :] += left[...].astype(F32)
    acc[:, BLK : 2 * BLK, :] += right[...].astype(F32)
    for b in range(BITS):
        rows = pl.ds(pl.multiple_of(where[b] * BLK, BLK), BLK)
        acc[:, rows, :] += rand[b][...].astype(F32)
    for g in range(GLOB):
        here = where[6 + g]

        @pl.when(here >= 0)
        def _():
            rows = pl.ds(pl.multiple_of(jnp.maximum(here, 0) * BLK, BLK), BLK)
            acc[:, rows, :] += glob[:, g].astype(F32)

    dk[...] = acc[0].astype(BF)
    dv[...] = acc[1].astype(BF)


def finish(where, own, left, right, rand, glob, mine, other):
    wide = 256
    pair = pl.BlockSpec((2, BLK, wide), lambda i: (0, 0, i))
    flat = pl.BlockSpec((TOK, wide), lambda i: (0, i))
    rows = pl.BlockSpec((4, 2 * wide), lambda i: (0, i))
    return pl.pallas_call(
        finish_kernel,
        grid=(WIDTH // wide,),
        in_specs=[smem(), pl.BlockSpec((2, TOK, wide), lambda i: (0, 0, i)), pair, pair]
        + [pair] * BITS
        + [pl.BlockSpec((2, GLOB, BLK, wide), lambda i: (0, 0, 0, i)), rows, rows],
        out_specs=[flat, flat, rows],
        out_shape=[far((TOK, WIDTH)), far((TOK, WIDTH)), far((4, D), F32)],
        scratch_shapes=[pltpu.VMEM((2, TOK, wide), F32)],
        compiler_params=params(dimension_semantics=("arbitrary",)),
        name="finish",
    )(where, *from_hbm(own), left, right, *rand, glob, mine, other)


def feature_order(rep):
    new = jnp.arange(WIDTH, dtype=jnp.int32)
    r, y, x, z, j = (new // 256) ^ rep, (new // 64) % 4, (new // 4) % 2, (new // 8) % 8, new % 4
    old = y * 256 + z * 32 + x * 16 + r * 4 + j
    return (jnp.arange(WIDTH, dtype=jnp.int32)[:, None] == old[None, :]).astype(BF)


def together(*values):
    return lax.optimization_barrier(values)


def per_device(queries, keys, values, w_out, d_out, rand_slot, global_ids):
    q, k, v, grad_out = queries[0], keys[0], values[0], d_out[0]
    where = where_of(rand_slot[0, 0], global_ids[0])
    *chosen, first, last, picked = pick(where, k, v)
    spread = trade(picked.reshape(8, 32, WIDTH), Z_GROUPS)
    mixed = jnp.concatenate([w_out[:HEAD_DIM], grad_out])
    upper = w_out[HEAD_DIM:]
    mixed2 = across(mixed, 2)
    upper2 = beside(upper)
    mixed1 = across(mixed, 1)
    upper1 = across(upper, 1)
    rand = [swapped(chosen[b], b) for b in range(BITS)]
    lo = shifted(last, 1)
    hi = shifted(first, -1)
    spread, rand[4], rand[1], mixed1, upper1 = together(spread, rand[4], rand[1], mixed1, upper1)
    spread = trade(relay(spread), YX_GROUPS)
    spread, rand[3], rand[5], mixed2, upper2 = together(spread, rand[3], rand[5], mixed2, upper2)
    mixed3 = across(mixed2, 1)
    upper3 = across(upper2, 1)
    glob = trade(relay(spread), Z_GROUPS).reshape(2, GLOB * BLK, WIDTH)
    parts = (w_out, upper, mixed1, upper1, mixed2, upper2, mixed3, upper3)
    d_attn = project(where, parts, grad_out)
    order = feature_order(lax.axis_index("rep"))
    glob, d_attn, order = together(glob, d_attn, order)
    early = from_hbm(rand[1], rand[3], rand[4], rand[5])
    mixed_rand = [rand[0], early[0], rand[2], early[1], early[2], early[3]]
    attn, stats, *ordered = forward(
        where, *from_hbm(q, k, v), lo, hi, mixed_rand, glob, *from_hbm(order)
    )
    cols = [ordered[0]] + [across(ordered[a], a) for a in range(1, 4)]
    layer = layer_of(where, parts, attn)
    layer, *cols = together(layer, *cols)
    weight = weight_payload(cols, (grad_out, mixed1, mixed2, mixed3))
    weight, d_attn = together(weight, d_attn)
    weight = lax.psum_scatter(
        weight, "seq", scatter_dimension=0, axis_index_groups=Y_GROUPS, tiled=True
    )
    (dq, down, dlo, dhi), drand, dglob = backward(
        where, q, k, v, lo, hi, rand, glob, stats, d_attn
    )
    payload = trade(dglob.reshape(8, 32, WIDTH), YX_GROUPS)
    back = [swapped(drand[b], b) for b in range(BITS)]
    right = shifted(dlo, -1)
    left = shifted(dhi, 1)
    payload, weight, back[3] = together(payload, weight, back[3])
    payload = trade(route_z(where, payload, weight), Z_GROUPS)
    payload, back[0], back[4], back[5], left = together(
        payload, back[0], back[4], back[5], left
    )
    payload, mine, other = route_yx(where, payload)
    glob_total = trade(payload, YX_GROUPS).reshape(2, GLOB, BLK, WIDTH)
    other = swapped(other, 0)
    dk, dv, weight_grad = finish(where, down, left, right, back, glob_total, mine, other)
    return (layer[None], dq[None], dk[None], dv[None], weight_grad)


def solution(mesh):
    return jax.shard_map(
        per_device,
        mesh=mesh,
        in_specs=(
            P("rep", "seq", None),
            P("rep", "seq", None),
            P("rep", "seq", None),
            P("rep", None),
            P("rep", "seq", None),
            P("rep", "seq", None),
            P("rep", None),
        ),
        out_specs=(
            P("rep", "seq", None),
            P("rep", "seq", None),
            P("rep", "seq", None),
            P("rep", "seq", None),
            P(("seq", "rep"), None),
        ),
        check_vma=False,
    )
```

time: 261 us -> 232 us (0.89); the launches traced: 257 us -> 231 us
  blocking collectives: 80 us -> 0 us
  waiting for transfers between devices: 48.5 us -> 88 us
  starting transfers between devices: 48.6 us -> 78 us
  local copies, waits for them, and re-layouts: 31.1 us -> 9.39 us
  Pallas kernels: 31.9 us -> 37.6 us
    all_to_all x3 -> x0, blocking collectives: 80 us -> none  [trade(): lax.all_to_all(value, 'seq', 0, 0, axis_index_groups=groups, tiled=True)]
    ppermute x12 -> x13, waiting for transfers between devices: 16.1 us -> 61.8 us  [swapped(): return lax.ppermute(value, 'seq', [(s, s ^ 1 << bit) for s in range(64)])]
    all_to_all x3 -> x6, starting transfers between devices: 12.1 us -> 39.1 us  [trade(): lax.all_to_all(value, 'seq', 0, 0, axis_index_groups=groups, tiled=True)]
    unnamed x90 -> x62, local copies, waits for them, and re-layouts: 30.4 us -> 7.94 us
    all_to_all x3 -> x6, waiting for transfers between devices: 16.1 us -> 0.02 us  [trade(): lax.all_to_all(value, 'seq', 0, 0, axis_index_groups=groups, tiled=True)]
    ppermute x4, waiting for transfers between devices: 14.9 us -> 26.2 us  [shifted(): lax.ppermute(value, 'seq', [(s, (s + steps) % 64) for s in range(64)])]
    ppermute x0 -> x9, starting transfers between devices: none -> 5.87 us  [the longest x8 3.77 us: across(): return lax.ppermute(value, 'rep', [(r, r ^ flip) for r in range(4)])]
    ppermute x4, starting transfers between devices: 13.9 us -> 9.43 us  [shifted(): lax.ppermute(value, 'seq', [(s, (s + steps) % 64) for s in range(64)])]
  transfers between devices with their start and end apart: 22 -> 33, of which waited for: 8 -> 13; matrix products, arithmetic and copies ran while one was open for 1% -> 1% of each run, Pallas kernels for 10% -> 10%
where the time goes in v3:
time: 232 us; the launch traced here: 231 us
  waiting for transfers between devices  88 us (38%)
  starting transfers between devices  78 us (34%)
  Pallas kernels  37.6 us (16%)
  between operations  14.3 us (6%)
  local copies, waits for them, and re-layouts  9.39 us (4%)
  other arithmetic  3.4 us (1%)
    ppermute x13, waiting for transfers between devices, swapped(): return lax.ppermute(value, 'seq', [(s, s ^ 1 << bit) for s in range(64)])  61.8 us
    all_to_all x6, starting transfers between devices, trade(): lax.all_to_all(value, 'seq', 0, 0, axis_index_groups=groups, tiled=True)  39.1 us
    ppermute x4, waiting for transfers between devices, shifted(): lax.ppermute(value, 'seq', [(s, (s + steps) % 64) for s in range(64)])  26.2 us
    ppermute x13, starting transfers between devices, swapped(): return lax.ppermute(value, 'seq', [(s, s ^ 1 << bit) for s in range(64)])  23.5 us
    pallas_call x2, Pallas kernels, head_call(): pl.pallas_call(kernel, grid_spec=pltpu.PrefetchScalarGridSpec(num_scalar_...  11.1 us
    ppermute x4, starting transfers between devices, shifted(): lax.ppermute(value, 'seq', [(s, (s + steps) % 64) for s in range(64)])  9.43 us
    unnamed x62, local copies, waits for them, and re-layouts  7.94 us
    pallas_call x1, Pallas kernels, backward(): pl.pallas_call(backward_kernel, grid=(HEADS // STEP,), in_specs=[smem(),...  7.08 us
  transfers between devices with their start and end apart: 33, of which 13 were waited for; matrix products, arithmetic and copies ran while one was open for 1% of the time, Pallas kernels for 10%

profile of v3, /device:TPU:8, one launch (start us, length us, event | category | flops | bytes accessed | tf_op | source)
XLA Modules:
  0.0 230.7 jit_solution(7335153850017650289)
XLA Ops:
  7.2 1.4 fusion.28
  8.6 1.2 pad_maximum_fusion
  9.8 0.1 concatenate.6.where
  9.9 2.2 pick.1
  12.2 8.5 %all-to-all-start = ((bf16[8,32,1024]{2,1,0:T(8,128)(2,1)}), bf16[8,32,1024]{2,1,0:T(8,128)(2,1)S(1)}, u32[]{:S(2)}, u32[]{:S(2)}) async-start(bf16[8,32,1024]{2,1,0:T(8,128)(2,1)} %bitcast.45), calls=%async_computation | async-start | bytes 1048576 | tf_op jit(solution)/shard_map/all_to_all | solution.py:42
  20.6 1.5 collective-permute-start.6
  22.1 0.4 collective-permute-start
  22.6 2.0 collective-permute-start.1
  24.6 6.5 %collective-permute-done.rest_4_ = bf16[2,64,1024]{2,1,0:T(8,128)(2,1)S(1)} collective-permute-done((bf16[2,64,1024]{2,1,0:T(8,128)(2,1)}, bf16[2,64,1024]{2,1,0:T(8,128)(2,1)S(1)}, u32[]{:S(2)}, u32[]{:S(2)}) %collective-permute-start) | collective-permute-done | bytes 262176 | tf_op jit(solution)/shard_map/ppermute | solution.py:50
  31.0 2.1 collective-permute-start.7
  33.1 7.4 %collective-permute-done.1.rest_1_ = bf16[2,64,1024]{2,1,0:T(8,128)(2,1)S(1)} collective-permute-done((bf16[2,64,1024]{2,1,0:T(8,128)(2,1)}, bf16[2,64,1024]{2,1,0:T(8,128)(2,1)S(1)}, u32[]{:S(2)}, u32[]{:S(2)}) %collective-permute-start.1) | collective-permute-done | bytes 262176 | tf_op jit(solution)/shard_map/ppermute | solution.py:50
  40.5 0.7 copy-done.22
  41.2 0.8 copy-done.10
  42.0 0.9 relay.2
  42.9 7.4 %all-to-all-start.1 = ((bf16[8,32,1024]{2,1,0:T(8,128)(2,1)}), bf16[8,32,1024]{2,1,0:T(8,128)(2,1)S(1)}, u32[]{:S(2)}, u32[]{:S(2)}) async-start(bf16[8,32,1024]{2,1,0:T(8,128)(2,1)} %relay.2), calls=%async_computation.1 | async-start | bytes 1048576 | tf_op jit(solution)/shard_map/all_to_all | solution.py:42
  50.3 4.5 %collective-permute-start.4 = (bf16[2,64,1024]{2,1,0:T(8,128)(2,1)}, bf16[2,64,1024]{2,1,0:T(8,128)(2,1)S(1)}, u32[]{:S(2)}, u32[]{:S(2)}) collective-permute-start(bf16[2,64,1024]{2,1,0:T(8,128)(2,1)} %get-tuple-element.71), channel_id=1, source_target_pairs={{0,32},{4,36},{8,40},{12,44},{16,48},{20,52},{24,56},{28,60},{32,0... | collective-permute-start | bytes 786440 | tf_op jit(solution)/shard_map/ppermute | solution.py:50
  54.7 2.1 collective-permute-start.5
  56.8 8.8 %collective-permute-done.4.rest_3_ = bf16[2,64,1024]{2,1,0:T(8,128)(2,1)S(1)} collective-permute-done((bf16[2,64,1024]{2,1,0:T(8,128)(2,1)}, bf16[2,64,1024]{2,1,0:T(8,128)(2,1)S(1)}, u32[]{:S(2)}, u32[]{:S(2)}) %collective-permute-start.4) | collective-permute-done | bytes 262176 | tf_op jit(solution)/shard_map/ppermute | solution.py:50
  65.6 0.7 copy-done.23
  66.3 0.1 copy-done.24
  66.4 0.8 copy-done.15
  67.3 1.0 copy-done.16
  68.3 0.9 relay.3
  69.2 7.5 %all-to-all-start.2 = ((bf16[8,32,1024]{2,1,0:T(8,128)(2,1)}), bf16[8,32,1024]{2,1,0:T(8,128)(2,1)}, u32[]{:S(2)}, u32[]{:S(2)}) async-start(bf16[8,32,1024]{2,1,0:T(8,128)(2,1)} %relay.3), calls=%async_computation.2 | async-start | bytes 1048576 | tf_op jit(solution)/shard_map/all_to_all | solution.py:42
  76.8 0.3 collective-permute-start.9
  77.1 3.0 %collective-permute-start.10 = (bf16[2,64,1024]{2,1,0:T(8,128)(2,1)}, bf16[2,64,1024]{2,1,0:T(8,128)(2,1)S(1)}, u32[]{:S(2)}, u32[]{:S(2)}) collective-permute-start(bf16[2,64,1024]{2,1,0:T(8,128)(2,1)} %get-tuple-element.75), channel_id=1, source_target_pairs={{0,4},{4,8},{8,12},{12,16},{16,20},{20,24},{24,28},{28,32},{32,36}... | collective-permute-start | bytes 786440 | tf_op jit(solution)/shard_map/ppermute | solution.py:46
  80.1 3.6 %collective-permute-start.11 = (bf16[2,64,1024]{2,1,0:T(8,128)(2,1)}, bf16[2,64,1024]{2,1,0:T(8,128)(2,1)}, u32[]{:S(2)}, u32[]{:S(2)}) collective-permute-start(bf16[2,64,1024]{2,1,0:T(8,128)(2,1)} %get-tuple-element.76), channel_id=1, source_target_pairs={{0,252},{4,0},{8,4},{12,8},{16,12},{20,16},{24,20},{28,24},{32,28}... | collective-permute-start | bytes 786440 | tf_op jit(solution)/shard_map/ppermute | solution.py:46
  83.7 3.0 %collective-permute-start.13 = (bf16[2,64,1024]{2,1,0:T(8,128)(2,1)}, bf16[2,64,1024]{2,1,0:T(8,128)(2,1)}, u32[]{:S(2)}, u32[]{:S(2)}) collective-permute-start(bf16[2,64,1024]{2,1,0:T(8,128)(2,1)} %get-tuple-element.79), channel_id=1, source_target_pairs={{0,16},{4,20},{8,24},{12,28},{16,0},{20,4},{24,8},{28,12},{32,48},... | collective-permute-start | bytes 786440 | tf_op jit(solution)/shard_map/ppermute | solution.py:50
  86.7 2.2 fusion.rest_7_
  88.9 1.0 copy-done.11
  89.9 5.8 %project.1.rest_8_ = bf16[128,1024]{1,0:T(8,128)(2,1)} custom-call(s32[15]{0:T(128)S(1)} %concatenate.6.where, bf16[256,2048]{1,0:T(8,128)(2,1)S(1)} %copy-done, bf16[128,2048]{1,0:T(8,128)(2,1)S(1)} %copy-done.3, bf16[256,2048]{1,0:T(8,128)(2,1)S(1)} %collective-permute-done.2.refs_2_.refs_5_, bf16[128,2048]{1,0:T(8,128)(2,1)S(1)} %copy-done.11, ...), custom_call_target="tpu_custom_call" | custom-call | tf_op jit(solution)/shard_map/project/pallas_call | solution.py:296
  95.8 4.5 %collective-permute-done.10.lo = bf16[2,64,1024]{2,1,0:T(8,128)(2,1)S(1)} collective-permute-done((bf16[2,64,1024]{2,1,0:T(8,128)(2,1)}, bf16[2,64,1024]{2,1,0:T(8,128)(2,1)S(1)}, u32[]{:S(2)}, u32[]{:S(2)}) %collective-permute-start.10) | collective-permute-done | bytes 262176 | tf_op jit(solution)/shard_map/ppermute | solution.py:46
  100.2 1.1 collective-permute-done.12.rest_0_
  101.4 7.5 %collective-permute-done.13.rest_2_ = bf16[2,64,1024]{2,1,0:T(8,128)(2,1)} collective-permute-done((bf16[2,64,1024]{2,1,0:T(8,128)(2,1)}, bf16[2,64,1024]{2,1,0:T(8,128)(2,1)}, u32[]{:S(2)}, u32[]{:S(2)}) %collective-permute-start.13) | collective-permute-done | bytes 262176 | tf_op jit(solution)/shard_map/ppermute | solution.py:50
  108.9 6.3 %forward.1 = (bf16[128,1024]{1,0:T(8,128)(2,1)}, f32[8,8,128]{2,1,0:T(8,128)}, bf16[128,256]{1,0:T(8,128)(2,1)S(1)}, bf16[128,256]{1,0:T(8,128)(2,1)S(1)}, bf16[...) custom-call(s32[15]{0:T(128)S(1)} %concatenate.6.where, bf16[128,1024]{1,0:T(8,128)(2,1)} %bitcast.42, ...), custom_call_target="tpu_custom_call" | custom-call | tf_op jit(solution)/shard_map/forward/pallas_call | solution.py:208
  115.1 0.1 collective-permute-start.14
  115.2 0.7 collective-permute-start.15
  115.9 1.2 collective-permute-start.16
  117.1 0.9 copy-done.18
  118.1 5.3 %layer.1 = bf16[128,2048]{1,0:T(8,128)(2,1)} custom-call(s32[15]{0:T(128)S(1)} %concatenate.6.where, bf16[256,2048]{1,0:T(8,128)(2,1)S(1)} %copy-done.1, bf16[128,2048]{1,0:T(8,128)(2,1)S(1)} %copy-done.4, bf16[256,2048]{1,0:T(8,128)(2,1)S(1)} %collective-permute-done.2.refs_2_.refs_5_, bf16[128,2048]{1,0:T(8,128)(2,1)S(1)} %copy-done.12, ...), custom_call_target="tpu_custom_call" | custom-call | tf_op jit(solution)/shard_map/layer/pallas_call | solution.py:296
  123.4 2.5 %weight.1 = bf16[256,2048]{1,0:T(8,128)(2,1)} custom-call(bf16[128,256]{1,0:T(8,128)(2,1)S(1)} %get-tuple-element.93.refs_0_, bf16[128,256]{1,0:T(8,128)(2,1)S(1)} %collective-permute-done.14.refs_1_, bf16[128,256]{1,0:T(8,128)(2,1)S(1)} %collective-permute-done.15.refs_2_, bf16[128,256]{1,0:T(8,128)(2,1)S(1)} %collective-permute-done.16.refs_3_, ...), custom_call_target="tpu_custom_call" | custom-call | tf_op jit(solution)/shard_map/weight/pallas_call | solution.py:372
  125.9 7.1 %backward.1 = (bf16[128,1024]{1,0:T(8,128)(2,1)}, f32[2,128,1024]{2,1,0:T(8,128)}, bf16[2,64,1024]{2,1,0:T(8,128)(2,1)}, bf16[2,64,1024]{2,1,0:T(8,128)(2,1)}, b...) custom-call(s32[15]{0:T(128)S(1)} %concatenate.6.where, ...), custom_call_target="tpu_custom_call" | custom-call | tf_op jit(solution)/shard_map/backward/pallas_call | solution.py:269
  133.0 5.0 %all-to-all-start.3 = ((bf16[8,32,1024]{2,1,0:T(8,128)(2,1)}), bf16[8,32,1024]{2,1,0:T(8,128)(2,1)S(1)}, u32[]{:S(2)}, u32[]{:S(2)}) async-start(bf16[8,32,1024]{2,1,0:T(8,128)(2,1)} %bitcast.46), calls=%async_computation.3 | async-start | bytes 1048576 | tf_op jit(solution)/shard_map/all_to_all | solution.py:42
  138.0 3.6 %collective-permute-start.17 = (bf16[2,64,1024]{2,1,0:T(8,128)(2,1)}, bf16[2,64,1024]{2,1,0:T(8,128)(2,1)S(1)}, u32[]{:S(2)}, u32[]{:S(2)}) collective-permute-start(bf16[2,64,1024]{2,1,0:T(8,128)(2,1)} %get-tuple-element.103), channel_id=1, source_target_pairs={{0,32},{4,36},{8,40},{12,44},{16,48},{20,52},{24,56},{28,60},{32,0... | collective-permute-start | bytes 786440 | tf_op jit(solution)/shard_map/ppermute | solution.py:50
  141.5 14.2 %collective-permute-done.17.rest_3_ = bf16[2,64,1024]{2,1,0:T(8,128)(2,1)S(1)} collective-permute-done((bf16[2,64,1024]{2,1,0:T(8,128)(2,1)}, bf16[2,64,1024]{2,1,0:T(8,128)(2,1)S(1)}, u32[]{:S(2)}, u32[]{:S(2)}) %collective-permute-start.17) | collective-permute-done | bytes 262176 | tf_op jit(solution)/shard_map/ppermute | solution.py:50
  155.7 0.9 copy-done.19
  156.7 1.5 route_z.1
  158.2 5.0 %all-to-all-start.4 = ((bf16[8,48,1024]{2,1,0:T(8,128)(2,1)}), bf16[8,48,1024]{2,1,0:T(8,128)(2,1)S(1)}, u32[]{:S(2)}, u32[]{:S(2)}) async-start(bf16[8,48,1024]{2,1,0:T(8,128)(2,1)} %route_z.1), calls=%async_computation.5 | async-start | bytes 1572864 | tf_op jit(solution)/shard_map/all_to_all | solution.py:42
  163.3 3.1 %collective-permute-start.18 = (bf16[2,64,1024]{2,1,0:T(8,128)(2,1)}, bf16[2,64,1024]{2,1,0:T(8,128)(2,1)S(1)}, u32[]{:S(2)}, u32[]{:S(2)}) collective-permute-start(bf16[2,64,1024]{2,1,0:T(8,128)(2,1)} %get-tuple-element.106), channel_id=1, source_target_pairs={{0,4},{4,0},{8,12},{12,8},{16,20},{20,16},{24,28},{28,24},{32,36},... | collective-permute-start | bytes 786440 | tf_op jit(solution)/shard_map/ppermute | solution.py:50
  166.4 1.9 collective-permute-start.19
  168.3 0.9 collective-permute-start.20
  169.2 0.5 collective-permute-start.21
  169.7 3.8 %collective-permute-done.18.rest_0_ = bf16[2,64,1024]{2,1,0:T(8,128)(2,1)S(1)} collective-permute-done((bf16[2,64,1024]{2,1,0:T(8,128)(2,1)}, bf16[2,64,1024]{2,1,0:T(8,128)(2,1)S(1)}, u32[]{:S(2)}, u32[]{:S(2)}) %collective-permute-start.18) | collective-permute-done | bytes 262176 | tf_op jit(solution)/shard_map/ppermute | solution.py:50
  173.5 2.4 %collective-permute-done.19.rest_4_ = bf16[2,64,1024]{2,1,0:T(8,128)(2,1)S(1)} collective-permute-done((bf16[2,64,1024]{2,1,0:T(8,128)(2,1)}, bf16[2,64,1024]{2,1,0:T(8,128)(2,1)S(1)}, u32[]{:S(2)}, u32[]{:S(2)}) %collective-permute-start.19) | collective-permute-done | bytes 262176 | tf_op jit(solution)/shard_map/ppermute | solution.py:50
  175.9 3.7 %collective-permute-done.20.rest_5_ = bf16[2,64,1024]{2,1,0:T(8,128)(2,1)S(1)} collective-permute-done((bf16[2,64,1024]{2,1,0:T(8,128)(2,1)S(1)}, bf16[2,64,1024]{2,1,0:T(8,128)(2,1)S(1)}, u32[]{:S(2)}, u32[]{:S(2)}) %collective-permute-start.20) | collective-permute-done | bytes 262176 | tf_op jit(solution)/shard_map/ppermute | solution.py:50
  179.5 11.8 %collective-permute-done.21.left = bf16[2,64,1024]{2,1,0:T(8,128)(2,1)S(1)} collective-permute-done((bf16[2,64,1024]{2,1,0:T(8,128)(2,1)S(1)}, bf16[2,64,1024]{2,1,0:T(8,128)(2,1)S(1)}, u32[]{:S(2)}, u32[]{:S(2)}) %collective-permute-start.21) | collective-permute-done | bytes 262176 | tf_op jit(solution)/shard_map/ppermute | solution.py:46
  191.4 1.5 route_yx.1
  192.9 5.8 %all-to-all-start.5 = ((bf16[8,32,1024]{2,1,0:T(8,128)(2,1)}), bf16[8,32,1024]{2,1,0:T(8,128)(2,1)S(1)}, u32[]{:S(2)}, u32[]{:S(2)}) async-start(bf16[8,32,1024]{2,1,0:T(8,128)(2,1)} %get-tuple-element.119), calls=%async_computation.6 | async-start | bytes 1048576 | tf_op jit(solution)/shard_map/all_to_all | solution.py:42
  198.7 2.4 %collective-permute-start.22 = (bf16[2,64,1024]{2,1,0:T(8,128)(2,1)}, bf16[2,64,1024]{2,1,0:T(8,128)(2,1)S(1)}, u32[]{:S(2)}, u32[]{:S(2)}) collective-permute-start(bf16[2,64,1024]{2,1,0:T(8,128)(2,1)} %get-tuple-element.111), channel_id=1, source_target_pairs={{0,252},{4,0},{8,4},{12,8},{16,12},{20,16},{24,20},{28,24},{32,28}... | collective-permute-start | bytes 786440 | tf_op jit(solution)/shard_map/ppermute | solution.py:46
  201.1 2.1 collective-permute-start.23
  203.1 9.9 %collective-permute-done.22.right = bf16[2,64,1024]{2,1,0:T(8,128)(2,1)S(1)} collective-permute-done((bf16[2,64,1024]{2,1,0:T(8,128)(2,1)}, bf16[2,64,1024]{2,1,0:T(8,128)(2,1)S(1)}, u32[]{:S(2)}, u32[]{:S(2)}) %collective-permute-start.22) | collective-permute-done | bytes 262176 | tf_op jit(solution)/shard_map/ppermute | solution.py:46
  213.1 6.5 %collective-permute-done.23.rest_1_ = bf16[2,64,1024]{2,1,0:T(8,128)(2,1)S(1)} collective-permute-done((bf16[2,64,1024]{2,1,0:T(8,128)(2,1)S(1)}, bf16[2,64,1024]{2,1,0:T(8,128)(2,1)S(1)}, u32[]{:S(2)}, u32[]{:S(2)}) %collective-permute-start.23) | collective-permute-done | bytes 262176 | tf_op jit(solution)/shard_map/ppermute | solution.py:50
  219.6 0.7 copy-done.20
  220.3 3.5 %finish.1 = (bf16[128,1024]{1,0:T(8,128)(2,1)}, bf16[128,1024]{1,0:T(8,128)(2,1)}, f32[4,2048]{1,0:T(4,128)}) custom-call(s32[15]{0:T(128)S(1)} %concatenate.6.where, f32[2,128,1024]{2,1,0:T(8,128)} %get-tuple-element.100.own, bf16[2,64,1024]{2,1,0:T(8,128)(2,1)S(1)} %collective-permute-done.21.left, bf16[2,64,1024]{2,1,0:T(8,128)(2,1)S(1)} %collective-permute-done.22.right, ...), custom_call_target="tpu_custom_call" | custom-call | tf_op jit(solution)/shard_map/finish/pallas_call | solution.py:463
  (83 shorter events, 0.3 us)
Async XLA Ops:
  7.2 1.4 copy-start.5
  7.2 2.6 %copy-start.25 = (s32[1,2]{1,0:T(1,128)S(1)}, s32[1,2]{1,0:T(1,128)}, u32[]{:S(2)}) copy-start(s32[1,2]{1,0:T(1,128)} %param.13) | copy-start | bytes 28
  7.2 2.6 %copy-start.26 = (s32[1,1,6]{2,1,0:T(1,128)S(1)}, s32[1,1,6]{2,1,0:T(1,128)}, u32[]{:S(2)}) copy-start(s32[1,1,6]{2,1,0:T(1,128)} %param.12) | copy-start | bytes 76
  7.2 2.7 %copy-start.9 = (bf16[1,128,1024]{2,1,0:T(8,128)(2,1)S(1)}, bf16[1,128,1024]{2,1,0:T(8,128)(2,1)}, u32[]{:S(2)}) copy-start(bf16[1,128,1024]{2,1,0:T(8,128)(2,1)} %param.9) | copy-start | bytes 786436
  7.2 2.7 %copy-start.8 = (bf16[1,128,1024]{2,1,0:T(8,128)(2,1)S(1)}, bf16[1,128,1024]{2,1,0:T(8,128)(2,1)}, u32[]{:S(2)}) copy-start(bf16[1,128,1024]{2,1,0:T(8,128)(2,1)} %param.8) | copy-start | bytes 786436
  8.6 34.3 %copy-start.2 = (bf16[128,2048]{1,0:T(8,128)(2,1)}, bf16[128,2048]{1,0:T(8,128)(2,1)S(1)}, u32[]{:S(2)}) copy-start(bf16[128,2048]{1,0:T(8,128)(2,1)S(1)} %get-tuple-element.128.refs_1_) | copy-start | bytes 1572868
  9.8 32.2 %collective-permute-start.2 = (bf16[256,2048]{1,0:T(8,128)(2,1)}, bf16[256,2048]{1,0:T(8,128)(2,1)S(1)}, u32[]{:S(2)}, u32[]{:S(2)}) collective-permute-start(bf16[256,2048]{1,0:T(8,128)(2,1)} %pad_maximum_fusion), channel_id=1, source_target_pairs={{0,1},{1,0},{2,3},{3,2},{4,5},{5,4},{6,7},{7,6},{8,9},{9,8},{10,11... | collective-permute-start | bytes 3145736 | tf_op jit(solution)/shard_map/ppermute | solution.py:54
  12.2 29.8 %all-to-all-start = ((bf16[8,32,1024]{2,1,0:T(8,128)(2,1)}), bf16[8,32,1024]{2,1,0:T(8,128)(2,1)S(1)}, u32[]{:S(2)}, u32[]{:S(2)}) async-start(bf16[8,32,1024]{2,1,0:T(8,128)(2,1)} %bitcast.45), calls=%async_computation | async-start | bytes 1048576 | tf_op jit(solution)/shard_map/all_to_all | solution.py:42
  20.6 45.8 %collective-permute-start.6 = (bf16[256,2048]{1,0:T(8,128)(2,1)}, bf16[256,2048]{1,0:T(8,128)(2,1)S(1)}, u32[]{:S(2)}, u32[]{:S(2)}) collective-permute-start(bf16[256,2048]{1,0:T(8,128)(2,1)} %pad_maximum_fusion), channel_id=1, source_target_pairs={{0,2},{1,3},{2,0},{3,1},{4,6},{5,7},{6,4},{7,5},{8,10},{9,11},{10,... | collective-permute-start | bytes 3145736 | tf_op jit(solution)/shard_map/ppermute | solution.py:54
  22.1 19.1 %collective-permute-start.3 = (bf16[128,2048]{1,0:T(8,128)(2,1)S(1)}, bf16[128,2048]{1,0:T(8,128)(2,1)S(1)}, u32[]{:S(2)}, u32[]{:S(2)}) collective-permute-start(bf16[128,2048]{1,0:T(8,128)(2,1)S(1)} %get-tuple-element.128.refs_1_), channel_id=1, source_target_pairs={{0,1},{1,0},{2,3},{3,2},{4,5},{5,4},{6,7},{7,6},{8,9},{9,8},{10,11... | collective-permute-start | bytes 1572872 | tf_op jit(solution)/shard_map/ppermute | solution.py:54
  22.1 8.9 %collective-permute-start = (bf16[2,64,1024]{2,1,0:T(8,128)(2,1)}, bf16[2,64,1024]{2,1,0:T(8,128)(2,1)S(1)}, u32[]{:S(2)}, u32[]{:S(2)}) collective-permute-start(bf16[2,64,1024]{2,1,0:T(8,128)(2,1)} %get-tuple-element.66), channel_id=1, source_target_pairs={{0,64},{4,68},{8,72},{12,76},{16,80},{20,84},{24,88},{28,92},{32,9... | collective-permute-start | bytes 786440 | tf_op jit(solution)/shard_map/ppermute | solution.py:50
  22.6 17.9 %collective-permute-start.1 = (bf16[2,64,1024]{2,1,0:T(8,128)(2,1)}, bf16[2,64,1024]{2,1,0:T(8,128)(2,1)S(1)}, u32[]{:S(2)}, u32[]{:S(2)}) collective-permute-start(bf16[2,64,1024]{2,1,0:T(8,128)(2,1)} %get-tuple-element.67), channel_id=1, source_target_pairs={{0,8},{4,12},{8,0},{12,4},{16,24},{20,28},{24,16},{28,20},{32,40},... | collective-permute-start | bytes 786440 | tf_op jit(solution)/shard_map/ppermute | solution.py:50
  31.0 46.1 %copy-start.21 = (bf16[2,64,1024]{2,1,0:T(8,128)(2,1)}, bf16[2,64,1024]{2,1,0:T(8,128)(2,1)S(1)}, u32[]{:S(2)}) copy-start(bf16[2,64,1024]{2,1,0:T(8,128)(2,1)S(1)} %collective-permute-done.rest_4_) | copy-start | bytes 786436
  31.0 34.6 %collective-permute-start.7 = (bf16[128,2048]{1,0:T(8,128)(2,1)S(1)}, bf16[128,2048]{1,0:T(8,128)(2,1)}, u32[]{:S(2)}, u32[]{:S(2)}) collective-permute-start(bf16[128,2048]{1,0:T(8,128)(2,1)S(1)} %get-tuple-element.128.refs_1_), channel_id=1, source_target_pairs={{0,6},{1,7},{2,4},{3,5},{4,2},{5,3},{6,0},{7,1},{8,14},{9,15},{10,... | collective-permute-start | bytes 1572872 | tf_op jit(solution)/shard_map/ppermute | solution.py:59
  40.5 0.7 copy-start.22
  41.2 0.8 copy-start.10
  42.9 23.6 %all-to-all-start.1 = ((bf16[8,32,1024]{2,1,0:T(8,128)(2,1)}), bf16[8,32,1024]{2,1,0:T(8,128)(2,1)S(1)}, u32[]{:S(2)}, u32[]{:S(2)}) async-start(bf16[8,32,1024]{2,1,0:T(8,128)(2,1)} %relay.2), calls=%async_computation.1 | async-start | bytes 1048576 | tf_op jit(solution)/shard_map/all_to_all | solution.py:42
  50.3 15.4 %collective-permute-start.4 = (bf16[2,64,1024]{2,1,0:T(8,128)(2,1)}, bf16[2,64,1024]{2,1,0:T(8,128)(2,1)S(1)}, u32[]{:S(2)}, u32[]{:S(2)}) collective-permute-start(bf16[2,64,1024]{2,1,0:T(8,128)(2,1)} %get-tuple-element.71), channel_id=1, source_target_pairs={{0,32},{4,36},{8,40},{12,44},{16,48},{20,52},{24,56},{28,60},{32,0... | collective-permute-start | bytes 786440 | tf_op jit(solution)/shard_map/ppermute | solution.py:50
  54.7 10.9 %collective-permute-start.5 = (bf16[2,64,1024]{2,1,0:T(8,128)(2,1)}, bf16[2,64,1024]{2,1,0:T(8,128)(2,1)S(1)}, u32[]{:S(2)}, u32[]{:S(2)}) collective-permute-start(bf16[2,64,1024]{2,1,0:T(8,128)(2,1)} %get-tuple-element.72), channel_id=1, source_target_pairs={{0,128},{4,132},{8,136},{12,140},{16,144},{20,148},{24,152},{28,15... | collective-permute-start | bytes 786440 | tf_op jit(solution)/shard_map/ppermute | solution.py:50
  65.6 0.7 copy-start.23
  65.6 0.8 copy-start.24
  66.4 0.8 copy-start.15
  67.3 21.6 %collective-permute-start.8 = (bf16[256,2048]{1,0:T(8,128)(2,1)S(1)}, bf16[256,2048]{1,0:T(8,128)(2,1)S(1)}, u32[]{:S(2)}, u32[]{:S(2)}) collective-permute-start(bf16[256,2048]{1,0:T(8,128)(2,1)S(1)} %collective-permute-done.6.refs_4_.refs_6_), channel_id=1, source_target_pairs={{0,1},{1,0},{2,3},{3,2},{4,5},{5,4},{6,7},{7,6},{8,9},{9,8},{10,11... | collective-permute-start | bytes 3145736 | tf_op jit(solution)/shard_map/ppermute | solution.py:54
  67.3 1.0 copy-start.16
  69.2 26.5 %all-to-all-start.2 = ((bf16[8,32,1024]{2,1,0:T(8,128)(2,1)}), bf16[8,32,1024]{2,1,0:T(8,128)(2,1)}, u32[]{:S(2)}, u32[]{:S(2)}) async-start(bf16[8,32,1024]{2,1,0:T(8,128)(2,1)} %relay.3), calls=%async_computation.2 | async-start | bytes 1048576 | tf_op jit(solution)/shard_map/all_to_all | solution.py:42
  76.7 79.0 %reduce-scatter.2.cloned.1.call-start = ((), (), s32[]{:S(2)}) async-start(), calls=%async_computation.7 | async-start | bytes 1310720 | tf_op jit(solution)/shard_map/reduce_scatter | solution.py:522
  76.8 12.1 %copy-start = (bf16[256,2048]{1,0:T(8,128)(2,1)S(1)}, bf16[256,2048]{1,0:T(8,128)(2,1)}, u32[]{:S(2)}) copy-start(bf16[256,2048]{1,0:T(8,128)(2,1)} %refs_0_.3) | copy-start | bytes 3145732
  76.8 12.1 %copy-start.3 = (bf16[128,2048]{1,0:T(8,128)(2,1)S(1)}, bf16[128,2048]{1,0:T(8,128)(2,1)}, u32[]{:S(2)}) copy-start(bf16[128,2048]{1,0:T(8,128)(2,1)} %copy-done.2) | copy-start | bytes 1572868
  76.8 12.1 %copy-start.6 = (bf16[1,128,2048]{2,1,0:T(8,128)(2,1)S(1)}, bf16[1,128,2048]{2,1,0:T(8,128)(2,1)}, u32[]{:S(2)}) copy-start(bf16[1,128,2048]{2,1,0:T(8,128)(2,1)} %param.11) | copy-start | bytes 1572868
  76.8 6.9 %collective-permute-start.9 = (bf16[128,2048]{1,0:T(8,128)(2,1)}, bf16[128,2048]{1,0:T(8,128)(2,1)S(1)}, u32[]{:S(2)}, u32[]{:S(2)}) collective-permute-start(bf16[128,2048]{1,0:T(8,128)(2,1)} %collective-permute-done.7.refs_5_), channel_id=1, source_target_pairs={{0,1},{1,0},{2,3},{3,2},{4,5},{5,4},{6,7},{7,6},{8,9},{9,8},{10,11... | collective-permute-start | bytes 1572872 | tf_op jit(solution)/shard_map/ppermute | solution.py:54
  77.1 23.1 %collective-permute-start.10 = (bf16[2,64,1024]{2,1,0:T(8,128)(2,1)}, bf16[2,64,1024]{2,1,0:T(8,128)(2,1)S(1)}, u32[]{:S(2)}, u32[]{:S(2)}) collective-permute-start(bf16[2,64,1024]{2,1,0:T(8,128)(2,1)} %get-tuple-element.75), channel_id=1, source_target_pairs={{0,4},{4,8},{8,12},{12,16},{16,20},{20,24},{24,28},{28,32},{32,36}... | collective-permute-start | bytes 786440 | tf_op jit(solution)/shard_map/ppermute | solution.py:46
  80.1 20.1 %collective-permute-start.11 = (bf16[2,64,1024]{2,1,0:T(8,128)(2,1)}, bf16[2,64,1024]{2,1,0:T(8,128)(2,1)}, u32[]{:S(2)}, u32[]{:S(2)}) collective-permute-start(bf16[2,64,1024]{2,1,0:T(8,128)(2,1)} %get-tuple-element.76), channel_id=1, source_target_pairs={{0,252},{4,0},{8,4},{12,8},{16,12},{20,16},{24,20},{28,24},{32,28}... | collective-permute-start | bytes 786440 | tf_op jit(solution)/shard_map/ppermute | solution.py:46
  83.7 17.7 %collective-permute-start.12 = (bf16[2,64,1024]{2,1,0:T(8,128)(2,1)}, bf16[2,64,1024]{2,1,0:T(8,128)(2,1)}, u32[]{:S(2)}, u32[]{:S(2)}) collective-permute-start(bf16[2,64,1024]{2,1,0:T(8,128)(2,1)} %get-tuple-element.77), channel_id=1, source_target_pairs={{0,4},{4,0},{8,12},{12,8},{16,20},{20,16},{24,28},{28,24},{32,36},... | collective-permute-start | bytes 786440 | tf_op jit(solution)/shard_map/ppermute | solution.py:50
  83.7 5.2 %copy-start.13 = (bf16[128,2048]{1,0:T(8,128)(2,1)}, bf16[128,2048]{1,0:T(8,128)(2,1)S(1)}, u32[]{:S(2)}) copy-start(bf16[128,2048]{1,0:T(8,128)(2,1)S(1)} %collective-permute-done.9.refs_7_) | copy-start | bytes 1572868
  83.7 25.1 %collective-permute-start.13 = (bf16[2,64,1024]{2,1,0:T(8,128)(2,1)}, bf16[2,64,1024]{2,1,0:T(8,128)(2,1)}, u32[]{:S(2)}, u32[]{:S(2)}) collective-permute-start(bf16[2,64,1024]{2,1,0:T(8,128)(2,1)} %get-tuple-element.79), channel_id=1, source_target_pairs={{0,16},{4,20},{8,24},{12,28},{16,0},{20,4},{24,8},{28,12},{32,48},... | collective-permute-start | bytes 786440 | tf_op jit(solution)/shard_map/ppermute | solution.py:50
  88.9 1.0 copy-start.11
  100.2 14.9 %copy-start.17 = (bf16[2,64,1024]{2,1,0:T(8,128)(2,1)}, bf16[2,64,1024]{2,1,0:T(8,128)(2,1)S(1)}, u32[]{:S(2)}) copy-start(bf16[2,64,1024]{2,1,0:T(8,128)(2,1)S(1)} %collective-permute-done.10.lo) | copy-start | bytes 786436
  108.8 8.2 %copy-start.1 = (bf16[256,2048]{1,0:T(8,128)(2,1)S(1)}, bf16[256,2048]{1,0:T(8,128)(2,1)}, u32[]{:S(2)}) copy-start(bf16[256,2048]{1,0:T(8,128)(2,1)} %refs_0_.3) | copy-start | bytes 3145732
  108.8 8.2 %copy-start.4 = (bf16[128,2048]{1,0:T(8,128)(2,1)S(1)}, bf16[128,2048]{1,0:T(8,128)(2,1)}, u32[]{:S(2)}) copy-start(bf16[128,2048]{1,0:T(8,128)(2,1)} %copy-done.2) | copy-start | bytes 1572868
  108.9 8.2 %copy-start.12 = (bf16[128,2048]{1,0:T(8,128)(2,1)S(1)}, bf16[128,2048]{1,0:T(8,128)(2,1)}, u32[]{:S(2)}) copy-start(bf16[128,2048]{1,0:T(8,128)(2,1)} %copy-done.10) | copy-start | bytes 1572868
  108.9 8.2 %copy-start.14 = (bf16[128,2048]{1,0:T(8,128)(2,1)S(1)}, bf16[128,2048]{1,0:T(8,128)(2,1)}, u32[]{:S(2)}) copy-start(bf16[128,2048]{1,0:T(8,128)(2,1)} %copy-done.13) | copy-start | bytes 1572868
  115.1 8.2 %collective-permute-start.14 = (bf16[128,256]{1,0:T(8,128)(2,1)S(1)}, bf16[128,256]{1,0:T(8,128)(2,1)S(1)}, u32[]{:S(2)}, u32[]{:S(2)}) collective-permute-start(bf16[128,256]{1,0:T(8,128)(2,1)S(1)} %get-tuple-element.88), channel_id=1, source_target_pairs={{0,1},{1,0},{2,3},{3,2},{4,5},{5,4},{6,7},{7,6},{8,9},{9,8},{10,11... | collective-permute-start | bytes 196616 | tf_op jit(solution)/shard_map/ppermute | solution.py:54
  115.2 8.1 %collective-permute-start.15 = (bf16[128,256]{1,0:T(8,128)(2,1)S(1)}, bf16[128,256]{1,0:T(8,128)(2,1)S(1)}, u32[]{:S(2)}, u32[]{:S(2)}) collective-permute-start(bf16[128,256]{1,0:T(8,128)(2,1)S(1)} %get-tuple-element.89), channel_id=1, source_target_pairs={{0,2},{1,3},{2,0},{3,1},{4,6},{5,7},{6,4},{7,5},{8,10},{9,11},{10,... | collective-permute-start | bytes 196616 | tf_op jit(solution)/shard_map/ppermute | solution.py:54
  115.9 7.4 %collective-permute-start.16 = (bf16[128,256]{1,0:T(8,128)(2,1)S(1)}, bf16[128,256]{1,0:T(8,128)(2,1)S(1)}, u32[]{:S(2)}, u32[]{:S(2)}) collective-permute-start(bf16[128,256]{1,0:T(8,128)(2,1)S(1)} %get-tuple-element.90), channel_id=1, source_target_pairs={{0,3},{1,2},{2,1},{3,0},{4,7},{5,6},{6,5},{7,4},{8,11},{9,10},{10,... | collective-permute-start | bytes 196616 | tf_op jit(solution)/shard_map/ppermute | solution.py:54
  117.1 1.0 copy-start.18
  118.1 5.3 %copy-start.7 = (bf16[1,128,2048]{2,1,0:T(8,128)(2,1)S(1)}, bf16[1,128,2048]{2,1,0:T(8,128)(2,1)}, u32[]{:S(2)}) copy-start(bf16[1,128,2048]{2,1,0:T(8,128)(2,1)} %param.11) | copy-start | bytes 1572868
  133.0 35.3 %copy-start.30 = (bf16[2,64,1024]{2,1,0:T(8,128)(2,1)S(1)}, bf16[2,64,1024]{2,1,0:T(8,128)(2,1)}, u32[]{:S(2)}) copy-start(bf16[2,64,1024]{2,1,0:T(8,128)(2,1)} %get-tuple-element.108) | copy-start | bytes 786436
  133.0 36.2 %copy-start.29 = (bf16[2,64,1024]{2,1,0:T(8,128)(2,1)S(1)}, bf16[2,64,1024]{2,1,0:T(8,128)(2,1)}, u32[]{:S(2)}) copy-start(bf16[2,64,1024]{2,1,0:T(8,128)(2,1)} %get-tuple-element.109) | copy-start | bytes 786436
  133.0 22.7 %all-to-all-start.3 = ((bf16[8,32,1024]{2,1,0:T(8,128)(2,1)}), bf16[8,32,1024]{2,1,0:T(8,128)(2,1)S(1)}, u32[]{:S(2)}, u32[]{:S(2)}) async-start(bf16[8,32,1024]{2,1,0:T(8,128)(2,1)} %bitcast.46), calls=%async_computation.3 | async-start | bytes 1048576 | tf_op jit(solution)/shard_map/all_to_all | solution.py:42
  138.0 17.7 %collective-permute-start.17 = (bf16[2,64,1024]{2,1,0:T(8,128)(2,1)}, bf16[2,64,1024]{2,1,0:T(8,128)(2,1)S(1)}, u32[]{:S(2)}, u32[]{:S(2)}) collective-permute-start(bf16[2,64,1024]{2,1,0:T(8,128)(2,1)} %get-tuple-element.103), channel_id=1, source_target_pairs={{0,32},{4,36},{8,40},{12,44},{16,48},{20,52},{24,56},{28,60},{32,0... | collective-permute-start | bytes 786440 | tf_op jit(solution)/shard_map/ppermute | solution.py:50
  155.7 1.0 copy-start.19
  158.2 42.8 %copy-start.28 = (bf16[2,64,1024]{2,1,0:T(8,128)(2,1)S(1)}, bf16[2,64,1024]{2,1,0:T(8,128)(2,1)}, u32[]{:S(2)}) copy-start(bf16[2,64,1024]{2,1,0:T(8,128)(2,1)} %get-tuple-element.113) | copy-start | bytes 786436
  158.2 44.9 %copy-start.27 = (bf16[2,64,1024]{2,1,0:T(8,128)(2,1)S(1)}, bf16[2,64,1024]{2,1,0:T(8,128)(2,1)}, u32[]{:S(2)}) copy-start(bf16[2,64,1024]{2,1,0:T(8,128)(2,1)} %get-tuple-element.114) | copy-start | bytes 786436
  158.2 33.1 %all-to-all-start.4 = ((bf16[8,48,1024]{2,1,0:T(8,128)(2,1)}), bf16[8,48,1024]{2,1,0:T(8,128)(2,1)S(1)}, u32[]{:S(2)}, u32[]{:S(2)}) async-start(bf16[8,48,1024]{2,1,0:T(8,128)(2,1)} %route_z.1), calls=%async_computation.5 | async-start | bytes 1572864 | tf_op jit(solution)/shard_map/all_to_all | solution.py:42
  163.3 10.2 %collective-permute-start.18 = (bf16[2,64,1024]{2,1,0:T(8,128)(2,1)}, bf16[2,64,1024]{2,1,0:T(8,128)(2,1)S(1)}, u32[]{:S(2)}, u32[]{:S(2)}) collective-permute-start(bf16[2,64,1024]{2,1,0:T(8,128)(2,1)} %get-tuple-element.106), channel_id=1, source_target_pairs={{0,4},{4,0},{8,12},{12,8},{16,20},{20,16},{24,28},{28,24},{32,36},... | collective-permute-start | bytes 786440 | tf_op jit(solution)/shard_map/ppermute | solution.py:50
  166.4 9.5 %collective-permute-start.19 = (bf16[2,64,1024]{2,1,0:T(8,128)(2,1)}, bf16[2,64,1024]{2,1,0:T(8,128)(2,1)S(1)}, u32[]{:S(2)}, u32[]{:S(2)}) collective-permute-start(bf16[2,64,1024]{2,1,0:T(8,128)(2,1)} %get-tuple-element.107), channel_id=1, source_target_pairs={{0,64},{4,68},{8,72},{12,76},{16,80},{20,84},{24,88},{28,92},{32,9... | collective-permute-start | bytes 786440 | tf_op jit(solution)/shard_map/ppermute | solution.py:50
  168.3 11.2 %collective-permute-start.20 = (bf16[2,64,1024]{2,1,0:T(8,128)(2,1)S(1)}, bf16[2,64,1024]{2,1,0:T(8,128)(2,1)S(1)}, u32[]{:S(2)}, u32[]{:S(2)}) collective-permute-start(bf16[2,64,1024]{2,1,0:T(8,128)(2,1)S(1)} %copy-done.30), channel_id=1, source_target_pairs={{0,128},{4,132},{8,136},{12,140},{16,144},{20,148},{24,152},{28,15... | collective-permute-start | bytes 786440 | tf_op jit(solution)/shard_map/ppermute | solution.py:50
  169.2 22.2 %collective-permute-start.21 = (bf16[2,64,1024]{2,1,0:T(8,128)(2,1)S(1)}, bf16[2,64,1024]{2,1,0:T(8,128)(2,1)S(1)}, u32[]{:S(2)}, u32[]{:S(2)}) collective-permute-start(bf16[2,64,1024]{2,1,0:T(8,128)(2,1)S(1)} %copy-done.29), channel_id=1, source_target_pairs={{0,4},{4,8},{8,12},{12,16},{16,20},{20,24},{24,28},{28,32},{32,36}... | collective-permute-start | bytes 786440 | tf_op jit(solution)/shard_map/ppermute | solution.py:46
  192.9 26.7 %all-to-all-start.5 = ((bf16[8,32,1024]{2,1,0:T(8,128)(2,1)}), bf16[8,32,1024]{2,1,0:T(8,128)(2,1)S(1)}, u32[]{:S(2)}, u32[]{:S(2)}) async-start(bf16[8,32,1024]{2,1,0:T(8,128)(2,1)} %get-tuple-element.119), calls=%async_computation.6 | async-start | bytes 1048576 | tf_op jit(solution)/shard_map/all_to_all | solution.py:42
  198.7 14.4 %collective-permute-start.22 = (bf16[2,64,1024]{2,1,0:T(8,128)(2,1)}, bf16[2,64,1024]{2,1,0:T(8,128)(2,1)S(1)}, u32[]{:S(2)}, u32[]{:S(2)}) collective-permute-start(bf16[2,64,1024]{2,1,0:T(8,128)(2,1)} %get-tuple-element.111), channel_id=1, source_target_pairs={{0,252},{4,0},{8,4},{12,8},{16,12},{20,16},{24,20},{28,24},{32,28}... | collective-permute-start | bytes 786440 | tf_op jit(solution)/shard_map/ppermute | solution.py:46
  201.1 18.5 %collective-permute-start.23 = (bf16[2,64,1024]{2,1,0:T(8,128)(2,1)S(1)}, bf16[2,64,1024]{2,1,0:T(8,128)(2,1)S(1)}, u32[]{:S(2)}, u32[]{:S(2)}) collective-permute-start(bf16[2,64,1024]{2,1,0:T(8,128)(2,1)S(1)} %copy-done.28), channel_id=1, source_target_pairs={{0,8},{4,12},{8,0},{12,4},{16,24},{20,28},{24,16},{28,20},{32,40},... | collective-permute-start | bytes 786440 | tf_op jit(solution)/shard_map/ppermute | solution.py:50
  203.1 16.4 %collective-permute-start.24 = (bf16[2,64,1024]{2,1,0:T(8,128)(2,1)S(1)}, bf16[2,64,1024]{2,1,0:T(8,128)(2,1)S(1)}, u32[]{:S(2)}, u32[]{:S(2)}) collective-permute-start(bf16[2,64,1024]{2,1,0:T(8,128)(2,1)S(1)} %copy-done.27), channel_id=1, source_target_pairs={{0,16},{4,20},{8,24},{12,28},{16,0},{20,4},{24,8},{28,12},{32,48},... | collective-permute-start | bytes 786440 | tf_op jit(solution)/shard_map/ppermute | solution.py:50
  203.1 16.4 %collective-permute-start.25 = (f32[4,2048]{1,0:T(4,128)}, f32[4,2048]{1,0:T(4,128)S(1)}, u32[]{:S(2)}, u32[]{:S(2)}) collective-permute-start(f32[4,2048]{1,0:T(4,128)} %get-tuple-element.121), channel_id=1, source_target_pairs={{0,4},{4,0},{8,12},{12,8},{16,20},{20,16},{24,28},{28,24},{32,36},... | collective-permute-start | bytes 98312 | tf_op jit(solution)/shard_map/ppermute | solution.py:50
  219.6 0.8 copy-start.20
Sparse Core Ops, SparseCore 0:
  126.0 27.6 reduce-scatter.1

commit v4 on v3

--- a/solution.py
+++ b/solution.py
@@ -29,17 +29,19 @@
     return y * 16 + z * 2 + x
 
 
-Z_GROUPS = [[stretch_id(y, z, x) for z in range(8)] for y in range(4) for x in range(2)]
-Y_GROUPS = [[stretch_id(y, z, x) for y in range(4)] for z in range(8) for x in range(2)]
 YX_GROUPS = [[stretch_id(y, z, x) for y in range(4) for x in range(2)] for z in range(8)]
+CHUNKS = 8
+HALF = WIDTH // 2
+Z_BITS = (1, 2, 3)
+FIRST, SECOND, THIRD = (3, 4, 0), (5, 1), (2,)
 
 
 def mm(left, right, dims):
     return lax.dot_general(left, right, dims, preferred_element_type=F32)
 
 
-def trade(value, groups):
-    return lax.all_to_all(value, "seq", 0, 0, axis_index_groups=groups, tiled=True)
+def trade(value):
+    return lax.all_to_all(value, "seq", 0, 0, axis_index_groups=YX_GROUPS, tiled=True)
 
 
 def shifted(value, steps):
@@ -77,13 +79,13 @@
 
 def where_of(rand_slot, global_ids):
     me = lax.axis_index("seq")
+    rep = lax.axis_index("rep")
     owner = global_ids // 2
     here = jnp.where(owner == me, global_ids % 2, -1)
-    my_m = (me // 16) * 2 + me % 2
-    tail = jnp.stack([(my_m // 2) % 2, lax.axis_index("rep"), me % 2])
-    return jnp.concatenate(
-        [rand_slot, here, (owner // 2) % 8, (owner // 16) * 2 + owner % 2, tail]
-    ).astype(jnp.int32)
+    tail = jnp.stack([me % 2, me, rep, rep])
+    return jnp.concatenate([rand_slot, here, (owner // 16) * 2 + owner % 2, tail]).astype(
+        jnp.int32
+    )
 
 
 def pick_kernel(where, k_ref, v_ref, *outs):
@@ -98,22 +100,16 @@
     last[1] = v_ref[BLK : 2 * BLK, :]
     for g in range(GLOB):
         here = where[6 + g]
-
-        @pl.when(here < 0)
-        def _():
-            picked[0, g] = jnp.zeros((BLK, WIDTH), BF)
-            picked[1, g] = jnp.zeros((BLK, WIDTH), BF)
-
-        @pl.when(here >= 0)
-        def _():
-            rows = pl.ds(pl.multiple_of(jnp.maximum(here, 0) * BLK, BLK), BLK)
-            picked[0, g] = k_ref[rows, :]
-            picked[1, g] = v_ref[rows, :]
+        rows = pl.ds(pl.multiple_of(jnp.maximum(here, 0) * BLK, BLK), BLK)
+        for c, src in enumerate((k_ref, v_ref)):
+            block = jnp.where(here >= 0, src[rows, :], jnp.zeros((BLK, WIDTH), BF))
+            for half in range(2):
+                picked[half * 4 + c * 2 + g] = block[:, half * HALF : (half + 1) * HALF]
 
 
 def pick(where, keys, values):
     block = far((2, BLK, WIDTH))
-    outs = [block] * (BITS + 2) + [far((2, GLOB, BLK, WIDTH))]
+    outs = [block] * (BITS + 2) + [far((CHUNKS, BLK, HALF))]
     vm = pl.BlockSpec(memory_space=pltpu.VMEM)
     return pl.pallas_call(
         pick_kernel,
@@ -125,26 +121,42 @@
     )(where, keys, values)
 
 
-def relay_kernel(x_ref, o_ref):
-    total = jnp.sum(x_ref[...].astype(F32), axis=0).astype(BF)
-    for j in range(8):
-        o_ref[j] = total
-
-
-def relay(x):
+def gathered_kernel(x_ref, o_ref):
+    o_ref[...] = jnp.sum(x_ref[...].astype(F32), axis=0).astype(BF)
+
+
+def gathered(x):
+    return pl.pallas_call(
+        gathered_kernel,
+        out_shape=far((BLK, HALF)),
+        compiler_params=params(),
+        name="gathered",
+    )(x)
+
+
+def relay_kernel(mine, other, out):
+    total = (mine[...].astype(F32) + other[...].astype(F32)).astype(BF)
+    if len(out.shape) == 2:
+        out[...] = total
+    else:
+        for j in range(CHUNKS):
+            out[j] = total
+
+
+def relay(mine, other, shape):
     return pl.pallas_call(
         relay_kernel,
-        out_shape=far(x.shape),
+        out_shape=far(shape),
         compiler_params=params(),
         name="relay",
-    )(x)
+    )(mine, other)
 
 
 def gather_heads(dst, c, cols, own, lo, hi, rand, glob):
     dst[0:64, :] = lo[c, :, cols]
     dst[64:192, :] = own[:, cols]
     dst[192:256, :] = hi[c, :, cols]
-    dst[256:384, :] = glob[c, :, cols]
+    dst[256:384, :] = glob[0, c * TOK : (c + 1) * TOK, cols]
     for b in range(BITS):
         dst[384 + 64 * b : 448 + 64 * b, :] = rand[b][c, :, cols]
 
@@ -200,17 +212,18 @@
     flat = pl.BlockSpec((TOK, WIDE), lambda h: (0, h))
     pair = pl.BlockSpec((2, BLK, WIDE), lambda h: (0, 0, h))
     both = pl.BlockSpec((2, TOK, WIDE), lambda h: (0, 0, h))
-    return flat, pair, both
+    half = pl.BlockSpec((1, 2 * TOK, WIDE), lambda h: (h, 0, 0))
+    return flat, pair, both, half
 
 
 def forward(where, q, k, v, lo, hi, rand, glob, perm):
-    flat, pair, both = head_specs()
+    flat, pair, both, half = head_specs()
     return pl.pallas_call(
         forward_kernel,
         grid=(HEADS // STEP,),
         in_specs=[smem(), flat, flat, flat, pair, pair]
         + [pair] * BITS
-        + [both, pl.BlockSpec((WIDE, WIDTH), lambda h: (h, 0))],
+        + [half, pl.BlockSpec((WIDE, WIDTH), lambda h: (h, 0))],
         out_specs=[
             flat,
             pl.BlockSpec((STEP, 8, TOK), lambda h: (h, 0, 0)),
@@ -258,24 +271,24 @@
             dlo[c, :, cols] = grad[0:64].astype(BF)
             down[c, :, cols] = grad[64:192]
             dhi[c, :, cols] = grad[192:256].astype(BF)
-            dglob[c, :, cols] = grad[256:384].astype(BF)
+            dglob[0, c * TOK : (c + 1) * TOK, cols] = grad[256:384].astype(BF)
             for b in range(BITS):
                 drand[b][c, :, cols] = grad[384 + 64 * b : 448 + 64 * b].astype(BF)
 
 
 def backward(where, q, k, v, lo, hi, rand, glob, stats, d_attn):
-    flat, pair, both = head_specs()
+    flat, pair, both, half = head_specs()
     block = far((2, BLK, WIDTH))
     outs = pl.pallas_call(
         backward_kernel,
         grid=(HEADS // STEP,),
         in_specs=[smem(), flat, flat, flat, pair, pair]
         + [pair] * BITS
-        + [both, pl.BlockSpec((STEP, 8, TOK), lambda h: (h, 0, 0)), flat],
-        out_specs=[flat, both, pair, pair] + [pair] * BITS + [both],
+        + [half, pl.BlockSpec((STEP, 8, TOK), lambda h: (h, 0, 0)), flat],
+        out_specs=[flat, both, pair, pair] + [pair] * BITS + [half],
         out_shape=[far((TOK, WIDTH)), far((2, TOK, WIDTH), F32), block, block]
         + [block] * BITS
-        + [far((2, TOK, WIDTH))],
+        + [far((2, 2 * TOK, HALF))],
         scratch_shapes=[
             pltpu.VMEM((STEP, KEYS, HEAD_DIM), BF),
             pltpu.VMEM((STEP, KEYS, HEAD_DIM), BF),
@@ -305,7 +318,7 @@
         out_shape=out_shape,
         compiler_params=params(dimension_semantics=("arbitrary",)),
         name=name,
-    )(where, *parts, extra)
+    )(where, *from_hbm(*parts, extra))
 
 
 def project_kernel(where, *refs):
@@ -361,82 +374,112 @@
 
 
 def weight_kernel(*refs):
-    cols, grads, out = refs[:4], refs[4:8], refs[8]
-    total = mm(cols[0][...], grads[0][...], COLS)
-    for a in range(1, 4):
-        total += mm(cols[a][...], grads[a][...], COLS)
-    out[...] = total.astype(BF)
-
-
-def weight_payload(cols, grads):
+    cols, grads, (dglob, out) = refs[:4], refs[4:8], refs[8:]
+    step = pl.program_id(0)
+
+    @pl.when(step < 2)
+    def _():
+        out[...] = dglob[...]
+
+    @pl.when(step >= 2)
+    def _():
+        part = mm(cols[0][...], grads[0][...], COLS)
+        for a in range(1, 4):
+            part += mm(cols[a][...], grads[a][...], COLS)
+        out[...] = part.astype(BF).reshape(CHUNKS, 32, HALF)
+
+
+def weight_payload(cols, grads, dglob):
     return pl.pallas_call(
         weight_kernel,
-        grid=(2,),
+        grid=(6,),
         in_specs=[pl.BlockSpec((TOK, 256), lambda i: (0, 0))] * 4
-        + [pl.BlockSpec((TOK, 1024), lambda i: (0, i))]
-        + [pl.BlockSpec((TOK, 1024), lambda i: (1, i))] * 3,
-        out_specs=pl.BlockSpec((256, 1024), lambda i: (0, i)),
-        out_shape=far((256, D)),
+        + [pl.BlockSpec((TOK, HALF), lambda i: (0, jnp.maximum(i - 2, 0)))]
+        + [pl.BlockSpec((TOK, HALF), lambda i: (1, jnp.maximum(i - 2, 0)))] * 3
+        + [pl.BlockSpec((CHUNKS, 32, HALF), lambda i: (0, jnp.minimum(i, 1), 0))],
+        out_specs=pl.BlockSpec((CHUNKS, 32, HALF), lambda i: (0, i, 0)),
+        out_shape=far((CHUNKS, 192, HALF)),
         compiler_params=params(dimension_semantics=("arbitrary",)),
         name="weight",
-    )(*cols, *grads)
-
-
-def route_z_kernel(where, x, w, out, rows, small):
-    chunk = jnp.sum(x[...].astype(F32), axis=0)
-    rows[...] = w[...].astype(F32)
-    target = jnp.where(where[12] == 0, where[8], where[9])
-    for j in range(8):
-        out[j, 0:32] = jnp.where(target == j, chunk, 0.0).astype(BF)
-        small[0:8, :] = rows[8 * j : 8 * j + 8, 0:1024]
-        small[8:16, :] = rows[8 * j : 8 * j + 8, 1024:2048]
-        out[j, 32:48] = small[...].astype(BF)
-
-
-def route_z(where, x, w):
+    )(*cols, *from_hbm(*grads, dglob))
+
+
+def halve(where, bit, total, keep, stage):
+    rows = keep.shape[0] // 4
+    side = (where[11] // (1 << bit)) % 2
+    for part in range(4):
+        lower = total[2 * rows * part : 2 * rows * part + rows, :]
+        upper = total[2 * rows * part + rows : 2 * rows * (part + 1), :]
+        keep[rows * part : rows * (part + 1), :] = jnp.where(side == 0, lower, upper)
+        stage[rows * part : rows * (part + 1), :] = jnp.where(side == 0, upper, lower)
+
+
+def first_kernel(bit, where, x, glob, keep, send, total, stage):
+    added = jnp.sum(x[...].astype(F32), axis=0)
+    glob[...] = added[0:BLK]
+    send[0:BLK, :] = added[0:BLK].astype(BF)
+    total[...] = added[BLK:]
+    halve(where, bit, total, keep, stage)
+    send[BLK:, :] = stage[...].astype(BF)
+
+
+def fold_kernel(bit, where, glob, kept, came, glob_out, keep, send, total, stage):
+    added = came[...].astype(F32)
+    glob_out[...] = glob[...] + added[0:BLK]
+    send[0:BLK, :] = glob_out[...].astype(BF)
+    total[...] = kept[...] + added[BLK:]
+    halve(where, bit, total, keep, stage)
+    send[BLK:, :] = stage[...].astype(BF)
+
+
+def last_kernel(where, glob, kept, came, out, weight, total):
+    added = came[...].astype(F32)
+    chunk = (glob[...] + added[0:BLK]).astype(BF)
+    target = jnp.where(where[10] == 0, where[8], where[9])
+    for j in range(CHUNKS):
+        out[j] = jnp.where(target == j, chunk, jnp.zeros_like(chunk))
+    total[...] = kept[...] + added[BLK:]
+    for part in range(4):
+        weight[:, part * HALF : (part + 1) * HALF] = total[4 * part : 4 * part + 4, :]
+
+
+def fold_call(kernel, where, args, rows, name):
     vm = pl.BlockSpec(memory_space=pltpu.VMEM)
     return pl.pallas_call(
-        route_z_kernel,
-        out_shape=far((8, 48, 1024)),
-        in_specs=[smem(), vm, vm],
-        out_specs=vm,
-        scratch_shapes=[pltpu.VMEM((64, D), F32), pltpu.VMEM((16, 1024), F32)],
+        kernel,
+        out_shape=[far((BLK, HALF), F32), far((rows, HALF), F32), far((BLK + rows, HALF))],
+        in_specs=[smem()] + [vm] * len(args),
+        out_specs=[vm] * 3,
+        scratch_shapes=[pltpu.VMEM((2 * rows, HALF), F32), pltpu.VMEM((rows, HALF), F32)],
         compiler_params=params(),
-        name="route_z",
-    )(where, x, w)
-
-
-def route_yx_kernel(where, x, out, mine, other, total):
-    total[...] = jnp.sum(x[...].astype(F32), axis=0)
-    target = jnp.where(where[12] == 0, where[10], where[11])
-    chunk = total[0:32, :]
-    for j in range(8):
-        out[j] = jnp.where(target == j, chunk, 0.0).astype(BF)
-    left = where[14] == 0
-    for half in range(2):
-        cols = slice(half * 1024, (half + 1) * 1024)
-        one = total[32 + 8 * half : 36 + 8 * half, :]
-        two = total[36 + 8 * half : 40 + 8 * half, :]
-        mine[:, cols] = jnp.where(left, one, two)
-        other[:, cols] = jnp.where(left, two, one)
-
-
-def route_yx(where, x):
+        name=name,
+    )(where, *args)
+
+
+def first(where, x):
+    return fold_call(lambda *refs: first_kernel(Z_BITS[0], *refs), where, (x,), 64, "first")
+
+
+def fold(where, bit, glob, kept, came):
+    rows = kept.shape[0] // 2
+    return fold_call(lambda *refs: fold_kernel(bit, *refs), where, (glob, kept, came), rows, "fold")
+
+
+def last(where, glob, kept, came):
     vm = pl.BlockSpec(memory_space=pltpu.VMEM)
     return pl.pallas_call(
-        route_yx_kernel,
-        out_shape=[far((8, 32, 1024)), far((4, D), F32), far((4, D), F32)],
-        in_specs=[smem(), vm],
-        out_specs=[vm] * 3,
-        scratch_shapes=[pltpu.VMEM((48, 1024), F32)],
+        last_kernel,
+        out_shape=[far((CHUNKS, BLK, HALF)), far((4, D), F32)],
+        in_specs=[smem()] + [vm] * 3,
+        out_specs=[vm] * 2,
+        scratch_shapes=[pltpu.VMEM((16, HALF), F32)],
         compiler_params=params(),
-        name="route_yx",
-    )(where, x)
+        name="last",
+    )(where, glob, kept, came)
 
 
 def finish_kernel(where, own, left, right, *rest):
-    rand, (glob, mine, other, dk, dv, weight, acc) = rest[:BITS], rest[BITS:]
-    weight[...] = mine[...] + other[...]
+    rand, (glob, dk, dv, acc) = rest[:BITS], rest[BITS:]
     acc[...] = own[...]
     acc[:, 0:BLK, :] += left[...].astype(F32)
     acc[:, BLK : 2 * BLK, :] += right[...].astype(F32)
@@ -449,35 +492,36 @@
         @pl.when(here >= 0)
         def _():
             rows = pl.ds(pl.multiple_of(jnp.maximum(here, 0) * BLK, BLK), BLK)
-            acc[:, rows, :] += glob[:, g].astype(F32)
+            acc[:, rows, :] += glob[0, :, g].astype(F32)
 
     dk[...] = acc[0].astype(BF)
     dv[...] = acc[1].astype(BF)
 
 
-def finish(where, own, left, right, rand, glob, mine, other):
+def finish(where, own, left, right, rand, glob):
     wide = 256
     pair = pl.BlockSpec((2, BLK, wide), lambda i: (0, 0, i))
     flat = pl.BlockSpec((TOK, wide), lambda i: (0, i))
-    rows = pl.BlockSpec((4, 2 * wide), lambda i: (0, i))
     return pl.pallas_call(
         finish_kernel,
         grid=(WIDTH // wide,),
         in_specs=[smem(), pl.BlockSpec((2, TOK, wide), lambda i: (0, 0, i)), pair, pair]
         + [pair] * BITS
-        + [pl.BlockSpec((2, GLOB, BLK, wide), lambda i: (0, 0, 0, i)), rows, rows],
-        out_specs=[flat, flat, rows],
-        out_shape=[far((TOK, WIDTH)), far((TOK, WIDTH)), far((4, D), F32)],
+        + [pl.BlockSpec((1, 2, GLOB, BLK, wide), lambda i: (i // 2, 0, 0, 0, i % 2))],
+        out_specs=[flat, flat],
+        out_shape=[far((TOK, WIDTH)), far((TOK, WIDTH))],
         scratch_shapes=[pltpu.VMEM((2, TOK, wide), F32)],
         compiler_params=params(dimension_semantics=("arbitrary",)),
         name="finish",
-    )(where, *from_hbm(own), left, right, *rand, glob, mine, other)
+    )(where, *from_hbm(own, left, right, *rand), glob)
 
 
 def feature_order(rep):
     new = jnp.arange(WIDTH, dtype=jnp.int32)
-    r, y, x, z, j = (new // 256) ^ rep, (new // 64) % 4, (new // 4) % 2, (new // 8) % 8, new % 4
-    old = y * 256 + z * 32 + x * 16 + r * 4 + j
+    stretch = ((new // 64) % 4) * 16 + (new // 32) % 2
+    for i, bit in enumerate(Z_BITS):
+        stretch = stretch + ((new // (16 >> i)) % 2) * (1 << bit)
+    old = stretch * 16 + ((new // 256) ^ rep) * 4 + new % 4
     return (jnp.arange(WIDTH, dtype=jnp.int32)[:, None] == old[None, :]).astype(BF)
 
 
@@ -488,56 +532,94 @@
 def per_device(queries, keys, values, w_out, d_out, rand_slot, global_ids):
     q, k, v, grad_out = queries[0], keys[0], values[0], d_out[0]
     where = where_of(rand_slot[0, 0], global_ids[0])
-    *chosen, first, last, picked = pick(where, k, v)
-    spread = trade(picked.reshape(8, 32, WIDTH), Z_GROUPS)
+    *chosen, low_edge, high_edge, picked = pick(where, k, v)
+    spread = trade(picked)
     mixed = jnp.concatenate([w_out[:HEAD_DIM], grad_out])
     upper = w_out[HEAD_DIM:]
     mixed2 = across(mixed, 2)
     upper2 = beside(upper)
+    rand = [None] * BITS
+    for b in FIRST:
+        rand[b] = swapped(chosen[b], b)
+    tied = together(spread, *[rand[b] for b in FIRST], low_edge, high_edge, *chosen)
+    spread, tied = tied[0], tied[1:]
+    for b in FIRST:
+        rand[b], tied = tied[0], tied[1:]
+    low_edge, high_edge, *chosen = tied
+    mine = gathered(spread)
+    for b in SECOND:
+        rand[b] = swapped(chosen[b], b)
+    for b in Z_BITS[:2]:
+        mine = relay(mine, swapped(mine, b), (BLK, HALF))
+    other = swapped(mine, Z_BITS[2])
+    tied = together(
+        mine, other, mixed2, upper2, *[rand[b] for b in SECOND], low_edge, high_edge, *chosen
+    )
+    mine, other, mixed2, upper2, *tied = tied
+    for b in SECOND:
+        rand[b], tied = tied[0], tied[1:]
+    low_edge, high_edge, *chosen = tied
+    glob = trade(relay(mine, other, (CHUNKS, BLK, HALF))).reshape(2, 2 * TOK, HALF)
+    mixed3 = across(mixed2, 1)
+    upper3 = across(upper2, 1)
     mixed1 = across(mixed, 1)
     upper1 = across(upper, 1)
-    rand = [swapped(chosen[b], b) for b in range(BITS)]
-    lo = shifted(last, 1)
-    hi = shifted(first, -1)
-    spread, rand[4], rand[1], mixed1, upper1 = together(spread, rand[4], rand[1], mixed1, upper1)
-    spread = trade(relay(spread), YX_GROUPS)
-    spread, rand[3], rand[5], mixed2, upper2 = together(spread, rand[3], rand[5], mixed2, upper2)
-    mixed3 = across(mixed2, 1)
-    upper3 = across(upper2, 1)
-    glob = trade(relay(spread), Z_GROUPS).reshape(2, GLOB * BLK, WIDTH)
+    for b in THIRD:
+        rand[b] = swapped(chosen[b], b)
+    lo = shifted(high_edge, 1)
+    hi = shifted(low_edge, -1)
     parts = (w_out, upper, mixed1, upper1, mixed2, upper2, mixed3, upper3)
     d_attn = project(where, parts, grad_out)
     order = feature_order(lax.axis_index("rep"))
-    glob, d_attn, order = together(glob, d_attn, order)
-    early = from_hbm(rand[1], rand[3], rand[4], rand[5])
-    mixed_rand = [rand[0], early[0], rand[2], early[1], early[2], early[3]]
+    glob, lo, hi, d_attn, order, *tied = together(
+        glob, lo, hi, d_attn, order, *[rand[b] for b in THIRD]
+    )
+    for b in THIRD:
+        rand[b], tied = tied[0], tied[1:]
+    lo, hi, *rand = from_hbm(lo, hi, *rand)
     attn, stats, *ordered = forward(
-        where, *from_hbm(q, k, v), lo, hi, mixed_rand, glob, *from_hbm(order)
+        where, *from_hbm(q, k, v), lo, hi, rand, glob, *from_hbm(order)
     )
     cols = [ordered[0]] + [across(ordered[a], a) for a in range(1, 4)]
-    layer = layer_of(where, parts, attn)
-    layer, *cols = together(layer, *cols)
-    weight = weight_payload(cols, (grad_out, mixed1, mixed2, mixed3))
-    weight, d_attn = together(weight, d_attn)
-    weight = lax.psum_scatter(
-        weight, "seq", scatter_dimension=0, axis_index_groups=Y_GROUPS, tiled=True
-    )
     (dq, down, dlo, dhi), drand, dglob = backward(
         where, q, k, v, lo, hi, rand, glob, stats, d_attn
     )
-    payload = trade(dglob.reshape(8, 32, WIDTH), YX_GROUPS)
-    back = [swapped(drand[b], b) for b in range(BITS)]
+    cols[1], cols[2], cols[3], dglob = together(cols[1], cols[2], cols[3], dglob)
+    payload = weight_payload(
+        cols, (grad_out, mixed1, mixed2, mixed3), dglob.reshape(CHUNKS, BLK, HALF)
+    )
+    payload = trade(payload)
+    back = [None] * BITS
+    for b in FIRST:
+        back[b] = swapped(drand[b], b)
+    payload, attn, dlo, dhi, *tied = together(
+        payload, attn, dlo, dhi, *[back[b] for b in FIRST], *drand
+    )
+    for b in FIRST:
+        back[b], tied = tied[0], tied[1:]
+    drand = tied
+    for b in SECOND:
+        back[b] = swapped(drand[b], b)
+    glob_sum, keep, send = first(where, payload)
+    for step, bit in enumerate(Z_BITS[1:]):
+        came = swapped(send, Z_BITS[step])
+        glob_sum, keep, send = fold(where, bit, glob_sum, keep, came)
+    came = swapped(send, Z_BITS[2])
+    came, attn, dlo, dhi, *tied = together(
+        came, attn, dlo, dhi, *[back[b] for b in SECOND], *drand
+    )
+    for b in SECOND:
+        back[b], tied = tied[0], tied[1:]
+    drand = tied
+    routed, weight_grad = last(where, glob_sum, keep, came)
+    glob_total = trade(routed).reshape(2, 2, GLOB, BLK, HALF)
+    for b in THIRD:
+        back[b] = swapped(drand[b], b)
     right = shifted(dlo, -1)
     left = shifted(dhi, 1)
-    payload, weight, back[3] = together(payload, weight, back[3])
-    payload = trade(route_z(where, payload, weight), Z_GROUPS)
-    payload, back[0], back[4], back[5], left = together(
-        payload, back[0], back[4], back[5], left
-    )
-    payload, mine, other = route_yx(where, payload)
-    glob_total = trade(payload, YX_GROUPS).reshape(2, GLOB, BLK, WIDTH)
-    other = swapped(other, 0)
-    dk, dv, weight_grad = finish(where, down, left, right, back, glob_total, mine, other)
+    layer = layer_of(where, parts, attn)
+    glob_total, layer = together(glob_total, layer)
+    dk, dv = finish(where, down, left, right, back, glob_total)
     return (layer[None], dq[None], dk[None], dv[None], weight_grad)
 
 

time: 232 us -> 215 us (0.927)
  waiting for transfers between devices: 88 us -> 68.3 us
  between operations: 14.3 us -> 1.12 us
  Pallas kernels: 37.6 us -> 47.9 us
  starting transfers between devices: 78 us -> 82.5 us
    ppermute x13 -> x18, starting transfers between devices: 23.5 us -> 42.7 us  [swapped(): return lax.ppermute(value, 'seq', [(s, s ^ 1 << bit) for s in range(64)])]
    ppermute x4, waiting for transfers between devices: 26.2 us -> 7.91 us  [shifted(): lax.ppermute(value, 'seq', [(s, (s + steps) % 64) for s in range(64)])]
    all_to_all x6 -> x4, starting transfers between devices: 39.1 us -> 22.5 us  [trade(): lax.all_to_all(value, 'seq', 0, 0, axis_index_groups=YX_GROUPS, tiled=True)]
    pallas_call x5 -> x9, Pallas kernels: 7.39 us -> 14.1 us  [the longest x1 5.95 us: weight_payload(): pl.pallas_call(weight_kernel, grid=(6,), in_specs=[pl.BlockSpec((TOK, 256...]
    ppermute x4, starting transfers between devices: 9.43 us -> 13.2 us  [shifted(): lax.ppermute(value, 'seq', [(s, (s + steps) % 64) for s in range(64)])]
    pallas_call x2, Pallas kernels: 11.1 us -> 14.5 us  [head_call(): pl.pallas_call(kernel, grid_spec=pltpu.PrefetchScalarGridSpec(num_scalar_...]
    ppermute x13 -> x18, waiting for transfers between devices: 61.8 us -> 60.4 us  [swapped(): return lax.ppermute(value, 'seq', [(s, s ^ 1 << bit) for s in range(64)])]
    unnamed x62 -> x76, local copies, waits for them, and re-layouts: 7.94 us -> 9.26 us
  transfers between devices with their start and end apart: 33 -> 35, of which waited for: 13 -> 17; matrix products, arithmetic and copies ran while one was open for 1% -> 1% of each run, Pallas kernels for 10% -> 14%
where the time goes in v4:
time: 215 us; the launch traced here: 214 us
  starting transfers between devices  82.5 us (38%)
  waiting for transfers between devices  68.3 us (32%)
  Pallas kernels  47.9 us (22%)
  local copies, waits for them, and re-layouts  10.7 us (5%)
  other arithmetic  3.39 us (2%)
    ppermute x18, waiting for transfers between devices, swapped(): return lax.ppermute(value, 'seq', [(s, s ^ 1 << bit) for s in range(64)])  60.4 us
    ppermute x18, starting transfers between devices, swapped(): return lax.ppermute(value, 'seq', [(s, s ^ 1 << bit) for s in range(64)])  42.7 us
    all_to_all x4, starting transfers between devices, trade(): lax.all_to_all(value, 'seq', 0, 0, axis_index_groups=YX_GROUPS, tiled=True)  22.5 us
    pallas_call x2, Pallas kernels, head_call(): pl.pallas_call(kernel, grid_spec=pltpu.PrefetchScalarGridSpec(num_scalar_...  14.5 us
    ppermute x4, starting transfers between devices, shifted(): lax.ppermute(value, 'seq', [(s, (s + steps) % 64) for s in range(64)])  13.2 us
    unnamed x76, local copies, waits for them, and re-layouts  9.26 us
    ppermute x4, waiting for transfers between devices, shifted(): lax.ppermute(value, 'seq', [(s, (s + steps) % 64) for s in range(64)])  7.91 us
    pallas_call x1, Pallas kernels, backward(): pl.pallas_call(backward_kernel, grid=(HEADS // STEP,), in_specs=[smem(),...  7.05 us
  transfers between devices with their start and end apart: 35, of which 17 were waited for; matrix products, arithmetic and copies ran while one was open for 1% of the time, Pallas kernels for 14%

profile of v4, /device:TPU:8, one launch (start us, length us, event | category | flops | bytes accessed | tf_op | source)
XLA Modules:
  0.0 213.9 jit_solution(7889262056714450179)
XLA Ops:
  0.7 1.4 fusion.37
  2.1 1.2 pad_maximum_fusion
  3.2 1.5 collective-permute-start.6
  4.9 2.2 %pick.1 = (bf16[2,64,1024]{2,1,0:T(8,128)(2,1)}, bf16[2,64,1024]{2,1,0:T(8,128)(2,1)}, bf16[2,64,1024]{2,1,0:T(8,128)(2,1)}, bf16[2,64,1024]{2,1,0:T(8,128)(2,1)...) custom-call(s32[14]{0:T(128)S(1)} %concatenate.6.where.refs_0_, ...), custom_call_target="tpu_custom_call" | custom-call | tf_op jit(solution)/shard_map/pick/pallas_call | solution.py:114
  7.1 7.1 %all-to-all-start = ((bf16[8,64,512]{2,1,0:T(8,128)(2,1)}), bf16[8,64,512]{2,1,0:T(8,128)(2,1)S(1)}, u32[]{:S(2)}, u32[]{:S(2)}) async-start(bf16[8,64,512]{2,1,0:T(8,128)(2,1)} %get-tuple-element.91), calls=%async_computation | async-start | bytes 1048576 | tf_op jit(solution)/shard_map/all_to_all | solution.py:44
  14.2 7.2 %collective-permute-start = (bf16[2,64,1024]{2,1,0:T(8,128)(2,1)}, bf16[2,64,1024]{2,1,0:T(8,128)(2,1)S(1)}, u32[]{:S(2)}, u32[]{:S(2)}) collective-permute-start(bf16[2,64,1024]{2,1,0:T(8,128)(2,1)} %get-tuple-element.92), channel_id=1, source_target_pairs={{0,32},{4,36},{8,40},{12,44},{16,48},{20,52},{24,56},{28,60},{32,0... | collective-permute-start | bytes 786440 | tf_op jit(solution)/shard_map/ppermute | solution.py:52
  21.3 3.5 %collective-permute-start.2 = (bf16[2,64,1024]{2,1,0:T(8,128)(2,1)}, bf16[2,64,1024]{2,1,0:T(8,128)(2,1)S(1)}, u32[]{:S(2)}, u32[]{:S(2)}) collective-permute-start(bf16[2,64,1024]{2,1,0:T(8,128)(2,1)} %get-tuple-element.94), channel_id=1, source_target_pairs={{0,4},{4,0},{8,12},{12,8},{16,20},{20,16},{24,28},{28,24},{32,36},... | collective-permute-start | bytes 786440 | tf_op jit(solution)/shard_map/ppermute | solution.py:52
  24.9 3.3 %collective-permute-done.rest_3_ = bf16[2,64,1024]{2,1,0:T(8,128)(2,1)S(1)} collective-permute-done((bf16[2,64,1024]{2,1,0:T(8,128)(2,1)}, bf16[2,64,1024]{2,1,0:T(8,128)(2,1)S(1)}, u32[]{:S(2)}, u32[]{:S(2)}) %collective-permute-start) | collective-permute-done | bytes 262176 | tf_op jit(solution)/shard_map/ppermute | solution.py:52
  28.5 13.4 %collective-permute-done.2.rest_0_ = bf16[2,64,1024]{2,1,0:T(8,128)(2,1)S(1)} collective-permute-done((bf16[2,64,1024]{2,1,0:T(8,128)(2,1)}, bf16[2,64,1024]{2,1,0:T(8,128)(2,1)S(1)}, u32[]{:S(2)}, u32[]{:S(2)}) %collective-permute-start.2) | collective-permute-done | bytes 262176 | tf_op jit(solution)/shard_map/ppermute | solution.py:52
  41.9 0.7 gathered.1.mine
  42.6 1.9 collective-permute-start.3
  44.5 2.6 %collective-permute-done.3.other = bf16[64,512]{1,0:T(8,128)(2,1)S(1)} collective-permute-done((bf16[64,512]{1,0:T(8,128)(2,1)}, bf16[64,512]{1,0:T(8,128)(2,1)S(1)}, u32[]{:S(2)}, u32[]{:S(2)}) %collective-permute-start.3) | collective-permute-done | bytes 65568 | tf_op jit(solution)/shard_map/ppermute | solution.py:52
  47.1 0.8 copy-done.5
  48.6 3.3 %collective-permute-start.4 = (bf16[64,512]{1,0:T(8,128)(2,1)}, bf16[64,512]{1,0:T(8,128)(2,1)S(1)}, u32[]{:S(2)}, u32[]{:S(2)}) collective-permute-start(bf16[64,512]{1,0:T(8,128)(2,1)} %relay.3.mine), channel_id=1, source_target_pairs={{0,16},{4,20},{8,24},{12,28},{16,0},{20,4},{24,8},{28,12},{32,48},... | collective-permute-start | bytes 196616 | tf_op jit(solution)/shard_map/ppermute | solution.py:52
  51.8 2.3 %collective-permute-start.8 = (bf16[2,64,1024]{2,1,0:T(8,128)(2,1)}, bf16[2,64,1024]{2,1,0:T(8,128)(2,1)S(1)}, u32[]{:S(2)}, u32[]{:S(2)}) collective-permute-start(bf16[2,64,1024]{2,1,0:T(8,128)(2,1)} %get-tuple-element.101), channel_id=1, source_target_pairs={{0,128},{4,132},{8,136},{12,140},{16,144},{20,148},{24,152},{28,15... | collective-permute-start | bytes 786440 | tf_op jit(solution)/shard_map/ppermute | solution.py:52
  54.3 1.9 collective-permute-start.9
  56.2 0.8 copy-done.4
  57.7 6.0 %collective-permute-start.5 = (bf16[64,512]{1,0:T(8,128)(2,1)}, bf16[64,512]{1,0:T(8,128)(2,1)S(1)}, u32[]{:S(2)}, u32[]{:S(2)}) collective-permute-start(bf16[64,512]{1,0:T(8,128)(2,1)} %relay.4.mine), channel_id=1, source_target_pairs={{0,32},{4,36},{8,40},{12,44},{16,48},{20,52},{24,56},{28,60},{32,0... | collective-permute-start | bytes 196616 | tf_op jit(solution)/shard_map/ppermute | solution.py:52
  63.7 5.5 %collective-permute-done.5.other = bf16[64,512]{1,0:T(8,128)(2,1)S(1)} collective-permute-done((bf16[64,512]{1,0:T(8,128)(2,1)}, bf16[64,512]{1,0:T(8,128)(2,1)S(1)}, u32[]{:S(2)}, u32[]{:S(2)}) %collective-permute-start.5) | collective-permute-done | bytes 65568 | tf_op jit(solution)/shard_map/ppermute | solution.py:52
  70.0 0.8 copy-done.3
  70.9 0.8 relay.5
  71.7 4.8 %all-to-all-start.1 = ((bf16[8,64,512]{2,1,0:T(8,128)(2,1)}), bf16[8,64,512]{2,1,0:T(8,128)(2,1)S(1)}, u32[]{:S(2)}, u32[]{:S(2)}) async-start(bf16[8,64,512]{2,1,0:T(8,128)(2,1)} %relay.5), calls=%async_computation.1 | async-start | bytes 1048576 | tf_op jit(solution)/shard_map/all_to_all | solution.py:44
  76.5 3.0 %collective-permute-start.10 = (bf16[2,64,1024]{2,1,0:T(8,128)(2,1)}, bf16[2,64,1024]{2,1,0:T(8,128)(2,1)S(1)}, u32[]{:S(2)}, u32[]{:S(2)}) collective-permute-start(bf16[2,64,1024]{2,1,0:T(8,128)(2,1)} %get-tuple-element.108), channel_id=1, source_target_pairs={{0,4},{4,8},{8,12},{12,16},{16,20},{20,24},{24,28},{28,32},{32,36}... | collective-permute-start | bytes 786440 | tf_op jit(solution)/shard_map/ppermute | solution.py:48
  79.5 3.6 %collective-permute-start.11 = (bf16[2,64,1024]{2,1,0:T(8,128)(2,1)}, bf16[2,64,1024]{2,1,0:T(8,128)(2,1)S(1)}, u32[]{:S(2)}, u32[]{:S(2)}) collective-permute-start(bf16[2,64,1024]{2,1,0:T(8,128)(2,1)} %get-tuple-element.109), channel_id=1, source_target_pairs={{0,252},{4,0},{8,4},{12,8},{16,12},{20,16},{24,20},{28,24},{32,28}... | collective-permute-start | bytes 786440 | tf_op jit(solution)/shard_map/ppermute | solution.py:48
  83.1 2.2 %fusion.rest_7_ = bf16[1024,1024]{1,0:T(8,128)(2,1)} fusion(s32[1024]{0:T(1024)S(1)} %fusion.15), kind=kLoop, calls=%fused_computation.1 | loop fusion | flops 2097152 | bytes 2101248 | tf_op jit(solution)/shard_map/convert_element_type | solution.py:525
  85.3 7.0 %project.1.rest_8_ = bf16[128,1024]{1,0:T(8,128)(2,1)} custom-call(s32[14]{0:T(128)S(1)} %concatenate.6.where.refs_0_, bf16[256,2048]{1,0:T(8,128)(2,1)} %refs_0_.3, bf16[128,2048]{1,0:T(8,128)(2,1)} %copy-done.14, bf16[256,2048]{1,0:T(8,128)(2,1)} %copy-done.13, bf16[128,2048]{1,0:T(8,128)(2,1)} %collective-permute-done.13.refs_3_, ...), custom_call_target="tpu_custom_call" | custom-call | tf_op jit(solution)/shard_map/project/pallas_call | solution.py:309
  92.4 1.8 collective-permute-done.10.lo
  94.2 3.3 %collective-permute-done.11.hi = bf16[2,64,1024]{2,1,0:T(8,128)(2,1)S(1)} collective-permute-done((bf16[2,64,1024]{2,1,0:T(8,128)(2,1)}, bf16[2,64,1024]{2,1,0:T(8,128)(2,1)S(1)}, u32[]{:S(2)}, u32[]{:S(2)}) %collective-permute-start.11) | collective-permute-done | bytes 262176 | tf_op jit(solution)/shard_map/ppermute | solution.py:48
  97.5 2.5 %collective-permute-done.16.rest_2_ = bf16[2,64,1024]{2,1,0:T(8,128)(2,1)S(1)} collective-permute-done((bf16[2,64,1024]{2,1,0:T(8,128)(2,1)}, bf16[2,64,1024]{2,1,0:T(8,128)(2,1)S(1)}, u32[]{:S(2)}, u32[]{:S(2)}) %collective-permute-start.16) | collective-permute-done | bytes 262176 | tf_op jit(solution)/shard_map/ppermute | solution.py:52
  100.0 0.7 copy-done.23
  100.7 6.1 %forward.1 = (bf16[128,1024]{1,0:T(8,128)(2,1)}, f32[8,8,128]{2,1,0:T(8,128)}, bf16[128,256]{1,0:T(8,128)(2,1)S(1)}, bf16[128,256]{1,0:T(8,128)(2,1)S(1)}, bf16[...) custom-call(s32[14]{0:T(128)S(1)} %concatenate.6.where.refs_0_, bf16[128,1024]{1,0:T(8,128)(2,1)} %bitcast.43, ...), custom_call_target="tpu_custom_call" | custom-call | tf_op jit(solution)/shard_map/forward/pallas_call | solution.py:221
  107.1 1.7 collective-permute-start.19
  108.8 7.0 %backward.1 = (bf16[128,1024]{1,0:T(8,128)(2,1)}, f32[2,128,1024]{2,1,0:T(8,128)}, bf16[2,64,1024]{2,1,0:T(8,128)(2,1)}, bf16[2,64,1024]{2,1,0:T(8,128)(2,1)}, b...) custom-call(s32[14]{0:T(128)S(1)} %concatenate.6.where.refs_0_, ...), custom_call_target="tpu_custom_call" | custom-call | tf_op jit(solution)/shard_map/backward/pallas_call | solution.py:282
  115.9 6.0 %weight.1 = bf16[8,192,512]{2,1,0:T(8,128)(2,1)} custom-call(bf16[128,256]{1,0:T(8,128)(2,1)S(1)} %get-tuple-element.123.refs_0_, bf16[128,256]{1,0:T(8,128)(2,1)S(1)} %collective-permute-done.17.refs_1_, bf16[128,256]{1,0:T(8,128)(2,1)S(1)} %collective-permute-done.18.refs_2_, bf16[128,256]{1,0:T(8,128)(2,1)S(1)} %collective-permute-done.19.refs_3_, ...), custom_call_target="tpu_custom_call" | custom-call | tf_op jit(solution)/shard_map/weight/pallas_call | solution.py:393
  121.8 5.0 %all-to-all-start.2 = ((bf16[8,192,512]{2,1,0:T(8,128)(2,1)}), bf16[8,192,512]{2,1,0:T(8,128)(2,1)S(1)}, u32[]{:S(2)}, u32[]{:S(2)}) async-start(bf16[8,192,512]{2,1,0:T(8,128)(2,1)} %weight.1), calls=%async_computation.2 | async-start | bytes 3145728 | tf_op jit(solution)/shard_map/all_to_all | solution.py:44
  126.8 4.5 %collective-permute-start.20 = (bf16[2,64,1024]{2,1,0:T(8,128)(2,1)}, bf16[2,64,1024]{2,1,0:T(8,128)(2,1)S(1)}, u32[]{:S(2)}, u32[]{:S(2)}) collective-permute-start(bf16[2,64,1024]{2,1,0:T(8,128)(2,1)} %get-tuple-element.137), channel_id=1, source_target_pairs={{0,32},{4,36},{8,40},{12,44},{16,48},{20,52},{24,56},{28,60},{32,0... | collective-permute-start | bytes 786440 | tf_op jit(solution)/shard_map/ppermute | solution.py:52
  131.3 3.5 %collective-permute-start.22 = (bf16[2,64,1024]{2,1,0:T(8,128)(2,1)}, bf16[2,64,1024]{2,1,0:T(8,128)(2,1)S(1)}, u32[]{:S(2)}, u32[]{:S(2)}) collective-permute-start(bf16[2,64,1024]{2,1,0:T(8,128)(2,1)} %get-tuple-element.139), channel_id=1, source_target_pairs={{0,4},{4,0},{8,12},{12,8},{16,20},{20,16},{24,28},{28,24},{32,36},... | collective-permute-start | bytes 786440 | tf_op jit(solution)/shard_map/ppermute | solution.py:52
  134.8 9.8 %collective-permute-done.20.rest_3_ = bf16[2,64,1024]{2,1,0:T(8,128)(2,1)S(1)} collective-permute-done((bf16[2,64,1024]{2,1,0:T(8,128)(2,1)}, bf16[2,64,1024]{2,1,0:T(8,128)(2,1)S(1)}, u32[]{:S(2)}, u32[]{:S(2)}) %collective-permute-start.20) | collective-permute-done | bytes 262176 | tf_op jit(solution)/shard_map/ppermute | solution.py:52
  144.7 5.8 %collective-permute-done.21.rest_4_ = bf16[2,64,1024]{2,1,0:T(8,128)(2,1)S(1)} collective-permute-done((bf16[2,64,1024]{2,1,0:T(8,128)(2,1)}, bf16[2,64,1024]{2,1,0:T(8,128)(2,1)S(1)}, u32[]{:S(2)}, u32[]{:S(2)}) %collective-permute-start.21) | collective-permute-done | bytes 262176 | tf_op jit(solution)/shard_map/ppermute | solution.py:52
  150.4 2.7 %collective-permute-done.22.rest_0_ = bf16[2,64,1024]{2,1,0:T(8,128)(2,1)S(1)} collective-permute-done((bf16[2,64,1024]{2,1,0:T(8,128)(2,1)}, bf16[2,64,1024]{2,1,0:T(8,128)(2,1)S(1)}, u32[]{:S(2)}, u32[]{:S(2)}) %collective-permute-start.22) | collective-permute-done | bytes 262176 | tf_op jit(solution)/shard_map/ppermute | solution.py:52
  153.1 1.4 first.1
  154.6 2.1 collective-permute-start.26
  156.6 2.0 collective-permute-start.27
  158.7 2.5 %collective-permute-done.23.refs_3_ = bf16[128,512]{1,0:T(8,128)(2,1)S(1)} collective-permute-done((bf16[128,512]{1,0:T(8,128)(2,1)}, bf16[128,512]{1,0:T(8,128)(2,1)S(1)}, u32[]{:S(2)}, u32[]{:S(2)}) %collective-permute-start.23) | collective-permute-done | bytes 131104 | tf_op jit(solution)/shard_map/ppermute | solution.py:52
  161.1 0.9 copy-done.6
  162.1 0.9 copy-done.7
  163.0 1.3 fold.2
  164.2 5.9 %collective-permute-done.24.refs_3_ = bf16[96,512]{1,0:T(8,128)(2,1)S(1)} collective-permute-done((bf16[96,512]{1,0:T(8,128)(2,1)}, bf16[96,512]{1,0:T(8,128)(2,1)S(1)}, u32[]{:S(2)}, u32[]{:S(2)}) %collective-permute-start.24) | collective-permute-done | bytes 98336 | tf_op jit(solution)/shard_map/ppermute | solution.py:52
  170.1 0.9 copy-done.8
  171.0 0.8 copy-done.10
  171.8 1.3 fold.3
  173.1 4.4 %collective-permute-start.25 = (bf16[80,512]{1,0:T(8,128)(2,1)}, bf16[80,512]{1,0:T(8,128)(2,1)S(1)}, u32[]{:S(2)}, u32[]{:S(2)}) collective-permute-start(bf16[80,512]{1,0:T(8,128)(2,1)} %get-tuple-element.152), channel_id=1, source_target_pairs={{0,32},{4,36},{8,40},{12,44},{16,48},{20,52},{24,56},{28,60},{32,0... | collective-permute-start | bytes 245768 | tf_op jit(solution)/shard_map/ppermute | solution.py:52
  177.5 4.1 %collective-permute-done.25.came = bf16[80,512]{1,0:T(8,128)(2,1)S(1)} collective-permute-done((bf16[80,512]{1,0:T(8,128)(2,1)}, bf16[80,512]{1,0:T(8,128)(2,1)S(1)}, u32[]{:S(2)}, u32[]{:S(2)}) %collective-permute-start.25) | collective-permute-done | bytes 81952 | tf_op jit(solution)/shard_map/ppermute | solution.py:52
  181.7 0.9 copy-done.9
  182.6 0.8 copy-done.11
  183.3 1.4 last.1
  184.7 5.7 %all-to-all-start.3 = ((bf16[8,64,512]{2,1,0:T(8,128)(2,1)}), bf16[8,64,512]{2,1,0:T(8,128)(2,1)S(1)}, u32[]{:S(2)}, u32[]{:S(2)}) async-start(bf16[8,64,512]{2,1,0:T(8,128)(2,1)} %get-tuple-element.160), calls=%async_computation.3 | async-start | bytes 1048576 | tf_op jit(solution)/shard_map/all_to_all | solution.py:44
  190.4 3.0 %collective-permute-start.28 = (bf16[2,64,1024]{2,1,0:T(8,128)(2,1)S(1)}, bf16[2,64,1024]{2,1,0:T(8,128)(2,1)S(1)}, u32[]{:S(2)}, u32[]{:S(2)}) collective-permute-start(bf16[2,64,1024]{2,1,0:T(8,128)(2,1)S(1)} %copy-done.36), channel_id=1, source_target_pairs={{0,4},{4,8},{8,12},{12,16},{16,20},{20,24},{24,28},{28,32},{32,36}... | collective-permute-start | bytes 786440 | tf_op jit(solution)/shard_map/ppermute | solution.py:48
  193.4 3.6 %collective-permute-start.29 = (bf16[2,64,1024]{2,1,0:T(8,128)(2,1)S(1)}, bf16[2,64,1024]{2,1,0:T(8,128)(2,1)S(1)}, u32[]{:S(2)}, u32[]{:S(2)}) collective-permute-start(bf16[2,64,1024]{2,1,0:T(8,128)(2,1)S(1)} %copy-done.35), channel_id=1, source_target_pairs={{0,252},{4,0},{8,4},{12,8},{16,12},{20,16},{24,20},{28,24},{32,28}... | collective-permute-start | bytes 786440 | tf_op jit(solution)/shard_map/ppermute | solution.py:48
  196.9 7.5 %layer.1 = bf16[128,2048]{1,0:T(8,128)(2,1)} custom-call(s32[14]{0:T(128)S(1)} %concatenate.6.where.refs_0_, bf16[256,2048]{1,0:T(8,128)(2,1)} %refs_0_.3, bf16[128,2048]{1,0:T(8,128)(2,1)} %copy-done.14, bf16[256,2048]{1,0:T(8,128)(2,1)} %copy-done.13, bf16[128,2048]{1,0:T(8,128)(2,1)} %collective-permute-done.13.refs_3_, bf16[256,2048]{1,0:T(8,128)(2,1)} %copy-done.12, ...), custom_call_target="tpu_custom_call" | custom-call | tf_op jit(solution)/shard_map/layer/pallas_call | solution.py:309
  204.5 2.8 %collective-permute-done.29.right = bf16[2,64,1024]{2,1,0:T(8,128)(2,1)S(1)} collective-permute-done((bf16[2,64,1024]{2,1,0:T(8,128)(2,1)S(1)}, bf16[2,64,1024]{2,1,0:T(8,128)(2,1)S(1)}, u32[]{:S(2)}, u32[]{:S(2)}) %collective-permute-start.29) | collective-permute-done | bytes 262176 | tf_op jit(solution)/shard_map/ppermute | solution.py:48
  207.3 1.9 collective-permute-done.30.rest_2_
  209.2 0.7 copy-done.31
  209.9 3.8 %finish.1 = (bf16[128,1024]{1,0:T(8,128)(2,1)}, bf16[128,1024]{1,0:T(8,128)(2,1)}) custom-call(s32[14]{0:T(128)S(1)} %concatenate.6.where.refs_0_, f32[2,128,1024]{2,1,0:T(8,128)} %get-tuple-element.164.own, bf16[2,64,1024]{2,1,0:T(8,128)(2,1)} %copy-done.29, bf16[2,64,1024]{2,1,0:T(8,128)(2,1)} %copy-done.30, bf16[2,64,1024]{2,1,0:T(8,128)(2,1)} %copy-done.26, ...), custom_call_target="tpu_custom_call" | custom-call | tf_op jit(solution)/shard_map/finish/pallas_call | solution.py:505
  (104 shorter events, 3.1 us)
Async XLA Ops:
  0.6 1.4 copy-start.15
  0.6 4.1 %copy-start.32 = (s32[1,2]{1,0:T(1,128)S(1)}, s32[1,2]{1,0:T(1,128)}, u32[]{:S(2)}) copy-start(s32[1,2]{1,0:T(1,128)} %param.13) | copy-start | bytes 28
  0.7 4.1 %copy-start.33 = (s32[1,1,6]{2,1,0:T(1,128)S(1)}, s32[1,1,6]{2,1,0:T(1,128)}, u32[]{:S(2)}) copy-start(s32[1,1,6]{2,1,0:T(1,128)} %param.12) | copy-start | bytes 76
  0.7 4.2 %copy-start.1 = (bf16[1,128,1024]{2,1,0:T(8,128)(2,1)S(1)}, bf16[1,128,1024]{2,1,0:T(8,128)(2,1)}, u32[]{:S(2)}) copy-start(bf16[1,128,1024]{2,1,0:T(8,128)(2,1)} %param.8) | copy-start | bytes 786436
  0.7 4.2 %copy-start.2 = (bf16[1,128,1024]{2,1,0:T(8,128)(2,1)S(1)}, bf16[1,128,1024]{2,1,0:T(8,128)(2,1)}, u32[]{:S(2)}) copy-start(bf16[1,128,1024]{2,1,0:T(8,128)(2,1)} %param.9) | copy-start | bytes 786436
  2.1 67.4 %copy-start.14 = (bf16[128,2048]{1,0:T(8,128)(2,1)}, bf16[128,2048]{1,0:T(8,128)(2,1)S(1)}, u32[]{:S(2)}) copy-start(bf16[128,2048]{1,0:T(8,128)(2,1)S(1)} %get-tuple-element.179.refs_1_) | copy-start | bytes 1572868
  3.2 66.1 %collective-permute-start.6 = (bf16[256,2048]{1,0:T(8,128)(2,1)}, bf16[256,2048]{1,0:T(8,128)(2,1)S(1)}, u32[]{:S(2)}, u32[]{:S(2)}) collective-permute-start(bf16[256,2048]{1,0:T(8,128)(2,1)} %pad_maximum_fusion), channel_id=1, source_target_pairs={{0,2},{1,3},{2,0},{3,1},{4,6},{5,7},{6,4},{7,5},{8,10},{9,11},{10,... | collective-permute-start | bytes 3145736 | tf_op jit(solution)/shard_map/ppermute | solution.py:56
  7.1 34.8 %all-to-all-start = ((bf16[8,64,512]{2,1,0:T(8,128)(2,1)}), bf16[8,64,512]{2,1,0:T(8,128)(2,1)S(1)}, u32[]{:S(2)}, u32[]{:S(2)}) async-start(bf16[8,64,512]{2,1,0:T(8,128)(2,1)} %get-tuple-element.91), calls=%async_computation | async-start | bytes 1048576 | tf_op jit(solution)/shard_map/all_to_all | solution.py:44
  14.2 14.0 %collective-permute-start = (bf16[2,64,1024]{2,1,0:T(8,128)(2,1)}, bf16[2,64,1024]{2,1,0:T(8,128)(2,1)S(1)}, u32[]{:S(2)}, u32[]{:S(2)}) collective-permute-start(bf16[2,64,1024]{2,1,0:T(8,128)(2,1)} %get-tuple-element.92), channel_id=1, source_target_pairs={{0,32},{4,36},{8,40},{12,44},{16,48},{20,52},{24,56},{28,60},{32,0... | collective-permute-start | bytes 786440 | tf_op jit(solution)/shard_map/ppermute | solution.py:52
  21.3 7.1 %collective-permute-start.1 = (bf16[2,64,1024]{2,1,0:T(8,128)(2,1)}, bf16[2,64,1024]{2,1,0:T(8,128)(2,1)S(1)}, u32[]{:S(2)}, u32[]{:S(2)}) collective-permute-start(bf16[2,64,1024]{2,1,0:T(8,128)(2,1)} %get-tuple-element.93), channel_id=1, source_target_pairs={{0,64},{4,68},{8,72},{12,76},{16,80},{20,84},{24,88},{28,92},{32,9... | collective-permute-start | bytes 786440 | tf_op jit(solution)/shard_map/ppermute | solution.py:52
  21.3 20.5 %collective-permute-start.2 = (bf16[2,64,1024]{2,1,0:T(8,128)(2,1)}, bf16[2,64,1024]{2,1,0:T(8,128)(2,1)S(1)}, u32[]{:S(2)}, u32[]{:S(2)}) collective-permute-start(bf16[2,64,1024]{2,1,0:T(8,128)(2,1)} %get-tuple-element.94), channel_id=1, source_target_pairs={{0,4},{4,0},{8,12},{12,8},{16,20},{20,16},{24,28},{28,24},{32,36},... | collective-permute-start | bytes 786440 | tf_op jit(solution)/shard_map/ppermute | solution.py:52
  24.9 32.8 %collective-permute-start.7 = (bf16[128,2048]{1,0:T(8,128)(2,1)S(1)}, bf16[128,2048]{1,0:T(8,128)(2,1)}, u32[]{:S(2)}, u32[]{:S(2)}) collective-permute-start(bf16[128,2048]{1,0:T(8,128)(2,1)S(1)} %get-tuple-element.179.refs_1_), channel_id=1, source_target_pairs={{0,6},{1,7},{2,4},{3,5},{4,2},{5,3},{6,0},{7,1},{8,14},{9,15},{10,... | collective-permute-start | bytes 1572872 | tf_op jit(solution)/shard_map/ppermute | solution.py:61
  28.1 57.2 %copy-start.16 = (bf16[2,64,1024]{2,1,0:T(8,128)(2,1)}, bf16[2,64,1024]{2,1,0:T(8,128)(2,1)S(1)}, u32[]{:S(2)}) copy-start(bf16[2,64,1024]{2,1,0:T(8,128)(2,1)S(1)} %collective-permute-done.rest_3_) | copy-start | bytes 786436
  28.5 20.1 %copy-start.17 = (bf16[2,64,1024]{2,1,0:T(8,128)(2,1)}, bf16[2,64,1024]{2,1,0:T(8,128)(2,1)S(1)}, u32[]{:S(2)}) copy-start(bf16[2,64,1024]{2,1,0:T(8,128)(2,1)S(1)} %collective-permute-done.1.rest_4_) | copy-start | bytes 786436
  41.9 6.7 %copy-start.18 = (bf16[2,64,1024]{2,1,0:T(8,128)(2,1)}, bf16[2,64,1024]{2,1,0:T(8,128)(2,1)S(1)}, u32[]{:S(2)}) copy-start(bf16[2,64,1024]{2,1,0:T(8,128)(2,1)S(1)} %collective-permute-done.2.rest_0_) | copy-start | bytes 786436
  42.6 4.5 %collective-permute-start.3 = (bf16[64,512]{1,0:T(8,128)(2,1)}, bf16[64,512]{1,0:T(8,128)(2,1)S(1)}, u32[]{:S(2)}, u32[]{:S(2)}) collective-permute-start(bf16[64,512]{1,0:T(8,128)(2,1)} %gathered.1.mine), channel_id=1, source_target_pairs={{0,8},{4,12},{8,0},{12,4},{16,24},{20,28},{24,16},{28,20},{32,40},... | collective-permute-start | bytes 196616 | tf_op jit(solution)/shard_map/ppermute | solution.py:52
  48.6 5.7 %collective-permute-start.4 = (bf16[64,512]{1,0:T(8,128)(2,1)}, bf16[64,512]{1,0:T(8,128)(2,1)S(1)}, u32[]{:S(2)}, u32[]{:S(2)}) collective-permute-start(bf16[64,512]{1,0:T(8,128)(2,1)} %relay.3.mine), channel_id=1, source_target_pairs={{0,16},{4,20},{8,24},{12,28},{16,0},{20,4},{24,8},{28,12},{32,48},... | collective-permute-start | bytes 196616 | tf_op jit(solution)/shard_map/ppermute | solution.py:52
  51.8 31.3 %collective-permute-start.12 = (bf16[256,2048]{1,0:T(8,128)(2,1)}, bf16[256,2048]{1,0:T(8,128)(2,1)S(1)}, u32[]{:S(2)}, u32[]{:S(2)}) collective-permute-start(bf16[256,2048]{1,0:T(8,128)(2,1)} %pad_maximum_fusion), channel_id=1, source_target_pairs={{0,1},{1,0},{2,3},{3,2},{4,5},{5,4},{6,7},{7,6},{8,9},{9,8},{10,11... | collective-permute-start | bytes 3145736 | tf_op jit(solution)/shard_map/ppermute | solution.py:56
  51.8 17.4 %collective-permute-start.8 = (bf16[2,64,1024]{2,1,0:T(8,128)(2,1)}, bf16[2,64,1024]{2,1,0:T(8,128)(2,1)S(1)}, u32[]{:S(2)}, u32[]{:S(2)}) collective-permute-start(bf16[2,64,1024]{2,1,0:T(8,128)(2,1)} %get-tuple-element.101), channel_id=1, source_target_pairs={{0,128},{4,132},{8,136},{12,140},{16,144},{20,148},{24,152},{28,15... | collective-permute-start | bytes 786440 | tf_op jit(solution)/shard_map/ppermute | solution.py:52
  54.3 15.0 %collective-permute-start.9 = (bf16[2,64,1024]{2,1,0:T(8,128)(2,1)}, bf16[2,64,1024]{2,1,0:T(8,128)(2,1)S(1)}, u32[]{:S(2)}, u32[]{:S(2)}) collective-permute-start(bf16[2,64,1024]{2,1,0:T(8,128)(2,1)} %get-tuple-element.102), channel_id=1, source_target_pairs={{0,8},{4,12},{8,0},{12,4},{16,24},{20,28},{24,16},{28,20},{32,40},... | collective-permute-start | bytes 786440 | tf_op jit(solution)/shard_map/ppermute | solution.py:52
  57.7 11.6 %collective-permute-start.5 = (bf16[64,512]{1,0:T(8,128)(2,1)}, bf16[64,512]{1,0:T(8,128)(2,1)S(1)}, u32[]{:S(2)}, u32[]{:S(2)}) collective-permute-start(bf16[64,512]{1,0:T(8,128)(2,1)} %relay.4.mine), channel_id=1, source_target_pairs={{0,32},{4,36},{8,40},{12,44},{16,48},{20,52},{24,56},{28,60},{32,0... | collective-permute-start | bytes 196616 | tf_op jit(solution)/shard_map/ppermute | solution.py:52
  69.3 2.4 %copy-start.19 = (bf16[2,64,1024]{2,1,0:T(8,128)(2,1)}, bf16[2,64,1024]{2,1,0:T(8,128)(2,1)S(1)}, u32[]{:S(2)}) copy-start(bf16[2,64,1024]{2,1,0:T(8,128)(2,1)S(1)} %collective-permute-done.8.rest_5_) | copy-start | bytes 786436
  69.3 2.4 %copy-start.20 = (bf16[2,64,1024]{2,1,0:T(8,128)(2,1)}, bf16[2,64,1024]{2,1,0:T(8,128)(2,1)S(1)}, u32[]{:S(2)}) copy-start(bf16[2,64,1024]{2,1,0:T(8,128)(2,1)S(1)} %collective-permute-done.9.rest_1_) | copy-start | bytes 786436
  69.3 16.0 %copy-start.12 = (bf16[256,2048]{1,0:T(8,128)(2,1)}, bf16[256,2048]{1,0:T(8,128)(2,1)S(1)}, u32[]{:S(2)}) copy-start(bf16[256,2048]{1,0:T(8,128)(2,1)S(1)} %collective-permute-done.6.refs_4_.refs_6_) | copy-start | bytes 3145732
  69.3 16.0 %collective-permute-start.14 = (bf16[256,2048]{1,0:T(8,128)(2,1)S(1)}, bf16[256,2048]{1,0:T(8,128)(2,1)}, u32[]{:S(2)}, u32[]{:S(2)}) collective-permute-start(bf16[256,2048]{1,0:T(8,128)(2,1)S(1)} %collective-permute-done.6.refs_4_.refs_6_), channel_id=1, source_target_pairs={{0,1},{1,0},{2,3},{3,2},{4,5},{5,4},{6,7},{7,6},{8,9},{9,8},{10,11... | collective-permute-start | bytes 3145736 | tf_op jit(solution)/shard_map/ppermute | solution.py:56
  69.4 10.1 %collective-permute-start.13 = (bf16[128,2048]{1,0:T(8,128)(2,1)S(1)}, bf16[128,2048]{1,0:T(8,128)(2,1)}, u32[]{:S(2)}, u32[]{:S(2)}) collective-permute-start(bf16[128,2048]{1,0:T(8,128)(2,1)S(1)} %get-tuple-element.179.refs_1_), channel_id=1, source_target_pairs={{0,1},{1,0},{2,3},{3,2},{4,5},{5,4},{6,7},{7,6},{8,9},{9,8},{10,11... | collective-permute-start | bytes 1572872 | tf_op jit(solution)/shard_map/ppermute | solution.py:56
  69.9 15.4 %collective-permute-start.15 = (bf16[128,2048]{1,0:T(8,128)(2,1)}, bf16[128,2048]{1,0:T(8,128)(2,1)}, u32[]{:S(2)}, u32[]{:S(2)}) collective-permute-start(bf16[128,2048]{1,0:T(8,128)(2,1)} %collective-permute-done.7.refs_5_), channel_id=1, source_target_pairs={{0,1},{1,0},{2,3},{3,2},{4,5},{5,4},{6,7},{7,6},{8,9},{9,8},{10,11... | collective-permute-start | bytes 1572872 | tf_op jit(solution)/shard_map/ppermute | solution.py:56
  71.7 28.3 %all-to-all-start.1 = ((bf16[8,64,512]{2,1,0:T(8,128)(2,1)}), bf16[8,64,512]{2,1,0:T(8,128)(2,1)S(1)}, u32[]{:S(2)}, u32[]{:S(2)}) async-start(bf16[8,64,512]{2,1,0:T(8,128)(2,1)} %relay.5), calls=%async_computation.1 | async-start | bytes 1048576 | tf_op jit(solution)/shard_map/all_to_all | solution.py:44
  76.5 17.7 %collective-permute-start.10 = (bf16[2,64,1024]{2,1,0:T(8,128)(2,1)}, bf16[2,64,1024]{2,1,0:T(8,128)(2,1)S(1)}, u32[]{:S(2)}, u32[]{:S(2)}) collective-permute-start(bf16[2,64,1024]{2,1,0:T(8,128)(2,1)} %get-tuple-element.108), channel_id=1, source_target_pairs={{0,4},{4,8},{8,12},{12,16},{16,20},{20,24},{24,28},{28,32},{32,36}... | collective-permute-start | bytes 786440 | tf_op jit(solution)/shard_map/ppermute | solution.py:48
  79.5 18.0 %collective-permute-start.11 = (bf16[2,64,1024]{2,1,0:T(8,128)(2,1)}, bf16[2,64,1024]{2,1,0:T(8,128)(2,1)S(1)}, u32[]{:S(2)}, u32[]{:S(2)}) collective-permute-start(bf16[2,64,1024]{2,1,0:T(8,128)(2,1)} %get-tuple-element.109), channel_id=1, source_target_pairs={{0,252},{4,0},{8,4},{12,8},{16,12},{20,16},{24,20},{28,24},{32,28}... | collective-permute-start | bytes 786440 | tf_op jit(solution)/shard_map/ppermute | solution.py:48
  83.1 2.2 %copy-start.13 = (bf16[256,2048]{1,0:T(8,128)(2,1)}, bf16[256,2048]{1,0:T(8,128)(2,1)S(1)}, u32[]{:S(2)}) copy-start(bf16[256,2048]{1,0:T(8,128)(2,1)S(1)} %collective-permute-done.12.refs_2_.refs_5_) | copy-start | bytes 3145732
  83.1 16.9 %collective-permute-start.16 = (bf16[2,64,1024]{2,1,0:T(8,128)(2,1)}, bf16[2,64,1024]{2,1,0:T(8,128)(2,1)S(1)}, u32[]{:S(2)}, u32[]{:S(2)}) collective-permute-start(bf16[2,64,1024]{2,1,0:T(8,128)(2,1)} %get-tuple-element.112), channel_id=1, source_target_pairs={{0,16},{4,20},{8,24},{12,28},{16,0},{20,4},{24,8},{28,12},{32,48},... | collective-permute-start | bytes 786440 | tf_op jit(solution)/shard_map/ppermute | solution.py:52
  94.2 3.3 %copy-start.21 = (bf16[2,64,1024]{2,1,0:T(8,128)(2,1)}, bf16[2,64,1024]{2,1,0:T(8,128)(2,1)S(1)}, u32[]{:S(2)}) copy-start(bf16[2,64,1024]{2,1,0:T(8,128)(2,1)S(1)} %collective-permute-done.10.lo) | copy-start | bytes 786436
  97.5 2.5 %copy-start.22 = (bf16[2,64,1024]{2,1,0:T(8,128)(2,1)}, bf16[2,64,1024]{2,1,0:T(8,128)(2,1)S(1)}, u32[]{:S(2)}) copy-start(bf16[2,64,1024]{2,1,0:T(8,128)(2,1)S(1)} %collective-permute-done.11.hi) | copy-start | bytes 786436
  100.0 6.8 %copy-start = (bf16[8,64,512]{2,1,0:T(8,128)(2,1)}, bf16[8,64,512]{2,1,0:T(8,128)(2,1)S(1)}, u32[]{:S(2)}) copy-start(bf16[8,64,512]{2,1,0:T(8,128)(2,1)S(1)} %all-to-all-done.1) | copy-start | bytes 1572868
  106.8 9.0 %collective-permute-start.17 = (bf16[128,256]{1,0:T(8,128)(2,1)S(1)}, bf16[128,256]{1,0:T(8,128)(2,1)S(1)}, u32[]{:S(2)}, u32[]{:S(2)}) collective-permute-start(bf16[128,256]{1,0:T(8,128)(2,1)S(1)} %get-tuple-element.124), channel_id=1, source_target_pairs={{0,1},{1,0},{2,3},{3,2},{4,5},{5,4},{6,7},{7,6},{8,9},{9,8},{10,11... | collective-permute-start | bytes 196616 | tf_op jit(solution)/shard_map/ppermute | solution.py:56
  106.9 8.9 %collective-permute-start.18 = (bf16[128,256]{1,0:T(8,128)(2,1)S(1)}, bf16[128,256]{1,0:T(8,128)(2,1)S(1)}, u32[]{:S(2)}, u32[]{:S(2)}) collective-permute-start(bf16[128,256]{1,0:T(8,128)(2,1)S(1)} %get-tuple-element.125), channel_id=1, source_target_pairs={{0,2},{1,3},{2,0},{3,1},{4,6},{5,7},{6,4},{7,5},{8,10},{9,11},{10,... | collective-permute-start | bytes 196616 | tf_op jit(solution)/shard_map/ppermute | solution.py:56
  107.1 8.7 %collective-permute-start.19 = (bf16[128,256]{1,0:T(8,128)(2,1)S(1)}, bf16[128,256]{1,0:T(8,128)(2,1)S(1)}, u32[]{:S(2)}, u32[]{:S(2)}) collective-permute-start(bf16[128,256]{1,0:T(8,128)(2,1)S(1)} %get-tuple-element.126), channel_id=1, source_target_pairs={{0,3},{1,2},{2,1},{3,0},{4,7},{5,6},{6,5},{7,4},{8,11},{9,10},{10,... | collective-permute-start | bytes 196616 | tf_op jit(solution)/shard_map/ppermute | solution.py:56
  121.8 34.8 %copy-start.37 = (bf16[2,64,1024]{2,1,0:T(8,128)(2,1)S(1)}, bf16[2,64,1024]{2,1,0:T(8,128)(2,1)}, u32[]{:S(2)}) copy-start(bf16[2,64,1024]{2,1,0:T(8,128)(2,1)} %get-tuple-element.157) | copy-start | bytes 786436
  121.8 31.3 %all-to-all-start.2 = ((bf16[8,192,512]{2,1,0:T(8,128)(2,1)}), bf16[8,192,512]{2,1,0:T(8,128)(2,1)S(1)}, u32[]{:S(2)}, u32[]{:S(2)}) async-start(bf16[8,192,512]{2,1,0:T(8,128)(2,1)} %weight.1), calls=%async_computation.2 | async-start | bytes 3145728 | tf_op jit(solution)/shard_map/all_to_all | solution.py:44
  126.8 63.6 %copy-start.36 = (bf16[2,64,1024]{2,1,0:T(8,128)(2,1)S(1)}, bf16[2,64,1024]{2,1,0:T(8,128)(2,1)}, u32[]{:S(2)}) copy-start(bf16[2,64,1024]{2,1,0:T(8,128)(2,1)} %get-tuple-element.165) | copy-start | bytes 786436
  126.8 66.6 %copy-start.35 = (bf16[2,64,1024]{2,1,0:T(8,128)(2,1)S(1)}, bf16[2,64,1024]{2,1,0:T(8,128)(2,1)}, u32[]{:S(2)}) copy-start(bf16[2,64,1024]{2,1,0:T(8,128)(2,1)} %get-tuple-element.166) | copy-start | bytes 786436
  126.8 70.1 %copy-start.34 = (bf16[2,64,1024]{2,1,0:T(8,128)(2,1)S(1)}, bf16[2,64,1024]{2,1,0:T(8,128)(2,1)}, u32[]{:S(2)}) copy-start(bf16[2,64,1024]{2,1,0:T(8,128)(2,1)} %get-tuple-element.169) | copy-start | bytes 786436
  126.8 17.9 %collective-permute-start.20 = (bf16[2,64,1024]{2,1,0:T(8,128)(2,1)}, bf16[2,64,1024]{2,1,0:T(8,128)(2,1)S(1)}, u32[]{:S(2)}, u32[]{:S(2)}) collective-permute-start(bf16[2,64,1024]{2,1,0:T(8,128)(2,1)} %get-tuple-element.137), channel_id=1, source_target_pairs={{0,32},{4,36},{8,40},{12,44},{16,48},{20,52},{24,56},{28,60},{32,0... | collective-permute-start | bytes 786440 | tf_op jit(solution)/shard_map/ppermute | solution.py:52
  131.3 19.1 %collective-permute-start.21 = (bf16[2,64,1024]{2,1,0:T(8,128)(2,1)}, bf16[2,64,1024]{2,1,0:T(8,128)(2,1)S(1)}, u32[]{:S(2)}, u32[]{:S(2)}) collective-permute-start(bf16[2,64,1024]{2,1,0:T(8,128)(2,1)} %get-tuple-element.138), channel_id=1, source_target_pairs={{0,64},{4,68},{8,72},{12,76},{16,80},{20,84},{24,88},{28,92},{32,9... | collective-permute-start | bytes 786440 | tf_op jit(solution)/shard_map/ppermute | solution.py:52
  131.3 21.8 %collective-permute-start.22 = (bf16[2,64,1024]{2,1,0:T(8,128)(2,1)}, bf16[2,64,1024]{2,1,0:T(8,128)(2,1)S(1)}, u32[]{:S(2)}, u32[]{:S(2)}) collective-permute-start(bf16[2,64,1024]{2,1,0:T(8,128)(2,1)} %get-tuple-element.139), channel_id=1, source_target_pairs={{0,4},{4,0},{8,12},{12,8},{16,20},{20,16},{24,28},{28,24},{32,36},... | collective-permute-start | bytes 786440 | tf_op jit(solution)/shard_map/ppermute | solution.py:52
  144.7 59.8 %copy-start.24 = (bf16[2,64,1024]{2,1,0:T(8,128)(2,1)}, bf16[2,64,1024]{2,1,0:T(8,128)(2,1)S(1)}, u32[]{:S(2)}) copy-start(bf16[2,64,1024]{2,1,0:T(8,128)(2,1)S(1)} %collective-permute-done.20.rest_3_) | copy-start | bytes 786436
  150.4 54.0 %copy-start.25 = (bf16[2,64,1024]{2,1,0:T(8,128)(2,1)}, bf16[2,64,1024]{2,1,0:T(8,128)(2,1)S(1)}, u32[]{:S(2)}) copy-start(bf16[2,64,1024]{2,1,0:T(8,128)(2,1)S(1)} %collective-permute-done.21.rest_4_) | copy-start | bytes 786436
  153.1 51.3 %copy-start.26 = (bf16[2,64,1024]{2,1,0:T(8,128)(2,1)}, bf16[2,64,1024]{2,1,0:T(8,128)(2,1)S(1)}, u32[]{:S(2)}) copy-start(bf16[2,64,1024]{2,1,0:T(8,128)(2,1)S(1)} %collective-permute-done.22.rest_0_) | copy-start | bytes 786436
  154.6 6.6 %collective-permute-start.23 = (bf16[128,512]{1,0:T(8,128)(2,1)}, bf16[128,512]{1,0:T(8,128)(2,1)S(1)}, u32[]{:S(2)}, u32[]{:S(2)}) collective-permute-start(bf16[128,512]{1,0:T(8,128)(2,1)} %get-tuple-element.146), channel_id=1, source_target_pairs={{0,8},{4,12},{8,0},{12,4},{16,24},{20,28},{24,16},{28,20},{32,40},... | collective-permute-start | bytes 393224 | tf_op jit(solution)/shard_map/ppermute | solution.py:52
  154.6 23.0 %collective-permute-start.26 = (bf16[2,64,1024]{2,1,0:T(8,128)(2,1)}, bf16[2,64,1024]{2,1,0:T(8,128)(2,1)S(1)}, u32[]{:S(2)}, u32[]{:S(2)}) collective-permute-start(bf16[2,64,1024]{2,1,0:T(8,128)(2,1)} %get-tuple-element.156), channel_id=1, source_target_pairs={{0,128},{4,132},{8,136},{12,140},{16,144},{20,148},{24,152},{28,15... | collective-permute-start | bytes 786440 | tf_op jit(solution)/shard_map/ppermute | solution.py:52
  156.6 20.9 %collective-permute-start.27 = (bf16[2,64,1024]{2,1,0:T(8,128)(2,1)S(1)}, bf16[2,64,1024]{2,1,0:T(8,128)(2,1)S(1)}, u32[]{:S(2)}, u32[]{:S(2)}) collective-permute-start(bf16[2,64,1024]{2,1,0:T(8,128)(2,1)S(1)} %copy-done.37), channel_id=1, source_target_pairs={{0,8},{4,12},{8,0},{12,4},{16,24},{20,28},{24,16},{28,20},{32,40},... | collective-permute-start | bytes 786440 | tf_op jit(solution)/shard_map/ppermute | solution.py:52
  161.1 0.9 copy-start.6
  164.2 5.9 %collective-permute-start.24 = (bf16[96,512]{1,0:T(8,128)(2,1)}, bf16[96,512]{1,0:T(8,128)(2,1)S(1)}, u32[]{:S(2)}, u32[]{:S(2)}) collective-permute-start(bf16[96,512]{1,0:T(8,128)(2,1)} %get-tuple-element.149), channel_id=1, source_target_pairs={{0,16},{4,20},{8,24},{12,28},{16,0},{20,4},{24,8},{28,12},{32,48},... | collective-permute-start | bytes 294920 | tf_op jit(solution)/shard_map/ppermute | solution.py:52
  170.1 0.9 copy-start.8
  173.1 8.6 %collective-permute-start.25 = (bf16[80,512]{1,0:T(8,128)(2,1)}, bf16[80,512]{1,0:T(8,128)(2,1)S(1)}, u32[]{:S(2)}, u32[]{:S(2)}) collective-permute-start(bf16[80,512]{1,0:T(8,128)(2,1)} %get-tuple-element.152), channel_id=1, source_target_pairs={{0,32},{4,36},{8,40},{12,44},{16,48},{20,52},{24,56},{28,60},{32,0... | collective-permute-start | bytes 245768 | tf_op jit(solution)/shard_map/ppermute | solution.py:52
  177.5 26.9 %copy-start.27 = (bf16[2,64,1024]{2,1,0:T(8,128)(2,1)}, bf16[2,64,1024]{2,1,0:T(8,128)(2,1)S(1)}, u32[]{:S(2)}) copy-start(bf16[2,64,1024]{2,1,0:T(8,128)(2,1)S(1)} %collective-permute-done.26.rest_5_) | copy-start | bytes 786436
  177.5 26.9 %copy-start.28 = (bf16[2,64,1024]{2,1,0:T(8,128)(2,1)}, bf16[2,64,1024]{2,1,0:T(8,128)(2,1)S(1)}, u32[]{:S(2)}) copy-start(bf16[2,64,1024]{2,1,0:T(8,128)(2,1)S(1)} %collective-permute-done.27.rest_1_) | copy-start | bytes 786436
  184.7 19.8 %all-to-all-start.3 = ((bf16[8,64,512]{2,1,0:T(8,128)(2,1)}), bf16[8,64,512]{2,1,0:T(8,128)(2,1)S(1)}, u32[]{:S(2)}, u32[]{:S(2)}) async-start(bf16[8,64,512]{2,1,0:T(8,128)(2,1)} %get-tuple-element.160), calls=%async_computation.3 | async-start | bytes 1048576 | tf_op jit(solution)/shard_map/all_to_all | solution.py:44
  190.4 14.1 %collective-permute-start.28 = (bf16[2,64,1024]{2,1,0:T(8,128)(2,1)S(1)}, bf16[2,64,1024]{2,1,0:T(8,128)(2,1)S(1)}, u32[]{:S(2)}, u32[]{:S(2)}) collective-permute-start(bf16[2,64,1024]{2,1,0:T(8,128)(2,1)S(1)} %copy-done.36), channel_id=1, source_target_pairs={{0,4},{4,8},{8,12},{12,16},{16,20},{20,24},{24,28},{28,32},{32,36}... | collective-permute-start | bytes 786440 | tf_op jit(solution)/shard_map/ppermute | solution.py:48
  193.4 13.9 %collective-permute-start.29 = (bf16[2,64,1024]{2,1,0:T(8,128)(2,1)S(1)}, bf16[2,64,1024]{2,1,0:T(8,128)(2,1)S(1)}, u32[]{:S(2)}, u32[]{:S(2)}) collective-permute-start(bf16[2,64,1024]{2,1,0:T(8,128)(2,1)S(1)} %copy-done.35), channel_id=1, source_target_pairs={{0,252},{4,0},{8,4},{12,8},{16,12},{20,16},{24,20},{28,24},{32,28}... | collective-permute-start | bytes 786440 | tf_op jit(solution)/shard_map/ppermute | solution.py:48
  196.9 12.3 %collective-permute-start.30 = (bf16[2,64,1024]{2,1,0:T(8,128)(2,1)S(1)}, bf16[2,64,1024]{2,1,0:T(8,128)(2,1)S(1)}, u32[]{:S(2)}, u32[]{:S(2)}) collective-permute-start(bf16[2,64,1024]{2,1,0:T(8,128)(2,1)S(1)} %copy-done.34), channel_id=1, source_target_pairs={{0,16},{4,20},{8,24},{12,28},{16,0},{20,4},{24,8},{28,12},{32,48},... | collective-permute-start | bytes 786440 | tf_op jit(solution)/shard_map/ppermute | solution.py:52
  204.5 4.7 %copy-start.29 = (bf16[2,64,1024]{2,1,0:T(8,128)(2,1)}, bf16[2,64,1024]{2,1,0:T(8,128)(2,1)S(1)}, u32[]{:S(2)}) copy-start(bf16[2,64,1024]{2,1,0:T(8,128)(2,1)S(1)} %collective-permute-done.28.left) | copy-start | bytes 786436
  207.3 1.9 copy-start.30
  (9 other events, 7.4 us)

commit v5 on v4

--- a/solution.py
+++ b/solution.py
@@ -33,7 +33,7 @@
 CHUNKS = 8
 HALF = WIDTH // 2
 Z_BITS = (1, 2, 3)
-FIRST, SECOND, THIRD = (3, 4, 0), (5, 1), (2,)
+FIRST, SECOND, THIRD = (3, 4, 1), (5, 0), (2,)
 
 
 def mm(left, right, dims):
@@ -50,6 +50,11 @@
 
 def swapped(value, bit):
     return lax.ppermute(value, "seq", [(s, s ^ (1 << bit)) for s in range(64)])
+
+
+def along_z(value, steps):
+    pairs = [(s, s // 16 * 16 + (s // 2 + steps) % 8 * 2 + s % 2) for s in range(64)]
+    return lax.ppermute(value, "seq", pairs)
 
 
 def across(value, flip):
@@ -128,28 +133,40 @@
 def gathered(x):
     return pl.pallas_call(
         gathered_kernel,
-        out_shape=far((BLK, HALF)),
+        out_shape=jax.ShapeDtypeStruct((BLK, HALF), BF),
         compiler_params=params(),
         name="gathered",
     )(x)
 
 
-def relay_kernel(mine, other, out):
-    total = (mine[...].astype(F32) + other[...].astype(F32)).astype(BF)
-    if len(out.shape) == 2:
-        out[...] = total
-    else:
-        for j in range(CHUNKS):
-            out[j] = total
-
-
-def relay(mine, other, shape):
+def near_kernel(mine, below, above, two, three):
+    added = mine[...].astype(F32) + below[...].astype(F32)
+    two[...] = added.astype(BF)
+    three[...] = (added + above[...].astype(F32)).astype(BF)
+
+
+def near(mine, below, above):
+    return pl.pallas_call(
+        near_kernel,
+        out_shape=[jax.ShapeDtypeStruct((BLK, HALF), BF)] * 2,
+        compiler_params=params(),
+        name="near",
+    )(mine, below, above)
+
+
+def relay_kernel(mine, below, above, out):
+    total = (mine[...].astype(F32) + below[...].astype(F32) + above[...].astype(F32)).astype(BF)
+    for j in range(CHUNKS):
+        out[j] = total
+
+
+def relay(mine, below, above):
     return pl.pallas_call(
         relay_kernel,
-        out_shape=far(shape),
+        out_shape=far((CHUNKS, BLK, HALF)),
         compiler_params=params(),
         name="relay",
-    )(mine, other)
+    )(mine, below, above)
 
 
 def gather_heads(dst, c, cols, own, lo, hi, rand, glob):
@@ -377,27 +394,31 @@
     cols, grads, (dglob, out) = refs[:4], refs[4:8], refs[8:]
     step = pl.program_id(0)
 
-    @pl.when(step < 2)
+    @pl.when(step == 0)
     def _():
         out[...] = dglob[...]
 
-    @pl.when(step >= 2)
+    @pl.when(step > 0)
     def _():
         part = mm(cols[0][...], grads[0][...], COLS)
         for a in range(1, 4):
             part += mm(cols[a][...], grads[a][...], COLS)
-        out[...] = part.astype(BF).reshape(CHUNKS, 32, HALF)
+        part = part.astype(BF)
+        for i in range(2):
+            out[:, 32 * i : 32 * i + 32, :] = part[:, HALF * i : HALF * (i + 1)].reshape(
+                CHUNKS, 32, HALF
+            )
 
 
 def weight_payload(cols, grads, dglob):
     return pl.pallas_call(
         weight_kernel,
-        grid=(6,),
+        grid=(3,),
         in_specs=[pl.BlockSpec((TOK, 256), lambda i: (0, 0))] * 4
-        + [pl.BlockSpec((TOK, HALF), lambda i: (0, jnp.maximum(i - 2, 0)))]
-        + [pl.BlockSpec((TOK, HALF), lambda i: (1, jnp.maximum(i - 2, 0)))] * 3
-        + [pl.BlockSpec((CHUNKS, 32, HALF), lambda i: (0, jnp.minimum(i, 1), 0))],
-        out_specs=pl.BlockSpec((CHUNKS, 32, HALF), lambda i: (0, i, 0)),
+        + [pl.BlockSpec((TOK, WIDTH), lambda i: (0, jnp.maximum(i - 1, 0)))]
+        + [pl.BlockSpec((TOK, WIDTH), lambda i: (1, jnp.maximum(i - 1, 0)))] * 3
+        + [pl.BlockSpec((CHUNKS, BLK, HALF), lambda i: (0, 0, 0))],
+        out_specs=pl.BlockSpec((CHUNKS, BLK, HALF), lambda i: (0, i, 0)),
         out_shape=far((CHUNKS, 192, HALF)),
         compiler_params=params(dimension_semantics=("arbitrary",)),
         name="weight",
@@ -447,7 +468,11 @@
     vm = pl.BlockSpec(memory_space=pltpu.VMEM)
     return pl.pallas_call(
         kernel,
-        out_shape=[far((BLK, HALF), F32), far((rows, HALF), F32), far((BLK + rows, HALF))],
+        out_shape=[
+            jax.ShapeDtypeStruct((BLK, HALF), F32),
+            jax.ShapeDtypeStruct((rows, HALF), F32),
+            jax.ShapeDtypeStruct((BLK + rows, HALF), BF),
+        ],
         in_specs=[smem()] + [vm] * len(args),
         out_specs=[vm] * 3,
         scratch_shapes=[pltpu.VMEM((2 * rows, HALF), F32), pltpu.VMEM((rows, HALF), F32)],
@@ -538,42 +563,48 @@
     upper = w_out[HEAD_DIM:]
     mixed2 = across(mixed, 2)
     upper2 = beside(upper)
+    order = feature_order(lax.axis_index("rep"))
     rand = [None] * BITS
     for b in FIRST:
         rand[b] = swapped(chosen[b], b)
-    tied = together(spread, *[rand[b] for b in FIRST], low_edge, high_edge, *chosen)
-    spread, tied = tied[0], tied[1:]
+    spread, mixed, upper, mixed2, upper2, order, *tied = together(
+        spread,
+        mixed,
+        upper,
+        mixed2,
+        upper2,
+        order,
+        *[rand[b] for b in FIRST],
+        low_edge,
+        high_edge,
+        *chosen,
+    )
     for b in FIRST:
         rand[b], tied = tied[0], tied[1:]
     low_edge, high_edge, *chosen = tied
     mine = gathered(spread)
+    mixed1 = across(mixed, 1)
+    upper1 = across(upper, 1)
+    mixed3 = across(mixed2, 1)
+    upper3 = across(upper2, 1)
     for b in SECOND:
         rand[b] = swapped(chosen[b], b)
-    for b in Z_BITS[:2]:
-        mine = relay(mine, swapped(mine, b), (BLK, HALF))
-    other = swapped(mine, Z_BITS[2])
-    tied = together(
-        mine, other, mixed2, upper2, *[rand[b] for b in SECOND], low_edge, high_edge, *chosen
-    )
-    mine, other, mixed2, upper2, *tied = tied
+    two, three = near(mine, along_z(mine, 1), along_z(mine, -1))
+    below, above = along_z(three, 3), along_z(two, -3)
+    parts = (w_out, upper, mixed1, upper1, mixed2, upper2, mixed3, upper3)
+    d_attn = project(where, parts, grad_out)
+    below, above, d_attn, *tied = together(
+        below, above, d_attn, *[rand[b] for b in SECOND], low_edge, high_edge, *chosen
+    )
     for b in SECOND:
         rand[b], tied = tied[0], tied[1:]
     low_edge, high_edge, *chosen = tied
-    glob = trade(relay(mine, other, (CHUNKS, BLK, HALF))).reshape(2, 2 * TOK, HALF)
-    mixed3 = across(mixed2, 1)
-    upper3 = across(upper2, 1)
-    mixed1 = across(mixed, 1)
-    upper1 = across(upper, 1)
+    glob = trade(relay(three, below, above)).reshape(2, 2 * TOK, HALF)
     for b in THIRD:
         rand[b] = swapped(chosen[b], b)
     lo = shifted(high_edge, 1)
     hi = shifted(low_edge, -1)
-    parts = (w_out, upper, mixed1, upper1, mixed2, upper2, mixed3, upper3)
-    d_attn = project(where, parts, grad_out)
-    order = feature_order(lax.axis_index("rep"))
-    glob, lo, hi, d_attn, order, *tied = together(
-        glob, lo, hi, d_attn, order, *[rand[b] for b in THIRD]
-    )
+    glob, lo, hi, *tied = together(glob, lo, hi, *[rand[b] for b in THIRD])
     for b in THIRD:
         rand[b], tied = tied[0], tied[1:]
     lo, hi, *rand = from_hbm(lo, hi, *rand)
@@ -592,8 +623,9 @@
     back = [None] * BITS
     for b in FIRST:
         back[b] = swapped(drand[b], b)
-    payload, attn, dlo, dhi, *tied = together(
-        payload, attn, dlo, dhi, *[back[b] for b in FIRST], *drand
+    layer = layer_of(where, parts, attn)
+    payload, layer, dlo, dhi, *tied = together(
+        payload, layer, dlo, dhi, *[back[b] for b in FIRST], *drand
     )
     for b in FIRST:
         back[b], tied = tied[0], tied[1:]
@@ -605,9 +637,7 @@
         came = swapped(send, Z_BITS[step])
         glob_sum, keep, send = fold(where, bit, glob_sum, keep, came)
     came = swapped(send, Z_BITS[2])
-    came, attn, dlo, dhi, *tied = together(
-        came, attn, dlo, dhi, *[back[b] for b in SECOND], *drand
-    )
+    came, dlo, dhi, *tied = together(came, dlo, dhi, *[back[b] for b in SECOND], *drand)
     for b in SECOND:
         back[b], tied = tied[0], tied[1:]
     drand = tied
@@ -617,8 +647,6 @@
         back[b] = swapped(drand[b], b)
     right = shifted(dlo, -1)
     left = shifted(dhi, 1)
-    layer = layer_of(where, parts, attn)
-    glob_total, layer = together(glob_total, layer)
     dk, dv = finish(where, down, left, right, back, glob_total)
     return (layer[None], dq[None], dk[None], dv[None], weight_grad)
 

time: 215 us -> 201 us (0.935)
  local copies, waits for them, and re-layouts: 10.7 us -> 3.82 us
  Pallas kernels: 47.9 us -> 42.5 us
  starting transfers between devices: 82.5 us -> 78.6 us
    ppermute x18 -> x15, waiting for transfers between devices: 60.4 us -> 40 us  [swapped(): return lax.ppermute(value, 'seq', [(s, s ^ 1 << bit) for s in range(64)])]
    ppermute x18 -> x15, starting transfers between devices: 42.7 us -> 26.2 us  [swapped(): return lax.ppermute(value, 'seq', [(s, s ^ 1 << bit) for s in range(64)])]
    ppermute x4, waiting for transfers between devices: 7.91 us -> 22.5 us  [shifted(): lax.ppermute(value, 'seq', [(s, (s + steps) % 64) for s in range(64)])]
    ppermute x0 -> x4, waiting for transfers between devices: none -> 7.72 us  [along_z(): return lax.ppermute(value, 'seq', pairs)]
    ppermute x0 -> x4, starting transfers between devices: none -> 7.39 us  [along_z(): return lax.ppermute(value, 'seq', pairs)]
    unnamed x76 -> x68, local copies, waits for them, and re-layouts: 9.26 us -> 2.36 us
    pallas_call x8 -> x7, Pallas kernels: 12.8 us -> 7.31 us  [the longest x1 4.38 us: weight_payload(): pl.pallas_call(weight_kernel, grid=(3,), in_specs=[pl.BlockSpec((TOK, 256...]
    all_to_all x4, starting transfers between devices: 22.5 us -> 25.3 us  [trade(): lax.all_to_all(value, 'seq', 0, 0, axis_index_groups=YX_GROUPS, tiled=True)]
  transfers between devices with their start and end apart: 35 -> 36, of which waited for: 17 -> 14; matrix products, arithmetic and copies ran while one was open for 1% -> 1% of each run, Pallas kernels for 14% -> 13%
where the time goes in v5:
time: 201 us; the launch traced here: 200 us
  starting transfers between devices  78.6 us (39%)
  waiting for transfers between devices  70.3 us (35%)
  Pallas kernels  42.5 us (21%)
  local copies, waits for them, and re-layouts  3.82 us (2%)
  other arithmetic  3.4 us (2%)
    ppermute x15, waiting for transfers between devices, swapped(): return lax.ppermute(value, 'seq', [(s, s ^ 1 << bit) for s in range(64)])  40 us
    ppermute x15, starting transfers between devices, swapped(): return lax.ppermute(value, 'seq', [(s, s ^ 1 << bit) for s in range(64)])  26.2 us
    all_to_all x4, starting transfers between devices, trade(): lax.all_to_all(value, 'seq', 0, 0, axis_index_groups=YX_GROUPS, tiled=True)  25.3 us
    ppermute x4, waiting for transfers between devices, shifted(): lax.ppermute(value, 'seq', [(s, (s + steps) % 64) for s in range(64)])  22.5 us
    pallas_call x2, Pallas kernels, head_call(): pl.pallas_call(kernel, grid_spec=pltpu.PrefetchScalarGridSpec(num_scalar_...  14.6 us
    ppermute x4, starting transfers between devices, shifted(): lax.ppermute(value, 'seq', [(s, (s + steps) % 64) for s in range(64)])  13.1 us
    ppermute x4, waiting for transfers between devices, along_z(): return lax.ppermute(value, 'seq', pairs)  7.72 us
    ppermute x4, starting transfers between devices, along_z(): return lax.ppermute(value, 'seq', pairs)  7.39 us
  transfers between devices with their start and end apart: 36, of which 14 were waited for; matrix products, arithmetic and copies ran while one was open for 1% of the time, Pallas kernels for 13%

profile of v5, /device:TPU:8, one launch (start us, length us, event | category | flops | bytes accessed | tf_op | source)
XLA Modules:
  0.0 199.8 jit_solution(661255426253490635)
XLA Ops:
  0.7 1.4 fusion.37
  2.1 1.2 pad_maximum_fusion
  3.2 1.5 collective-permute-start
  4.7 2.1 %collective-permute-start.1 = (bf16[128,2048]{1,0:T(8,128)(2,1)S(1)}, bf16[128,2048]{1,0:T(8,128)(2,1)S(1)}, u32[]{:S(2)}, u32[]{:S(2)}) collective-permute-start(bf16[128,2048]{1,0:T(8,128)(2,1)S(1)} %get-tuple-element.104.refs_1_), channel_id=1, source_target_pairs={{0,6},{1,7},{2,4},{3,5},{4,2},{5,3},{6,0},{7,1},{8,14},{9,15},{10,... | collective-permute-start | bytes 1572872 | tf_op jit(solution)/shard_map/ppermute | solution.py:66
  6.9 0.1 concatenate.6.where.refs_0_
  7.0 2.2 %pick.1 = (bf16[2,64,1024]{2,1,0:T(8,128)(2,1)}, bf16[2,64,1024]{2,1,0:T(8,128)(2,1)}, bf16[2,64,1024]{2,1,0:T(8,128)(2,1)}, bf16[2,64,1024]{2,1,0:T(8,128)(2,1)...) custom-call(s32[14]{0:T(128)S(1)} %concatenate.6.where.refs_0_, ...), custom_call_target="tpu_custom_call" | custom-call | tf_op jit(solution)/shard_map/pick/pallas_call | solution.py:119
  9.2 5.0 %all-to-all-start = ((bf16[8,64,512]{2,1,0:T(8,128)(2,1)}), bf16[8,64,512]{2,1,0:T(8,128)(2,1)S(1)}, u32[]{:S(2)}, u32[]{:S(2)}) async-start(bf16[8,64,512]{2,1,0:T(8,128)(2,1)} %get-tuple-element.92), calls=%async_computation | async-start | bytes 1048576 | tf_op jit(solution)/shard_map/all_to_all | solution.py:44
  14.2 7.2 %collective-permute-start.2 = (bf16[2,64,1024]{2,1,0:T(8,128)(2,1)}, bf16[2,64,1024]{2,1,0:T(8,128)(2,1)S(1)}, u32[]{:S(2)}, u32[]{:S(2)}) collective-permute-start(bf16[2,64,1024]{2,1,0:T(8,128)(2,1)} %get-tuple-element.93), channel_id=1, source_target_pairs={{0,32},{4,36},{8,40},{12,44},{16,48},{20,52},{24,56},{28,60},{32,0... | collective-permute-start | bytes 786440 | tf_op jit(solution)/shard_map/ppermute | solution.py:52
  21.4 1.0 collective-permute-start.4
  22.4 2.2 %fusion.rest_7_ = bf16[1024,1024]{1,0:T(8,128)(2,1)} fusion(s32[1024]{0:T(1024)S(1)} %fusion.15), kind=kLoop, calls=%fused_computation.1 | loop fusion | flops 2097152 | bytes 2101248 | tf_op jit(solution)/shard_map/convert_element_type | solution.py:550
  24.6 8.7 %collective-permute-done.2.rest_3_ = bf16[2,64,1024]{2,1,0:T(8,128)(2,1)S(1)} collective-permute-done((bf16[2,64,1024]{2,1,0:T(8,128)(2,1)}, bf16[2,64,1024]{2,1,0:T(8,128)(2,1)S(1)}, u32[]{:S(2)}, u32[]{:S(2)}) %collective-permute-start.2) | collective-permute-done | bytes 262176 | tf_op jit(solution)/shard_map/ppermute | solution.py:52
  33.3 5.7 %collective-permute-done.4.rest_1_ = bf16[2,64,1024]{2,1,0:T(8,128)(2,1)S(1)} collective-permute-done((bf16[2,64,1024]{2,1,0:T(8,128)(2,1)}, bf16[2,64,1024]{2,1,0:T(8,128)(2,1)S(1)}, u32[]{:S(2)}, u32[]{:S(2)}) %collective-permute-start.4) | collective-permute-done | bytes 262176 | tf_op jit(solution)/shard_map/ppermute | solution.py:52
  39.0 0.1 collective-permute-start.9
  39.1 0.5 collective-permute-start.11
  39.6 0.1 collective-permute-start.10
  39.7 0.4 collective-permute-start.12
  40.2 3.5 %collective-permute-start.6 = (bf16[64,512]{1,0:T(8,128)(2,1)S(1)}, bf16[64,512]{1,0:T(8,128)(2,1)S(1)}, u32[]{:S(2)}, u32[]{:S(2)}) collective-permute-start(bf16[64,512]{1,0:T(8,128)(2,1)S(1)} %gathered.1.mine), channel_id=1, source_target_pairs={{0,56},{4,60},{8,0},{12,4},{16,8},{20,12},{24,16},{28,20},{32,24},... | collective-permute-start | bytes 196616 | tf_op jit(solution)/shard_map/ppermute | solution.py:57
  43.7 1.9 collective-permute-done.6.above
  45.6 5.8 %collective-permute-done.5.below = bf16[64,512]{1,0:T(8,128)(2,1)S(1)} collective-permute-done((bf16[64,512]{1,0:T(8,128)(2,1)S(1)}, bf16[64,512]{1,0:T(8,128)(2,1)S(1)}, u32[]{:S(2)}, u32[]{:S(2)}) %collective-permute-start.5) | collective-permute-done | bytes 65568 | tf_op jit(solution)/shard_map/ppermute | solution.py:57
  51.4 2.1 %collective-permute-start.13 = (bf16[2,64,1024]{2,1,0:T(8,128)(2,1)}, bf16[2,64,1024]{2,1,0:T(8,128)(2,1)S(1)}, u32[]{:S(2)}, u32[]{:S(2)}) collective-permute-start(bf16[2,64,1024]{2,1,0:T(8,128)(2,1)} %get-tuple-element.108), channel_id=1, source_target_pairs={{0,128},{4,132},{8,136},{12,140},{16,144},{20,148},{24,152},{28,15... | collective-permute-start | bytes 786440 | tf_op jit(solution)/shard_map/ppermute | solution.py:52
  53.5 1.6 collective-permute-start.14
  55.1 0.8 collective-permute-start.8
  56.0 3.1 %collective-permute-start.7 = (bf16[64,512]{1,0:T(8,128)(2,1)S(1)}, bf16[64,512]{1,0:T(8,128)(2,1)S(1)}, u32[]{:S(2)}, u32[]{:S(2)}) collective-permute-start(bf16[64,512]{1,0:T(8,128)(2,1)S(1)} %get-tuple-element.102.mine), channel_id=1, source_target_pairs={{0,24},{4,28},{8,32},{12,36},{16,40},{20,44},{24,48},{28,52},{32,5... | collective-permute-start | bytes 196616 | tf_op jit(solution)/shard_map/ppermute | solution.py:57
  59.1 1.0 copy-done.5
  60.1 7.1 %project.1.rest_8_ = bf16[128,1024]{1,0:T(8,128)(2,1)} custom-call(s32[14]{0:T(128)S(1)} %concatenate.6.where.refs_0_, bf16[256,2048]{1,0:T(8,128)(2,1)} %refs_0_.3, bf16[128,2048]{1,0:T(8,128)(2,1)} %copy-done.6, bf16[256,2048]{1,0:T(8,128)(2,1)} %copy-done.4, bf16[128,2048]{1,0:T(8,128)(2,1)} %copy-done.9, bf16[256,2048]{1,0:T(8,128)(2,1)} %copy-done.3, ...), custom_call_target="tpu_custom_call" | custom-call | tf_op jit(solution)/shard_map/project/pallas_call | solution.py:326
  67.2 0.9 relay.1
  68.1 6.6 %all-to-all-start.1 = ((bf16[8,64,512]{2,1,0:T(8,128)(2,1)}), bf16[8,64,512]{2,1,0:T(8,128)(2,1)S(1)}, u32[]{:S(2)}, u32[]{:S(2)}) async-start(bf16[8,64,512]{2,1,0:T(8,128)(2,1)} %relay.1), calls=%async_computation.1 | async-start | bytes 1048576 | tf_op jit(solution)/shard_map/all_to_all | solution.py:44
  74.8 3.0 %collective-permute-start.15 = (bf16[2,64,1024]{2,1,0:T(8,128)(2,1)}, bf16[2,64,1024]{2,1,0:T(8,128)(2,1)S(1)}, u32[]{:S(2)}, u32[]{:S(2)}) collective-permute-start(bf16[2,64,1024]{2,1,0:T(8,128)(2,1)} %get-tuple-element.115), channel_id=1, source_target_pairs={{0,4},{4,8},{8,12},{12,16},{16,20},{20,24},{24,28},{28,32},{32,36}... | collective-permute-start | bytes 786440 | tf_op jit(solution)/shard_map/ppermute | solution.py:48
  77.7 3.6 %collective-permute-start.16 = (bf16[2,64,1024]{2,1,0:T(8,128)(2,1)}, bf16[2,64,1024]{2,1,0:T(8,128)(2,1)S(1)}, u32[]{:S(2)}, u32[]{:S(2)}) collective-permute-start(bf16[2,64,1024]{2,1,0:T(8,128)(2,1)} %get-tuple-element.116), channel_id=1, source_target_pairs={{0,252},{4,0},{8,4},{12,8},{16,12},{20,16},{24,20},{28,24},{32,28}... | collective-permute-start | bytes 786440 | tf_op jit(solution)/shard_map/ppermute | solution.py:48
  81.3 7.4 %collective-permute-done.15.lo = bf16[2,64,1024]{2,1,0:T(8,128)(2,1)S(1)} collective-permute-done((bf16[2,64,1024]{2,1,0:T(8,128)(2,1)}, bf16[2,64,1024]{2,1,0:T(8,128)(2,1)S(1)}, u32[]{:S(2)}, u32[]{:S(2)}) %collective-permute-start.15) | collective-permute-done | bytes 262176 | tf_op jit(solution)/shard_map/ppermute | solution.py:48
  88.7 3.5 %collective-permute-done.16.hi = bf16[2,64,1024]{2,1,0:T(8,128)(2,1)S(1)} collective-permute-done((bf16[2,64,1024]{2,1,0:T(8,128)(2,1)}, bf16[2,64,1024]{2,1,0:T(8,128)(2,1)S(1)}, u32[]{:S(2)}, u32[]{:S(2)}) %collective-permute-start.16) | collective-permute-done | bytes 262176 | tf_op jit(solution)/shard_map/ppermute | solution.py:48
  92.2 2.4 %collective-permute-done.17.rest_2_ = bf16[2,64,1024]{2,1,0:T(8,128)(2,1)S(1)} collective-permute-done((bf16[2,64,1024]{2,1,0:T(8,128)(2,1)S(1)}, bf16[2,64,1024]{2,1,0:T(8,128)(2,1)S(1)}, u32[]{:S(2)}, u32[]{:S(2)}) %collective-permute-start.17) | collective-permute-done | bytes 262176 | tf_op jit(solution)/shard_map/ppermute | solution.py:52
  94.7 0.6 copy-done.18
  95.4 6.1 %forward.1 = (bf16[128,1024]{1,0:T(8,128)(2,1)}, f32[8,8,128]{2,1,0:T(8,128)}, bf16[128,256]{1,0:T(8,128)(2,1)S(1)}, bf16[128,256]{1,0:T(8,128)(2,1)S(1)}, bf16[...) custom-call(s32[14]{0:T(128)S(1)} %concatenate.6.where.refs_0_, bf16[128,1024]{1,0:T(8,128)(2,1)} %bitcast.43, ...), custom_call_target="tpu_custom_call" | custom-call | tf_op jit(solution)/shard_map/forward/pallas_call | solution.py:238
  101.5 0.1 collective-permute-start.18
  101.6 0.3 collective-permute-start.19
  101.9 1.6 collective-permute-start.20
  103.5 7.0 %backward.1 = (bf16[128,1024]{1,0:T(8,128)(2,1)}, f32[2,128,1024]{2,1,0:T(8,128)}, bf16[2,64,1024]{2,1,0:T(8,128)(2,1)}, bf16[2,64,1024]{2,1,0:T(8,128)(2,1)}, b...) custom-call(s32[14]{0:T(128)S(1)} %concatenate.6.where.refs_0_, ...), custom_call_target="tpu_custom_call" | custom-call | tf_op jit(solution)/shard_map/backward/pallas_call | solution.py:299
  110.5 4.4 %weight.1 = bf16[8,192,512]{2,1,0:T(8,128)(2,1)} custom-call(bf16[128,256]{1,0:T(8,128)(2,1)S(1)} %get-tuple-element.128.refs_0_, bf16[128,256]{1,0:T(8,128)(2,1)S(1)} %collective-permute-done.18.refs_1_, bf16[128,256]{1,0:T(8,128)(2,1)S(1)} %collective-permute-done.19.refs_2_, bf16[128,256]{1,0:T(8,128)(2,1)S(1)} %collective-permute-done.20.refs_3_, ...), custom_call_target="tpu_custom_call" | custom-call | tf_op jit(solution)/shard_map/weight/pallas_call | solution.py:414
  114.9 4.8 %all-to-all-start.2 = ((bf16[8,192,512]{2,1,0:T(8,128)(2,1)}), bf16[8,192,512]{2,1,0:T(8,128)(2,1)S(1)}, u32[]{:S(2)}, u32[]{:S(2)}) async-start(bf16[8,192,512]{2,1,0:T(8,128)(2,1)} %weight.1), calls=%async_computation.2 | async-start | bytes 3145728 | tf_op jit(solution)/shard_map/all_to_all | solution.py:44
  119.7 3.0 %collective-permute-start.21 = (bf16[2,64,1024]{2,1,0:T(8,128)(2,1)}, bf16[2,64,1024]{2,1,0:T(8,128)(2,1)S(1)}, u32[]{:S(2)}, u32[]{:S(2)}) collective-permute-start(bf16[2,64,1024]{2,1,0:T(8,128)(2,1)} %get-tuple-element.142), channel_id=1, source_target_pairs={{0,32},{4,36},{8,40},{12,44},{16,48},{20,52},{24,56},{28,60},{32,0... | collective-permute-start | bytes 786440 | tf_op jit(solution)/shard_map/ppermute | solution.py:52
  122.8 0.2 collective-permute-start.23
  123.0 7.5 %layer.1 = bf16[128,2048]{1,0:T(8,128)(2,1)} custom-call(s32[14]{0:T(128)S(1)} %concatenate.6.where.refs_0_, bf16[256,2048]{1,0:T(8,128)(2,1)} %refs_0_.3, bf16[128,2048]{1,0:T(8,128)(2,1)} %copy-done.6, bf16[256,2048]{1,0:T(8,128)(2,1)} %copy-done.4, bf16[128,2048]{1,0:T(8,128)(2,1)} %copy-done.9, bf16[256,2048]{1,0:T(8,128)(2,1)} %copy-done.3, ...), custom_call_target="tpu_custom_call" | custom-call | tf_op jit(solution)/shard_map/layer/pallas_call | solution.py:326
  130.5 6.7 %collective-permute-done.21.rest_3_ = bf16[2,64,1024]{2,1,0:T(8,128)(2,1)S(1)} collective-permute-done((bf16[2,64,1024]{2,1,0:T(8,128)(2,1)}, bf16[2,64,1024]{2,1,0:T(8,128)(2,1)S(1)}, u32[]{:S(2)}, u32[]{:S(2)}) %collective-permute-start.21) | collective-permute-done | bytes 262176 | tf_op jit(solution)/shard_map/ppermute | solution.py:52
  137.2 6.2 %collective-permute-done.22.rest_4_ = bf16[2,64,1024]{2,1,0:T(8,128)(2,1)S(1)} collective-permute-done((bf16[2,64,1024]{2,1,0:T(8,128)(2,1)}, bf16[2,64,1024]{2,1,0:T(8,128)(2,1)S(1)}, u32[]{:S(2)}, u32[]{:S(2)}) %collective-permute-start.22) | collective-permute-done | bytes 262176 | tf_op jit(solution)/shard_map/ppermute | solution.py:52
  143.4 0.7 first.1
  144.2 0.3 collective-permute-start.24
  144.5 2.6 %collective-permute-start.27 = (bf16[2,64,1024]{2,1,0:T(8,128)(2,1)}, bf16[2,64,1024]{2,1,0:T(8,128)(2,1)S(1)}, u32[]{:S(2)}, u32[]{:S(2)}) collective-permute-start(bf16[2,64,1024]{2,1,0:T(8,128)(2,1)} %get-tuple-element.161), channel_id=1, source_target_pairs={{0,128},{4,132},{8,136},{12,140},{16,144},{20,148},{24,152},{28,15... | collective-permute-start | bytes 786440 | tf_op jit(solution)/shard_map/ppermute | solution.py:52
  147.1 3.0 %collective-permute-start.28 = (bf16[2,64,1024]{2,1,0:T(8,128)(2,1)S(1)}, bf16[2,64,1024]{2,1,0:T(8,128)(2,1)S(1)}, u32[]{:S(2)}, u32[]{:S(2)}) collective-permute-start(bf16[2,64,1024]{2,1,0:T(8,128)(2,1)S(1)} %copy-done.33), channel_id=1, source_target_pairs={{0,4},{4,0},{8,12},{12,8},{16,20},{20,16},{24,28},{28,24},{32,36},... | collective-permute-start | bytes 786440 | tf_op jit(solution)/shard_map/ppermute | solution.py:52
  150.1 0.6 fold.2
  150.6 2.1 %collective-permute-start.25 = (bf16[96,512]{1,0:T(8,128)(2,1)S(1)}, bf16[96,512]{1,0:T(8,128)(2,1)S(1)}, u32[]{:S(2)}, u32[]{:S(2)}) collective-permute-start(bf16[96,512]{1,0:T(8,128)(2,1)S(1)} %get-tuple-element.157), channel_id=1, source_target_pairs={{0,16},{4,20},{8,24},{12,28},{16,0},{20,4},{24,8},{28,12},{32,48},... | collective-permute-start | bytes 294920 | tf_op jit(solution)/shard_map/ppermute | solution.py:52
  152.7 3.5 %collective-permute-done.25.refs_3_ = bf16[96,512]{1,0:T(8,128)(2,1)S(1)} collective-permute-done((bf16[96,512]{1,0:T(8,128)(2,1)S(1)}, bf16[96,512]{1,0:T(8,128)(2,1)S(1)}, u32[]{:S(2)}, u32[]{:S(2)}) %collective-permute-start.25) | collective-permute-done | bytes 98336 | tf_op jit(solution)/shard_map/ppermute | solution.py:52
  156.2 0.6 fold.3
  156.8 3.1 %collective-permute-start.26 = (bf16[80,512]{1,0:T(8,128)(2,1)S(1)}, bf16[80,512]{1,0:T(8,128)(2,1)S(1)}, u32[]{:S(2)}, u32[]{:S(2)}) collective-permute-start(bf16[80,512]{1,0:T(8,128)(2,1)S(1)} %get-tuple-element.158), channel_id=1, source_target_pairs={{0,32},{4,36},{8,40},{12,44},{16,48},{20,52},{24,56},{28,60},{32,0... | collective-permute-start | bytes 245768 | tf_op jit(solution)/shard_map/ppermute | solution.py:52
  160.0 5.9 %collective-permute-done.26.came = bf16[80,512]{1,0:T(8,128)(2,1)S(1)} collective-permute-done((bf16[80,512]{1,0:T(8,128)(2,1)S(1)}, bf16[80,512]{1,0:T(8,128)(2,1)S(1)}, u32[]{:S(2)}, u32[]{:S(2)}) %collective-permute-start.26) | collective-permute-done | bytes 81952 | tf_op jit(solution)/shard_map/ppermute | solution.py:52
  165.8 1.4 last.1
  167.2 8.9 %all-to-all-start.3 = ((bf16[8,64,512]{2,1,0:T(8,128)(2,1)}), bf16[8,64,512]{2,1,0:T(8,128)(2,1)S(1)}, u32[]{:S(2)}, u32[]{:S(2)}) async-start(bf16[8,64,512]{2,1,0:T(8,128)(2,1)} %get-tuple-element.175), calls=%async_computation.3 | async-start | bytes 1048576 | tf_op jit(solution)/shard_map/all_to_all | solution.py:44
  176.1 3.0 %collective-permute-start.29 = (bf16[2,64,1024]{2,1,0:T(8,128)(2,1)S(1)}, bf16[2,64,1024]{2,1,0:T(8,128)(2,1)S(1)}, u32[]{:S(2)}, u32[]{:S(2)}) collective-permute-start(bf16[2,64,1024]{2,1,0:T(8,128)(2,1)S(1)} %copy-done.31), channel_id=1, source_target_pairs={{0,4},{4,8},{8,12},{12,16},{16,20},{20,24},{24,28},{28,32},{32,36}... | collective-permute-start | bytes 786440 | tf_op jit(solution)/shard_map/ppermute | solution.py:48
  179.1 3.6 %collective-permute-start.30 = (bf16[2,64,1024]{2,1,0:T(8,128)(2,1)S(1)}, bf16[2,64,1024]{2,1,0:T(8,128)(2,1)S(1)}, u32[]{:S(2)}, u32[]{:S(2)}) collective-permute-start(bf16[2,64,1024]{2,1,0:T(8,128)(2,1)S(1)} %copy-done.30), channel_id=1, source_target_pairs={{0,252},{4,0},{8,4},{12,8},{16,12},{20,16},{24,20},{28,24},{32,28}... | collective-permute-start | bytes 786440 | tf_op jit(solution)/shard_map/ppermute | solution.py:48
  182.7 8.1 %collective-permute-done.29.left = bf16[2,64,1024]{2,1,0:T(8,128)(2,1)S(1)} collective-permute-done((bf16[2,64,1024]{2,1,0:T(8,128)(2,1)S(1)}, bf16[2,64,1024]{2,1,0:T(8,128)(2,1)S(1)}, u32[]{:S(2)}, u32[]{:S(2)}) %collective-permute-start.29) | collective-permute-done | bytes 262176 | tf_op jit(solution)/shard_map/ppermute | solution.py:48
  190.8 3.4 %collective-permute-done.30.right = bf16[2,64,1024]{2,1,0:T(8,128)(2,1)S(1)} collective-permute-done((bf16[2,64,1024]{2,1,0:T(8,128)(2,1)S(1)}, bf16[2,64,1024]{2,1,0:T(8,128)(2,1)S(1)}, u32[]{:S(2)}, u32[]{:S(2)}) %collective-permute-start.30) | collective-permute-done | bytes 262176 | tf_op jit(solution)/shard_map/ppermute | solution.py:48
  194.2 0.9 collective-permute-done.31.rest_2_
  195.2 0.6 copy-done.26
  195.8 3.8 %finish.1 = (bf16[128,1024]{1,0:T(8,128)(2,1)}, bf16[128,1024]{1,0:T(8,128)(2,1)}) custom-call(s32[14]{0:T(128)S(1)} %concatenate.6.where.refs_0_, f32[2,128,1024]{2,1,0:T(8,128)} %get-tuple-element.150.own, bf16[2,64,1024]{2,1,0:T(8,128)(2,1)} %copy-done.24, bf16[2,64,1024]{2,1,0:T(8,128)(2,1)} %copy-done.25, bf16[2,64,1024]{2,1,0:T(8,128)(2,1)} %copy-done.23, ...), custom_call_target="tpu_custom_call" | custom-call | tf_op jit(solution)/shard_map/finish/pallas_call | solution.py:530
  (97 shorter events, 0.3 us)
Async XLA Ops:
  0.6 6.2 %copy-start.27 = (s32[1,2]{1,0:T(1,128)S(1)}, s32[1,2]{1,0:T(1,128)}, u32[]{:S(2)}) copy-start(s32[1,2]{1,0:T(1,128)} %param.13) | copy-start | bytes 28
  0.7 6.2 %copy-start.28 = (s32[1,1,6]{2,1,0:T(1,128)S(1)}, s32[1,1,6]{2,1,0:T(1,128)}, u32[]{:S(2)}) copy-start(s32[1,1,6]{2,1,0:T(1,128)} %param.12) | copy-start | bytes 76
  0.7 6.3 %copy-start.2 = (bf16[1,128,1024]{2,1,0:T(8,128)(2,1)S(1)}, bf16[1,128,1024]{2,1,0:T(8,128)(2,1)}, u32[]{:S(2)}) copy-start(bf16[1,128,1024]{2,1,0:T(8,128)(2,1)} %param.9) | copy-start | bytes 786436
  0.7 6.3 %copy-start.1 = (bf16[1,128,1024]{2,1,0:T(8,128)(2,1)S(1)}, bf16[1,128,1024]{2,1,0:T(8,128)(2,1)}, u32[]{:S(2)}) copy-start(bf16[1,128,1024]{2,1,0:T(8,128)(2,1)} %param.8) | copy-start | bytes 786436
  2.1 37.6 %copy-start.6 = (bf16[128,2048]{1,0:T(8,128)(2,1)}, bf16[128,2048]{1,0:T(8,128)(2,1)S(1)}, u32[]{:S(2)}) copy-start(bf16[128,2048]{1,0:T(8,128)(2,1)S(1)} %get-tuple-element.104.refs_1_) | copy-start | bytes 1572868
  3.2 35.8 %collective-permute-start = (bf16[256,2048]{1,0:T(8,128)(2,1)}, bf16[256,2048]{1,0:T(8,128)(2,1)S(1)}, u32[]{:S(2)}, u32[]{:S(2)}) collective-permute-start(bf16[256,2048]{1,0:T(8,128)(2,1)} %pad_maximum_fusion), channel_id=1, source_target_pairs={{0,2},{1,3},{2,0},{3,1},{4,6},{5,7},{6,4},{7,5},{8,10},{9,11},{10,... | collective-permute-start | bytes 3145736 | tf_op jit(solution)/shard_map/ppermute | solution.py:61
  4.7 34.3 %collective-permute-start.1 = (bf16[128,2048]{1,0:T(8,128)(2,1)S(1)}, bf16[128,2048]{1,0:T(8,128)(2,1)S(1)}, u32[]{:S(2)}, u32[]{:S(2)}) collective-permute-start(bf16[128,2048]{1,0:T(8,128)(2,1)S(1)} %get-tuple-element.104.refs_1_), channel_id=1, source_target_pairs={{0,6},{1,7},{2,4},{3,5},{4,2},{5,3},{6,0},{7,1},{8,14},{9,15},{10,... | collective-permute-start | bytes 1572872 | tf_op jit(solution)/shard_map/ppermute | solution.py:66
  9.2 29.8 %all-to-all-start = ((bf16[8,64,512]{2,1,0:T(8,128)(2,1)}), bf16[8,64,512]{2,1,0:T(8,128)(2,1)S(1)}, u32[]{:S(2)}, u32[]{:S(2)}) async-start(bf16[8,64,512]{2,1,0:T(8,128)(2,1)} %get-tuple-element.92), calls=%async_computation | async-start | bytes 1048576 | tf_op jit(solution)/shard_map/all_to_all | solution.py:44
  14.2 19.2 %collective-permute-start.2 = (bf16[2,64,1024]{2,1,0:T(8,128)(2,1)}, bf16[2,64,1024]{2,1,0:T(8,128)(2,1)S(1)}, u32[]{:S(2)}, u32[]{:S(2)}) collective-permute-start(bf16[2,64,1024]{2,1,0:T(8,128)(2,1)} %get-tuple-element.93), channel_id=1, source_target_pairs={{0,32},{4,36},{8,40},{12,44},{16,48},{20,52},{24,56},{28,60},{32,0... | collective-permute-start | bytes 786440 | tf_op jit(solution)/shard_map/ppermute | solution.py:52
  21.4 12.0 %collective-permute-start.3 = (bf16[2,64,1024]{2,1,0:T(8,128)(2,1)}, bf16[2,64,1024]{2,1,0:T(8,128)(2,1)S(1)}, u32[]{:S(2)}, u32[]{:S(2)}) collective-permute-start(bf16[2,64,1024]{2,1,0:T(8,128)(2,1)} %get-tuple-element.94), channel_id=1, source_target_pairs={{0,64},{4,68},{8,72},{12,76},{16,80},{20,84},{24,88},{28,92},{32,9... | collective-permute-start | bytes 786440 | tf_op jit(solution)/shard_map/ppermute | solution.py:52
  21.4 17.6 %collective-permute-start.4 = (bf16[2,64,1024]{2,1,0:T(8,128)(2,1)}, bf16[2,64,1024]{2,1,0:T(8,128)(2,1)S(1)}, u32[]{:S(2)}, u32[]{:S(2)}) collective-permute-start(bf16[2,64,1024]{2,1,0:T(8,128)(2,1)} %get-tuple-element.95), channel_id=1, source_target_pairs={{0,8},{4,12},{8,0},{12,4},{16,24},{20,28},{24,16},{28,20},{32,40},... | collective-permute-start | bytes 786440 | tf_op jit(solution)/shard_map/ppermute | solution.py:52
  33.3 33.8 %copy-start.11 = (bf16[2,64,1024]{2,1,0:T(8,128)(2,1)}, bf16[2,64,1024]{2,1,0:T(8,128)(2,1)S(1)}, u32[]{:S(2)}) copy-start(bf16[2,64,1024]{2,1,0:T(8,128)(2,1)S(1)} %collective-permute-done.2.rest_3_) | copy-start | bytes 786436
  33.3 61.4 %copy-start.12 = (bf16[2,64,1024]{2,1,0:T(8,128)(2,1)}, bf16[2,64,1024]{2,1,0:T(8,128)(2,1)S(1)}, u32[]{:S(2)}) copy-start(bf16[2,64,1024]{2,1,0:T(8,128)(2,1)S(1)} %collective-permute-done.3.rest_4_) | copy-start | bytes 786436
  39.0 55.7 %copy-start.13 = (bf16[2,64,1024]{2,1,0:T(8,128)(2,1)}, bf16[2,64,1024]{2,1,0:T(8,128)(2,1)S(1)}, u32[]{:S(2)}) copy-start(bf16[2,64,1024]{2,1,0:T(8,128)(2,1)S(1)} %collective-permute-done.4.rest_1_) | copy-start | bytes 786436
  39.0 20.0 %copy-start.8 = (bf16[128,2048]{1,0:T(8,128)(2,1)}, bf16[128,2048]{1,0:T(8,128)(2,1)S(1)}, u32[]{:S(2)}) copy-start(bf16[128,2048]{1,0:T(8,128)(2,1)S(1)} %collective-permute-done.1.refs_5_) | copy-start | bytes 1572868
  39.0 20.0 %copy-start.3 = (bf16[256,2048]{1,0:T(8,128)(2,1)}, bf16[256,2048]{1,0:T(8,128)(2,1)S(1)}, u32[]{:S(2)}) copy-start(bf16[256,2048]{1,0:T(8,128)(2,1)S(1)} %collective-permute-done.refs_4_.refs_6_) | copy-start | bytes 3145732
  39.0 16.9 %collective-permute-start.9 = (bf16[256,2048]{1,0:T(8,128)(2,1)}, bf16[256,2048]{1,0:T(8,128)(2,1)S(1)}, u32[]{:S(2)}, u32[]{:S(2)}) collective-permute-start(bf16[256,2048]{1,0:T(8,128)(2,1)} %pad_maximum_fusion), channel_id=1, source_target_pairs={{0,1},{1,0},{2,3},{3,2},{4,5},{5,4},{6,7},{7,6},{8,9},{9,8},{10,11... | collective-permute-start | bytes 3145736 | tf_op jit(solution)/shard_map/ppermute | solution.py:61
  39.1 19.9 %collective-permute-start.11 = (bf16[256,2048]{1,0:T(8,128)(2,1)S(1)}, bf16[256,2048]{1,0:T(8,128)(2,1)S(1)}, u32[]{:S(2)}, u32[]{:S(2)}) collective-permute-start(bf16[256,2048]{1,0:T(8,128)(2,1)S(1)} %collective-permute-done.refs_4_.refs_6_), channel_id=1, source_target_pairs={{0,1},{1,0},{2,3},{3,2},{4,5},{5,4},{6,7},{7,6},{8,9},{9,8},{10,11... | collective-permute-start | bytes 3145736 | tf_op jit(solution)/shard_map/ppermute | solution.py:61
  39.6 13.9 %collective-permute-start.10 = (bf16[128,2048]{1,0:T(8,128)(2,1)S(1)}, bf16[128,2048]{1,0:T(8,128)(2,1)S(1)}, u32[]{:S(2)}, u32[]{:S(2)}) collective-permute-start(bf16[128,2048]{1,0:T(8,128)(2,1)S(1)} %get-tuple-element.104.refs_1_), channel_id=1, source_target_pairs={{0,1},{1,0},{2,3},{3,2},{4,5},{5,4},{6,7},{7,6},{8,9},{9,8},{10,11... | collective-permute-start | bytes 1572872 | tf_op jit(solution)/shard_map/ppermute | solution.py:61
  39.7 15.4 %collective-permute-start.12 = (bf16[128,2048]{1,0:T(8,128)(2,1)S(1)}, bf16[128,2048]{1,0:T(8,128)(2,1)S(1)}, u32[]{:S(2)}, u32[]{:S(2)}) collective-permute-start(bf16[128,2048]{1,0:T(8,128)(2,1)S(1)} %collective-permute-done.1.refs_5_), channel_id=1, source_target_pairs={{0,1},{1,0},{2,3},{3,2},{4,5},{5,4},{6,7},{7,6},{8,9},{9,8},{10,11... | collective-permute-start | bytes 1572872 | tf_op jit(solution)/shard_map/ppermute | solution.py:61
  40.2 5.4 %collective-permute-start.6 = (bf16[64,512]{1,0:T(8,128)(2,1)S(1)}, bf16[64,512]{1,0:T(8,128)(2,1)S(1)}, u32[]{:S(2)}, u32[]{:S(2)}) collective-permute-start(bf16[64,512]{1,0:T(8,128)(2,1)S(1)} %gathered.1.mine), channel_id=1, source_target_pairs={{0,56},{4,60},{8,0},{12,4},{16,8},{20,12},{24,16},{28,20},{32,24},... | collective-permute-start | bytes 196616 | tf_op jit(solution)/shard_map/ppermute | solution.py:57
  45.6 5.8 %collective-permute-start.5 = (bf16[64,512]{1,0:T(8,128)(2,1)S(1)}, bf16[64,512]{1,0:T(8,128)(2,1)S(1)}, u32[]{:S(2)}, u32[]{:S(2)}) collective-permute-start(bf16[64,512]{1,0:T(8,128)(2,1)S(1)} %gathered.1.mine), channel_id=1, source_target_pairs={{0,8},{4,12},{8,16},{12,20},{16,24},{20,28},{24,32},{28,36},{32,40... | collective-permute-start | bytes 196616 | tf_op jit(solution)/shard_map/ppermute | solution.py:57
  51.4 15.8 %collective-permute-start.13 = (bf16[2,64,1024]{2,1,0:T(8,128)(2,1)}, bf16[2,64,1024]{2,1,0:T(8,128)(2,1)S(1)}, u32[]{:S(2)}, u32[]{:S(2)}) collective-permute-start(bf16[2,64,1024]{2,1,0:T(8,128)(2,1)} %get-tuple-element.108), channel_id=1, source_target_pairs={{0,128},{4,132},{8,136},{12,140},{16,144},{20,148},{24,152},{28,15... | collective-permute-start | bytes 786440 | tf_op jit(solution)/shard_map/ppermute | solution.py:52
  53.5 5.6 %copy-start.9 = (bf16[128,2048]{1,0:T(8,128)(2,1)}, bf16[128,2048]{1,0:T(8,128)(2,1)S(1)}, u32[]{:S(2)}) copy-start(bf16[128,2048]{1,0:T(8,128)(2,1)S(1)} %collective-permute-done.10.refs_3_) | copy-start | bytes 1572868
  53.5 13.7 %collective-permute-start.14 = (bf16[2,64,1024]{2,1,0:T(8,128)(2,1)}, bf16[2,64,1024]{2,1,0:T(8,128)(2,1)S(1)}, u32[]{:S(2)}, u32[]{:S(2)}) collective-permute-start(bf16[2,64,1024]{2,1,0:T(8,128)(2,1)} %get-tuple-element.109), channel_id=1, source_target_pairs={{0,4},{4,0},{8,12},{12,8},{16,20},{20,16},{24,28},{28,24},{32,36},... | collective-permute-start | bytes 786440 | tf_op jit(solution)/shard_map/ppermute | solution.py:52
  55.1 3.9 %copy-start.10 = (bf16[128,2048]{1,0:T(8,128)(2,1)}, bf16[128,2048]{1,0:T(8,128)(2,1)S(1)}, u32[]{:S(2)}) copy-start(bf16[128,2048]{1,0:T(8,128)(2,1)S(1)} %collective-permute-done.12.refs_7_) | copy-start | bytes 1572868
  55.1 12.0 %collective-permute-start.8 = (bf16[64,512]{1,0:T(8,128)(2,1)S(1)}, bf16[64,512]{1,0:T(8,128)(2,1)S(1)}, u32[]{:S(2)}, u32[]{:S(2)}) collective-permute-start(bf16[64,512]{1,0:T(8,128)(2,1)S(1)} %get-tuple-element.103), channel_id=1, source_target_pairs={{0,40},{4,44},{8,48},{12,52},{16,56},{20,60},{24,0},{28,4},{32,8},... | collective-permute-start | bytes 196616 | tf_op jit(solution)/shard_map/ppermute | solution.py:57
  56.0 3.1 %copy-start.4 = (bf16[256,2048]{1,0:T(8,128)(2,1)}, bf16[256,2048]{1,0:T(8,128)(2,1)S(1)}, u32[]{:S(2)}) copy-start(bf16[256,2048]{1,0:T(8,128)(2,1)S(1)} %collective-permute-done.9.refs_2_.refs_5_) | copy-start | bytes 3145732
  56.0 25.3 %copy-start.32 = (bf16[2,64,1024]{2,1,0:T(8,128)(2,1)S(1)}, bf16[2,64,1024]{2,1,0:T(8,128)(2,1)}, u32[]{:S(2)}) copy-start(bf16[2,64,1024]{2,1,0:T(8,128)(2,1)} %get-tuple-element.117) | copy-start | bytes 786436
  56.0 11.2 %collective-permute-start.7 = (bf16[64,512]{1,0:T(8,128)(2,1)S(1)}, bf16[64,512]{1,0:T(8,128)(2,1)S(1)}, u32[]{:S(2)}, u32[]{:S(2)}) collective-permute-start(bf16[64,512]{1,0:T(8,128)(2,1)S(1)} %get-tuple-element.102.mine), channel_id=1, source_target_pairs={{0,24},{4,28},{8,32},{12,36},{16,40},{20,44},{24,48},{28,52},{32,5... | collective-permute-start | bytes 196616 | tf_op jit(solution)/shard_map/ppermute | solution.py:57
  67.2 27.5 %copy-start.14 = (bf16[2,64,1024]{2,1,0:T(8,128)(2,1)}, bf16[2,64,1024]{2,1,0:T(8,128)(2,1)S(1)}, u32[]{:S(2)}) copy-start(bf16[2,64,1024]{2,1,0:T(8,128)(2,1)S(1)} %collective-permute-done.13.rest_5_) | copy-start | bytes 786436
  67.2 27.5 %copy-start.15 = (bf16[2,64,1024]{2,1,0:T(8,128)(2,1)}, bf16[2,64,1024]{2,1,0:T(8,128)(2,1)S(1)}, u32[]{:S(2)}) copy-start(bf16[2,64,1024]{2,1,0:T(8,128)(2,1)S(1)} %collective-permute-done.14.rest_0_) | copy-start | bytes 786436
  68.1 26.5 %all-to-all-start.1 = ((bf16[8,64,512]{2,1,0:T(8,128)(2,1)}), bf16[8,64,512]{2,1,0:T(8,128)(2,1)S(1)}, u32[]{:S(2)}, u32[]{:S(2)}) async-start(bf16[8,64,512]{2,1,0:T(8,128)(2,1)} %relay.1), calls=%async_computation.1 | async-start | bytes 1048576 | tf_op jit(solution)/shard_map/all_to_all | solution.py:44
  74.8 14.0 %collective-permute-start.15 = (bf16[2,64,1024]{2,1,0:T(8,128)(2,1)}, bf16[2,64,1024]{2,1,0:T(8,128)(2,1)S(1)}, u32[]{:S(2)}, u32[]{:S(2)}) collective-permute-start(bf16[2,64,1024]{2,1,0:T(8,128)(2,1)} %get-tuple-element.115), channel_id=1, source_target_pairs={{0,4},{4,8},{8,12},{12,16},{16,20},{20,24},{24,28},{28,32},{32,36}... | collective-permute-start | bytes 786440 | tf_op jit(solution)/shard_map/ppermute | solution.py:48
  77.7 14.5 %collective-permute-start.16 = (bf16[2,64,1024]{2,1,0:T(8,128)(2,1)}, bf16[2,64,1024]{2,1,0:T(8,128)(2,1)S(1)}, u32[]{:S(2)}, u32[]{:S(2)}) collective-permute-start(bf16[2,64,1024]{2,1,0:T(8,128)(2,1)} %get-tuple-element.116), channel_id=1, source_target_pairs={{0,252},{4,0},{8,4},{12,8},{16,12},{20,16},{24,20},{28,24},{32,28}... | collective-permute-start | bytes 786440 | tf_op jit(solution)/shard_map/ppermute | solution.py:48
  81.3 13.4 %collective-permute-start.17 = (bf16[2,64,1024]{2,1,0:T(8,128)(2,1)S(1)}, bf16[2,64,1024]{2,1,0:T(8,128)(2,1)S(1)}, u32[]{:S(2)}, u32[]{:S(2)}) collective-permute-start(bf16[2,64,1024]{2,1,0:T(8,128)(2,1)S(1)} %copy-done.32), channel_id=1, source_target_pairs={{0,16},{4,20},{8,24},{12,28},{16,0},{20,4},{24,8},{28,12},{32,48},... | collective-permute-start | bytes 786440 | tf_op jit(solution)/shard_map/ppermute | solution.py:52
  88.7 6.0 %copy-start.16 = (bf16[2,64,1024]{2,1,0:T(8,128)(2,1)}, bf16[2,64,1024]{2,1,0:T(8,128)(2,1)S(1)}, u32[]{:S(2)}) copy-start(bf16[2,64,1024]{2,1,0:T(8,128)(2,1)S(1)} %collective-permute-done.15.lo) | copy-start | bytes 786436
  94.7 6.8 %copy-start = (bf16[8,64,512]{2,1,0:T(8,128)(2,1)}, bf16[8,64,512]{2,1,0:T(8,128)(2,1)S(1)}, u32[]{:S(2)}) copy-start(bf16[8,64,512]{2,1,0:T(8,128)(2,1)S(1)} %all-to-all-done.1) | copy-start | bytes 1572868
  101.5 9.0 %collective-permute-start.18 = (bf16[128,256]{1,0:T(8,128)(2,1)S(1)}, bf16[128,256]{1,0:T(8,128)(2,1)S(1)}, u32[]{:S(2)}, u32[]{:S(2)}) collective-permute-start(bf16[128,256]{1,0:T(8,128)(2,1)S(1)} %get-tuple-element.129), channel_id=1, source_target_pairs={{0,1},{1,0},{2,3},{3,2},{4,5},{5,4},{6,7},{7,6},{8,9},{9,8},{10,11... | collective-permute-start | bytes 196616 | tf_op jit(solution)/shard_map/ppermute | solution.py:61
  101.6 8.9 %collective-permute-start.19 = (bf16[128,256]{1,0:T(8,128)(2,1)S(1)}, bf16[128,256]{1,0:T(8,128)(2,1)S(1)}, u32[]{:S(2)}, u32[]{:S(2)}) collective-permute-start(bf16[128,256]{1,0:T(8,128)(2,1)S(1)} %get-tuple-element.130), channel_id=1, source_target_pairs={{0,2},{1,3},{2,0},{3,1},{4,6},{5,7},{6,4},{7,5},{8,10},{9,11},{10,... | collective-permute-start | bytes 196616 | tf_op jit(solution)/shard_map/ppermute | solution.py:61
  101.9 8.6 %collective-permute-start.20 = (bf16[128,256]{1,0:T(8,128)(2,1)S(1)}, bf16[128,256]{1,0:T(8,128)(2,1)S(1)}, u32[]{:S(2)}, u32[]{:S(2)}) collective-permute-start(bf16[128,256]{1,0:T(8,128)(2,1)S(1)} %get-tuple-element.131), channel_id=1, source_target_pairs={{0,3},{1,2},{2,1},{3,0},{4,7},{5,6},{6,5},{7,4},{8,11},{9,10},{10,... | collective-permute-start | bytes 196616 | tf_op jit(solution)/shard_map/ppermute | solution.py:61
  114.9 28.5 %all-to-all-start.2 = ((bf16[8,192,512]{2,1,0:T(8,128)(2,1)}), bf16[8,192,512]{2,1,0:T(8,128)(2,1)S(1)}, u32[]{:S(2)}, u32[]{:S(2)}) async-start(bf16[8,192,512]{2,1,0:T(8,128)(2,1)} %weight.1), calls=%async_computation.2 | async-start | bytes 3145728 | tf_op jit(solution)/shard_map/all_to_all | solution.py:44
  119.7 17.5 %collective-permute-start.21 = (bf16[2,64,1024]{2,1,0:T(8,128)(2,1)}, bf16[2,64,1024]{2,1,0:T(8,128)(2,1)S(1)}, u32[]{:S(2)}, u32[]{:S(2)}) collective-permute-start(bf16[2,64,1024]{2,1,0:T(8,128)(2,1)} %get-tuple-element.142), channel_id=1, source_target_pairs={{0,32},{4,36},{8,40},{12,44},{16,48},{20,52},{24,56},{28,60},{32,0... | collective-permute-start | bytes 786440 | tf_op jit(solution)/shard_map/ppermute | solution.py:52
  122.8 20.6 %collective-permute-start.22 = (bf16[2,64,1024]{2,1,0:T(8,128)(2,1)}, bf16[2,64,1024]{2,1,0:T(8,128)(2,1)S(1)}, u32[]{:S(2)}, u32[]{:S(2)}) collective-permute-start(bf16[2,64,1024]{2,1,0:T(8,128)(2,1)} %get-tuple-element.143), channel_id=1, source_target_pairs={{0,64},{4,68},{8,72},{12,76},{16,80},{20,84},{24,88},{28,92},{32,9... | collective-permute-start | bytes 786440 | tf_op jit(solution)/shard_map/ppermute | solution.py:52
  122.8 20.6 %collective-permute-start.23 = (bf16[2,64,1024]{2,1,0:T(8,128)(2,1)}, bf16[2,64,1024]{2,1,0:T(8,128)(2,1)S(1)}, u32[]{:S(2)}, u32[]{:S(2)}) collective-permute-start(bf16[2,64,1024]{2,1,0:T(8,128)(2,1)} %get-tuple-element.144), channel_id=1, source_target_pairs={{0,8},{4,12},{8,0},{12,4},{16,24},{20,28},{24,16},{28,20},{32,40},... | collective-permute-start | bytes 786440 | tf_op jit(solution)/shard_map/ppermute | solution.py:52
  123.0 24.1 %copy-start.33 = (bf16[2,64,1024]{2,1,0:T(8,128)(2,1)S(1)}, bf16[2,64,1024]{2,1,0:T(8,128)(2,1)}, u32[]{:S(2)}) copy-start(bf16[2,64,1024]{2,1,0:T(8,128)(2,1)} %get-tuple-element.162) | copy-start | bytes 786436
  130.5 45.6 %copy-start.31 = (bf16[2,64,1024]{2,1,0:T(8,128)(2,1)S(1)}, bf16[2,64,1024]{2,1,0:T(8,128)(2,1)}, u32[]{:S(2)}) copy-start(bf16[2,64,1024]{2,1,0:T(8,128)(2,1)} %get-tuple-element.164) | copy-start | bytes 786436
  130.5 48.6 %copy-start.30 = (bf16[2,64,1024]{2,1,0:T(8,128)(2,1)S(1)}, bf16[2,64,1024]{2,1,0:T(8,128)(2,1)}, u32[]{:S(2)}) copy-start(bf16[2,64,1024]{2,1,0:T(8,128)(2,1)} %get-tuple-element.165) | copy-start | bytes 786436
  130.5 52.2 %copy-start.29 = (bf16[2,64,1024]{2,1,0:T(8,128)(2,1)S(1)}, bf16[2,64,1024]{2,1,0:T(8,128)(2,1)}, u32[]{:S(2)}) copy-start(bf16[2,64,1024]{2,1,0:T(8,128)(2,1)} %get-tuple-element.168) | copy-start | bytes 786436
  137.2 57.9 %copy-start.19 = (bf16[2,64,1024]{2,1,0:T(8,128)(2,1)}, bf16[2,64,1024]{2,1,0:T(8,128)(2,1)S(1)}, u32[]{:S(2)}) copy-start(bf16[2,64,1024]{2,1,0:T(8,128)(2,1)S(1)} %collective-permute-done.21.rest_3_) | copy-start | bytes 786436
  143.4 51.7 %copy-start.20 = (bf16[2,64,1024]{2,1,0:T(8,128)(2,1)}, bf16[2,64,1024]{2,1,0:T(8,128)(2,1)S(1)}, u32[]{:S(2)}) copy-start(bf16[2,64,1024]{2,1,0:T(8,128)(2,1)S(1)} %collective-permute-done.22.rest_4_) | copy-start | bytes 786436
  143.4 51.8 %copy-start.21 = (bf16[2,64,1024]{2,1,0:T(8,128)(2,1)}, bf16[2,64,1024]{2,1,0:T(8,128)(2,1)S(1)}, u32[]{:S(2)}) copy-start(bf16[2,64,1024]{2,1,0:T(8,128)(2,1)S(1)} %collective-permute-done.23.rest_1_) | copy-start | bytes 786436
  144.2 5.9 %collective-permute-start.24 = (bf16[128,512]{1,0:T(8,128)(2,1)S(1)}, bf16[128,512]{1,0:T(8,128)(2,1)S(1)}, u32[]{:S(2)}, u32[]{:S(2)}) collective-permute-start(bf16[128,512]{1,0:T(8,128)(2,1)S(1)} %get-tuple-element.154), channel_id=1, source_target_pairs={{0,8},{4,12},{8,0},{12,4},{16,24},{20,28},{24,16},{28,20},{32,40},... | collective-permute-start | bytes 393224 | tf_op jit(solution)/shard_map/ppermute | solution.py:52
  144.5 15.5 %collective-permute-start.27 = (bf16[2,64,1024]{2,1,0:T(8,128)(2,1)}, bf16[2,64,1024]{2,1,0:T(8,128)(2,1)S(1)}, u32[]{:S(2)}, u32[]{:S(2)}) collective-permute-start(bf16[2,64,1024]{2,1,0:T(8,128)(2,1)} %get-tuple-element.161), channel_id=1, source_target_pairs={{0,128},{4,132},{8,136},{12,140},{16,144},{20,148},{24,152},{28,15... | collective-permute-start | bytes 786440 | tf_op jit(solution)/shard_map/ppermute | solution.py:52
  147.1 12.9 %collective-permute-start.28 = (bf16[2,64,1024]{2,1,0:T(8,128)(2,1)S(1)}, bf16[2,64,1024]{2,1,0:T(8,128)(2,1)S(1)}, u32[]{:S(2)}, u32[]{:S(2)}) collective-permute-start(bf16[2,64,1024]{2,1,0:T(8,128)(2,1)S(1)} %copy-done.33), channel_id=1, source_target_pairs={{0,4},{4,0},{8,12},{12,8},{16,20},{20,16},{24,28},{28,24},{32,36},... | collective-permute-start | bytes 786440 | tf_op jit(solution)/shard_map/ppermute | solution.py:52
  150.6 5.6 %collective-permute-start.25 = (bf16[96,512]{1,0:T(8,128)(2,1)S(1)}, bf16[96,512]{1,0:T(8,128)(2,1)S(1)}, u32[]{:S(2)}, u32[]{:S(2)}) collective-permute-start(bf16[96,512]{1,0:T(8,128)(2,1)S(1)} %get-tuple-element.157), channel_id=1, source_target_pairs={{0,16},{4,20},{8,24},{12,28},{16,0},{20,4},{24,8},{28,12},{32,48},... | collective-permute-start | bytes 294920 | tf_op jit(solution)/shard_map/ppermute | solution.py:52
  156.8 9.0 %collective-permute-start.26 = (bf16[80,512]{1,0:T(8,128)(2,1)S(1)}, bf16[80,512]{1,0:T(8,128)(2,1)S(1)}, u32[]{:S(2)}, u32[]{:S(2)}) collective-permute-start(bf16[80,512]{1,0:T(8,128)(2,1)S(1)} %get-tuple-element.158), channel_id=1, source_target_pairs={{0,32},{4,36},{8,40},{12,44},{16,48},{20,52},{24,56},{28,60},{32,0... | collective-permute-start | bytes 245768 | tf_op jit(solution)/shard_map/ppermute | solution.py:52
  159.9 35.2 %copy-start.22 = (bf16[2,64,1024]{2,1,0:T(8,128)(2,1)}, bf16[2,64,1024]{2,1,0:T(8,128)(2,1)S(1)}, u32[]{:S(2)}) copy-start(bf16[2,64,1024]{2,1,0:T(8,128)(2,1)S(1)} %collective-permute-done.27.rest_5_) | copy-start | bytes 786436
  160.0 35.2 %copy-start.23 = (bf16[2,64,1024]{2,1,0:T(8,128)(2,1)}, bf16[2,64,1024]{2,1,0:T(8,128)(2,1)S(1)}, u32[]{:S(2)}) copy-start(bf16[2,64,1024]{2,1,0:T(8,128)(2,1)S(1)} %collective-permute-done.28.rest_0_) | copy-start | bytes 786436
  167.2 27.9 %all-to-all-start.3 = ((bf16[8,64,512]{2,1,0:T(8,128)(2,1)}), bf16[8,64,512]{2,1,0:T(8,128)(2,1)S(1)}, u32[]{:S(2)}, u32[]{:S(2)}) async-start(bf16[8,64,512]{2,1,0:T(8,128)(2,1)} %get-tuple-element.175), calls=%async_computation.3 | async-start | bytes 1048576 | tf_op jit(solution)/shard_map/all_to_all | solution.py:44
  176.1 14.7 %collective-permute-start.29 = (bf16[2,64,1024]{2,1,0:T(8,128)(2,1)S(1)}, bf16[2,64,1024]{2,1,0:T(8,128)(2,1)S(1)}, u32[]{:S(2)}, u32[]{:S(2)}) collective-permute-start(bf16[2,64,1024]{2,1,0:T(8,128)(2,1)S(1)} %copy-done.31), channel_id=1, source_target_pairs={{0,4},{4,8},{8,12},{12,16},{16,20},{20,24},{24,28},{28,32},{32,36}... | collective-permute-start | bytes 786440 | tf_op jit(solution)/shard_map/ppermute | solution.py:48
  179.1 15.1 %collective-permute-start.30 = (bf16[2,64,1024]{2,1,0:T(8,128)(2,1)S(1)}, bf16[2,64,1024]{2,1,0:T(8,128)(2,1)S(1)}, u32[]{:S(2)}, u32[]{:S(2)}) collective-permute-start(bf16[2,64,1024]{2,1,0:T(8,128)(2,1)S(1)} %copy-done.30), channel_id=1, source_target_pairs={{0,252},{4,0},{8,4},{12,8},{16,12},{20,16},{24,20},{28,24},{32,28}... | collective-permute-start | bytes 786440 | tf_op jit(solution)/shard_map/ppermute | solution.py:48
  182.7 12.5 %collective-permute-start.31 = (bf16[2,64,1024]{2,1,0:T(8,128)(2,1)S(1)}, bf16[2,64,1024]{2,1,0:T(8,128)(2,1)S(1)}, u32[]{:S(2)}, u32[]{:S(2)}) collective-permute-start(bf16[2,64,1024]{2,1,0:T(8,128)(2,1)S(1)} %copy-done.29), channel_id=1, source_target_pairs={{0,16},{4,20},{8,24},{12,28},{16,0},{20,4},{24,8},{28,12},{32,48},... | collective-permute-start | bytes 786440 | tf_op jit(solution)/shard_map/ppermute | solution.py:52
  190.8 4.4 %copy-start.24 = (bf16[2,64,1024]{2,1,0:T(8,128)(2,1)}, bf16[2,64,1024]{2,1,0:T(8,128)(2,1)S(1)}, u32[]{:S(2)}) copy-start(bf16[2,64,1024]{2,1,0:T(8,128)(2,1)S(1)} %collective-permute-done.29.left) | copy-start | bytes 786436
  (6 other events, 7.3 us)

commit v6 on v5

--- a/solution.py
+++ b/solution.py
@@ -31,9 +31,10 @@
 
 YX_GROUPS = [[stretch_id(y, z, x) for y in range(4) for x in range(2)] for z in range(8)]
 CHUNKS = 8
+PARTS = 4
 HALF = WIDTH // 2
 Z_BITS = (1, 2, 3)
-FIRST, SECOND, THIRD = (3, 4, 1), (5, 0), (2,)
+FIRST, THIRD = (3, 4), (2, 1, 5)
 
 
 def mm(left, right, dims):
@@ -42,10 +43,6 @@
 
 def trade(value):
     return lax.all_to_all(value, "seq", 0, 0, axis_index_groups=YX_GROUPS, tiled=True)
-
-
-def shifted(value, steps):
-    return lax.ppermute(value, "seq", [(s, (s + steps) % 64) for s in range(64)])
 
 
 def swapped(value, bit):
@@ -59,11 +56,6 @@
 
 def across(value, flip):
     return lax.ppermute(value, "rep", [(r, r ^ flip) for r in range(4)])
-
-
-def beside(value):
-    pairs = [(s * 4 + r, (s ^ 1) * 4 + (r ^ 2)) for s in range(64) for r in range(4)]
-    return lax.ppermute(value, ("seq", "rep"), pairs)
 
 
 def far(shape, dtype=BF):
@@ -93,16 +85,30 @@
     )
 
 
-def pick_kernel(where, k_ref, v_ref, *outs):
-    for b in range(BITS):
-        rows = pl.ds(pl.multiple_of(where[b] * BLK, BLK), BLK)
-        outs[b][0] = k_ref[rows, :]
-        outs[b][1] = v_ref[rows, :]
-    first, last, picked = outs[BITS:]
-    first[0] = k_ref[0:BLK, :]
-    first[1] = v_ref[0:BLK, :]
-    last[0] = k_ref[BLK : 2 * BLK, :]
-    last[1] = v_ref[BLK : 2 * BLK, :]
+def paired(value):
+    return swapped(value, 0)
+
+
+def neighboured(value):
+    return lax.ppermute(value, "seq", [(s, (s - 1 + s % 2 * 2) % 64) for s in range(64)])
+
+
+def inner_block(where):
+    return 1 - where[11] % 2
+
+
+def pick_kernel(where, k_ref, v_ref, pair, outer, *outs):
+    def block(index):
+        return pl.ds(pl.multiple_of(index * BLK, BLK), BLK)
+
+    inner = inner_block(where)
+    for c, src in enumerate((k_ref, v_ref)):
+        pair[0, c] = src[block(where[0]), :]
+        pair[1, c] = src[block(inner), :]
+        outer[c] = src[block(1 - inner), :]
+        for b in range(1, BITS):
+            outs[b - 1][c] = src[block(where[b]), :]
+    picked = outs[BITS - 1]
     for g in range(GLOB):
         here = where[6 + g]
         rows = pl.ds(pl.multiple_of(jnp.maximum(here, 0) * BLK, BLK), BLK)
@@ -114,7 +120,7 @@
 
 def pick(where, keys, values):
     block = far((2, BLK, WIDTH))
-    outs = [block] * (BITS + 2) + [far((CHUNKS, BLK, HALF))]
+    outs = [far((2, 2, BLK, WIDTH))] + [block] * BITS + [far((CHUNKS, BLK, HALF))]
     vm = pl.BlockSpec(memory_space=pltpu.VMEM)
     return pl.pallas_call(
         pick_kernel,
@@ -123,7 +129,7 @@
         out_specs=[vm] * len(outs),
         compiler_params=params(),
         name="pick",
-    )(where, keys, values)
+    )(where, *from_hbm(keys, values))
 
 
 def gathered_kernel(x_ref, o_ref):
@@ -169,13 +175,15 @@
     )(mine, below, above)
 
 
-def gather_heads(dst, c, cols, own, lo, hi, rand, glob):
-    dst[0:64, :] = lo[c, :, cols]
+def gather_heads(where, dst, c, cols, own, pair, outer, rand, glob):
+    inner = inner_block(where)
+    dst[pl.ds(pl.multiple_of(inner * 192, 64), BLK), :] = pair[1, c, :, cols]
+    dst[pl.ds(pl.multiple_of((1 - inner) * 192, 64), BLK), :] = outer[c, :, cols]
     dst[64:192, :] = own[:, cols]
-    dst[192:256, :] = hi[c, :, cols]
     dst[256:384, :] = glob[0, c * TOK : (c + 1) * TOK, cols]
-    for b in range(BITS):
-        dst[384 + 64 * b : 448 + 64 * b, :] = rand[b][c, :, cols]
+    dst[384:448, :] = pair[0, c, :, cols]
+    for b in range(1, BITS):
+        dst[384 + 64 * b : 448 + 64 * b, :] = rand[b - 1][c, :, cols]
 
 
 def fill_bias(where, bias):
@@ -190,8 +198,8 @@
         bias[kb * BLK : (kb + 1) * BLK, :] = jnp.where(keep, 0.0, -1e30).astype(F32)
 
 
-def forward_kernel(where, q, k, v, lo, hi, *rest):
-    rand, rest = rest[:BITS], rest[BITS:]
+def forward_kernel(where, q, k, v, pair, outer, *rest):
+    rand, rest = rest[: BITS - 1], rest[BITS - 1 :]
     glob, perm, attn, stats, *ordered, ks, vs, bias, acc = rest
     step = pl.program_id(0)
 
@@ -201,8 +209,8 @@
 
     for i in range(STEP):
         cols = slice(i * HEAD_DIM, (i + 1) * HEAD_DIM)
-        gather_heads(ks.at[i], 0, cols, k, lo, hi, rand, glob)
-        gather_heads(vs.at[i], 1, cols, v, lo, hi, rand, glob)
+        gather_heads(where, ks.at[i], 0, cols, k, pair, outer, rand, glob)
+        gather_heads(where, vs.at[i], 1, cols, v, pair, outer, rand, glob)
         scores = mm(ks[i], q[:, cols], ROWS) * SCALE + bias[...]
         top = jnp.max(scores, axis=0, keepdims=True)
         expd = jnp.exp(scores - top)
@@ -230,16 +238,17 @@
     pair = pl.BlockSpec((2, BLK, WIDE), lambda h: (0, 0, h))
     both = pl.BlockSpec((2, TOK, WIDE), lambda h: (0, 0, h))
     half = pl.BlockSpec((1, 2 * TOK, WIDE), lambda h: (h, 0, 0))
-    return flat, pair, both, half
-
-
-def forward(where, q, k, v, lo, hi, rand, glob, perm):
-    flat, pair, both, half = head_specs()
+    two = pl.BlockSpec((2, 2, BLK, WIDE), lambda h: (0, 0, 0, h))
+    return flat, pair, both, half, two
+
+
+def forward(where, q, k, v, pair, outer, rand, glob, perm):
+    flat, block, both, half, two = head_specs()
     return pl.pallas_call(
         forward_kernel,
         grid=(HEADS // STEP,),
-        in_specs=[smem(), flat, flat, flat, pair, pair]
-        + [pair] * BITS
+        in_specs=[smem(), flat, flat, flat, two]
+        + [block] * BITS
         + [half, pl.BlockSpec((WIDE, WIDTH), lambda h: (h, 0))],
         out_specs=[
             flat,
@@ -259,13 +268,14 @@
         ],
         compiler_params=params(dimension_semantics=("arbitrary",)),
         name="forward",
-    )(where, q, k, v, lo, hi, *rand, glob, perm)
-
-
-def backward_kernel(where, q, k, v, lo, hi, *rest):
-    rand, rest = rest[:BITS], rest[BITS:]
-    glob, stats, d_attn_ref, dq, down, dlo, dhi = rest[:7]
-    drand, rest = rest[7 : 7 + BITS], rest[7 + BITS :]
+    )(where, q, k, v, pair, outer, *rand, glob, perm)
+
+
+def backward_kernel(where, q, k, v, pair, outer, *rest):
+    rand, rest = rest[: BITS - 1], rest[BITS - 1 :]
+    low = inner_block(where) == 0
+    glob, stats, d_attn_ref, dq, down, dpair, douter = rest[:7]
+    drand, rest = rest[7 : 6 + BITS], rest[6 + BITS :]
     dglob, ks, vs, bias = rest
 
     @pl.when(pl.program_id(0) == 0)
@@ -274,8 +284,8 @@
 
     for i in range(STEP):
         cols = slice(i * HEAD_DIM, (i + 1) * HEAD_DIM)
-        gather_heads(ks.at[i], 0, cols, k, lo, hi, rand, glob)
-        gather_heads(vs.at[i], 1, cols, v, lo, hi, rand, glob)
+        gather_heads(where, ks.at[i], 0, cols, k, pair, outer, rand, glob)
+        gather_heads(where, vs.at[i], 1, cols, v, pair, outer, rand, glob)
         d_attn = d_attn_ref[:, cols]
         scores = mm(ks[i], q[:, cols], ROWS) * SCALE + bias[...]
         probs = jnp.exp(scores - stats[i, 0:1, :]) * stats[i, 1:2, :]
@@ -285,26 +295,28 @@
         dscore = (probs * (dprob - delta) * SCALE).astype(BF)
         dq[:, cols] = mm(dscore, ks[i], COLS).astype(BF)
         for c, grad in ((0, mm(dscore, q[:, cols], PLAIN)), (1, mm(probs_b, d_attn, PLAIN))):
-            dlo[c, :, cols] = grad[0:64].astype(BF)
+            before, after = grad[0:64], grad[192:256]
+            dpair[0, c, :, cols] = grad[384:448].astype(BF)
+            dpair[1, c, :, cols] = jnp.where(low, before, after).astype(BF)
+            douter[c, :, cols] = jnp.where(low, after, before).astype(BF)
             down[c, :, cols] = grad[64:192]
-            dhi[c, :, cols] = grad[192:256].astype(BF)
             dglob[0, c * TOK : (c + 1) * TOK, cols] = grad[256:384].astype(BF)
-            for b in range(BITS):
-                drand[b][c, :, cols] = grad[384 + 64 * b : 448 + 64 * b].astype(BF)
-
-
-def backward(where, q, k, v, lo, hi, rand, glob, stats, d_attn):
-    flat, pair, both, half = head_specs()
-    block = far((2, BLK, WIDTH))
+            for b in range(1, BITS):
+                drand[b - 1][c, :, cols] = grad[384 + 64 * b : 448 + 64 * b].astype(BF)
+
+
+def backward(where, q, k, v, pair, outer, rand, glob, stats, d_attn):
+    flat, block, both, half, two = head_specs()
+    out = far((2, BLK, WIDTH))
     outs = pl.pallas_call(
         backward_kernel,
         grid=(HEADS // STEP,),
-        in_specs=[smem(), flat, flat, flat, pair, pair]
-        + [pair] * BITS
+        in_specs=[smem(), flat, flat, flat, two]
+        + [block] * BITS
         + [half, pl.BlockSpec((STEP, 8, TOK), lambda h: (h, 0, 0)), flat],
-        out_specs=[flat, both, pair, pair] + [pair] * BITS + [half],
-        out_shape=[far((TOK, WIDTH)), far((2, TOK, WIDTH), F32), block, block]
-        + [block] * BITS
+        out_specs=[flat, both, two] + [block] * BITS + [half],
+        out_shape=[far((TOK, WIDTH)), far((2, TOK, WIDTH), F32), far((2, 2, BLK, WIDTH))]
+        + [out] * BITS
         + [far((2, 2 * TOK, HALF))],
         scratch_shapes=[
             pltpu.VMEM((STEP, KEYS, HEAD_DIM), BF),
@@ -313,81 +325,52 @@
         ],
         compiler_params=params(dimension_semantics=("arbitrary",)),
         name="backward",
-    )(where, *from_hbm(q, k, v, lo, hi, *rand, glob, stats, d_attn))
-    return outs[:4], outs[4 : 4 + BITS], outs[4 + BITS]
-
-
-def head_of(i, where):
-    return ((i // 2) ^ where[13]) * 2 + i % 2
-
-
-def head_call(kernel, where, parts, extra, extra_spec, out_shape, out_spec, scratch, name):
-    w_spec = pl.BlockSpec((HEAD_DIM, D), lambda i, at: (0, 0))
+    )(where, *from_hbm(q, k, v, pair, outer, *rand, glob, stats, d_attn))
+    return outs[:4], outs[4 : 3 + BITS], outs[3 + BITS]
+
+
+def place_weights(where, parts, w, sems):
+    copies = []
+    for i in range(PARTS):
+        rows = pl.ds(pl.multiple_of((i ^ where[13]) * 256, 256), 256)
+        copies.append(pltpu.make_async_copy(parts[i], w.at[rows, :], sems.at[i]))
+    for copy in copies:
+        copy.start()
+    for copy in copies:
+        copy.wait()
+
+
+def project_kernel(where, *refs):
+    parts, (d_out, out, w, sems) = refs[:PARTS], refs[PARTS:]
+    place_weights(where, parts, w, sems)
+    out[...] = mm(d_out[...], w[...], ROWS).astype(BF)
+
+
+def layer_kernel(where, *refs):
+    parts, (attn, out, w, sems) = refs[:PARTS], refs[PARTS:]
+    place_weights(where, parts, w, sems)
+    out[...] = mm(attn[...], w[...], PLAIN).astype(BF)
+
+
+def weights_call(kernel, where, parts, rows, width, name):
+    vm = pl.BlockSpec(memory_space=pltpu.VMEM)
     return pl.pallas_call(
         kernel,
-        grid_spec=pltpu.PrefetchScalarGridSpec(
-            num_scalar_prefetch=1,
-            grid=(HEADS,),
-            in_specs=[w_spec] * HEADS + [extra_spec],
-            out_specs=out_spec,
-            scratch_shapes=scratch,
-        ),
-        out_shape=out_shape,
-        compiler_params=params(dimension_semantics=("arbitrary",)),
+        out_shape=far((TOK, width)),
+        in_specs=[smem()] + [pl.BlockSpec(memory_space=pl.ANY)] * PARTS + [vm],
+        out_specs=vm,
+        scratch_shapes=[pltpu.VMEM((WIDTH, D), BF), pltpu.SemaphoreType.DMA((PARTS,))],
+        compiler_params=params(),
         name=name,
-    )(where, *from_hbm(*parts, extra))
-
-
-def project_kernel(where, *refs):
-    w, (d_out, out) = refs[:HEADS], refs[HEADS:]
-    for i in range(HEADS):
-
-        @pl.when(pl.program_id(0) == i)
-        def _():
-            out[...] = mm(d_out[...], w[i][...], ROWS).astype(BF)
+    )(where, *from_hbm(*parts), rows)
 
 
 def project(where, parts, d_out):
-    return head_call(
-        project_kernel,
-        where,
-        parts,
-        d_out,
-        pl.BlockSpec((TOK, D), lambda i, at: (0, 0)),
-        far((TOK, WIDTH)),
-        pl.BlockSpec((TOK, HEAD_DIM), lambda i, at: (0, head_of(i, at))),
-        [],
-        "project",
-    )
-
-
-def layer_kernel(where, *refs):
-    w, (attn, out, acc) = refs[:HEADS], refs[HEADS:]
-    for i in range(HEADS):
-
-        @pl.when(pl.program_id(0) == i)
-        def _():
-            part = mm(attn[...], w[i][...], PLAIN)
-            if i == 0:
-                acc[...] = part
-            elif i < HEADS - 1:
-                acc[...] += part
-            else:
-                out[...] = (acc[...] + part).astype(BF)
+    return weights_call(project_kernel, where, parts, d_out, WIDTH, "project")
 
 
 def layer_of(where, parts, attn):
-    return head_call(
-        layer_kernel,
-        where,
-        parts,
-        attn,
-        pl.BlockSpec((TOK, HEAD_DIM), lambda i, at: (0, head_of(i, at))),
-        far((TOK, D)),
-        pl.BlockSpec((TOK, D), lambda i, at: (0, 0)),
-        [pltpu.VMEM((TOK, D), F32)],
-        "layer",
-    )
+    return weights_call(layer_kernel, where, parts, attn, D, "layer")
 
 
 def weight_kernel(*refs):
@@ -415,8 +398,7 @@
         weight_kernel,
         grid=(3,),
         in_specs=[pl.BlockSpec((TOK, 256), lambda i: (0, 0))] * 4
-        + [pl.BlockSpec((TOK, WIDTH), lambda i: (0, jnp.maximum(i - 1, 0)))]
-        + [pl.BlockSpec((TOK, WIDTH), lambda i: (1, jnp.maximum(i - 1, 0)))] * 3
+        + [pl.BlockSpec((TOK, WIDTH), lambda i: (0, jnp.maximum(i - 1, 0)))] * 4
         + [pl.BlockSpec((CHUNKS, BLK, HALF), lambda i: (0, 0, 0))],
         out_specs=pl.BlockSpec((CHUNKS, BLK, HALF), lambda i: (0, i, 0)),
         out_shape=far((CHUNKS, 192, HALF)),
@@ -503,14 +485,19 @@
     )(where, glob, kept, came)
 
 
-def finish_kernel(where, own, left, right, *rest):
-    rand, (glob, dk, dv, acc) = rest[:BITS], rest[BITS:]
+def finish_kernel(where, own, pair, outer, *rest):
+    rand, (glob, dk, dv, acc) = rest[: BITS - 1], rest[BITS - 1 :]
+
+    def block(index):
+        return pl.ds(pl.multiple_of(index * BLK, BLK), BLK)
+
+    inner = inner_block(where)
     acc[...] = own[...]
-    acc[:, 0:BLK, :] += left[...].astype(F32)
-    acc[:, BLK : 2 * BLK, :] += right[...].astype(F32)
-    for b in range(BITS):
-        rows = pl.ds(pl.multiple_of(where[b] * BLK, BLK), BLK)
-        acc[:, rows, :] += rand[b][...].astype(F32)
+    acc[:, block(inner), :] += pair[1].astype(F32)
+    acc[:, block(1 - inner), :] += outer[...].astype(F32)
+    acc[:, block(where[0]), :] += pair[0].astype(F32)
+    for b in range(1, BITS):
+        acc[:, block(where[b]), :] += rand[b - 1][...].astype(F32)
     for g in range(GLOB):
         here = where[6 + g]
 
@@ -523,22 +510,23 @@
     dv[...] = acc[1].astype(BF)
 
 
-def finish(where, own, left, right, rand, glob):
-    wide = 256
-    pair = pl.BlockSpec((2, BLK, wide), lambda i: (0, 0, i))
+def finish(where, own, pair, outer, rand, glob):
+    wide = 512
+    block = pl.BlockSpec((2, BLK, wide), lambda i: (0, 0, i))
+    two = pl.BlockSpec((2, 2, BLK, wide), lambda i: (0, 0, 0, i))
     flat = pl.BlockSpec((TOK, wide), lambda i: (0, i))
     return pl.pallas_call(
         finish_kernel,
         grid=(WIDTH // wide,),
-        in_specs=[smem(), pl.BlockSpec((2, TOK, wide), lambda i: (0, 0, i)), pair, pair]
-        + [pair] * BITS
-        + [pl.BlockSpec((1, 2, GLOB, BLK, wide), lambda i: (i // 2, 0, 0, 0, i % 2))],
+        in_specs=[smem(), pl.BlockSpec((2, TOK, wide), lambda i: (0, 0, i)), two]
+        + [block] * BITS
+        + [pl.BlockSpec((1, 2, GLOB, BLK, wide), lambda i: (i, 0, 0, 0, 0))],
         out_specs=[flat, flat],
         out_shape=[far((TOK, WIDTH)), far((TOK, WIDTH))],
         scratch_shapes=[pltpu.VMEM((2, TOK, wide), F32)],
         compiler_params=params(dimension_semantics=("arbitrary",)),
         name="finish",
-    )(where, *from_hbm(own, left, right, *rand), glob)
+    )(where, *from_hbm(own, pair, outer, *rand), glob)
 
 
 def feature_order(rep):
@@ -557,97 +545,66 @@
 def per_device(queries, keys, values, w_out, d_out, rand_slot, global_ids):
     q, k, v, grad_out = queries[0], keys[0], values[0], d_out[0]
     where = where_of(rand_slot[0, 0], global_ids[0])
-    *chosen, low_edge, high_edge, picked = pick(where, k, v)
+    pair, outer, *chosen, picked = pick(where, k, v)
+    rand = dict(zip(range(1, BITS), chosen))
     spread = trade(picked)
-    mixed = jnp.concatenate([w_out[:HEAD_DIM], grad_out])
-    upper = w_out[HEAD_DIM:]
-    mixed2 = across(mixed, 2)
-    upper2 = beside(upper)
+    picked, rows = together(picked, w_out)
+    parts = [w_out, across(rows, 1), across(rows, 2)]
     order = feature_order(lax.axis_index("rep"))
-    rand = [None] * BITS
     for b in FIRST:
-        rand[b] = swapped(chosen[b], b)
-    spread, mixed, upper, mixed2, upper2, order, *tied = together(
-        spread,
-        mixed,
-        upper,
-        mixed2,
-        upper2,
-        order,
-        *[rand[b] for b in FIRST],
-        low_edge,
-        high_edge,
-        *chosen,
+        rand[b] = swapped(rand[b], b)
+    spread, order, parts[1], own_grad, pair, outer, rand = together(
+        spread, order, parts[1], grad_out, pair, outer, rand
     )
-    for b in FIRST:
-        rand[b], tied = tied[0], tied[1:]
-    low_edge, high_edge, *chosen = tied
     mine = gathered(spread)
-    mixed1 = across(mixed, 1)
-    upper1 = across(upper, 1)
-    mixed3 = across(mixed2, 1)
-    upper3 = across(upper2, 1)
-    for b in SECOND:
-        rand[b] = swapped(chosen[b], b)
+    pair = paired(pair)
+    outer = neighboured(outer)
     two, three = near(mine, along_z(mine, 1), along_z(mine, -1))
     below, above = along_z(three, 3), along_z(two, -3)
-    parts = (w_out, upper, mixed1, upper1, mixed2, upper2, mixed3, upper3)
+    below, above, pair, outer, parts[2], own_grad, rand = together(
+        below, above, pair, outer, parts[2], own_grad, rand
+    )
+    glob = trade(relay(three, below, above)).reshape(2, 2 * TOK, HALF)
+    parts.append(across(parts[2], 1))
+    grads = [grad_out, across(own_grad, 1), across(own_grad, 2)]
+    for b in THIRD:
+        rand[b] = swapped(rand[b], b)
     d_attn = project(where, parts, grad_out)
-    below, above, d_attn, *tied = together(
-        below, above, d_attn, *[rand[b] for b in SECOND], low_edge, high_edge, *chosen
-    )
-    for b in SECOND:
-        rand[b], tied = tied[0], tied[1:]
-    low_edge, high_edge, *chosen = tied
-    glob = trade(relay(three, below, above)).reshape(2, 2 * TOK, HALF)
-    for b in THIRD:
-        rand[b] = swapped(chosen[b], b)
-    lo = shifted(high_edge, 1)
-    hi = shifted(low_edge, -1)
-    glob, lo, hi, *tied = together(glob, lo, hi, *[rand[b] for b in THIRD])
-    for b in THIRD:
-        rand[b], tied = tied[0], tied[1:]
-    lo, hi, *rand = from_hbm(lo, hi, *rand)
+    glob, d_attn, rand = together(glob, d_attn, rand)
+    rand = [rand[b] for b in range(1, BITS)]
+    pair, outer, *rand = from_hbm(pair, outer, *rand)
     attn, stats, *ordered = forward(
-        where, *from_hbm(q, k, v), lo, hi, rand, glob, *from_hbm(order)
+        where, *from_hbm(q, k, v), pair, outer, rand, glob, *from_hbm(order)
     )
     cols = [ordered[0]] + [across(ordered[a], a) for a in range(1, 4)]
-    (dq, down, dlo, dhi), drand, dglob = backward(
-        where, q, k, v, lo, hi, rand, glob, stats, d_attn
+    grads.append(across(grads[2], 1))
+    (dq, down, pair, outer), drand, dglob = backward(
+        where, q, k, v, pair, outer, rand, glob, stats, d_attn
     )
-    cols[1], cols[2], cols[3], dglob = together(cols[1], cols[2], cols[3], dglob)
-    payload = weight_payload(
-        cols, (grad_out, mixed1, mixed2, mixed3), dglob.reshape(CHUNKS, BLK, HALF)
+    back = dict(zip(range(1, BITS), drand))
+    cols[1], cols[2], cols[3], grads[1], grads[2], grads[3], dglob = together(
+        cols[1], cols[2], cols[3], grads[1], grads[2], grads[3], dglob
     )
+    payload = weight_payload(cols, grads, dglob.reshape(CHUNKS, BLK, HALF))
     payload = trade(payload)
-    back = [None] * BITS
     for b in FIRST:
-        back[b] = swapped(drand[b], b)
+        back[b] = swapped(back[b], b)
     layer = layer_of(where, parts, attn)
-    payload, layer, dlo, dhi, *tied = together(
-        payload, layer, dlo, dhi, *[back[b] for b in FIRST], *drand
-    )
-    for b in FIRST:
-        back[b], tied = tied[0], tied[1:]
-    drand = tied
-    for b in SECOND:
-        back[b] = swapped(drand[b], b)
+    payload, layer, pair, outer, back = together(payload, layer, pair, outer, back)
+    pair = paired(pair)
+    outer = neighboured(outer)
     glob_sum, keep, send = first(where, payload)
     for step, bit in enumerate(Z_BITS[1:]):
         came = swapped(send, Z_BITS[step])
         glob_sum, keep, send = fold(where, bit, glob_sum, keep, came)
     came = swapped(send, Z_BITS[2])
-    came, dlo, dhi, *tied = together(came, dlo, dhi, *[back[b] for b in SECOND], *drand)
-    for b in SECOND:
-        back[b], tied = tied[0], tied[1:]
-    drand = tied
+    came, pair, outer, back = together(came, pair, outer, back)
     routed, weight_grad = last(where, glob_sum, keep, came)
     glob_total = trade(routed).reshape(2, 2, GLOB, BLK, HALF)
     for b in THIRD:
-        back[b] = swapped(drand[b], b)
-    right = shifted(dlo, -1)
-    left = shifted(dhi, 1)
-    dk, dv = finish(where, down, left, right, back, glob_total)
+        back[b] = swapped(back[b], b)
+    back = [back[b] for b in range(1, BITS)]
+    dk, dv = finish(where, down, pair, outer, back, glob_total)
     return (layer[None], dq[None], dk[None], dv[None], weight_grad)
 
 

time: 201 us -> 200 us (level)
  waiting for transfers between devices: 70.3 us -> 80.6 us
  Pallas kernels: 42.5 us -> 36.9 us
  starting transfers between devices: 78.6 us -> 75.5 us
    ppermute x5 -> x2, waiting for transfers between devices: 22.5 us -> 0.01 us  [neighboured(): lax.ppermute(value, 'seq', [(s, (s - 1 + s % 2 * 2) % 64) for s in range(...]
    ppermute x15, waiting for transfers between devices: 40 us -> 55 us  [swapped(): return lax.ppermute(value, 'seq', [(s, s ^ 1 << bit) for s in range(64)])]
    all_to_all x4, waiting for transfers between devices: 0.01 us -> 10.2 us  [trade(): lax.all_to_all(value, 'seq', 0, 0, axis_index_groups=YX_GROUPS, tiled=True)]
    ppermute x8 -> x9, waiting for transfers between devices: 0.02 us -> 8.69 us  [across(): return lax.ppermute(value, 'rep', [(r, r ^ flip) for r in range(4)])]
    pallas_call x2, Pallas kernels: 14.6 us -> 9.26 us  [weights_call(): pl.pallas_call(kernel, out_shape=far((TOK, width)), in_specs=[smem()] + [...]
    ppermute x5 -> x2, starting transfers between devices: 15.2 us -> 10.2 us  [neighboured(): lax.ppermute(value, 'seq', [(s, (s - 1 + s % 2 * 2) % 64) for s in range(...]
    ppermute x15, starting transfers between devices: 26.2 us -> 29.3 us  [swapped(): return lax.ppermute(value, 'seq', [(s, s ^ 1 << bit) for s in range(64)])]
    ppermute x8 -> x9, starting transfers between devices: 4.55 us -> 3.82 us  [across(): return lax.ppermute(value, 'rep', [(r, r ^ flip) for r in range(4)])]
  transfers between devices with their start and end apart: 36 -> 34, of which waited for: 14 -> 16; matrix products, arithmetic and copies ran while one was open for 1% -> 1% of each run, Pallas kernels for 13% -> 13%
where the time goes in v6:
time: 200 us
  waiting for transfers between devices  80.6 us (40%)
  starting transfers between devices  75.5 us (38%)
  Pallas kernels  36.9 us (18%)
  other arithmetic  3.56 us (2%)
  local copies, waits for them, and re-layouts  2.15 us (1%)
    ppermute x15, waiting for transfers between devices, swapped(): return lax.ppermute(value, 'seq', [(s, s ^ 1 << bit) for s in range(64)])  55 us
    ppermute x15, starting transfers between devices, swapped(): return lax.ppermute(value, 'seq', [(s, s ^ 1 << bit) for s in range(64)])  29.3 us
    all_to_all x4, starting transfers between devices, trade(): lax.all_to_all(value, 'seq', 0, 0, axis_index_groups=YX_GROUPS, tiled=True)  23.8 us
    all_to_all x4, waiting for transfers between devices, trade(): lax.all_to_all(value, 'seq', 0, 0, axis_index_groups=YX_GROUPS, tiled=True)  10.2 us
    ppermute x2, starting transfers between devices, neighboured(): lax.ppermute(value, 'seq', [(s, (s - 1 + s % 2 * 2) % 64) for s in range(...  10.2 us
    pallas_call x2, Pallas kernels, weights_call(): pl.pallas_call(kernel, out_shape=far((TOK, width)), in_specs=[smem()] + [...  9.26 us
    ppermute x9, waiting for transfers between devices, across(): return lax.ppermute(value, 'rep', [(r, r ^ flip) for r in range(4)])  8.69 us
    ppermute x4, starting transfers between devices, along_z(): return lax.ppermute(value, 'seq', pairs)  8.41 us
  transfers between devices with their start and end apart: 34, of which 16 were waited for; matrix products, arithmetic and copies ran while one was open for 1% of the time, Pallas kernels for 13%

profile of v6, /device:TPU:8, one launch (start us, length us, event | category | flops | bytes accessed | tf_op | source)
XLA Modules:
  0.0 199.7 jit_solution(14628011583687079969)
XLA Ops:
  0.6 0.7 fusion.36
  1.3 0.7 compare_select_fusion
  2.0 0.7 concatenate.3.where.refs_0_
  2.7 2.7 %pick.1 = (bf16[2,2,64,1024]{3,2,1,0:T(8,128)(2,1)}, bf16[2,64,1024]{2,1,0:T(8,128)(2,1)}, bf16[2,64,1024]{2,1,0:T(8,128)(2,1)}, bf16[2,64,1024]{2,1,0:T(8,128)(...) custom-call(s32[14]{0:T(128)S(1)} %concatenate.3.where.refs_0_, ...), custom_call_target="tpu_custom_call" | custom-call | tf_op jit(solution)/shard_map/pick/pallas_call | solution.py:125
  5.5 1.6 collective-permute-start.9
  7.0 7.1 %all-to-all-start = ((bf16[8,64,512]{2,1,0:T(8,128)(2,1)}), bf16[8,64,512]{2,1,0:T(8,128)(2,1)S(1)}, u32[]{:S(2)}, u32[]{:S(2)}) async-start(bf16[8,64,512]{2,1,0:T(8,128)(2,1)} %get-tuple-element.98), calls=%async_computation | async-start | bytes 1048576 | tf_op jit(solution)/shard_map/all_to_all | solution.py:45
  14.1 7.2 %collective-permute-start.1 = (bf16[2,64,1024]{2,1,0:T(8,128)(2,1)}, bf16[2,64,1024]{2,1,0:T(8,128)(2,1)S(1)}, u32[]{:S(2)}, u32[]{:S(2)}) collective-permute-start(bf16[2,64,1024]{2,1,0:T(8,128)(2,1)} %get-tuple-element.104), channel_id=1, source_target_pairs={{0,32},{4,36},{8,40},{12,44},{16,48},{20,52},{24,56},{28,60},{32,0... | collective-permute-start | bytes 786440 | tf_op jit(solution)/shard_map/ppermute | solution.py:49
  21.3 2.2 %fusion.rest_6_ = bf16[1024,1024]{1,0:T(8,128)(2,1)} fusion(s32[1024]{0:T(1024)S(1)} %fusion.15), kind=kLoop, calls=%fused_computation.1 | loop fusion | flops 2097152 | bytes 2101248 | tf_op jit(solution)/shard_map/convert_element_type | solution.py:538
  23.5 5.2 %collective-permute-done.1.rest_2_ = bf16[2,64,1024]{2,1,0:T(8,128)(2,1)S(1)} collective-permute-done((bf16[2,64,1024]{2,1,0:T(8,128)(2,1)}, bf16[2,64,1024]{2,1,0:T(8,128)(2,1)S(1)}, u32[]{:S(2)}, u32[]{:S(2)}) %collective-permute-start.1) | collective-permute-done | bytes 262176 | tf_op jit(solution)/shard_map/ppermute | solution.py:49
  28.7 0.3 collective-permute-done.2.rest_3_
  29.1 10.2 %all-to-all-done.x_ref = bf16[8,64,512]{2,1,0:T(8,128)(2,1)S(1)} async-done(((bf16[8,64,512]{2,1,0:T(8,128)(2,1)}), bf16[8,64,512]{2,1,0:T(8,128)(2,1)S(1)}, u32[]{:S(2)}, u32[]{:S(2)}) %all-to-all-start) | async-done | bytes 524320 | tf_op jit(solution)/shard_map/all_to_all | solution.py:45
  39.3 1.4 collective-permute-start.7
  40.7 9.6 %collective-permute-start.8 = (bf16[2,64,1024]{2,1,0:T(8,128)(2,1)}, bf16[2,64,1024]{2,1,0:T(8,128)(2,1)S(1)}, u32[]{:S(2)}, u32[]{:S(2)}) collective-permute-start(bf16[2,64,1024]{2,1,0:T(8,128)(2,1)} %get-tuple-element.111), channel_id=1, source_target_pairs={{0,252},{4,8},{8,4},{12,16},{16,12},{20,24},{24,20},{28,32},{32,28... | collective-permute-start | bytes 786440 | tf_op jit(solution)/shard_map/ppermute | solution.py:93
  50.3 0.1 collective-permute-start.3
  50.4 3.2 %collective-permute-start.4 = (bf16[64,512]{1,0:T(8,128)(2,1)S(1)}, bf16[64,512]{1,0:T(8,128)(2,1)S(1)}, u32[]{:S(2)}, u32[]{:S(2)}) collective-permute-start(bf16[64,512]{1,0:T(8,128)(2,1)S(1)} %gathered.1.mine), channel_id=1, source_target_pairs={{0,56},{4,60},{8,0},{12,4},{16,8},{20,12},{24,16},{28,20},{32,24},... | collective-permute-start | bytes 196616 | tf_op jit(solution)/shard_map/ppermute | solution.py:54
  53.6 2.2 %collective-permute-done.3.below = bf16[64,512]{1,0:T(8,128)(2,1)S(1)} collective-permute-done((bf16[64,512]{1,0:T(8,128)(2,1)S(1)}, bf16[64,512]{1,0:T(8,128)(2,1)S(1)}, u32[]{:S(2)}, u32[]{:S(2)}) %collective-permute-start.3) | collective-permute-done | bytes 65568 | tf_op jit(solution)/shard_map/ppermute | solution.py:54
  55.9 1.1 collective-permute-done.4.above
  57.0 0.1 collective-permute-start.5
  57.1 5.0 %collective-permute-start.6 = (bf16[64,512]{1,0:T(8,128)(2,1)S(1)}, bf16[64,512]{1,0:T(8,128)(2,1)S(1)}, u32[]{:S(2)}, u32[]{:S(2)}) collective-permute-start(bf16[64,512]{1,0:T(8,128)(2,1)S(1)} %get-tuple-element.109), channel_id=1, source_target_pairs={{0,40},{4,44},{8,48},{12,52},{16,56},{20,60},{24,0},{28,4},{32,8},... | collective-permute-start | bytes 196616 | tf_op jit(solution)/shard_map/ppermute | solution.py:54
  62.1 3.3 %collective-permute-done.5.below = bf16[64,512]{1,0:T(8,128)(2,1)S(1)} collective-permute-done((bf16[64,512]{1,0:T(8,128)(2,1)S(1)}, bf16[64,512]{1,0:T(8,128)(2,1)S(1)}, u32[]{:S(2)}, u32[]{:S(2)}) %collective-permute-start.5) | collective-permute-done | bytes 65568 | tf_op jit(solution)/shard_map/ppermute | solution.py:54
  65.5 0.1 collective-permute-start.10
  65.6 0.2 collective-permute-start.18
  65.8 0.9 relay.1
  66.7 5.2 %all-to-all-start.1 = ((bf16[8,64,512]{2,1,0:T(8,128)(2,1)}), bf16[8,64,512]{2,1,0:T(8,128)(2,1)S(1)}, u32[]{:S(2)}, u32[]{:S(2)}) async-start(bf16[8,64,512]{2,1,0:T(8,128)(2,1)} %relay.1), calls=%async_computation.1 | async-start | bytes 1048576 | tf_op jit(solution)/shard_map/all_to_all | solution.py:45
  71.8 8.7 %collective-permute-done.18.refs_6_ = bf16[128,2048]{1,0:T(8,128)(2,1)} collective-permute-done((bf16[128,2048]{1,0:T(8,128)(2,1)S(1)}, bf16[128,2048]{1,0:T(8,128)(2,1)}, u32[]{:S(2)}, u32[]{:S(2)}) %collective-permute-start.18) | collective-permute-done | bytes 524320 | tf_op jit(solution)/shard_map/ppermute | solution.py:58
  80.5 2.7 %collective-permute-start.11 = (bf16[2,64,1024]{2,1,0:T(8,128)(2,1)}, bf16[2,64,1024]{2,1,0:T(8,128)(2,1)S(1)}, u32[]{:S(2)}, u32[]{:S(2)}) collective-permute-start(bf16[2,64,1024]{2,1,0:T(8,128)(2,1)} %get-tuple-element.124), channel_id=1, source_target_pairs={{0,8},{4,12},{8,0},{12,4},{16,24},{20,28},{24,16},{28,20},{32,40},... | collective-permute-start | bytes 786440 | tf_op jit(solution)/shard_map/ppermute | solution.py:49
  83.2 3.6 %collective-permute-start.13 = (bf16[2,64,1024]{2,1,0:T(8,128)(2,1)}, bf16[2,64,1024]{2,1,0:T(8,128)(2,1)}, u32[]{:S(2)}, u32[]{:S(2)}) collective-permute-start(bf16[2,64,1024]{2,1,0:T(8,128)(2,1)} %get-tuple-element.128), channel_id=1, source_target_pairs={{0,128},{4,132},{8,136},{12,140},{16,144},{20,148},{24,152},{28,15... | collective-permute-start | bytes 786440 | tf_op jit(solution)/shard_map/ppermute | solution.py:49
  86.8 5.0 %project.1.rest_7_ = bf16[128,1024]{1,0:T(8,128)(2,1)} custom-call(s32[14]{0:T(128)S(1)} %concatenate.3.where.refs_0_, bf16[256,2048]{1,0:T(8,128)(2,1)} %refs_0_.3, bf16[256,2048]{1,0:T(8,128)(2,1)} %copy-done.3, bf16[256,2048]{1,0:T(8,128)(2,1)} %collective-permute-done.9.refs_2_, bf16[256,2048]{1,0:T(8,128)(2,1)} %collective-permute-done.10.refs_3_, ...), custom_call_target="tpu_custom_call" | custom-call | tf_op jit(solution)/shard_map/project/pallas_call | solution.py:357
  91.9 2.6 %collective-permute-done.11.rest_0_ = bf16[2,64,1024]{2,1,0:T(8,128)(2,1)S(1)} collective-permute-done((bf16[2,64,1024]{2,1,0:T(8,128)(2,1)}, bf16[2,64,1024]{2,1,0:T(8,128)(2,1)S(1)}, u32[]{:S(2)}, u32[]{:S(2)}) %collective-permute-start.11) | collective-permute-done | bytes 262176 | tf_op jit(solution)/shard_map/ppermute | solution.py:49
  94.4 4.0 %collective-permute-done.12.rest_1_ = bf16[2,64,1024]{2,1,0:T(8,128)(2,1)S(1)} collective-permute-done((bf16[2,64,1024]{2,1,0:T(8,128)(2,1)}, bf16[2,64,1024]{2,1,0:T(8,128)(2,1)S(1)}, u32[]{:S(2)}, u32[]{:S(2)}) %collective-permute-start.12) | collective-permute-done | bytes 262176 | tf_op jit(solution)/shard_map/ppermute | solution.py:49
  98.4 0.7 copy-done.9
  99.1 6.2 %forward.1 = (bf16[128,1024]{1,0:T(8,128)(2,1)}, f32[8,8,128]{2,1,0:T(8,128)}, bf16[128,256]{1,0:T(8,128)(2,1)S(1)}, bf16[128,256]{1,0:T(8,128)(2,1)S(1)}, bf16[...) custom-call(s32[14]{0:T(128)S(1)} %concatenate.3.where.refs_0_, bf16[128,1024]{1,0:T(8,128)(2,1)} %bitcast.44, ...), custom_call_target="tpu_custom_call" | custom-call | tf_op jit(solution)/shard_map/forward/pallas_call | solution.py:247
  105.4 0.1 collective-permute-start.14
  105.5 0.2 collective-permute-start.15
  105.7 1.7 collective-permute-start.16
  107.3 7.1 %backward.1 = (bf16[128,1024]{1,0:T(8,128)(2,1)}, f32[2,128,1024]{2,1,0:T(8,128)}, bf16[2,2,64,1024]{3,2,1,0:T(8,128)(2,1)}, bf16[2,64,1024]{2,1,0:T(8,128)(2,1)...) custom-call(s32[14]{0:T(128)S(1)} %concatenate.3.where.refs_0_, ...), custom_call_target="tpu_custom_call" | custom-call | tf_op jit(solution)/shard_map/backward/pallas_call | solution.py:311
  114.5 4.4 %weight.1 = bf16[8,192,512]{2,1,0:T(8,128)(2,1)} custom-call(bf16[128,256]{1,0:T(8,128)(2,1)S(1)} %get-tuple-element.136.refs_0_, bf16[128,256]{1,0:T(8,128)(2,1)S(1)} %collective-permute-done.14.refs_1_, bf16[128,256]{1,0:T(8,128)(2,1)S(1)} %collective-permute-done.15.refs_2_, bf16[128,256]{1,0:T(8,128)(2,1)S(1)} %collective-permute-done.16.refs_3_, ...), custom_call_target="tpu_custom_call" | custom-call | tf_op jit(solution)/shard_map/weight/pallas_call | solution.py:397
  118.9 6.1 %all-to-all-start.2 = ((bf16[8,192,512]{2,1,0:T(8,128)(2,1)}), bf16[8,192,512]{2,1,0:T(8,128)(2,1)S(1)}, u32[]{:S(2)}, u32[]{:S(2)}) async-start(bf16[8,192,512]{2,1,0:T(8,128)(2,1)} %weight.1), calls=%async_computation.2 | async-start | bytes 3145728 | tf_op jit(solution)/shard_map/all_to_all | solution.py:45
  125.0 1.4 collective-permute-start.20
  126.3 0.2 collective-permute-start.21
  126.5 4.3 %layer.1 = bf16[128,2048]{1,0:T(8,128)(2,1)} custom-call(s32[14]{0:T(128)S(1)} %concatenate.3.where.refs_0_, bf16[256,2048]{1,0:T(8,128)(2,1)} %refs_0_.3, bf16[256,2048]{1,0:T(8,128)(2,1)} %copy-done.3, bf16[256,2048]{1,0:T(8,128)(2,1)} %collective-permute-done.9.refs_2_, bf16[256,2048]{1,0:T(8,128)(2,1)} %collective-permute-done.10.refs_3_, ...), custom_call_target="tpu_custom_call" | custom-call | tf_op jit(solution)/shard_map/layer/pallas_call | solution.py:357
  130.8 11.0 %collective-permute-done.20.rest_2_ = bf16[2,64,1024]{2,1,0:T(8,128)(2,1)S(1)} collective-permute-done((bf16[2,64,1024]{2,1,0:T(8,128)(2,1)}, bf16[2,64,1024]{2,1,0:T(8,128)(2,1)S(1)}, u32[]{:S(2)}, u32[]{:S(2)}) %collective-permute-start.20) | collective-permute-done | bytes 262176 | tf_op jit(solution)/shard_map/ppermute | solution.py:49
  141.8 7.1 %collective-permute-done.21.rest_3_ = bf16[2,64,1024]{2,1,0:T(8,128)(2,1)S(1)} collective-permute-done((bf16[2,64,1024]{2,1,0:T(8,128)(2,1)S(1)}, bf16[2,64,1024]{2,1,0:T(8,128)(2,1)S(1)}, u32[]{:S(2)}, u32[]{:S(2)}) %collective-permute-start.21) | collective-permute-done | bytes 262176 | tf_op jit(solution)/shard_map/ppermute | solution.py:49
  149.0 3.4 %collective-permute-start.25 = (bf16[2,2,64,1024]{3,2,1,0:T(8,128)(2,1)S(1)}, bf16[2,2,64,1024]{3,2,1,0:T(8,128)(2,1)S(1)}, u32[]{:S(2)}, u32[]{:S(2)}) collective-permute-start(bf16[2,2,64,1024]{3,2,1,0:T(8,128)(2,1)S(1)} %copy-done.17), channel_id=1, source_target_pairs={{0,4},{4,0},{8,12},{12,8},{16,20},{20,16},{24,28},{28,24},{32,36},... | collective-permute-start | bytes 1572872 | tf_op jit(solution)/shard_map/ppermute | solution.py:49
  152.4 0.7 first.1
  153.1 0.1 collective-permute-start.22
  153.2 0.6 collective-permute-start.26
  153.8 5.8 %collective-permute-done.22.refs_3_ = bf16[128,512]{1,0:T(8,128)(2,1)S(1)} collective-permute-done((bf16[128,512]{1,0:T(8,128)(2,1)S(1)}, bf16[128,512]{1,0:T(8,128)(2,1)S(1)}, u32[]{:S(2)}, u32[]{:S(2)}) %collective-permute-start.22) | collective-permute-done | bytes 131104 | tf_op jit(solution)/shard_map/ppermute | solution.py:49
  159.6 0.6 fold.2
  160.2 0.3 collective-permute-start.23
  160.5 6.2 %collective-permute-done.23.refs_3_ = bf16[96,512]{1,0:T(8,128)(2,1)S(1)} collective-permute-done((bf16[96,512]{1,0:T(8,128)(2,1)S(1)}, bf16[96,512]{1,0:T(8,128)(2,1)S(1)}, u32[]{:S(2)}, u32[]{:S(2)}) %collective-permute-start.23) | collective-permute-done | bytes 98336 | tf_op jit(solution)/shard_map/ppermute | solution.py:49
  166.8 0.6 fold.3
  167.4 1.5 collective-permute-start.24
  168.8 7.0 %collective-permute-done.24.came = bf16[80,512]{1,0:T(8,128)(2,1)S(1)} collective-permute-done((bf16[80,512]{1,0:T(8,128)(2,1)S(1)}, bf16[80,512]{1,0:T(8,128)(2,1)S(1)}, u32[]{:S(2)}, u32[]{:S(2)}) %collective-permute-start.24) | collective-permute-done | bytes 81952 | tf_op jit(solution)/shard_map/ppermute | solution.py:49
  175.8 1.4 last.1
  177.2 5.5 %all-to-all-start.3 = ((bf16[8,64,512]{2,1,0:T(8,128)(2,1)}), bf16[8,64,512]{2,1,0:T(8,128)(2,1)S(1)}, u32[]{:S(2)}, u32[]{:S(2)}) async-start(bf16[8,64,512]{2,1,0:T(8,128)(2,1)} %get-tuple-element.187), calls=%async_computation.3 | async-start | bytes 1048576 | tf_op jit(solution)/shard_map/all_to_all | solution.py:45
  182.7 2.0 %collective-permute-start.27 = (bf16[2,64,1024]{2,1,0:T(8,128)(2,1)}, bf16[2,64,1024]{2,1,0:T(8,128)(2,1)S(1)}, u32[]{:S(2)}, u32[]{:S(2)}) collective-permute-start(bf16[2,64,1024]{2,1,0:T(8,128)(2,1)} %get-tuple-element.179), channel_id=1, source_target_pairs={{0,8},{4,12},{8,0},{12,4},{16,24},{20,28},{24,16},{28,20},{32,40},... | collective-permute-start | bytes 786440 | tf_op jit(solution)/shard_map/ppermute | solution.py:49
  184.7 3.4 %collective-permute-start.28 = (bf16[2,64,1024]{2,1,0:T(8,128)(2,1)}, bf16[2,64,1024]{2,1,0:T(8,128)(2,1)S(1)}, u32[]{:S(2)}, u32[]{:S(2)}) collective-permute-start(bf16[2,64,1024]{2,1,0:T(8,128)(2,1)} %get-tuple-element.180), channel_id=1, source_target_pairs={{0,16},{4,20},{8,24},{12,28},{16,0},{20,4},{24,8},{28,12},{32,48},... | collective-permute-start | bytes 786440 | tf_op jit(solution)/shard_map/ppermute | solution.py:49
  188.1 2.1 %collective-permute-start.29 = (bf16[2,64,1024]{2,1,0:T(8,128)(2,1)S(1)}, bf16[2,64,1024]{2,1,0:T(8,128)(2,1)S(1)}, u32[]{:S(2)}, u32[]{:S(2)}) collective-permute-start(bf16[2,64,1024]{2,1,0:T(8,128)(2,1)S(1)} %copy-done.18), channel_id=1, source_target_pairs={{0,128},{4,132},{8,136},{12,140},{16,144},{20,148},{24,152},{28,15... | collective-permute-start | bytes 786440 | tf_op jit(solution)/shard_map/ppermute | solution.py:49
  190.2 5.3 %collective-permute-done.28.rest_1_ = bf16[2,64,1024]{2,1,0:T(8,128)(2,1)S(1)} collective-permute-done((bf16[2,64,1024]{2,1,0:T(8,128)(2,1)}, bf16[2,64,1024]{2,1,0:T(8,128)(2,1)S(1)}, u32[]{:S(2)}, u32[]{:S(2)}) %collective-permute-start.28) | collective-permute-done | bytes 262176 | tf_op jit(solution)/shard_map/ppermute | solution.py:49
  195.5 0.5 collective-permute-done.29.rest_4_
  196.0 0.1 copy-done.15
  196.2 0.5 copy-done.16
  196.7 2.9 %finish.1 = (bf16[128,1024]{1,0:T(8,128)(2,1)}, bf16[128,1024]{1,0:T(8,128)(2,1)}) custom-call(s32[14]{0:T(128)S(1)} %concatenate.3.where.refs_0_, f32[2,128,1024]{2,1,0:T(8,128)} %get-tuple-element.161.own, bf16[2,2,64,1024]{3,2,1,0:T(8,128)(2,1)} %copy-done.10, bf16[2,64,1024]{2,1,0:T(8,128)(2,1)} %copy-done.13, bf16[2,64,1024]{2,1,0:T(8,128)(2,1)} %copy-done.14, ...), custom_call_target="tpu_custom_call" | custom-call | tf_op jit(solution)/shard_map/finish/pallas_call | solution.py:518
  (63 shorter events, 0.2 us)
Async XLA Ops:
  5.5 60.1 %copy-start.1 = (bf16[1,128,2048]{2,1,0:T(8,128)(2,1)S(1)}, bf16[1,128,2048]{2,1,0:T(8,128)(2,1)}, u32[]{:S(2)}) copy-start(bf16[1,128,2048]{2,1,0:T(8,128)(2,1)} %param.11) | copy-start | bytes 1572868
  5.5 33.8 %collective-permute-start = (bf16[256,2048]{1,0:T(8,128)(2,1)}, bf16[256,2048]{1,0:T(8,128)(2,1)S(1)}, u32[]{:S(2)}, u32[]{:S(2)}) collective-permute-start(bf16[256,2048]{1,0:T(8,128)(2,1)} %refs_0_.3), channel_id=1, source_target_pairs={{0,1},{1,0},{2,3},{3,2},{4,5},{5,4},{6,7},{7,6},{8,9},{9,8},{10,11... | collective-permute-start | bytes 3145736 | tf_op jit(solution)/shard_map/ppermute | solution.py:58
  5.5 56.7 %collective-permute-start.9 = (bf16[256,2048]{1,0:T(8,128)(2,1)}, bf16[256,2048]{1,0:T(8,128)(2,1)}, u32[]{:S(2)}, u32[]{:S(2)}) collective-permute-start(bf16[256,2048]{1,0:T(8,128)(2,1)} %refs_0_.3), channel_id=1, source_target_pairs={{0,2},{1,3},{2,0},{3,1},{4,6},{5,7},{6,4},{7,5},{8,10},{9,11},{10,... | collective-permute-start | bytes 3145736 | tf_op jit(solution)/shard_map/ppermute | solution.py:58
  7.0 32.2 %all-to-all-start = ((bf16[8,64,512]{2,1,0:T(8,128)(2,1)}), bf16[8,64,512]{2,1,0:T(8,128)(2,1)S(1)}, u32[]{:S(2)}, u32[]{:S(2)}) async-start(bf16[8,64,512]{2,1,0:T(8,128)(2,1)} %get-tuple-element.98), calls=%async_computation | async-start | bytes 1048576 | tf_op jit(solution)/shard_map/all_to_all | solution.py:45
  14.1 14.6 %collective-permute-start.1 = (bf16[2,64,1024]{2,1,0:T(8,128)(2,1)}, bf16[2,64,1024]{2,1,0:T(8,128)(2,1)S(1)}, u32[]{:S(2)}, u32[]{:S(2)}) collective-permute-start(bf16[2,64,1024]{2,1,0:T(8,128)(2,1)} %get-tuple-element.104), channel_id=1, source_target_pairs={{0,32},{4,36},{8,40},{12,44},{16,48},{20,52},{24,56},{28,60},{32,0... | collective-permute-start | bytes 786440 | tf_op jit(solution)/shard_map/ppermute | solution.py:49
  21.3 7.7 %collective-permute-start.2 = (bf16[2,64,1024]{2,1,0:T(8,128)(2,1)}, bf16[2,64,1024]{2,1,0:T(8,128)(2,1)S(1)}, u32[]{:S(2)}, u32[]{:S(2)}) collective-permute-start(bf16[2,64,1024]{2,1,0:T(8,128)(2,1)} %get-tuple-element.105), channel_id=1, source_target_pairs={{0,64},{4,68},{8,72},{12,76},{16,80},{20,84},{24,88},{28,92},{32,9... | collective-permute-start | bytes 786440 | tf_op jit(solution)/shard_map/ppermute | solution.py:49
  28.7 63.1 %copy-start.5 = (bf16[2,64,1024]{2,1,0:T(8,128)(2,1)}, bf16[2,64,1024]{2,1,0:T(8,128)(2,1)S(1)}, u32[]{:S(2)}) copy-start(bf16[2,64,1024]{2,1,0:T(8,128)(2,1)S(1)} %collective-permute-done.1.rest_2_) | copy-start | bytes 786436
  29.1 62.8 %copy-start.6 = (bf16[2,64,1024]{2,1,0:T(8,128)(2,1)}, bf16[2,64,1024]{2,1,0:T(8,128)(2,1)S(1)}, u32[]{:S(2)}) copy-start(bf16[2,64,1024]{2,1,0:T(8,128)(2,1)S(1)} %collective-permute-done.2.rest_3_) | copy-start | bytes 786436
  39.3 47.6 %copy-start.3 = (bf16[256,2048]{1,0:T(8,128)(2,1)}, bf16[256,2048]{1,0:T(8,128)(2,1)S(1)}, u32[]{:S(2)}) copy-start(bf16[256,2048]{1,0:T(8,128)(2,1)S(1)} %collective-permute-done.refs_1_) | copy-start | bytes 3145732
  39.3 26.2 %collective-permute-start.7 = (bf16[2,2,64,1024]{3,2,1,0:T(8,128)(2,1)}, bf16[2,2,64,1024]{3,2,1,0:T(8,128)(2,1)S(1)}, u32[]{:S(2)}, u32[]{:S(2)}) collective-permute-start(bf16[2,2,64,1024]{3,2,1,0:T(8,128)(2,1)} %get-tuple-element.110), channel_id=1, source_target_pairs={{0,4},{4,0},{8,12},{12,8},{16,20},{20,16},{24,28},{28,24},{32,36},... | collective-permute-start | bytes 1572872 | tf_op jit(solution)/shard_map/ppermute | solution.py:49
  40.7 24.8 %collective-permute-start.8 = (bf16[2,64,1024]{2,1,0:T(8,128)(2,1)}, bf16[2,64,1024]{2,1,0:T(8,128)(2,1)S(1)}, u32[]{:S(2)}, u32[]{:S(2)}) collective-permute-start(bf16[2,64,1024]{2,1,0:T(8,128)(2,1)} %get-tuple-element.111), channel_id=1, source_target_pairs={{0,252},{4,8},{8,4},{12,16},{16,12},{20,24},{24,20},{28,32},{32,28... | collective-permute-start | bytes 786440 | tf_op jit(solution)/shard_map/ppermute | solution.py:93
  50.3 5.6 %collective-permute-start.3 = (bf16[64,512]{1,0:T(8,128)(2,1)S(1)}, bf16[64,512]{1,0:T(8,128)(2,1)S(1)}, u32[]{:S(2)}, u32[]{:S(2)}) collective-permute-start(bf16[64,512]{1,0:T(8,128)(2,1)S(1)} %gathered.1.mine), channel_id=1, source_target_pairs={{0,8},{4,12},{8,16},{12,20},{16,24},{20,28},{24,32},{28,36},{32,40... | collective-permute-start | bytes 196616 | tf_op jit(solution)/shard_map/ppermute | solution.py:54
  50.4 6.6 %collective-permute-start.4 = (bf16[64,512]{1,0:T(8,128)(2,1)S(1)}, bf16[64,512]{1,0:T(8,128)(2,1)S(1)}, u32[]{:S(2)}, u32[]{:S(2)}) collective-permute-start(bf16[64,512]{1,0:T(8,128)(2,1)S(1)} %gathered.1.mine), channel_id=1, source_target_pairs={{0,56},{4,60},{8,0},{12,4},{16,8},{20,12},{24,16},{28,20},{32,24},... | collective-permute-start | bytes 196616 | tf_op jit(solution)/shard_map/ppermute | solution.py:54
  57.0 8.4 %collective-permute-start.5 = (bf16[64,512]{1,0:T(8,128)(2,1)S(1)}, bf16[64,512]{1,0:T(8,128)(2,1)S(1)}, u32[]{:S(2)}, u32[]{:S(2)}) collective-permute-start(bf16[64,512]{1,0:T(8,128)(2,1)S(1)} %get-tuple-element.108.mine), channel_id=1, source_target_pairs={{0,24},{4,28},{8,32},{12,36},{16,40},{20,44},{24,48},{28,52},{32,5... | collective-permute-start | bytes 196616 | tf_op jit(solution)/shard_map/ppermute | solution.py:54
  57.1 8.3 %collective-permute-start.6 = (bf16[64,512]{1,0:T(8,128)(2,1)S(1)}, bf16[64,512]{1,0:T(8,128)(2,1)S(1)}, u32[]{:S(2)}, u32[]{:S(2)}) collective-permute-start(bf16[64,512]{1,0:T(8,128)(2,1)S(1)} %get-tuple-element.109), channel_id=1, source_target_pairs={{0,40},{4,44},{8,48},{12,52},{16,56},{20,60},{24,0},{28,4},{32,8},... | collective-permute-start | bytes 196616 | tf_op jit(solution)/shard_map/ppermute | solution.py:54
  65.4 26.4 %copy-start.7 = (bf16[2,64,1024]{2,1,0:T(8,128)(2,1)}, bf16[2,64,1024]{2,1,0:T(8,128)(2,1)S(1)}, u32[]{:S(2)}) copy-start(bf16[2,64,1024]{2,1,0:T(8,128)(2,1)S(1)} %collective-permute-done.8.outer) | copy-start | bytes 786436
  65.5 26.4 %copy-start.4 = (bf16[2,2,64,1024]{3,2,1,0:T(8,128)(2,1)}, bf16[2,2,64,1024]{3,2,1,0:T(8,128)(2,1)S(1)}, u32[]{:S(2)}) copy-start(bf16[2,2,64,1024]{3,2,1,0:T(8,128)(2,1)S(1)} %collective-permute-done.7.pair) | copy-start | bytes 1572868
  65.5 17.8 %collective-permute-start.10 = (bf16[256,2048]{1,0:T(8,128)(2,1)}, bf16[256,2048]{1,0:T(8,128)(2,1)}, u32[]{:S(2)}, u32[]{:S(2)}) collective-permute-start(bf16[256,2048]{1,0:T(8,128)(2,1)} %collective-permute-done.9.refs_2_), channel_id=1, source_target_pairs={{0,1},{1,0},{2,3},{3,2},{4,5},{5,4},{6,7},{7,6},{8,9},{9,8},{10,11... | collective-permute-start | bytes 3145736 | tf_op jit(solution)/shard_map/ppermute | solution.py:58
  65.6 14.9 %collective-permute-start.18 = (bf16[128,2048]{1,0:T(8,128)(2,1)S(1)}, bf16[128,2048]{1,0:T(8,128)(2,1)}, u32[]{:S(2)}, u32[]{:S(2)}) collective-permute-start(bf16[128,2048]{1,0:T(8,128)(2,1)S(1)} %bitcast.34), channel_id=1, source_target_pairs={{0,2},{1,3},{2,0},{3,1},{4,6},{5,7},{6,4},{7,5},{8,10},{9,11},{10,... | collective-permute-start | bytes 1572872 | tf_op jit(solution)/shard_map/ppermute | solution.py:58
  66.7 32.5 %all-to-all-start.1 = ((bf16[8,64,512]{2,1,0:T(8,128)(2,1)}), bf16[8,64,512]{2,1,0:T(8,128)(2,1)S(1)}, u32[]{:S(2)}, u32[]{:S(2)}) async-start(bf16[8,64,512]{2,1,0:T(8,128)(2,1)} %relay.1), calls=%async_computation.1 | async-start | bytes 1048576 | tf_op jit(solution)/shard_map/all_to_all | solution.py:45
  71.8 42.6 %collective-permute-start.17 = (bf16[128,2048]{1,0:T(8,128)(2,1)S(1)}, bf16[128,2048]{1,0:T(8,128)(2,1)}, u32[]{:S(2)}, u32[]{:S(2)}) collective-permute-start(bf16[128,2048]{1,0:T(8,128)(2,1)S(1)} %bitcast.35), channel_id=1, source_target_pairs={{0,1},{1,0},{2,3},{3,2},{4,5},{5,4},{6,7},{7,6},{8,9},{9,8},{10,11... | collective-permute-start | bytes 1572872 | tf_op jit(solution)/shard_map/ppermute | solution.py:58
  80.5 34.0 %collective-permute-start.19 = (bf16[128,2048]{1,0:T(8,128)(2,1)}, bf16[128,2048]{1,0:T(8,128)(2,1)}, u32[]{:S(2)}, u32[]{:S(2)}) collective-permute-start(bf16[128,2048]{1,0:T(8,128)(2,1)} %collective-permute-done.18.refs_6_), channel_id=1, source_target_pairs={{0,1},{1,0},{2,3},{3,2},{4,5},{5,4},{6,7},{7,6},{8,9},{9,8},{10,11... | collective-permute-start | bytes 1572872 | tf_op jit(solution)/shard_map/ppermute | solution.py:58
  80.5 13.9 %collective-permute-start.11 = (bf16[2,64,1024]{2,1,0:T(8,128)(2,1)}, bf16[2,64,1024]{2,1,0:T(8,128)(2,1)S(1)}, u32[]{:S(2)}, u32[]{:S(2)}) collective-permute-start(bf16[2,64,1024]{2,1,0:T(8,128)(2,1)} %get-tuple-element.124), channel_id=1, source_target_pairs={{0,8},{4,12},{8,0},{12,4},{16,24},{20,28},{24,16},{28,20},{32,40},... | collective-permute-start | bytes 786440 | tf_op jit(solution)/shard_map/ppermute | solution.py:49
  83.2 15.2 %collective-permute-start.12 = (bf16[2,64,1024]{2,1,0:T(8,128)(2,1)}, bf16[2,64,1024]{2,1,0:T(8,128)(2,1)S(1)}, u32[]{:S(2)}, u32[]{:S(2)}) collective-permute-start(bf16[2,64,1024]{2,1,0:T(8,128)(2,1)} %get-tuple-element.125), channel_id=1, source_target_pairs={{0,16},{4,20},{8,24},{12,28},{16,0},{20,4},{24,8},{28,12},{32,48},... | collective-permute-start | bytes 786440 | tf_op jit(solution)/shard_map/ppermute | solution.py:49
  83.2 15.9 %collective-permute-start.13 = (bf16[2,64,1024]{2,1,0:T(8,128)(2,1)}, bf16[2,64,1024]{2,1,0:T(8,128)(2,1)}, u32[]{:S(2)}, u32[]{:S(2)}) collective-permute-start(bf16[2,64,1024]{2,1,0:T(8,128)(2,1)} %get-tuple-element.128), channel_id=1, source_target_pairs={{0,128},{4,132},{8,136},{12,140},{16,144},{20,148},{24,152},{28,15... | collective-permute-start | bytes 786440 | tf_op jit(solution)/shard_map/ppermute | solution.py:49
  94.4 4.0 %copy-start.8 = (bf16[2,64,1024]{2,1,0:T(8,128)(2,1)}, bf16[2,64,1024]{2,1,0:T(8,128)(2,1)S(1)}, u32[]{:S(2)}) copy-start(bf16[2,64,1024]{2,1,0:T(8,128)(2,1)S(1)} %collective-permute-done.11.rest_0_) | copy-start | bytes 786436
  98.4 0.7 copy-start.9
  99.1 6.2 %copy-start = (bf16[8,64,512]{2,1,0:T(8,128)(2,1)}, bf16[8,64,512]{2,1,0:T(8,128)(2,1)S(1)}, u32[]{:S(2)}) copy-start(bf16[8,64,512]{2,1,0:T(8,128)(2,1)S(1)} %all-to-all-done.1) | copy-start | bytes 1572868
  105.4 9.1 %collective-permute-start.14 = (bf16[128,256]{1,0:T(8,128)(2,1)S(1)}, bf16[128,256]{1,0:T(8,128)(2,1)S(1)}, u32[]{:S(2)}, u32[]{:S(2)}) collective-permute-start(bf16[128,256]{1,0:T(8,128)(2,1)S(1)} %get-tuple-element.137), channel_id=1, source_target_pairs={{0,1},{1,0},{2,3},{3,2},{4,5},{5,4},{6,7},{7,6},{8,9},{9,8},{10,11... | collective-permute-start | bytes 196616 | tf_op jit(solution)/shard_map/ppermute | solution.py:58
  105.5 9.0 %collective-permute-start.15 = (bf16[128,256]{1,0:T(8,128)(2,1)S(1)}, bf16[128,256]{1,0:T(8,128)(2,1)S(1)}, u32[]{:S(2)}, u32[]{:S(2)}) collective-permute-start(bf16[128,256]{1,0:T(8,128)(2,1)S(1)} %get-tuple-element.138), channel_id=1, source_target_pairs={{0,2},{1,3},{2,0},{3,1},{4,6},{5,7},{6,4},{7,5},{8,10},{9,11},{10,... | collective-permute-start | bytes 196616 | tf_op jit(solution)/shard_map/ppermute | solution.py:58
  105.7 8.9 %collective-permute-start.16 = (bf16[128,256]{1,0:T(8,128)(2,1)S(1)}, bf16[128,256]{1,0:T(8,128)(2,1)S(1)}, u32[]{:S(2)}, u32[]{:S(2)}) collective-permute-start(bf16[128,256]{1,0:T(8,128)(2,1)S(1)} %get-tuple-element.139), channel_id=1, source_target_pairs={{0,3},{1,2},{2,1},{3,0},{4,7},{5,6},{6,5},{7,4},{8,11},{9,10},{10,... | collective-permute-start | bytes 196616 | tf_op jit(solution)/shard_map/ppermute | solution.py:58
  118.9 7.5 %copy-start.19 = (bf16[2,64,1024]{2,1,0:T(8,128)(2,1)S(1)}, bf16[2,64,1024]{2,1,0:T(8,128)(2,1)}, u32[]{:S(2)}) copy-start(bf16[2,64,1024]{2,1,0:T(8,128)(2,1)} %get-tuple-element.157) | copy-start | bytes 786436
  118.9 7.6 %copy-start.2 = (bf16[128,1024]{1,0:T(8,128)(2,1)S(1)}, bf16[128,1024]{1,0:T(8,128)(2,1)}, u32[]{:S(2)}) copy-start(bf16[128,1024]{1,0:T(8,128)(2,1)} %get-tuple-element.151.refs_4_) | copy-start | bytes 786436
  118.9 30.1 %all-to-all-start.2 = ((bf16[8,192,512]{2,1,0:T(8,128)(2,1)}), bf16[8,192,512]{2,1,0:T(8,128)(2,1)S(1)}, u32[]{:S(2)}, u32[]{:S(2)}) async-start(bf16[8,192,512]{2,1,0:T(8,128)(2,1)} %weight.1), calls=%async_computation.2 | async-start | bytes 3145728 | tf_op jit(solution)/shard_map/all_to_all | solution.py:45
  125.0 16.9 %collective-permute-start.20 = (bf16[2,64,1024]{2,1,0:T(8,128)(2,1)}, bf16[2,64,1024]{2,1,0:T(8,128)(2,1)S(1)}, u32[]{:S(2)}, u32[]{:S(2)}) collective-permute-start(bf16[2,64,1024]{2,1,0:T(8,128)(2,1)} %get-tuple-element.156), channel_id=1, source_target_pairs={{0,32},{4,36},{8,40},{12,44},{16,48},{20,52},{24,56},{28,60},{32,0... | collective-permute-start | bytes 786440 | tf_op jit(solution)/shard_map/ppermute | solution.py:49
  126.3 22.6 %collective-permute-start.21 = (bf16[2,64,1024]{2,1,0:T(8,128)(2,1)S(1)}, bf16[2,64,1024]{2,1,0:T(8,128)(2,1)S(1)}, u32[]{:S(2)}, u32[]{:S(2)}) collective-permute-start(bf16[2,64,1024]{2,1,0:T(8,128)(2,1)S(1)} %copy-done.19), channel_id=1, source_target_pairs={{0,64},{4,68},{8,72},{12,76},{16,80},{20,84},{24,88},{28,92},{32,9... | collective-permute-start | bytes 786440 | tf_op jit(solution)/shard_map/ppermute | solution.py:49
  126.5 22.4 %copy-start.17 = (bf16[2,2,64,1024]{3,2,1,0:T(8,128)(2,1)S(1)}, bf16[2,2,64,1024]{3,2,1,0:T(8,128)(2,1)}, u32[]{:S(2)}) copy-start(bf16[2,2,64,1024]{3,2,1,0:T(8,128)(2,1)} %get-tuple-element.170) | copy-start | bytes 1572868
  130.8 57.3 %copy-start.18 = (bf16[2,64,1024]{2,1,0:T(8,128)(2,1)S(1)}, bf16[2,64,1024]{2,1,0:T(8,128)(2,1)}, u32[]{:S(2)}) copy-start(bf16[2,64,1024]{2,1,0:T(8,128)(2,1)} %get-tuple-element.183) | copy-start | bytes 786436
  141.8 54.2 %copy-start.11 = (bf16[2,64,1024]{2,1,0:T(8,128)(2,1)}, bf16[2,64,1024]{2,1,0:T(8,128)(2,1)S(1)}, u32[]{:S(2)}) copy-start(bf16[2,64,1024]{2,1,0:T(8,128)(2,1)S(1)} %collective-permute-done.20.rest_2_) | copy-start | bytes 786436
  149.0 47.0 %copy-start.12 = (bf16[2,64,1024]{2,1,0:T(8,128)(2,1)}, bf16[2,64,1024]{2,1,0:T(8,128)(2,1)S(1)}, u32[]{:S(2)}) copy-start(bf16[2,64,1024]{2,1,0:T(8,128)(2,1)S(1)} %collective-permute-done.21.rest_3_) | copy-start | bytes 786436
  149.0 26.8 %collective-permute-start.25 = (bf16[2,2,64,1024]{3,2,1,0:T(8,128)(2,1)S(1)}, bf16[2,2,64,1024]{3,2,1,0:T(8,128)(2,1)S(1)}, u32[]{:S(2)}, u32[]{:S(2)}) collective-permute-start(bf16[2,2,64,1024]{3,2,1,0:T(8,128)(2,1)S(1)} %copy-done.17), channel_id=1, source_target_pairs={{0,4},{4,0},{8,12},{12,8},{16,20},{20,16},{24,28},{28,24},{32,36},... | collective-permute-start | bytes 1572872 | tf_op jit(solution)/shard_map/ppermute | solution.py:49
  153.1 6.5 %collective-permute-start.22 = (bf16[128,512]{1,0:T(8,128)(2,1)S(1)}, bf16[128,512]{1,0:T(8,128)(2,1)S(1)}, u32[]{:S(2)}, u32[]{:S(2)}) collective-permute-start(bf16[128,512]{1,0:T(8,128)(2,1)S(1)} %get-tuple-element.165), channel_id=1, source_target_pairs={{0,8},{4,12},{8,0},{12,4},{16,24},{20,28},{24,16},{28,20},{32,40},... | collective-permute-start | bytes 393224 | tf_op jit(solution)/shard_map/ppermute | solution.py:49
  153.2 15.6 %collective-permute-start.26 = (bf16[2,64,1024]{2,1,0:T(8,128)(2,1)}, bf16[2,64,1024]{2,1,0:T(8,128)(2,1)S(1)}, u32[]{:S(2)}, u32[]{:S(2)}) collective-permute-start(bf16[2,64,1024]{2,1,0:T(8,128)(2,1)} %get-tuple-element.171), channel_id=1, source_target_pairs={{0,252},{4,8},{8,4},{12,16},{16,12},{20,24},{24,20},{28,32},{32,28... | collective-permute-start | bytes 786440 | tf_op jit(solution)/shard_map/ppermute | solution.py:93
  160.2 6.5 %collective-permute-start.23 = (bf16[96,512]{1,0:T(8,128)(2,1)S(1)}, bf16[96,512]{1,0:T(8,128)(2,1)S(1)}, u32[]{:S(2)}, u32[]{:S(2)}) collective-permute-start(bf16[96,512]{1,0:T(8,128)(2,1)S(1)} %get-tuple-element.168), channel_id=1, source_target_pairs={{0,16},{4,20},{8,24},{12,28},{16,0},{20,4},{24,8},{28,12},{32,48},... | collective-permute-start | bytes 294920 | tf_op jit(solution)/shard_map/ppermute | solution.py:49
  167.4 8.4 %collective-permute-start.24 = (bf16[80,512]{1,0:T(8,128)(2,1)S(1)}, bf16[80,512]{1,0:T(8,128)(2,1)S(1)}, u32[]{:S(2)}, u32[]{:S(2)}) collective-permute-start(bf16[80,512]{1,0:T(8,128)(2,1)S(1)} %get-tuple-element.169), channel_id=1, source_target_pairs={{0,32},{4,36},{8,40},{12,44},{16,48},{20,52},{24,56},{28,60},{32,0... | collective-permute-start | bytes 245768 | tf_op jit(solution)/shard_map/ppermute | solution.py:49
  168.8 27.2 %copy-start.13 = (bf16[2,64,1024]{2,1,0:T(8,128)(2,1)}, bf16[2,64,1024]{2,1,0:T(8,128)(2,1)S(1)}, u32[]{:S(2)}) copy-start(bf16[2,64,1024]{2,1,0:T(8,128)(2,1)S(1)} %collective-permute-done.26.outer) | copy-start | bytes 786436
  175.8 20.2 %copy-start.10 = (bf16[2,2,64,1024]{3,2,1,0:T(8,128)(2,1)}, bf16[2,2,64,1024]{3,2,1,0:T(8,128)(2,1)S(1)}, u32[]{:S(2)}) copy-start(bf16[2,2,64,1024]{3,2,1,0:T(8,128)(2,1)S(1)} %collective-permute-done.25.pair) | copy-start | bytes 1572868
  177.2 18.8 %all-to-all-start.3 = ((bf16[8,64,512]{2,1,0:T(8,128)(2,1)}), bf16[8,64,512]{2,1,0:T(8,128)(2,1)S(1)}, u32[]{:S(2)}, u32[]{:S(2)}) async-start(bf16[8,64,512]{2,1,0:T(8,128)(2,1)} %get-tuple-element.187), calls=%async_computation.3 | async-start | bytes 1048576 | tf_op jit(solution)/shard_map/all_to_all | solution.py:45
  182.7 7.5 %collective-permute-start.27 = (bf16[2,64,1024]{2,1,0:T(8,128)(2,1)}, bf16[2,64,1024]{2,1,0:T(8,128)(2,1)S(1)}, u32[]{:S(2)}, u32[]{:S(2)}) collective-permute-start(bf16[2,64,1024]{2,1,0:T(8,128)(2,1)} %get-tuple-element.179), channel_id=1, source_target_pairs={{0,8},{4,12},{8,0},{12,4},{16,24},{20,28},{24,16},{28,20},{32,40},... | collective-permute-start | bytes 786440 | tf_op jit(solution)/shard_map/ppermute | solution.py:49
  184.7 10.8 %collective-permute-start.28 = (bf16[2,64,1024]{2,1,0:T(8,128)(2,1)}, bf16[2,64,1024]{2,1,0:T(8,128)(2,1)S(1)}, u32[]{:S(2)}, u32[]{:S(2)}) collective-permute-start(bf16[2,64,1024]{2,1,0:T(8,128)(2,1)} %get-tuple-element.180), channel_id=1, source_target_pairs={{0,16},{4,20},{8,24},{12,28},{16,0},{20,4},{24,8},{28,12},{32,48},... | collective-permute-start | bytes 786440 | tf_op jit(solution)/shard_map/ppermute | solution.py:49
  188.1 7.9 %collective-permute-start.29 = (bf16[2,64,1024]{2,1,0:T(8,128)(2,1)S(1)}, bf16[2,64,1024]{2,1,0:T(8,128)(2,1)S(1)}, u32[]{:S(2)}, u32[]{:S(2)}) collective-permute-start(bf16[2,64,1024]{2,1,0:T(8,128)(2,1)S(1)} %copy-done.18), channel_id=1, source_target_pairs={{0,128},{4,132},{8,136},{12,140},{16,144},{20,148},{24,152},{28,15... | collective-permute-start | bytes 786440 | tf_op jit(solution)/shard_map/ppermute | solution.py:49
  190.2 5.8 %copy-start.14 = (bf16[2,64,1024]{2,1,0:T(8,128)(2,1)}, bf16[2,64,1024]{2,1,0:T(8,128)(2,1)S(1)}, u32[]{:S(2)}) copy-start(bf16[2,64,1024]{2,1,0:T(8,128)(2,1)S(1)} %collective-permute-done.27.rest_0_) | copy-start | bytes 786436
  195.5 0.7 copy-start.15
  196.0 0.7 copy-start.16

commit v7 on v6

--- a/solution.py
+++ b/solution.py
@@ -31,7 +31,7 @@
 
 YX_GROUPS = [[stretch_id(y, z, x) for y in range(4) for x in range(2)] for z in range(8)]
 CHUNKS = 8
-PARTS = 4
+PARTS = 6
 HALF = WIDTH // 2
 Z_BITS = (1, 2, 3)
 FIRST, THIRD = (3, 4), (2, 1, 5)
@@ -56,6 +56,11 @@
 
 def across(value, flip):
     return lax.ppermute(value, "rep", [(r, r ^ flip) for r in range(4)])
+
+
+def beside(value):
+    pairs = [(s * 4 + r, (s ^ 1) * 4 + (r ^ 2)) for s in range(64) for r in range(4)]
+    return lax.ppermute(value, ("seq", "rep"), pairs)
 
 
 def far(shape, dtype=BF):
@@ -274,19 +279,23 @@
 def backward_kernel(where, q, k, v, pair, outer, *rest):
     rand, rest = rest[: BITS - 1], rest[BITS - 1 :]
     low = inner_block(where) == 0
-    glob, stats, d_attn_ref, dq, down, dpair, douter = rest[:7]
-    drand, rest = rest[7 : 6 + BITS], rest[6 + BITS :]
-    dglob, ks, vs, bias = rest
-
-    @pl.when(pl.program_id(0) == 0)
+    glob, stats, *pieces, dq, down, dpair, douter = rest[:10]
+    drand, rest = rest[10 : 9 + BITS], rest[9 + BITS :]
+    dglob, ks, vs, bias, d_attns = rest
+
+    step = pl.program_id(0)
+
+    @pl.when(step == 0)
     def _():
         fill_bias(where, bias)
+        for i in range(4):
+            d_attns[i ^ where[13]] = pieces[i][...]
 
     for i in range(STEP):
         cols = slice(i * HEAD_DIM, (i + 1) * HEAD_DIM)
         gather_heads(where, ks.at[i], 0, cols, k, pair, outer, rand, glob)
         gather_heads(where, vs.at[i], 1, cols, v, pair, outer, rand, glob)
-        d_attn = d_attn_ref[:, cols]
+        d_attn = d_attns[step * (STEP // 2) + i // 2, :, i % 2 * HEAD_DIM : (i % 2 + 1) * HEAD_DIM]
         scores = mm(ks[i], q[:, cols], ROWS) * SCALE + bias[...]
         probs = jnp.exp(scores - stats[i, 0:1, :]) * stats[i, 1:2, :]
         probs_b = probs.astype(BF)
@@ -305,7 +314,7 @@
                 drand[b - 1][c, :, cols] = grad[384 + 64 * b : 448 + 64 * b].astype(BF)
 
 
-def backward(where, q, k, v, pair, outer, rand, glob, stats, d_attn):
+def backward(where, q, k, v, pair, outer, rand, glob, stats, pieces):
     flat, block, both, half, two = head_specs()
     out = far((2, BLK, WIDTH))
     outs = pl.pallas_call(
@@ -313,7 +322,8 @@
         grid=(HEADS // STEP,),
         in_specs=[smem(), flat, flat, flat, two]
         + [block] * BITS
-        + [half, pl.BlockSpec((STEP, 8, TOK), lambda h: (h, 0, 0)), flat],
+        + [half, pl.BlockSpec((STEP, 8, TOK), lambda h: (h, 0, 0))]
+        + [pl.BlockSpec((TOK, 256), lambda h: (0, 0))] * 4,
         out_specs=[flat, both, two] + [block] * BITS + [half],
         out_shape=[far((TOK, WIDTH)), far((2, TOK, WIDTH), F32), far((2, 2, BLK, WIDTH))]
         + [out] * BITS
@@ -322,17 +332,19 @@
             pltpu.VMEM((STEP, KEYS, HEAD_DIM), BF),
             pltpu.VMEM((STEP, KEYS, HEAD_DIM), BF),
             pltpu.VMEM((KEYS, TOK), F32),
+            pltpu.VMEM((4, TOK, 256), BF),
         ],
         compiler_params=params(dimension_semantics=("arbitrary",)),
         name="backward",
-    )(where, *from_hbm(q, k, v, pair, outer, *rand, glob, stats, d_attn))
+    )(where, *from_hbm(q, k, v, pair, outer, *rand, glob, stats), *pieces)
     return outs[:4], outs[4 : 3 + BITS], outs[3 + BITS]
 
 
 def place_weights(where, parts, w, sems):
     copies = []
-    for i in range(PARTS):
-        rows = pl.ds(pl.multiple_of((i ^ where[13]) * 256, 256), 256)
+    for i, (rep, half) in enumerate([(0, 0), (1, 0), (2, 0), (2, 1), (3, 0), (3, 1)]):
+        head = (rep ^ where[13]) * 2 + half
+        rows = pl.ds(pl.multiple_of(head * HEAD_DIM, HEAD_DIM), parts[i].shape[0])
         copies.append(pltpu.make_async_copy(parts[i], w.at[rows, :], sems.at[i]))
     for copy in copies:
         copy.start()
@@ -340,10 +352,18 @@
         copy.wait()
 
 
-def project_kernel(where, *refs):
-    parts, (d_out, out, w, sems) = refs[:PARTS], refs[PARTS:]
-    place_weights(where, parts, w, sems)
-    out[...] = mm(d_out[...], w[...], ROWS).astype(BF)
+def project_kernel(w, *refs):
+    for i in range(4):
+        refs[4 + i][...] = mm(refs[i][...], w[...], ROWS).astype(BF)
+
+
+def project(w, grads):
+    return pl.pallas_call(
+        project_kernel,
+        out_shape=[jax.ShapeDtypeStruct((TOK, 256), BF)] * 4,
+        compiler_params=params(),
+        name="project",
+    )(*from_hbm(w, *grads))
 
 
 def layer_kernel(where, *refs):
@@ -363,10 +383,6 @@
         compiler_params=params(),
         name=name,
     )(where, *from_hbm(*parts), rows)
-
-
-def project(where, parts, d_out):
-    return weights_call(project_kernel, where, parts, d_out, WIDTH, "project")
 
 
 def layer_of(where, parts, attn):
@@ -548,62 +564,63 @@
     pair, outer, *chosen, picked = pick(where, k, v)
     rand = dict(zip(range(1, BITS), chosen))
     spread = trade(picked)
-    picked, rows = together(picked, w_out)
-    parts = [w_out, across(rows, 1), across(rows, 2)]
+    picked, own_grad = together(picked, grad_out)
+    grads = [grad_out, across(own_grad, 1), across(own_grad, 2)]
     order = feature_order(lax.axis_index("rep"))
     for b in FIRST:
         rand[b] = swapped(rand[b], b)
-    spread, order, parts[1], own_grad, pair, outer, rand = together(
-        spread, order, parts[1], grad_out, pair, outer, rand
+    spread, order, grads, pair, outer, rand, lower, upper = together(
+        spread, order, grads, pair, outer, rand, w_out[:HEAD_DIM], w_out[HEAD_DIM:]
     )
     mine = gathered(spread)
+    two, three = near(mine, along_z(mine, 1), along_z(mine, -1))
+    two, three, outer = together(two, three, outer)
+    below, above = along_z(three, 3), along_z(two, -3)
+    outer = neighboured(outer)
+    below, above, pair, grads, rand = together(below, above, pair, grads, rand)
+    glob = trade(relay(three, below, above)).reshape(2, 2 * TOK, HALF)
+    grads.append(across(grads[2], 1))
     pair = paired(pair)
-    outer = neighboured(outer)
-    two, three = near(mine, along_z(mine, 1), along_z(mine, -1))
-    below, above = along_z(three, 3), along_z(two, -3)
-    below, above, pair, outer, parts[2], own_grad, rand = together(
-        below, above, pair, outer, parts[2], own_grad, rand
-    )
-    glob = trade(relay(three, below, above)).reshape(2, 2 * TOK, HALF)
-    parts.append(across(parts[2], 1))
-    grads = [grad_out, across(own_grad, 1), across(own_grad, 2)]
     for b in THIRD:
         rand[b] = swapped(rand[b], b)
-    d_attn = project(where, parts, grad_out)
-    glob, d_attn, rand = together(glob, d_attn, rand)
+    pieces = project(w_out, grads)
+    glob, pieces, pair, outer, rand = together(glob, pieces, pair, outer, rand)
+    pieces = [pieces[0]] + [across(pieces[a], a) for a in range(1, 4)]
     rand = [rand[b] for b in range(1, BITS)]
     pair, outer, *rand = from_hbm(pair, outer, *rand)
     attn, stats, *ordered = forward(
         where, *from_hbm(q, k, v), pair, outer, rand, glob, *from_hbm(order)
     )
     cols = [ordered[0]] + [across(ordered[a], a) for a in range(1, 4)]
-    grads.append(across(grads[2], 1))
     (dq, down, pair, outer), drand, dglob = backward(
-        where, q, k, v, pair, outer, rand, glob, stats, d_attn
+        where, q, k, v, pair, outer, rand, glob, stats, pieces
     )
     back = dict(zip(range(1, BITS), drand))
-    cols[1], cols[2], cols[3], grads[1], grads[2], grads[3], dglob = together(
-        cols[1], cols[2], cols[3], grads[1], grads[2], grads[3], dglob
-    )
+    cols, dglob = together(cols, dglob)
     payload = weight_payload(cols, grads, dglob.reshape(CHUNKS, BLK, HALF))
     payload = trade(payload)
-    for b in FIRST:
-        back[b] = swapped(back[b], b)
-    layer = layer_of(where, parts, attn)
-    payload, layer, pair, outer, back = together(payload, layer, pair, outer, back)
-    pair = paired(pair)
+    back[3] = swapped(back[3], 3)
+    payload, pair, outer, back, lower, upper, w_own = together(
+        payload, pair, outer, back, lower, upper, w_out
+    )
+    parts = [w_out, across(w_own, 1), across(lower, 2), beside(upper)]
+    back[4] = swapped(back[4], 4)
     outer = neighboured(outer)
     glob_sum, keep, send = first(where, payload)
     for step, bit in enumerate(Z_BITS[1:]):
         came = swapped(send, Z_BITS[step])
         glob_sum, keep, send = fold(where, bit, glob_sum, keep, came)
     came = swapped(send, Z_BITS[2])
-    came, pair, outer, back = together(came, pair, outer, back)
+    came, pair, outer, back, parts = together(came, pair, outer, back, parts)
+    parts += [across(parts[2], 1), across(parts[3], 1)]
     routed, weight_grad = last(where, glob_sum, keep, came)
     glob_total = trade(routed).reshape(2, 2, GLOB, BLK, HALF)
+    pair = paired(pair)
     for b in THIRD:
         back[b] = swapped(back[b], b)
     back = [back[b] for b in range(1, BITS)]
+    layer = layer_of(where, parts, attn)
+    glob_total, layer = together(glob_total, layer)
     dk, dv = finish(where, down, pair, outer, back, glob_total)
     return (layer[None], dq[None], dk[None], dv[None], weight_grad)
 

time: 200 us -> 193 us (0.965)
  waiting for transfers between devices: 80.6 us -> 69.4 us
  local copies, waits for them, and re-layouts: 2.15 us -> 4.85 us
  starting transfers between devices: 75.5 us -> 78.1 us
  Pallas kernels: 36.9 us -> 34.9 us
    ppermute x15, waiting for transfers between devices: 55 us -> 41.3 us  [swapped(): return lax.ppermute(value, 'seq', [(s, s ^ 1 << bit) for s in range(64)])]
    ppermute x9 -> x13, waiting for transfers between devices: 8.69 us -> 1.37 us  [across(): return lax.ppermute(value, 'rep', [(r, r ^ flip) for r in range(4)])]
    pallas_call x2 -> x1, Pallas kernels: 9.26 us -> 4.26 us  [weights_call(): pl.pallas_call(kernel, out_shape=far((TOK, width)), in_specs=[smem()] + [...]
    ppermute x2, waiting for transfers between devices: 0.01 us -> 3.94 us  [neighboured(): lax.ppermute(value, 'seq', [(s, (s - 1 + s % 2 * 2) % 64) for s in range(...]
    ppermute x4, waiting for transfers between devices: 6.66 us -> 10.5 us  [along_z(): return lax.ppermute(value, 'seq', pairs)]
    ppermute x2, starting transfers between devices: 10.2 us -> 6.83 us  [neighboured(): lax.ppermute(value, 'seq', [(s, (s - 1 + s % 2 * 2) % 64) for s in range(...]
    pallas_call x0 -> x1, Pallas kernels: none -> 3.31 us  [project(): pl.pallas_call(project_kernel, out_shape=[jax.ShapeDtypeStruct((TOK, 256)...]
    all_to_all x4, waiting for transfers between devices: 10.2 us -> 12.4 us  [trade(): lax.all_to_all(value, 'seq', 0, 0, axis_index_groups=YX_GROUPS, tiled=True)]
  transfers between devices with their start and end apart: 34 -> 39, of which waited for: 16 -> 16; matrix products, arithmetic and copies ran while one was open for 1% -> 2% of each run, Pallas kernels for 13% -> 13%
where the time goes in v7:
time: 193 us; the launch traced here: 192 us
  starting transfers between devices  78.1 us (40%)
  waiting for transfers between devices  69.4 us (36%)
  Pallas kernels  34.9 us (18%)
  local copies, waits for them, and re-layouts  4.85 us (3%)
  other arithmetic  3.65 us (2%)
    ppermute x15, waiting for transfers between devices, swapped(): return lax.ppermute(value, 'seq', [(s, s ^ 1 << bit) for s in range(64)])  41.3 us
    ppermute x15, starting transfers between devices, swapped(): return lax.ppermute(value, 'seq', [(s, s ^ 1 << bit) for s in range(64)])  30.4 us
    all_to_all x4, starting transfers between devices, trade(): lax.all_to_all(value, 'seq', 0, 0, axis_index_groups=YX_GROUPS, tiled=True)  24.2 us
    all_to_all x4, waiting for transfers between devices, trade(): lax.all_to_all(value, 'seq', 0, 0, axis_index_groups=YX_GROUPS, tiled=True)  12.4 us
    ppermute x4, waiting for transfers between devices, along_z(): return lax.ppermute(value, 'seq', pairs)  10.5 us
    ppermute x4, starting transfers between devices, along_z(): return lax.ppermute(value, 'seq', pairs)  9.84 us
    pallas_call x1, Pallas kernels, backward(): pl.pallas_call(backward_kernel, grid=(HEADS // STEP,), in_specs=[smem(),...  7.11 us
    ppermute x2, starting transfers between devices, neighboured(): lax.ppermute(value, 'seq', [(s, (s - 1 + s % 2 * 2) % 64) for s in range(...  6.83 us
  transfers between devices with their start and end apart: 39, of which 16 were waited for; matrix products, arithmetic and copies ran while one was open for 2% of the time, Pallas kernels for 13%

profile of v7, /device:TPU:8, one launch (start us, length us, event | category | flops | bytes accessed | tf_op | source)
XLA Modules:
  0.0 191.9 jit_solution(3761088792734929177)
XLA Ops:
  0.7 0.8 fusion.36
  1.4 0.7 compare_select_fusion
  2.1 0.7 concatenate.3.where.refs_0_
  2.8 2.7 %pick.1 = (bf16[2,2,64,1024]{3,2,1,0:T(8,128)(2,1)}, bf16[2,64,1024]{2,1,0:T(8,128)(2,1)}, bf16[2,64,1024]{2,1,0:T(8,128)(2,1)}, bf16[2,64,1024]{2,1,0:T(8,128)(...) custom-call(s32[14]{0:T(128)S(1)} %concatenate.3.where.refs_0_, ...), custom_call_target="tpu_custom_call" | custom-call | tf_op jit(solution)/shard_map/pick/pallas_call | solution.py:130
  5.5 7.4 %all-to-all-start = ((bf16[8,64,512]{2,1,0:T(8,128)(2,1)}), bf16[8,64,512]{2,1,0:T(8,128)(2,1)S(1)}, u32[]{:S(2)}, u32[]{:S(2)}) async-start(bf16[8,64,512]{2,1,0:T(8,128)(2,1)} %get-tuple-element.119), calls=%async_computation | async-start | bytes 1048576 | tf_op jit(solution)/shard_map/all_to_all | solution.py:45
  12.9 0.6 collective-permute-start.1
  13.5 7.2 %collective-permute-start.2 = (bf16[2,64,1024]{2,1,0:T(8,128)(2,1)}, bf16[2,64,1024]{2,1,0:T(8,128)(2,1)S(1)}, u32[]{:S(2)}, u32[]{:S(2)}) collective-permute-start(bf16[2,64,1024]{2,1,0:T(8,128)(2,1)} %get-tuple-element.125), channel_id=1, source_target_pairs={{0,32},{4,36},{8,40},{12,44},{16,48},{20,52},{24,56},{28,60},{32,0... | collective-permute-start | bytes 786440 | tf_op jit(solution)/shard_map/ppermute | solution.py:49
  20.7 1.1 fusion.37
  21.8 2.2 %fusion.rest_6_ = bf16[1024,1024]{1,0:T(8,128)(2,1)} fusion(s32[1024]{0:T(1024)S(1)} %fusion.15), kind=kLoop, calls=%fused_computation.1 | loop fusion | flops 2097152 | bytes 2101248 | tf_op jit(solution)/shard_map/convert_element_type | solution.py:554
  24.0 5.0 %collective-permute-done.2.rest_2_ = bf16[2,64,1024]{2,1,0:T(8,128)(2,1)S(1)} collective-permute-done((bf16[2,64,1024]{2,1,0:T(8,128)(2,1)}, bf16[2,64,1024]{2,1,0:T(8,128)(2,1)S(1)}, u32[]{:S(2)}, u32[]{:S(2)}) %collective-permute-start.2) | collective-permute-done | bytes 262176 | tf_op jit(solution)/shard_map/ppermute | solution.py:49
  29.3 1.3 collective-permute-done.1.refs_2_.refs_6_
  30.8 5.9 %collective-permute-start.5 = (bf16[64,512]{1,0:T(8,128)(2,1)S(1)}, bf16[64,512]{1,0:T(8,128)(2,1)S(1)}, u32[]{:S(2)}, u32[]{:S(2)}) collective-permute-start(bf16[64,512]{1,0:T(8,128)(2,1)S(1)} %gathered.1.mine), channel_id=1, source_target_pairs={{0,56},{4,60},{8,0},{12,4},{16,8},{20,12},{24,16},{28,20},{32,24},... | collective-permute-start | bytes 196616 | tf_op jit(solution)/shard_map/ppermute | solution.py:54
  36.7 1.9 collective-permute-done.5.above
  38.6 3.6 %collective-permute-done.4.below = bf16[64,512]{1,0:T(8,128)(2,1)S(1)} collective-permute-done((bf16[64,512]{1,0:T(8,128)(2,1)S(1)}, bf16[64,512]{1,0:T(8,128)(2,1)S(1)}, u32[]{:S(2)}, u32[]{:S(2)}) %collective-permute-start.4) | collective-permute-done | bytes 65568 | tf_op jit(solution)/shard_map/ppermute | solution.py:54
  42.2 1.4 collective-permute-start.7
  43.6 2.5 %collective-permute-start.6 = (bf16[64,512]{1,0:T(8,128)(2,1)S(1)}, bf16[64,512]{1,0:T(8,128)(2,1)S(1)}, u32[]{:S(2)}, u32[]{:S(2)}) collective-permute-start(bf16[64,512]{1,0:T(8,128)(2,1)S(1)} %get-tuple-element.132.mine), channel_id=1, source_target_pairs={{0,24},{4,28},{8,32},{12,36},{16,40},{20,44},{24,48},{28,52},{32,5... | collective-permute-start | bytes 196616 | tf_op jit(solution)/shard_map/ppermute | solution.py:54
  46.1 2.8 %collective-permute-done.7.above = bf16[64,512]{1,0:T(8,128)(2,1)S(1)} collective-permute-done((bf16[64,512]{1,0:T(8,128)(2,1)S(1)}, bf16[64,512]{1,0:T(8,128)(2,1)S(1)}, u32[]{:S(2)}, u32[]{:S(2)}) %collective-permute-start.7) | collective-permute-done | bytes 65568 | tf_op jit(solution)/shard_map/ppermute | solution.py:54
  48.9 2.2 %collective-permute-done.6.below = bf16[64,512]{1,0:T(8,128)(2,1)S(1)} collective-permute-done((bf16[64,512]{1,0:T(8,128)(2,1)S(1)}, bf16[64,512]{1,0:T(8,128)(2,1)S(1)}, u32[]{:S(2)}, u32[]{:S(2)}) %collective-permute-start.6) | collective-permute-done | bytes 65568 | tf_op jit(solution)/shard_map/ppermute | solution.py:54
  51.1 3.6 %collective-permute-start.9 = (bf16[2,2,64,1024]{3,2,1,0:T(8,128)(2,1)}, bf16[2,2,64,1024]{3,2,1,0:T(8,128)(2,1)S(1)}, u32[]{:S(2)}, u32[]{:S(2)}) collective-permute-start(bf16[2,2,64,1024]{3,2,1,0:T(8,128)(2,1)} %get-tuple-element.152), channel_id=1, source_target_pairs={{0,4},{4,0},{8,12},{12,8},{16,20},{20,16},{24,28},{28,24},{32,36},... | collective-permute-start | bytes 1572872 | tf_op jit(solution)/shard_map/ppermute | solution.py:49
  54.7 0.8 relay.1
  55.5 4.8 %all-to-all-start.1 = ((bf16[8,64,512]{2,1,0:T(8,128)(2,1)}), bf16[8,64,512]{2,1,0:T(8,128)(2,1)S(1)}, u32[]{:S(2)}, u32[]{:S(2)}) async-start(bf16[8,64,512]{2,1,0:T(8,128)(2,1)} %relay.1), calls=%async_computation.1 | async-start | bytes 1048576 | tf_op jit(solution)/shard_map/all_to_all | solution.py:45
  60.3 3.7 %collective-permute-start.10 = (bf16[2,64,1024]{2,1,0:T(8,128)(2,1)}, bf16[2,64,1024]{2,1,0:T(8,128)(2,1)S(1)}, u32[]{:S(2)}, u32[]{:S(2)}) collective-permute-start(bf16[2,64,1024]{2,1,0:T(8,128)(2,1)} %get-tuple-element.153), channel_id=1, source_target_pairs={{0,252},{4,8},{8,4},{12,16},{16,12},{20,24},{24,20},{28,32},{32,28... | collective-permute-start | bytes 786440 | tf_op jit(solution)/shard_map/ppermute | solution.py:98
  64.0 0.7 collective-permute-start.11
  64.7 3.3 %collective-permute-start.12 = (bf16[2,64,1024]{2,1,0:T(8,128)(2,1)}, bf16[2,64,1024]{2,1,0:T(8,128)(2,1)S(1)}, u32[]{:S(2)}, u32[]{:S(2)}) collective-permute-start(bf16[2,64,1024]{2,1,0:T(8,128)(2,1)} %get-tuple-element.155), channel_id=1, source_target_pairs={{0,16},{4,20},{8,24},{12,28},{16,0},{20,4},{24,8},{28,12},{32,48},... | collective-permute-start | bytes 786440 | tf_op jit(solution)/shard_map/ppermute | solution.py:49
  68.0 2.1 %collective-permute-start.13 = (bf16[2,64,1024]{2,1,0:T(8,128)(2,1)}, bf16[2,64,1024]{2,1,0:T(8,128)(2,1)}, u32[]{:S(2)}, u32[]{:S(2)}) collective-permute-start(bf16[2,64,1024]{2,1,0:T(8,128)(2,1)} %get-tuple-element.158), channel_id=1, source_target_pairs={{0,128},{4,132},{8,136},{12,140},{16,144},{20,148},{24,152},{28,15... | collective-permute-start | bytes 786440 | tf_op jit(solution)/shard_map/ppermute | solution.py:49
  70.1 3.3 %project.1 = (bf16[128,256]{1,0:T(8,128)(2,1)S(1)}, bf16[128,256]{1,0:T(8,128)(2,1)S(1)}, bf16[128,256]{1,0:T(8,128)(2,1)S(1)}, bf16[128,256]{1,0:T(8,128)(2,1)S(1)}) custom-call(bf16[256,2048]{1,0:T(8,128)(2,1)} %refs_0_, bf16[128,2048]{1,0:T(8,128)(2,1)} %bitcast.42, bf16[128,2048]{1,0:T(8,128)(2,1)} %copy-done.5, bf16[128,2048]{1,0:T(8,128)(2,1)} %copy-done.4, ...), custom_call_target="tpu_custom_call" | custom-call | tf_op jit(solution)/shard_map/project/pallas_call | solution.py:361
  73.5 8.6 %collective-permute-done.11.rest_0_ = bf16[2,64,1024]{2,1,0:T(8,128)(2,1)S(1)} collective-permute-done((bf16[2,64,1024]{2,1,0:T(8,128)(2,1)}, bf16[2,64,1024]{2,1,0:T(8,128)(2,1)S(1)}, u32[]{:S(2)}, u32[]{:S(2)}) %collective-permute-start.11) | collective-permute-done | bytes 262176 | tf_op jit(solution)/shard_map/ppermute | solution.py:49
  82.1 0.7 copy-done.12
  82.8 0.7 copy-done.13
  83.6 0.9 collective-permute-start.18
  84.5 1.0 collective-permute-start.19
  85.5 6.0 %forward.1 = (bf16[128,1024]{1,0:T(8,128)(2,1)}, f32[8,8,128]{2,1,0:T(8,128)}, bf16[128,256]{1,0:T(8,128)(2,1)S(1)}, bf16[128,256]{1,0:T(8,128)(2,1)S(1)}, bf16[...) custom-call(s32[14]{0:T(128)S(1)} %concatenate.3.where.refs_0_, bf16[128,1024]{1,0:T(8,128)(2,1)} %bitcast.44, ...), custom_call_target="tpu_custom_call" | custom-call | tf_op jit(solution)/shard_map/forward/pallas_call | solution.py:252
  92.0 0.8 collective-permute-start.15
  92.8 0.7 collective-permute-start.16
  93.5 7.1 %backward.1 = (bf16[128,1024]{1,0:T(8,128)(2,1)}, f32[2,128,1024]{2,1,0:T(8,128)}, bf16[2,2,64,1024]{3,2,1,0:T(8,128)(2,1)}, bf16[2,64,1024]{2,1,0:T(8,128)(2,1)...) custom-call(s32[14]{0:T(128)S(1)} %concatenate.3.where.refs_0_, ...), custom_call_target="tpu_custom_call" | custom-call | tf_op jit(solution)/shard_map/backward/pallas_call | solution.py:320
  100.7 4.4 %weight.1 = bf16[8,192,512]{2,1,0:T(8,128)(2,1)} custom-call(bf16[128,256]{1,0:T(8,128)(2,1)S(1)} %get-tuple-element.178.refs_0_, bf16[128,256]{1,0:T(8,128)(2,1)S(1)} %collective-permute-done.14.refs_1_, bf16[128,256]{1,0:T(8,128)(2,1)S(1)} %collective-permute-done.15.refs_2_, bf16[128,256]{1,0:T(8,128)(2,1)S(1)} %collective-permute-done.16.refs_3_, ...), custom_call_target="tpu_custom_call" | custom-call | tf_op jit(solution)/shard_map/weight/pallas_call | solution.py:413
  105.0 5.0 %all-to-all-start.2 = ((bf16[8,192,512]{2,1,0:T(8,128)(2,1)}), bf16[8,192,512]{2,1,0:T(8,128)(2,1)S(1)}, u32[]{:S(2)}, u32[]{:S(2)}) async-start(bf16[8,192,512]{2,1,0:T(8,128)(2,1)} %weight.1), calls=%async_computation.2 | async-start | bytes 3145728 | tf_op jit(solution)/shard_map/all_to_all | solution.py:45
  110.0 1.9 collective-permute-start.20
  111.9 13.2 %collective-permute-done.20.rest_2_ = bf16[2,64,1024]{2,1,0:T(8,128)(2,1)} collective-permute-done((bf16[2,64,1024]{2,1,0:T(8,128)(2,1)S(1)}, bf16[2,64,1024]{2,1,0:T(8,128)(2,1)}, u32[]{:S(2)}, u32[]{:S(2)}) %collective-permute-start.20) | collective-permute-done | bytes 262176 | tf_op jit(solution)/shard_map/ppermute | solution.py:49
  125.1 6.7 %all-to-all-done.2.refs_1_ = bf16[8,192,512]{2,1,0:T(8,128)(2,1)S(1)} async-done(((bf16[8,192,512]{2,1,0:T(8,128)(2,1)}), bf16[8,192,512]{2,1,0:T(8,128)(2,1)S(1)}, u32[]{:S(2)}, u32[]{:S(2)}) %all-to-all-start.2) | async-done | bytes 1572896 | tf_op jit(solution)/shard_map/all_to_all | solution.py:45
  131.9 0.8 collective-permute-start.27
  132.7 0.9 collective-permute-start.28
  133.6 0.7 first.1
  134.4 2.6 %collective-permute-start.21 = (bf16[128,512]{1,0:T(8,128)(2,1)S(1)}, bf16[128,512]{1,0:T(8,128)(2,1)S(1)}, u32[]{:S(2)}, u32[]{:S(2)}) collective-permute-start(bf16[128,512]{1,0:T(8,128)(2,1)S(1)} %get-tuple-element.195), channel_id=1, source_target_pairs={{0,8},{4,12},{8,0},{12,4},{16,24},{20,28},{24,16},{28,20},{32,40},... | collective-permute-start | bytes 393224 | tf_op jit(solution)/shard_map/ppermute | solution.py:49
  137.0 3.6 %collective-permute-done.21.refs_3_ = bf16[128,512]{1,0:T(8,128)(2,1)S(1)} collective-permute-done((bf16[128,512]{1,0:T(8,128)(2,1)S(1)}, bf16[128,512]{1,0:T(8,128)(2,1)S(1)}, u32[]{:S(2)}, u32[]{:S(2)}) %collective-permute-start.21) | collective-permute-done | bytes 131104 | tf_op jit(solution)/shard_map/ppermute | solution.py:49
  141.2 1.7 collective-permute-start.22
  142.8 3.1 %collective-permute-start.24 = (bf16[2,64,1024]{2,1,0:T(8,128)(2,1)}, bf16[2,64,1024]{2,1,0:T(8,128)(2,1)S(1)}, u32[]{:S(2)}, u32[]{:S(2)}) collective-permute-start(bf16[2,64,1024]{2,1,0:T(8,128)(2,1)} %get-tuple-element.203), channel_id=1, source_target_pairs={{0,252},{4,8},{8,4},{12,16},{16,12},{20,24},{24,20},{28,32},{32,28... | collective-permute-start | bytes 786440 | tf_op jit(solution)/shard_map/ppermute | solution.py:98
  146.0 2.8 %collective-permute-done.22.refs_3_ = bf16[96,512]{1,0:T(8,128)(2,1)S(1)} collective-permute-done((bf16[96,512]{1,0:T(8,128)(2,1)S(1)}, bf16[96,512]{1,0:T(8,128)(2,1)S(1)}, u32[]{:S(2)}, u32[]{:S(2)}) %collective-permute-start.22) | collective-permute-done | bytes 98336 | tf_op jit(solution)/shard_map/ppermute | solution.py:49
  148.7 1.6 collective-permute-start.25
  150.3 0.6 fold.3
  150.9 3.9 %collective-permute-done.24.outer = bf16[2,64,1024]{2,1,0:T(8,128)(2,1)S(1)} collective-permute-done((bf16[2,64,1024]{2,1,0:T(8,128)(2,1)}, bf16[2,64,1024]{2,1,0:T(8,128)(2,1)S(1)}, u32[]{:S(2)}, u32[]{:S(2)}) %collective-permute-start.24) | collective-permute-done | bytes 262176 | tf_op jit(solution)/shard_map/ppermute | solution.py:98
  154.8 0.7 collective-permute-start.23
  155.6 4.8 %collective-permute-done.25.rest_3_ = bf16[2,64,1024]{2,1,0:T(8,128)(2,1)S(1)} collective-permute-done((bf16[2,64,1024]{2,1,0:T(8,128)(2,1)}, bf16[2,64,1024]{2,1,0:T(8,128)(2,1)S(1)}, u32[]{:S(2)}, u32[]{:S(2)}) %collective-permute-start.25) | collective-permute-done | bytes 262176 | tf_op jit(solution)/shard_map/ppermute | solution.py:49
  160.4 2.9 %collective-permute-done.23.came = bf16[80,512]{1,0:T(8,128)(2,1)S(1)} collective-permute-done((bf16[80,512]{1,0:T(8,128)(2,1)S(1)}, bf16[80,512]{1,0:T(8,128)(2,1)S(1)}, u32[]{:S(2)}, u32[]{:S(2)}) %collective-permute-start.23) | collective-permute-done | bytes 81952 | tf_op jit(solution)/shard_map/ppermute | solution.py:49
  163.9 1.0 collective-permute-start.31
  164.9 1.4 last.1
  166.3 7.0 %all-to-all-start.3 = ((bf16[8,64,512]{2,1,0:T(8,128)(2,1)}), bf16[8,64,512]{2,1,0:T(8,128)(2,1)S(1)}, u32[]{:S(2)}, u32[]{:S(2)}) async-start(bf16[8,64,512]{2,1,0:T(8,128)(2,1)} %get-tuple-element.213), calls=%async_computation.3 | async-start | bytes 1048576 | tf_op jit(solution)/shard_map/all_to_all | solution.py:45
  173.5 1.8 collective-permute-start.33
  175.3 2.1 %collective-permute-start.34 = (bf16[2,64,1024]{2,1,0:T(8,128)(2,1)}, bf16[2,64,1024]{2,1,0:T(8,128)(2,1)}, u32[]{:S(2)}, u32[]{:S(2)}) collective-permute-start(bf16[2,64,1024]{2,1,0:T(8,128)(2,1)} %get-tuple-element.228), channel_id=1, source_target_pairs={{0,128},{4,132},{8,136},{12,140},{16,144},{20,148},{24,152},{28,15... | collective-permute-start | bytes 786440 | tf_op jit(solution)/shard_map/ppermute | solution.py:49
  177.4 0.8 copy-done.16
  178.2 4.3 %layer.1 = bf16[128,2048]{1,0:T(8,128)(2,1)} custom-call(s32[14]{0:T(128)S(1)} %concatenate.3.where.refs_0_, bf16[256,2048]{1,0:T(8,128)(2,1)} %refs_0_, bf16[256,2048]{1,0:T(8,128)(2,1)} %copy-done.8, bf16[128,2048]{1,0:T(8,128)(2,1)} %copy-done.14, bf16[128,2048]{1,0:T(8,128)(2,1)} %collective-permute-done.28.refs_3_, bf16[128,2048]{1,0:T(8,128)(2,1)} %copy-done.15, ...), custom_call_target="tpu_custom_call" | custom-call | tf_op jit(solution)/shard_map/layer/pallas_call | solution.py:377
  182.5 5.6 %all-to-all-done.3 = bf16[8,64,512]{2,1,0:T(8,128)(2,1)S(1)} async-done(((bf16[8,64,512]{2,1,0:T(8,128)(2,1)}), bf16[8,64,512]{2,1,0:T(8,128)(2,1)S(1)}, u32[]{:S(2)}, u32[]{:S(2)}) %all-to-all-start.3) | async-done | bytes 524320 | tf_op jit(solution)/shard_map/all_to_all | solution.py:45
  188.2 0.8 copy-done.17
  188.9 2.9 %finish.1 = (bf16[128,1024]{1,0:T(8,128)(2,1)}, bf16[128,1024]{1,0:T(8,128)(2,1)}) custom-call(s32[14]{0:T(128)S(1)} %concatenate.3.where.refs_0_, f32[2,128,1024]{2,1,0:T(8,128)} %get-tuple-element.221.own, bf16[2,2,64,1024]{3,2,1,0:T(8,128)(2,1)} %copy-done.17, bf16[2,64,1024]{2,1,0:T(8,128)(2,1)} %copy-done.18, ...), custom_call_target="tpu_custom_call" | custom-call | tf_op jit(solution)/shard_map/finish/pallas_call | solution.py:534
  (76 shorter events, 2.4 us)
Async XLA Ops:
  0.6 20.1 %copy-start.2 = (bf16[256,2048]{1,0:T(8,128)(2,1)S(1)}, bf16[256,2048]{1,0:T(8,128)(2,1)}, u32[]{:S(2)}) copy-start(bf16[256,2048]{1,0:T(8,128)(2,1)} %refs_0_) | copy-start | bytes 3145732
  5.5 23.8 %all-to-all-start = ((bf16[8,64,512]{2,1,0:T(8,128)(2,1)}), bf16[8,64,512]{2,1,0:T(8,128)(2,1)S(1)}, u32[]{:S(2)}, u32[]{:S(2)}) async-start(bf16[8,64,512]{2,1,0:T(8,128)(2,1)} %get-tuple-element.119), calls=%async_computation | async-start | bytes 1048576 | tf_op jit(solution)/shard_map/all_to_all | solution.py:45
  12.9 17.8 %collective-permute-start.1 = (bf16[128,2048]{1,0:T(8,128)(2,1)}, bf16[128,2048]{1,0:T(8,128)(2,1)S(1)}, u32[]{:S(2)}, u32[]{:S(2)}) collective-permute-start(bf16[128,2048]{1,0:T(8,128)(2,1)} %bitcast.40), channel_id=1, source_target_pairs={{0,2},{1,3},{2,0},{3,1},{4,6},{5,7},{6,4},{7,5},{8,10},{9,11},{10,... | collective-permute-start | bytes 1572872 | tf_op jit(solution)/shard_map/ppermute | solution.py:58
  13.5 17.2 %collective-permute-start = (bf16[128,2048]{1,0:T(8,128)(2,1)}, bf16[128,2048]{1,0:T(8,128)(2,1)S(1)}, u32[]{:S(2)}, u32[]{:S(2)}) collective-permute-start(bf16[128,2048]{1,0:T(8,128)(2,1)} %bitcast.41), channel_id=1, source_target_pairs={{0,1},{1,0},{2,3},{3,2},{4,5},{5,4},{6,7},{7,6},{8,9},{9,8},{10,11... | collective-permute-start | bytes 1572872 | tf_op jit(solution)/shard_map/ppermute | solution.py:58
  13.5 15.5 %collective-permute-start.2 = (bf16[2,64,1024]{2,1,0:T(8,128)(2,1)}, bf16[2,64,1024]{2,1,0:T(8,128)(2,1)S(1)}, u32[]{:S(2)}, u32[]{:S(2)}) collective-permute-start(bf16[2,64,1024]{2,1,0:T(8,128)(2,1)} %get-tuple-element.125), channel_id=1, source_target_pairs={{0,32},{4,36},{8,40},{12,44},{16,48},{20,52},{24,56},{28,60},{32,0... | collective-permute-start | bytes 786440 | tf_op jit(solution)/shard_map/ppermute | solution.py:49
  20.7 8.6 %collective-permute-start.3 = (bf16[2,64,1024]{2,1,0:T(8,128)(2,1)}, bf16[2,64,1024]{2,1,0:T(8,128)(2,1)S(1)}, u32[]{:S(2)}, u32[]{:S(2)}) collective-permute-start(bf16[2,64,1024]{2,1,0:T(8,128)(2,1)} %get-tuple-element.126), channel_id=1, source_target_pairs={{0,64},{4,68},{8,72},{12,76},{16,80},{20,84},{24,88},{28,92},{32,9... | collective-permute-start | bytes 786440 | tf_op jit(solution)/shard_map/ppermute | solution.py:49
  29.0 44.4 %copy-start.9 = (bf16[2,64,1024]{2,1,0:T(8,128)(2,1)}, bf16[2,64,1024]{2,1,0:T(8,128)(2,1)S(1)}, u32[]{:S(2)}) copy-start(bf16[2,64,1024]{2,1,0:T(8,128)(2,1)S(1)} %collective-permute-done.2.rest_2_) | copy-start | bytes 786436
  29.3 44.1 %copy-start.10 = (bf16[2,64,1024]{2,1,0:T(8,128)(2,1)}, bf16[2,64,1024]{2,1,0:T(8,128)(2,1)S(1)}, u32[]{:S(2)}) copy-start(bf16[2,64,1024]{2,1,0:T(8,128)(2,1)S(1)} %collective-permute-done.3.rest_3_) | copy-start | bytes 786436
  30.7 39.4 %copy-start.4 = (bf16[128,2048]{1,0:T(8,128)(2,1)}, bf16[128,2048]{1,0:T(8,128)(2,1)S(1)}, u32[]{:S(2)}) copy-start(bf16[128,2048]{1,0:T(8,128)(2,1)S(1)} %collective-permute-done.1.refs_2_.refs_6_) | copy-start | bytes 1572868
  30.7 39.4 %copy-start.5 = (bf16[128,2048]{1,0:T(8,128)(2,1)}, bf16[128,2048]{1,0:T(8,128)(2,1)S(1)}, u32[]{:S(2)}) copy-start(bf16[128,2048]{1,0:T(8,128)(2,1)S(1)} %collective-permute-done.refs_1_.refs_5_) | copy-start | bytes 1572868
  30.8 7.8 %collective-permute-start.5 = (bf16[64,512]{1,0:T(8,128)(2,1)S(1)}, bf16[64,512]{1,0:T(8,128)(2,1)S(1)}, u32[]{:S(2)}, u32[]{:S(2)}) collective-permute-start(bf16[64,512]{1,0:T(8,128)(2,1)S(1)} %gathered.1.mine), channel_id=1, source_target_pairs={{0,56},{4,60},{8,0},{12,4},{16,8},{20,12},{24,16},{28,20},{32,24},... | collective-permute-start | bytes 196616 | tf_op jit(solution)/shard_map/ppermute | solution.py:54
  36.7 5.5 %collective-permute-start.4 = (bf16[64,512]{1,0:T(8,128)(2,1)S(1)}, bf16[64,512]{1,0:T(8,128)(2,1)S(1)}, u32[]{:S(2)}, u32[]{:S(2)}) collective-permute-start(bf16[64,512]{1,0:T(8,128)(2,1)S(1)} %gathered.1.mine), channel_id=1, source_target_pairs={{0,8},{4,12},{8,16},{12,20},{16,24},{20,28},{24,32},{28,36},{32,40... | collective-permute-start | bytes 196616 | tf_op jit(solution)/shard_map/ppermute | solution.py:54
  42.2 6.7 %collective-permute-start.7 = (bf16[64,512]{1,0:T(8,128)(2,1)S(1)}, bf16[64,512]{1,0:T(8,128)(2,1)S(1)}, u32[]{:S(2)}, u32[]{:S(2)}) collective-permute-start(bf16[64,512]{1,0:T(8,128)(2,1)S(1)} %get-tuple-element.133), channel_id=1, source_target_pairs={{0,40},{4,44},{8,48},{12,52},{16,56},{20,60},{24,0},{28,4},{32,8},... | collective-permute-start | bytes 196616 | tf_op jit(solution)/shard_map/ppermute | solution.py:54
  43.6 7.5 %collective-permute-start.6 = (bf16[64,512]{1,0:T(8,128)(2,1)S(1)}, bf16[64,512]{1,0:T(8,128)(2,1)S(1)}, u32[]{:S(2)}, u32[]{:S(2)}) collective-permute-start(bf16[64,512]{1,0:T(8,128)(2,1)S(1)} %get-tuple-element.132.mine), channel_id=1, source_target_pairs={{0,24},{4,28},{8,32},{12,36},{16,40},{20,44},{24,48},{28,52},{32,5... | collective-permute-start | bytes 196616 | tf_op jit(solution)/shard_map/ppermute | solution.py:54
  51.1 16.9 %collective-permute-start.8 = (bf16[128,2048]{1,0:T(8,128)(2,1)S(1)}, bf16[128,2048]{1,0:T(8,128)(2,1)S(1)}, u32[]{:S(2)}, u32[]{:S(2)}) collective-permute-start(bf16[128,2048]{1,0:T(8,128)(2,1)S(1)} %collective-permute-done.1.refs_2_.refs_6_), channel_id=1, source_target_pairs={{0,1},{1,0},{2,3},{3,2},{4,5},{5,4},{6,7},{7,6},{8,9},{9,8},{10,11... | collective-permute-start | bytes 1572872 | tf_op jit(solution)/shard_map/ppermute | solution.py:58
  51.1 32.4 %collective-permute-start.9 = (bf16[2,2,64,1024]{3,2,1,0:T(8,128)(2,1)}, bf16[2,2,64,1024]{3,2,1,0:T(8,128)(2,1)S(1)}, u32[]{:S(2)}, u32[]{:S(2)}) collective-permute-start(bf16[2,2,64,1024]{3,2,1,0:T(8,128)(2,1)} %get-tuple-element.152), channel_id=1, source_target_pairs={{0,4},{4,0},{8,12},{12,8},{16,20},{20,16},{24,28},{28,24},{32,36},... | collective-permute-start | bytes 1572872 | tf_op jit(solution)/shard_map/ppermute | solution.py:49
  55.5 28.0 %all-to-all-start.1 = ((bf16[8,64,512]{2,1,0:T(8,128)(2,1)}), bf16[8,64,512]{2,1,0:T(8,128)(2,1)S(1)}, u32[]{:S(2)}, u32[]{:S(2)}) async-start(bf16[8,64,512]{2,1,0:T(8,128)(2,1)} %relay.1), calls=%async_computation.1 | async-start | bytes 1048576 | tf_op jit(solution)/shard_map/all_to_all | solution.py:45
  60.3 13.1 %collective-permute-start.10 = (bf16[2,64,1024]{2,1,0:T(8,128)(2,1)}, bf16[2,64,1024]{2,1,0:T(8,128)(2,1)S(1)}, u32[]{:S(2)}, u32[]{:S(2)}) collective-permute-start(bf16[2,64,1024]{2,1,0:T(8,128)(2,1)} %get-tuple-element.153), channel_id=1, source_target_pairs={{0,252},{4,8},{8,4},{12,16},{16,12},{20,24},{24,20},{28,32},{32,28... | collective-permute-start | bytes 786440 | tf_op jit(solution)/shard_map/ppermute | solution.py:98
  64.0 18.1 %collective-permute-start.11 = (bf16[2,64,1024]{2,1,0:T(8,128)(2,1)}, bf16[2,64,1024]{2,1,0:T(8,128)(2,1)S(1)}, u32[]{:S(2)}, u32[]{:S(2)}) collective-permute-start(bf16[2,64,1024]{2,1,0:T(8,128)(2,1)} %get-tuple-element.154), channel_id=1, source_target_pairs={{0,8},{4,12},{8,0},{12,4},{16,24},{20,28},{24,16},{28,20},{32,40},... | collective-permute-start | bytes 786440 | tf_op jit(solution)/shard_map/ppermute | solution.py:49
  64.7 17.4 %collective-permute-start.12 = (bf16[2,64,1024]{2,1,0:T(8,128)(2,1)}, bf16[2,64,1024]{2,1,0:T(8,128)(2,1)S(1)}, u32[]{:S(2)}, u32[]{:S(2)}) collective-permute-start(bf16[2,64,1024]{2,1,0:T(8,128)(2,1)} %get-tuple-element.155), channel_id=1, source_target_pairs={{0,16},{4,20},{8,24},{12,28},{16,0},{20,4},{24,8},{28,12},{32,48},... | collective-permute-start | bytes 786440 | tf_op jit(solution)/shard_map/ppermute | solution.py:49
  68.0 2.1 %copy-start.6 = (bf16[128,2048]{1,0:T(8,128)(2,1)}, bf16[128,2048]{1,0:T(8,128)(2,1)S(1)}, u32[]{:S(2)}) copy-start(bf16[128,2048]{1,0:T(8,128)(2,1)S(1)} %collective-permute-done.8.refs_3_.refs_7_) | copy-start | bytes 1572868
  68.0 15.5 %collective-permute-start.13 = (bf16[2,64,1024]{2,1,0:T(8,128)(2,1)}, bf16[2,64,1024]{2,1,0:T(8,128)(2,1)}, u32[]{:S(2)}, u32[]{:S(2)}) collective-permute-start(bf16[2,64,1024]{2,1,0:T(8,128)(2,1)} %get-tuple-element.158), channel_id=1, source_target_pairs={{0,128},{4,132},{8,136},{12,140},{16,144},{20,148},{24,152},{28,15... | collective-permute-start | bytes 786440 | tf_op jit(solution)/shard_map/ppermute | solution.py:49
  73.4 8.7 %copy-start.11 = (bf16[2,64,1024]{2,1,0:T(8,128)(2,1)}, bf16[2,64,1024]{2,1,0:T(8,128)(2,1)S(1)}, u32[]{:S(2)}) copy-start(bf16[2,64,1024]{2,1,0:T(8,128)(2,1)S(1)} %collective-permute-done.10.outer) | copy-start | bytes 786436
  82.1 0.7 copy-start.12
  82.8 0.7 copy-start.13
  83.5 8.0 %copy-start = (bf16[8,64,512]{2,1,0:T(8,128)(2,1)}, bf16[8,64,512]{2,1,0:T(8,128)(2,1)S(1)}, u32[]{:S(2)}) copy-start(bf16[8,64,512]{2,1,0:T(8,128)(2,1)S(1)} %all-to-all-done.1) | copy-start | bytes 1572868
  83.5 2.0 %copy-start.7 = (bf16[2,2,64,1024]{3,2,1,0:T(8,128)(2,1)}, bf16[2,2,64,1024]{3,2,1,0:T(8,128)(2,1)S(1)}, u32[]{:S(2)}) copy-start(bf16[2,2,64,1024]{3,2,1,0:T(8,128)(2,1)S(1)} %collective-permute-done.9.pair) | copy-start | bytes 1572868
  83.5 9.3 %collective-permute-start.17 = (bf16[128,256]{1,0:T(8,128)(2,1)S(1)}, bf16[128,256]{1,0:T(8,128)(2,1)S(1)}, u32[]{:S(2)}, u32[]{:S(2)}) collective-permute-start(bf16[128,256]{1,0:T(8,128)(2,1)S(1)} %get-tuple-element.174), channel_id=1, source_target_pairs={{0,1},{1,0},{2,3},{3,2},{4,5},{5,4},{6,7},{7,6},{8,9},{9,8},{10,11... | collective-permute-start | bytes 196616 | tf_op jit(solution)/shard_map/ppermute | solution.py:58
  83.6 9.9 %collective-permute-start.18 = (bf16[128,256]{1,0:T(8,128)(2,1)S(1)}, bf16[128,256]{1,0:T(8,128)(2,1)S(1)}, u32[]{:S(2)}, u32[]{:S(2)}) collective-permute-start(bf16[128,256]{1,0:T(8,128)(2,1)S(1)} %get-tuple-element.175), channel_id=1, source_target_pairs={{0,2},{1,3},{2,0},{3,1},{4,6},{5,7},{6,4},{7,5},{8,10},{9,11},{10,... | collective-permute-start | bytes 196616 | tf_op jit(solution)/shard_map/ppermute | solution.py:58
  84.5 9.0 %collective-permute-start.19 = (bf16[128,256]{1,0:T(8,128)(2,1)S(1)}, bf16[128,256]{1,0:T(8,128)(2,1)S(1)}, u32[]{:S(2)}, u32[]{:S(2)}) collective-permute-start(bf16[128,256]{1,0:T(8,128)(2,1)S(1)} %get-tuple-element.176), channel_id=1, source_target_pairs={{0,3},{1,2},{2,1},{3,0},{4,7},{5,6},{6,5},{7,4},{8,11},{9,10},{10,... | collective-permute-start | bytes 196616 | tf_op jit(solution)/shard_map/ppermute | solution.py:58
  91.5 9.1 %collective-permute-start.14 = (bf16[128,256]{1,0:T(8,128)(2,1)S(1)}, bf16[128,256]{1,0:T(8,128)(2,1)S(1)}, u32[]{:S(2)}, u32[]{:S(2)}) collective-permute-start(bf16[128,256]{1,0:T(8,128)(2,1)S(1)} %get-tuple-element.169), channel_id=1, source_target_pairs={{0,1},{1,0},{2,3},{3,2},{4,5},{5,4},{6,7},{7,6},{8,9},{9,8},{10,11... | collective-permute-start | bytes 196616 | tf_op jit(solution)/shard_map/ppermute | solution.py:58
  92.0 8.6 %collective-permute-start.15 = (bf16[128,256]{1,0:T(8,128)(2,1)S(1)}, bf16[128,256]{1,0:T(8,128)(2,1)S(1)}, u32[]{:S(2)}, u32[]{:S(2)}) collective-permute-start(bf16[128,256]{1,0:T(8,128)(2,1)S(1)} %get-tuple-element.170), channel_id=1, source_target_pairs={{0,2},{1,3},{2,0},{3,1},{4,6},{5,7},{6,4},{7,5},{8,10},{9,11},{10,... | collective-permute-start | bytes 196616 | tf_op jit(solution)/shard_map/ppermute | solution.py:58
  92.8 7.8 %collective-permute-start.16 = (bf16[128,256]{1,0:T(8,128)(2,1)S(1)}, bf16[128,256]{1,0:T(8,128)(2,1)S(1)}, u32[]{:S(2)}, u32[]{:S(2)}) collective-permute-start(bf16[128,256]{1,0:T(8,128)(2,1)S(1)} %get-tuple-element.171), channel_id=1, source_target_pairs={{0,3},{1,2},{2,1},{3,0},{4,7},{5,6},{6,5},{7,4},{8,11},{9,10},{10,... | collective-permute-start | bytes 196616 | tf_op jit(solution)/shard_map/ppermute | solution.py:58
  105.0 5.0 %copy-start.20 = (bf16[2,64,1024]{2,1,0:T(8,128)(2,1)S(1)}, bf16[2,64,1024]{2,1,0:T(8,128)(2,1)}, u32[]{:S(2)}) copy-start(bf16[2,64,1024]{2,1,0:T(8,128)(2,1)} %get-tuple-element.187) | copy-start | bytes 786436
  105.0 26.9 %copy-start.3 = (bf16[256,2048]{1,0:T(8,128)(2,1)S(1)}, bf16[256,2048]{1,0:T(8,128)(2,1)}, u32[]{:S(2)}) copy-start(bf16[256,2048]{1,0:T(8,128)(2,1)} %refs_0_) | copy-start | bytes 3145732
  105.0 26.8 %all-to-all-start.2 = ((bf16[8,192,512]{2,1,0:T(8,128)(2,1)}), bf16[8,192,512]{2,1,0:T(8,128)(2,1)S(1)}, u32[]{:S(2)}, u32[]{:S(2)}) async-start(bf16[8,192,512]{2,1,0:T(8,128)(2,1)} %weight.1), calls=%async_computation.2 | async-start | bytes 3145728 | tf_op jit(solution)/shard_map/all_to_all | solution.py:45
  110.0 68.2 %copy-start.1 = (bf16[128,1024]{1,0:T(8,128)(2,1)S(1)}, bf16[128,1024]{1,0:T(8,128)(2,1)}, u32[]{:S(2)}) copy-start(bf16[128,1024]{1,0:T(8,128)(2,1)} %get-tuple-element.218.refs_6_) | copy-start | bytes 786436
  110.0 15.1 %collective-permute-start.20 = (bf16[2,64,1024]{2,1,0:T(8,128)(2,1)S(1)}, bf16[2,64,1024]{2,1,0:T(8,128)(2,1)}, u32[]{:S(2)}, u32[]{:S(2)}) collective-permute-start(bf16[2,64,1024]{2,1,0:T(8,128)(2,1)S(1)} %copy-done.20), channel_id=1, source_target_pairs={{0,32},{4,36},{8,40},{12,44},{16,48},{20,52},{24,56},{28,60},{32,0... | collective-permute-start | bytes 786440 | tf_op jit(solution)/shard_map/ppermute | solution.py:49
  131.9 31.4 %collective-permute-start.26 = (bf16[256,2048]{1,0:T(8,128)(2,1)S(1)}, bf16[256,2048]{1,0:T(8,128)(2,1)S(1)}, u32[]{:S(2)}, u32[]{:S(2)}) collective-permute-start(bf16[256,2048]{1,0:T(8,128)(2,1)S(1)} %copy-done.3), channel_id=1, source_target_pairs={{0,1},{1,0},{2,3},{3,2},{4,5},{5,4},{6,7},{7,6},{8,9},{9,8},{10,11... | collective-permute-start | bytes 3145736 | tf_op jit(solution)/shard_map/ppermute | solution.py:58
  131.9 31.4 %collective-permute-start.27 = (bf16[128,2048]{1,0:T(8,128)(2,1)}, bf16[128,2048]{1,0:T(8,128)(2,1)S(1)}, u32[]{:S(2)}, u32[]{:S(2)}) collective-permute-start(bf16[128,2048]{1,0:T(8,128)(2,1)} %get-tuple-element.210), channel_id=1, source_target_pairs={{0,2},{1,3},{2,0},{3,1},{4,6},{5,7},{6,4},{7,5},{8,10},{9,11},{10,... | collective-permute-start | bytes 1572872 | tf_op jit(solution)/shard_map/ppermute | solution.py:58
  132.7 30.6 %collective-permute-start.28 = (bf16[128,2048]{1,0:T(8,128)(2,1)}, bf16[128,2048]{1,0:T(8,128)(2,1)}, u32[]{:S(2)}, u32[]{:S(2)}) collective-permute-start(bf16[128,2048]{1,0:T(8,128)(2,1)} %get-tuple-element.211), channel_id=1, source_target_pairs={{0,6},{1,7},{2,4},{3,5},{4,2},{5,3},{6,0},{7,1},{8,14},{9,15},{10,... | collective-permute-start | bytes 1572872 | tf_op jit(solution)/shard_map/ppermute | solution.py:63
  134.4 6.2 %collective-permute-start.21 = (bf16[128,512]{1,0:T(8,128)(2,1)S(1)}, bf16[128,512]{1,0:T(8,128)(2,1)S(1)}, u32[]{:S(2)}, u32[]{:S(2)}) collective-permute-start(bf16[128,512]{1,0:T(8,128)(2,1)S(1)} %get-tuple-element.195), channel_id=1, source_target_pairs={{0,8},{4,12},{8,0},{12,4},{16,24},{20,28},{24,16},{28,20},{32,40},... | collective-permute-start | bytes 393224 | tf_op jit(solution)/shard_map/ppermute | solution.py:49
  141.2 7.6 %collective-permute-start.22 = (bf16[96,512]{1,0:T(8,128)(2,1)S(1)}, bf16[96,512]{1,0:T(8,128)(2,1)S(1)}, u32[]{:S(2)}, u32[]{:S(2)}) collective-permute-start(bf16[96,512]{1,0:T(8,128)(2,1)S(1)} %get-tuple-element.198), channel_id=1, source_target_pairs={{0,16},{4,20},{8,24},{12,28},{16,0},{20,4},{24,8},{28,12},{32,48},... | collective-permute-start | bytes 294920 | tf_op jit(solution)/shard_map/ppermute | solution.py:49
  142.8 12.0 %collective-permute-start.24 = (bf16[2,64,1024]{2,1,0:T(8,128)(2,1)}, bf16[2,64,1024]{2,1,0:T(8,128)(2,1)S(1)}, u32[]{:S(2)}, u32[]{:S(2)}) collective-permute-start(bf16[2,64,1024]{2,1,0:T(8,128)(2,1)} %get-tuple-element.203), channel_id=1, source_target_pairs={{0,252},{4,8},{8,4},{12,16},{16,12},{20,24},{24,20},{28,32},{32,28... | collective-permute-start | bytes 786440 | tf_op jit(solution)/shard_map/ppermute | solution.py:98
  148.7 11.6 %collective-permute-start.25 = (bf16[2,64,1024]{2,1,0:T(8,128)(2,1)}, bf16[2,64,1024]{2,1,0:T(8,128)(2,1)S(1)}, u32[]{:S(2)}, u32[]{:S(2)}) collective-permute-start(bf16[2,64,1024]{2,1,0:T(8,128)(2,1)} %get-tuple-element.207), channel_id=1, source_target_pairs={{0,64},{4,68},{8,72},{12,76},{16,80},{20,84},{24,88},{28,92},{32,9... | collective-permute-start | bytes 786440 | tf_op jit(solution)/shard_map/ppermute | solution.py:49
  154.8 33.3 %copy-start.18 = (bf16[2,64,1024]{2,1,0:T(8,128)(2,1)}, bf16[2,64,1024]{2,1,0:T(8,128)(2,1)S(1)}, u32[]{:S(2)}) copy-start(bf16[2,64,1024]{2,1,0:T(8,128)(2,1)S(1)} %collective-permute-done.24.outer) | copy-start | bytes 786436
  154.8 8.5 %collective-permute-start.23 = (bf16[80,512]{1,0:T(8,128)(2,1)S(1)}, bf16[80,512]{1,0:T(8,128)(2,1)S(1)}, u32[]{:S(2)}, u32[]{:S(2)}) collective-permute-start(bf16[80,512]{1,0:T(8,128)(2,1)S(1)} %get-tuple-element.201), channel_id=1, source_target_pairs={{0,32},{4,36},{8,40},{12,44},{16,48},{20,52},{24,56},{28,60},{32,0... | collective-permute-start | bytes 245768 | tf_op jit(solution)/shard_map/ppermute | solution.py:49
  160.3 27.8 %copy-start.19 = (bf16[2,64,1024]{2,1,0:T(8,128)(2,1)}, bf16[2,64,1024]{2,1,0:T(8,128)(2,1)S(1)}, u32[]{:S(2)}) copy-start(bf16[2,64,1024]{2,1,0:T(8,128)(2,1)S(1)} %collective-permute-done.25.rest_3_) | copy-start | bytes 786436
  163.3 14.1 %copy-start.14 = (bf16[128,2048]{1,0:T(8,128)(2,1)}, bf16[128,2048]{1,0:T(8,128)(2,1)S(1)}, u32[]{:S(2)}) copy-start(bf16[128,2048]{1,0:T(8,128)(2,1)S(1)} %collective-permute-done.27.refs_2_) | copy-start | bytes 1572868
  163.3 3.0 %copy-start.8 = (bf16[256,2048]{1,0:T(8,128)(2,1)}, bf16[256,2048]{1,0:T(8,128)(2,1)S(1)}, u32[]{:S(2)}) copy-start(bf16[256,2048]{1,0:T(8,128)(2,1)S(1)} %collective-permute-done.26.refs_1_) | copy-start | bytes 3145732
  163.3 12.0 %collective-permute-start.29 = (bf16[128,2048]{1,0:T(8,128)(2,1)S(1)}, bf16[128,2048]{1,0:T(8,128)(2,1)S(1)}, u32[]{:S(2)}, u32[]{:S(2)}) collective-permute-start(bf16[128,2048]{1,0:T(8,128)(2,1)S(1)} %collective-permute-done.27.refs_2_), channel_id=1, source_target_pairs={{0,1},{1,0},{2,3},{3,2},{4,5},{5,4},{6,7},{7,6},{8,9},{9,8},{10,11... | collective-permute-start | bytes 1572872 | tf_op jit(solution)/shard_map/ppermute | solution.py:58
  163.4 14.0 %collective-permute-start.30 = (bf16[128,2048]{1,0:T(8,128)(2,1)}, bf16[128,2048]{1,0:T(8,128)(2,1)S(1)}, u32[]{:S(2)}, u32[]{:S(2)}) collective-permute-start(bf16[128,2048]{1,0:T(8,128)(2,1)} %collective-permute-done.28.refs_3_), channel_id=1, source_target_pairs={{0,1},{1,0},{2,3},{3,2},{4,5},{5,4},{6,7},{7,6},{8,9},{9,8},{10,11... | collective-permute-start | bytes 1572872 | tf_op jit(solution)/shard_map/ppermute | solution.py:58
  163.9 24.2 %collective-permute-start.31 = (bf16[2,2,64,1024]{3,2,1,0:T(8,128)(2,1)}, bf16[2,2,64,1024]{3,2,1,0:T(8,128)(2,1)S(1)}, u32[]{:S(2)}, u32[]{:S(2)}) collective-permute-start(bf16[2,2,64,1024]{3,2,1,0:T(8,128)(2,1)} %get-tuple-element.222), channel_id=1, source_target_pairs={{0,4},{4,0},{8,12},{12,8},{16,20},{20,16},{24,28},{28,24},{32,36},... | collective-permute-start | bytes 1572872 | tf_op jit(solution)/shard_map/ppermute | solution.py:49
  166.3 21.8 %all-to-all-start.3 = ((bf16[8,64,512]{2,1,0:T(8,128)(2,1)}), bf16[8,64,512]{2,1,0:T(8,128)(2,1)S(1)}, u32[]{:S(2)}, u32[]{:S(2)}) async-start(bf16[8,64,512]{2,1,0:T(8,128)(2,1)} %get-tuple-element.213), calls=%async_computation.3 | async-start | bytes 1048576 | tf_op jit(solution)/shard_map/all_to_all | solution.py:45
  173.4 14.7 %collective-permute-start.32 = (bf16[2,64,1024]{2,1,0:T(8,128)(2,1)}, bf16[2,64,1024]{2,1,0:T(8,128)(2,1)}, u32[]{:S(2)}, u32[]{:S(2)}) collective-permute-start(bf16[2,64,1024]{2,1,0:T(8,128)(2,1)} %get-tuple-element.224), channel_id=1, source_target_pairs={{0,8},{4,12},{8,0},{12,4},{16,24},{20,28},{24,16},{28,20},{32,40},... | collective-permute-start | bytes 786440 | tf_op jit(solution)/shard_map/ppermute | solution.py:49
  173.5 14.6 %collective-permute-start.33 = (bf16[2,64,1024]{2,1,0:T(8,128)(2,1)}, bf16[2,64,1024]{2,1,0:T(8,128)(2,1)}, u32[]{:S(2)}, u32[]{:S(2)}) collective-permute-start(bf16[2,64,1024]{2,1,0:T(8,128)(2,1)} %get-tuple-element.225), channel_id=1, source_target_pairs={{0,16},{4,20},{8,24},{12,28},{16,0},{20,4},{24,8},{28,12},{32,48},... | collective-permute-start | bytes 786440 | tf_op jit(solution)/shard_map/ppermute | solution.py:49
  175.3 2.1 %copy-start.15 = (bf16[128,2048]{1,0:T(8,128)(2,1)}, bf16[128,2048]{1,0:T(8,128)(2,1)S(1)}, u32[]{:S(2)}) copy-start(bf16[128,2048]{1,0:T(8,128)(2,1)S(1)} %collective-permute-done.29.refs_4_) | copy-start | bytes 1572868
  175.3 12.8 %collective-permute-start.34 = (bf16[2,64,1024]{2,1,0:T(8,128)(2,1)}, bf16[2,64,1024]{2,1,0:T(8,128)(2,1)}, u32[]{:S(2)}, u32[]{:S(2)}) collective-permute-start(bf16[2,64,1024]{2,1,0:T(8,128)(2,1)} %get-tuple-element.228), channel_id=1, source_target_pairs={{0,128},{4,132},{8,136},{12,140},{16,144},{20,148},{24,152},{28,15... | collective-permute-start | bytes 786440 | tf_op jit(solution)/shard_map/ppermute | solution.py:49
  177.4 0.8 copy-start.16
  188.1 0.8 copy-start.17

commit v8 on v7

--- a/solution.py
+++ b/solution.py
@@ -102,20 +102,21 @@
     return 1 - where[11] % 2
 
 
-def pick_kernel(where, k_ref, v_ref, pair, outer, *outs):
+def pick_kernel(me_ref, slots, gids, k_ref, v_ref, pair, outer, *outs):
     def block(index):
         return pl.ds(pl.multiple_of(index * BLK, BLK), BLK)
 
-    inner = inner_block(where)
+    me = me_ref[0]
+    inner = 1 - me % 2
     for c, src in enumerate((k_ref, v_ref)):
-        pair[0, c] = src[block(where[0]), :]
+        pair[0, c] = src[block(slots[0]), :]
         pair[1, c] = src[block(inner), :]
         outer[c] = src[block(1 - inner), :]
         for b in range(1, BITS):
-            outs[b - 1][c] = src[block(where[b]), :]
+            outs[b - 1][c] = src[block(slots[b]), :]
     picked = outs[BITS - 1]
     for g in range(GLOB):
-        here = where[6 + g]
+        here = jnp.where(gids[g] // 2 == me, gids[g] % 2, -1)
         rows = pl.ds(pl.multiple_of(jnp.maximum(here, 0) * BLK, BLK), BLK)
         for c, src in enumerate((k_ref, v_ref)):
             block = jnp.where(here >= 0, src[rows, :], jnp.zeros((BLK, WIDTH), BF))
@@ -123,18 +124,18 @@
                 picked[half * 4 + c * 2 + g] = block[:, half * HALF : (half + 1) * HALF]
 
 
-def pick(where, keys, values):
+def pick(me, slots, gids, keys, values):
     block = far((2, BLK, WIDTH))
     outs = [far((2, 2, BLK, WIDTH))] + [block] * BITS + [far((CHUNKS, BLK, HALF))]
     vm = pl.BlockSpec(memory_space=pltpu.VMEM)
     return pl.pallas_call(
         pick_kernel,
         out_shape=outs,
-        in_specs=[smem(), vm, vm],
+        in_specs=[smem()] * 3 + [vm, vm],
         out_specs=[vm] * len(outs),
         compiler_params=params(),
         name="pick",
-    )(where, *from_hbm(keys, values))
+    )(me, slots, gids, *from_hbm(keys, values))
 
 
 def gathered_kernel(x_ref, o_ref):
@@ -399,10 +400,9 @@
 
     @pl.when(step > 0)
     def _():
-        part = mm(cols[0][...], grads[0][...], COLS)
-        for a in range(1, 4):
-            part += mm(cols[a][...], grads[a][...], COLS)
-        part = part.astype(BF)
+        left = jnp.concatenate([ref[...] for ref in cols])
+        right = jnp.concatenate([ref[...] for ref in grads])
+        part = mm(left, right, COLS).astype(BF)
         for i in range(2):
             out[:, 32 * i : 32 * i + 32, :] = part[:, HALF * i : HALF * (i + 1)].reshape(
                 CHUNKS, 32, HALF
@@ -560,11 +560,12 @@
 
 def per_device(queries, keys, values, w_out, d_out, rand_slot, global_ids):
     q, k, v, grad_out = queries[0], keys[0], values[0], d_out[0]
-    where = where_of(rand_slot[0, 0], global_ids[0])
-    pair, outer, *chosen, picked = pick(where, k, v)
+    me = jnp.full((1,), lax.axis_index("seq"), jnp.int32)
+    pair, outer, *chosen, picked = pick(me, rand_slot[0, 0], global_ids[0], k, v)
     rand = dict(zip(range(1, BITS), chosen))
     spread = trade(picked)
-    picked, own_grad = together(picked, grad_out)
+    picked, own_grad, slots, gids = together(picked, grad_out, rand_slot[0, 0], global_ids[0])
+    where = where_of(slots, gids)
     grads = [grad_out, across(own_grad, 1), across(own_grad, 2)]
     order = feature_order(lax.axis_index("rep"))
     for b in FIRST:
@@ -598,12 +599,14 @@
     back = dict(zip(range(1, BITS), drand))
     cols, dglob = together(cols, dglob)
     payload = weight_payload(cols, grads, dglob.reshape(CHUNKS, BLK, HALF))
+    payload, w_own = together(payload, w_out)
     payload = trade(payload)
     back[3] = swapped(back[3], 3)
-    payload, pair, outer, back, lower, upper, w_own = together(
-        payload, pair, outer, back, lower, upper, w_out
+    w_core = across(w_own, 1)
+    payload, pair, outer, back, lower, upper, w_core = together(
+        payload, pair, outer, back, lower, upper, w_core
     )
-    parts = [w_out, across(w_own, 1), across(lower, 2), beside(upper)]
+    parts = [w_out, w_core, across(lower, 2), beside(upper)]
     back[4] = swapped(back[4], 4)
     outer = neighboured(outer)
     glob_sum, keep, send = first(where, payload)

time: 193 us -> 189 us (0.979)
  waiting for transfers between devices: 69.4 us -> 66 us
    ppermute x2, waiting for transfers between devices: 3.94 us -> 0.01 us  [neighboured(): lax.ppermute(value, 'seq', [(s, (s - 1 + s % 2 * 2) % 64) for s in range(...]
    ppermute x15, waiting for transfers between devices: 41.3 us -> 44.7 us  [swapped(): return lax.ppermute(value, 'seq', [(s, s ^ 1 << bit) for s in range(64)])]
    all_to_all x4, waiting for transfers between devices: 12.4 us -> 9.46 us  [trade(): lax.all_to_all(value, 'seq', 0, 0, axis_index_groups=YX_GROUPS, tiled=True)]
    unnamed x42 -> x52, local copies, waits for them, and re-layouts: 3.05 us -> 5.11 us
  transfers between devices with their start and end apart: 39 -> 39, of which waited for: 16 -> 14; matrix products, arithmetic and copies ran while one was open for 2% -> 2% of each run, Pallas kernels for 13% -> 13%
where the time goes in v8:
time: 189 us; the launch traced here: 187 us
  starting transfers between devices  76.6 us (41%)
  waiting for transfers between devices  66 us (35%)
  Pallas kernels  34.7 us (18%)
  local copies, waits for them, and re-layouts  6.26 us (3%)
  other arithmetic  2.24 us (1%)
    ppermute x15, waiting for transfers between devices, swapped(): return lax.ppermute(value, 'seq', [(s, s ^ 1 << bit) for s in range(64)])  44.7 us
    ppermute x15, starting transfers between devices, swapped(): return lax.ppermute(value, 'seq', [(s, s ^ 1 << bit) for s in range(64)])  29.4 us
    all_to_all x4, starting transfers between devices, trade(): lax.all_to_all(value, 'seq', 0, 0, axis_index_groups=YX_GROUPS, tiled=True)  24.8 us
    ppermute x4, waiting for transfers between devices, along_z(): return lax.ppermute(value, 'seq', pairs)  10.5 us
    ppermute x4, starting transfers between devices, along_z(): return lax.ppermute(value, 'seq', pairs)  9.84 us
    all_to_all x4, waiting for transfers between devices, trade(): lax.all_to_all(value, 'seq', 0, 0, axis_index_groups=YX_GROUPS, tiled=True)  9.46 us
    pallas_call x1, Pallas kernels, backward(): pl.pallas_call(backward_kernel, grid=(HEADS // STEP,), in_specs=[smem(),...  7.12 us
    ppermute x13, starting transfers between devices, across(): return lax.ppermute(value, 'rep', [(r, r ^ flip) for r in range(4)])  6.29 us
  transfers between devices with their start and end apart: 39, of which 14 were waited for; matrix products, arithmetic and copies ran while one was open for 2% of the time, Pallas kernels for 13%

profile of v8, /device:TPU:8, one launch (start us, length us, event | category | flops | bytes accessed | tf_op | source)
XLA Modules:
  0.0 187.0 jit_solution(11625421621225498157)
XLA Ops:
  0.6 0.6 copy-done.2
  1.3 0.7 copy-done.4
  2.0 2.8 %pick.1 = (bf16[2,2,64,1024]{3,2,1,0:T(8,128)(2,1)}, bf16[2,64,1024]{2,1,0:T(8,128)(2,1)}, bf16[2,64,1024]{2,1,0:T(8,128)(2,1)}, bf16[2,64,1024]{2,1,0:T(8,128)(...) custom-call(s32[1]{0:T(128)} %bitcast.me_ref, ...), custom_call_target="tpu_custom_call" | custom-call | tf_op jit(solution)/shard_map/pick/pallas_call | solution.py:131
  4.8 7.4 %all-to-all-start = ((bf16[8,64,512]{2,1,0:T(8,128)(2,1)}), bf16[8,64,512]{2,1,0:T(8,128)(2,1)S(1)}, u32[]{:S(2)}, u32[]{:S(2)}) async-start(bf16[8,64,512]{2,1,0:T(8,128)(2,1)} %get-tuple-element.123), calls=%async_computation | async-start | bytes 1048576 | tf_op jit(solution)/shard_map/all_to_all | solution.py:45
  12.1 0.6 collective-permute-start.1
  12.7 7.2 %collective-permute-start.2 = (bf16[2,64,1024]{2,1,0:T(8,128)(2,1)}, bf16[2,64,1024]{2,1,0:T(8,128)(2,1)S(1)}, u32[]{:S(2)}, u32[]{:S(2)}) collective-permute-start(bf16[2,64,1024]{2,1,0:T(8,128)(2,1)} %get-tuple-element.131), channel_id=1, source_target_pairs={{0,32},{4,36},{8,40},{12,44},{16,48},{20,52},{24,56},{28,60},{32,0... | collective-permute-start | bytes 786440 | tf_op jit(solution)/shard_map/ppermute | solution.py:49
  19.9 1.1 fusion.37
  21.0 2.2 %fusion.rest_6_ = bf16[1024,1024]{1,0:T(8,128)(2,1)} fusion(s32[1024]{0:T(1024)S(1)} %fusion.15), kind=kLoop, calls=%fused_computation.1 | loop fusion | flops 2097152 | bytes 2101248 | tf_op jit(solution)/shard_map/convert_element_type | solution.py:554
  23.2 5.0 %collective-permute-done.2.rest_2_ = bf16[2,64,1024]{2,1,0:T(8,128)(2,1)S(1)} collective-permute-done((bf16[2,64,1024]{2,1,0:T(8,128)(2,1)}, bf16[2,64,1024]{2,1,0:T(8,128)(2,1)S(1)}, u32[]{:S(2)}, u32[]{:S(2)}) %collective-permute-start.2) | collective-permute-done | bytes 262176 | tf_op jit(solution)/shard_map/ppermute | solution.py:49
  28.2 0.3 collective-permute-done.3.rest_3_
  28.6 1.3 collective-permute-done.1.refs_2_.refs_6_
  30.0 5.9 %collective-permute-start.5 = (bf16[64,512]{1,0:T(8,128)(2,1)S(1)}, bf16[64,512]{1,0:T(8,128)(2,1)S(1)}, u32[]{:S(2)}, u32[]{:S(2)}) collective-permute-start(bf16[64,512]{1,0:T(8,128)(2,1)S(1)} %gathered.1.mine), channel_id=1, source_target_pairs={{0,56},{4,60},{8,0},{12,4},{16,8},{20,12},{24,16},{28,20},{32,24},... | collective-permute-start | bytes 196616 | tf_op jit(solution)/shard_map/ppermute | solution.py:54
  35.9 1.9 %collective-permute-done.5.above = bf16[64,512]{1,0:T(8,128)(2,1)S(1)} collective-permute-done((bf16[64,512]{1,0:T(8,128)(2,1)S(1)}, bf16[64,512]{1,0:T(8,128)(2,1)S(1)}, u32[]{:S(2)}, u32[]{:S(2)}) %collective-permute-start.5) | collective-permute-done | bytes 65568 | tf_op jit(solution)/shard_map/ppermute | solution.py:54
  37.8 3.6 %collective-permute-done.4.below = bf16[64,512]{1,0:T(8,128)(2,1)S(1)} collective-permute-done((bf16[64,512]{1,0:T(8,128)(2,1)S(1)}, bf16[64,512]{1,0:T(8,128)(2,1)S(1)}, u32[]{:S(2)}, u32[]{:S(2)}) %collective-permute-start.4) | collective-permute-done | bytes 65568 | tf_op jit(solution)/shard_map/ppermute | solution.py:54
  41.4 1.4 collective-permute-start.7
  42.9 2.5 %collective-permute-start.6 = (bf16[64,512]{1,0:T(8,128)(2,1)S(1)}, bf16[64,512]{1,0:T(8,128)(2,1)S(1)}, u32[]{:S(2)}, u32[]{:S(2)}) collective-permute-start(bf16[64,512]{1,0:T(8,128)(2,1)S(1)} %get-tuple-element.138.mine), channel_id=1, source_target_pairs={{0,24},{4,28},{8,32},{12,36},{16,40},{20,44},{24,48},{28,52},{32,5... | collective-permute-start | bytes 196616 | tf_op jit(solution)/shard_map/ppermute | solution.py:54
  45.3 2.8 %collective-permute-done.7.above = bf16[64,512]{1,0:T(8,128)(2,1)S(1)} collective-permute-done((bf16[64,512]{1,0:T(8,128)(2,1)S(1)}, bf16[64,512]{1,0:T(8,128)(2,1)S(1)}, u32[]{:S(2)}, u32[]{:S(2)}) %collective-permute-start.7) | collective-permute-done | bytes 65568 | tf_op jit(solution)/shard_map/ppermute | solution.py:54
  48.1 2.2 %collective-permute-done.6.below = bf16[64,512]{1,0:T(8,128)(2,1)S(1)} collective-permute-done((bf16[64,512]{1,0:T(8,128)(2,1)S(1)}, bf16[64,512]{1,0:T(8,128)(2,1)S(1)}, u32[]{:S(2)}, u32[]{:S(2)}) %collective-permute-start.6) | collective-permute-done | bytes 65568 | tf_op jit(solution)/shard_map/ppermute | solution.py:54
  50.4 3.6 %collective-permute-start.9 = (bf16[2,2,64,1024]{3,2,1,0:T(8,128)(2,1)}, bf16[2,2,64,1024]{3,2,1,0:T(8,128)(2,1)S(1)}, u32[]{:S(2)}, u32[]{:S(2)}) collective-permute-start(bf16[2,2,64,1024]{3,2,1,0:T(8,128)(2,1)} %get-tuple-element.158), channel_id=1, source_target_pairs={{0,4},{4,0},{8,12},{12,8},{16,20},{20,16},{24,28},{28,24},{32,36},... | collective-permute-start | bytes 1572872 | tf_op jit(solution)/shard_map/ppermute | solution.py:49
  53.9 0.8 relay.1
  54.8 4.9 %all-to-all-start.1 = ((bf16[8,64,512]{2,1,0:T(8,128)(2,1)}), bf16[8,64,512]{2,1,0:T(8,128)(2,1)S(1)}, u32[]{:S(2)}, u32[]{:S(2)}) async-start(bf16[8,64,512]{2,1,0:T(8,128)(2,1)} %relay.1), calls=%async_computation.1 | async-start | bytes 1048576 | tf_op jit(solution)/shard_map/all_to_all | solution.py:45
  59.7 3.7 %collective-permute-start.10 = (bf16[2,64,1024]{2,1,0:T(8,128)(2,1)}, bf16[2,64,1024]{2,1,0:T(8,128)(2,1)S(1)}, u32[]{:S(2)}, u32[]{:S(2)}) collective-permute-start(bf16[2,64,1024]{2,1,0:T(8,128)(2,1)} %get-tuple-element.159), channel_id=1, source_target_pairs={{0,252},{4,8},{8,4},{12,16},{16,12},{20,24},{24,20},{28,32},{32,28... | collective-permute-start | bytes 786440 | tf_op jit(solution)/shard_map/ppermute | solution.py:98
  63.4 0.7 collective-permute-start.11
  64.1 3.3 %collective-permute-start.12 = (bf16[2,64,1024]{2,1,0:T(8,128)(2,1)}, bf16[2,64,1024]{2,1,0:T(8,128)(2,1)S(1)}, u32[]{:S(2)}, u32[]{:S(2)}) collective-permute-start(bf16[2,64,1024]{2,1,0:T(8,128)(2,1)} %get-tuple-element.161), channel_id=1, source_target_pairs={{0,16},{4,20},{8,24},{12,28},{16,0},{20,4},{24,8},{28,12},{32,48},... | collective-permute-start | bytes 786440 | tf_op jit(solution)/shard_map/ppermute | solution.py:49
  67.4 2.1 %collective-permute-start.13 = (bf16[2,64,1024]{2,1,0:T(8,128)(2,1)}, bf16[2,64,1024]{2,1,0:T(8,128)(2,1)}, u32[]{:S(2)}, u32[]{:S(2)}) collective-permute-start(bf16[2,64,1024]{2,1,0:T(8,128)(2,1)} %get-tuple-element.164), channel_id=1, source_target_pairs={{0,128},{4,132},{8,136},{12,140},{16,144},{20,148},{24,152},{28,15... | collective-permute-start | bytes 786440 | tf_op jit(solution)/shard_map/ppermute | solution.py:49
  69.5 3.3 %project.1 = (bf16[128,256]{1,0:T(8,128)(2,1)S(1)}, bf16[128,256]{1,0:T(8,128)(2,1)S(1)}, bf16[128,256]{1,0:T(8,128)(2,1)S(1)}, bf16[128,256]{1,0:T(8,128)(2,1)S(1)}) custom-call(bf16[256,2048]{1,0:T(8,128)(2,1)} %refs_0_, bf16[128,2048]{1,0:T(8,128)(2,1)} %bitcast.32, bf16[128,2048]{1,0:T(8,128)(2,1)} %copy-done.9, bf16[128,2048]{1,0:T(8,128)(2,1)} %copy-done.8, ...), custom_call_target="tpu_custom_call" | custom-call | tf_op jit(solution)/shard_map/project/pallas_call | solution.py:362
  72.9 8.6 %collective-permute-done.11.rest_0_ = bf16[2,64,1024]{2,1,0:T(8,128)(2,1)S(1)} collective-permute-done((bf16[2,64,1024]{2,1,0:T(8,128)(2,1)}, bf16[2,64,1024]{2,1,0:T(8,128)(2,1)S(1)}, u32[]{:S(2)}, u32[]{:S(2)}) %collective-permute-start.11) | collective-permute-done | bytes 262176 | tf_op jit(solution)/shard_map/ppermute | solution.py:49
  81.5 0.7 copy-done.15
  82.2 0.7 copy-done.16
  83.1 0.9 collective-permute-start.18
  84.0 1.0 collective-permute-start.19
  85.0 6.0 %forward.1 = (bf16[128,1024]{1,0:T(8,128)(2,1)}, f32[8,8,128]{2,1,0:T(8,128)}, bf16[128,256]{1,0:T(8,128)(2,1)S(1)}, bf16[128,256]{1,0:T(8,128)(2,1)S(1)}, bf16[...) custom-call(s32[14]{0:T(128)S(1)} %concatenate.3.where.refs_0_, bf16[128,1024]{1,0:T(8,128)(2,1)} %bitcast.34, ...), custom_call_target="tpu_custom_call" | custom-call | tf_op jit(solution)/shard_map/forward/pallas_call | solution.py:253
  91.0 0.4 collective-permute-start.14
  91.4 0.8 collective-permute-start.15
  92.3 0.7 collective-permute-start.16
  93.0 7.1 %backward.1 = (bf16[128,1024]{1,0:T(8,128)(2,1)}, f32[2,128,1024]{2,1,0:T(8,128)}, bf16[2,2,64,1024]{3,2,1,0:T(8,128)(2,1)}, bf16[2,64,1024]{2,1,0:T(8,128)(2,1)...) custom-call(s32[14]{0:T(128)S(1)} %concatenate.3.where.refs_0_, ...), custom_call_target="tpu_custom_call" | custom-call | tf_op jit(solution)/shard_map/backward/pallas_call | solution.py:321
  100.1 4.1 %weight.1 = bf16[8,192,512]{2,1,0:T(8,128)(2,1)} custom-call(bf16[128,256]{1,0:T(8,128)(2,1)S(1)} %get-tuple-element.184.refs_0_, bf16[128,256]{1,0:T(8,128)(2,1)S(1)} %collective-permute-done.14.refs_1_, bf16[128,256]{1,0:T(8,128)(2,1)S(1)} %collective-permute-done.15.refs_2_, bf16[128,256]{1,0:T(8,128)(2,1)S(1)} %collective-permute-done.16.refs_3_, ...), custom_call_target="tpu_custom_call" | custom-call | tf_op jit(solution)/shard_map/weight/pallas_call | solution.py:413
  104.2 5.0 %all-to-all-start.2 = ((bf16[8,192,512]{2,1,0:T(8,128)(2,1)}), bf16[8,192,512]{2,1,0:T(8,128)(2,1)S(1)}, u32[]{:S(2)}, u32[]{:S(2)}) async-start(bf16[8,192,512]{2,1,0:T(8,128)(2,1)} %weight.1), calls=%async_computation.2 | async-start | bytes 3145728 | tf_op jit(solution)/shard_map/all_to_all | solution.py:45
  109.3 1.9 %collective-permute-start.20 = (bf16[2,64,1024]{2,1,0:T(8,128)(2,1)}, bf16[2,64,1024]{2,1,0:T(8,128)(2,1)S(1)}, u32[]{:S(2)}, u32[]{:S(2)}) collective-permute-start(bf16[2,64,1024]{2,1,0:T(8,128)(2,1)} %get-tuple-element.194), channel_id=1, source_target_pairs={{0,32},{4,36},{8,40},{12,44},{16,48},{20,52},{24,56},{28,60},{32,0... | collective-permute-start | bytes 786440 | tf_op jit(solution)/shard_map/ppermute | solution.py:49
  111.2 13.7 %collective-permute-done.20.rest_2_ = bf16[2,64,1024]{2,1,0:T(8,128)(2,1)S(1)} collective-permute-done((bf16[2,64,1024]{2,1,0:T(8,128)(2,1)}, bf16[2,64,1024]{2,1,0:T(8,128)(2,1)S(1)}, u32[]{:S(2)}, u32[]{:S(2)}) %collective-permute-start.20) | collective-permute-done | bytes 262176 | tf_op jit(solution)/shard_map/ppermute | solution.py:49
  124.9 0.7 copy-done.23
  125.6 5.4 %all-to-all-done.2.refs_1_ = bf16[8,192,512]{2,1,0:T(8,128)(2,1)S(1)} async-done(((bf16[8,192,512]{2,1,0:T(8,128)(2,1)}), bf16[8,192,512]{2,1,0:T(8,128)(2,1)S(1)}, u32[]{:S(2)}, u32[]{:S(2)}) %all-to-all-start.2) | async-done | bytes 1572896 | tf_op jit(solution)/shard_map/all_to_all | solution.py:45
  131.0 0.9 collective-permute-start.27
  131.9 0.9 collective-permute-start.28
  132.8 0.7 first.1
  133.5 2.6 %collective-permute-start.22 = (bf16[128,512]{1,0:T(8,128)(2,1)S(1)}, bf16[128,512]{1,0:T(8,128)(2,1)S(1)}, u32[]{:S(2)}, u32[]{:S(2)}) collective-permute-start(bf16[128,512]{1,0:T(8,128)(2,1)S(1)} %get-tuple-element.203), channel_id=1, source_target_pairs={{0,8},{4,12},{8,0},{12,4},{16,24},{20,28},{24,16},{28,20},{32,40},... | collective-permute-start | bytes 393224 | tf_op jit(solution)/shard_map/ppermute | solution.py:49
  136.2 1.8 collective-permute-start.25
  137.9 1.5 collective-permute-start.26
  139.4 0.6 fold.2
  140.0 2.0 %collective-permute-start.23 = (bf16[96,512]{1,0:T(8,128)(2,1)S(1)}, bf16[96,512]{1,0:T(8,128)(2,1)S(1)}, u32[]{:S(2)}, u32[]{:S(2)}) collective-permute-start(bf16[96,512]{1,0:T(8,128)(2,1)S(1)} %get-tuple-element.206), channel_id=1, source_target_pairs={{0,16},{4,20},{8,24},{12,28},{16,0},{20,4},{24,8},{28,12},{32,48},... | collective-permute-start | bytes 294920 | tf_op jit(solution)/shard_map/ppermute | solution.py:49
  142.0 8.0 %collective-permute-done.23.refs_3_ = bf16[96,512]{1,0:T(8,128)(2,1)S(1)} collective-permute-done((bf16[96,512]{1,0:T(8,128)(2,1)S(1)}, bf16[96,512]{1,0:T(8,128)(2,1)S(1)}, u32[]{:S(2)}, u32[]{:S(2)}) %collective-permute-start.23) | collective-permute-done | bytes 98336 | tf_op jit(solution)/shard_map/ppermute | solution.py:49
  150.0 0.6 fold.3
  150.8 8.3 %collective-permute-done.24.came = bf16[80,512]{1,0:T(8,128)(2,1)S(1)} collective-permute-done((bf16[80,512]{1,0:T(8,128)(2,1)S(1)}, bf16[80,512]{1,0:T(8,128)(2,1)S(1)}, u32[]{:S(2)}, u32[]{:S(2)}) %collective-permute-start.24) | collective-permute-done | bytes 81952 | tf_op jit(solution)/shard_map/ppermute | solution.py:49
  159.4 0.5 collective-permute-start.30
  159.9 1.4 last.1
  161.3 7.5 %all-to-all-start.3 = ((bf16[8,64,512]{2,1,0:T(8,128)(2,1)}), bf16[8,64,512]{2,1,0:T(8,128)(2,1)S(1)}, u32[]{:S(2)}, u32[]{:S(2)}) async-start(bf16[8,64,512]{2,1,0:T(8,128)(2,1)} %get-tuple-element.221), calls=%async_computation.3 | async-start | bytes 1048576 | tf_op jit(solution)/shard_map/all_to_all | solution.py:45
  168.8 2.3 %collective-permute-start.33 = (bf16[2,64,1024]{2,1,0:T(8,128)(2,1)}, bf16[2,64,1024]{2,1,0:T(8,128)(2,1)}, u32[]{:S(2)}, u32[]{:S(2)}) collective-permute-start(bf16[2,64,1024]{2,1,0:T(8,128)(2,1)} %get-tuple-element.233), channel_id=1, source_target_pairs={{0,16},{4,20},{8,24},{12,28},{16,0},{20,4},{24,8},{28,12},{32,48},... | collective-permute-start | bytes 786440 | tf_op jit(solution)/shard_map/ppermute | solution.py:49
  171.2 2.1 %collective-permute-start.34 = (bf16[2,64,1024]{2,1,0:T(8,128)(2,1)}, bf16[2,64,1024]{2,1,0:T(8,128)(2,1)}, u32[]{:S(2)}, u32[]{:S(2)}) collective-permute-start(bf16[2,64,1024]{2,1,0:T(8,128)(2,1)} %get-tuple-element.236), channel_id=1, source_target_pairs={{0,128},{4,132},{8,136},{12,140},{16,144},{20,148},{24,152},{28,15... | collective-permute-start | bytes 786440 | tf_op jit(solution)/shard_map/ppermute | solution.py:49
  173.3 0.8 copy-done.20
  174.1 4.3 %layer.1 = bf16[128,2048]{1,0:T(8,128)(2,1)} custom-call(s32[14]{0:T(128)S(1)} %concatenate.3.where.refs_0_, bf16[256,2048]{1,0:T(8,128)(2,1)} %refs_0_, bf16[256,2048]{1,0:T(8,128)(2,1)} %collective-permute-done.21.refs_1_, bf16[128,2048]{1,0:T(8,128)(2,1)} %copy-done.17, bf16[128,2048]{1,0:T(8,128)(2,1)} %copy-done.18, bf16[128,2048]{1,0:T(8,128)(2,1)} %copy-done.19, ...), custom_call_target="tpu_custom_call" | custom-call | tf_op jit(solution)/shard_map/layer/pallas_call | solution.py:378
  178.4 4.1 %all-to-all-done.3 = bf16[8,64,512]{2,1,0:T(8,128)(2,1)S(1)} async-done(((bf16[8,64,512]{2,1,0:T(8,128)(2,1)}), bf16[8,64,512]{2,1,0:T(8,128)(2,1)S(1)}, u32[]{:S(2)}, u32[]{:S(2)}) %all-to-all-start.3) | async-done | bytes 524320 | tf_op jit(solution)/shard_map/all_to_all | solution.py:45
  182.4 0.7 collective-permute-done.33.rest_1_
  183.2 0.8 copy-done.22
  184.0 2.9 %finish.1 = (bf16[128,1024]{1,0:T(8,128)(2,1)}, bf16[128,1024]{1,0:T(8,128)(2,1)}) custom-call(s32[14]{0:T(128)S(1)} %concatenate.3.where.refs_0_, f32[2,128,1024]{2,1,0:T(8,128)} %get-tuple-element.229.own, bf16[2,2,64,1024]{3,2,1,0:T(8,128)(2,1)} %copy-done.22, bf16[2,64,1024]{2,1,0:T(8,128)(2,1)} %copy-done.24, ...), custom_call_target="tpu_custom_call" | custom-call | tf_op jit(solution)/shard_map/finish/pallas_call | solution.py:534
  (86 shorter events, 1.0 us)
Async XLA Ops:
  0.6 0.7 copy-start.2
  2.0 18.0 %copy-start.6 = (bf16[256,2048]{1,0:T(8,128)(2,1)S(1)}, bf16[256,2048]{1,0:T(8,128)(2,1)}, u32[]{:S(2)}) copy-start(bf16[256,2048]{1,0:T(8,128)(2,1)} %refs_0_) | copy-start | bytes 3145732
  4.8 23.8 %all-to-all-start = ((bf16[8,64,512]{2,1,0:T(8,128)(2,1)}), bf16[8,64,512]{2,1,0:T(8,128)(2,1)S(1)}, u32[]{:S(2)}, u32[]{:S(2)}) async-start(bf16[8,64,512]{2,1,0:T(8,128)(2,1)} %get-tuple-element.123), calls=%async_computation | async-start | bytes 1048576 | tf_op jit(solution)/shard_map/all_to_all | solution.py:45
  12.1 17.8 %collective-permute-start.1 = (bf16[128,2048]{1,0:T(8,128)(2,1)}, bf16[128,2048]{1,0:T(8,128)(2,1)S(1)}, u32[]{:S(2)}, u32[]{:S(2)}) collective-permute-start(bf16[128,2048]{1,0:T(8,128)(2,1)} %bitcast.30), channel_id=1, source_target_pairs={{0,2},{1,3},{2,0},{3,1},{4,6},{5,7},{6,4},{7,5},{8,10},{9,11},{10,... | collective-permute-start | bytes 1572872 | tf_op jit(solution)/shard_map/ppermute | solution.py:58
  12.7 17.2 %collective-permute-start = (bf16[128,2048]{1,0:T(8,128)(2,1)}, bf16[128,2048]{1,0:T(8,128)(2,1)S(1)}, u32[]{:S(2)}, u32[]{:S(2)}) collective-permute-start(bf16[128,2048]{1,0:T(8,128)(2,1)} %bitcast.31), channel_id=1, source_target_pairs={{0,1},{1,0},{2,3},{3,2},{4,5},{5,4},{6,7},{7,6},{8,9},{9,8},{10,11... | collective-permute-start | bytes 1572872 | tf_op jit(solution)/shard_map/ppermute | solution.py:58
  12.7 15.5 %collective-permute-start.2 = (bf16[2,64,1024]{2,1,0:T(8,128)(2,1)}, bf16[2,64,1024]{2,1,0:T(8,128)(2,1)S(1)}, u32[]{:S(2)}, u32[]{:S(2)}) collective-permute-start(bf16[2,64,1024]{2,1,0:T(8,128)(2,1)} %get-tuple-element.131), channel_id=1, source_target_pairs={{0,32},{4,36},{8,40},{12,44},{16,48},{20,52},{24,56},{28,60},{32,0... | collective-permute-start | bytes 786440 | tf_op jit(solution)/shard_map/ppermute | solution.py:49
  19.9 8.6 %collective-permute-start.3 = (bf16[2,64,1024]{2,1,0:T(8,128)(2,1)}, bf16[2,64,1024]{2,1,0:T(8,128)(2,1)S(1)}, u32[]{:S(2)}, u32[]{:S(2)}) collective-permute-start(bf16[2,64,1024]{2,1,0:T(8,128)(2,1)} %get-tuple-element.132), channel_id=1, source_target_pairs={{0,64},{4,68},{8,72},{12,76},{16,80},{20,84},{24,88},{28,92},{32,9... | collective-permute-start | bytes 786440 | tf_op jit(solution)/shard_map/ppermute | solution.py:49
  21.0 48.5 %copy-start.3 = (s32[1,2]{1,0:T(1,128)S(1)}, s32[1,2]{1,0:T(1,128)}, u32[]{:S(2)}) copy-start(s32[1,2]{1,0:T(1,128)} %param.13) | copy-start | bytes 28
  28.2 44.6 %copy-start.12 = (bf16[2,64,1024]{2,1,0:T(8,128)(2,1)}, bf16[2,64,1024]{2,1,0:T(8,128)(2,1)S(1)}, u32[]{:S(2)}) copy-start(bf16[2,64,1024]{2,1,0:T(8,128)(2,1)S(1)} %collective-permute-done.2.rest_2_) | copy-start | bytes 786436
  28.6 44.3 %copy-start.13 = (bf16[2,64,1024]{2,1,0:T(8,128)(2,1)}, bf16[2,64,1024]{2,1,0:T(8,128)(2,1)S(1)}, u32[]{:S(2)}) copy-start(bf16[2,64,1024]{2,1,0:T(8,128)(2,1)S(1)} %collective-permute-done.3.rest_3_) | copy-start | bytes 786436
  29.9 39.6 %copy-start.8 = (bf16[128,2048]{1,0:T(8,128)(2,1)}, bf16[128,2048]{1,0:T(8,128)(2,1)S(1)}, u32[]{:S(2)}) copy-start(bf16[128,2048]{1,0:T(8,128)(2,1)S(1)} %collective-permute-done.1.refs_2_.refs_6_) | copy-start | bytes 1572868
  29.9 39.6 %copy-start.9 = (bf16[128,2048]{1,0:T(8,128)(2,1)}, bf16[128,2048]{1,0:T(8,128)(2,1)S(1)}, u32[]{:S(2)}) copy-start(bf16[128,2048]{1,0:T(8,128)(2,1)S(1)} %collective-permute-done.refs_1_.refs_5_) | copy-start | bytes 1572868
  30.0 7.8 %collective-permute-start.5 = (bf16[64,512]{1,0:T(8,128)(2,1)S(1)}, bf16[64,512]{1,0:T(8,128)(2,1)S(1)}, u32[]{:S(2)}, u32[]{:S(2)}) collective-permute-start(bf16[64,512]{1,0:T(8,128)(2,1)S(1)} %gathered.1.mine), channel_id=1, source_target_pairs={{0,56},{4,60},{8,0},{12,4},{16,8},{20,12},{24,16},{28,20},{32,24},... | collective-permute-start | bytes 196616 | tf_op jit(solution)/shard_map/ppermute | solution.py:54
  35.9 5.5 %collective-permute-start.4 = (bf16[64,512]{1,0:T(8,128)(2,1)S(1)}, bf16[64,512]{1,0:T(8,128)(2,1)S(1)}, u32[]{:S(2)}, u32[]{:S(2)}) collective-permute-start(bf16[64,512]{1,0:T(8,128)(2,1)S(1)} %gathered.1.mine), channel_id=1, source_target_pairs={{0,8},{4,12},{8,16},{12,20},{16,24},{20,28},{24,32},{28,36},{32,40... | collective-permute-start | bytes 196616 | tf_op jit(solution)/shard_map/ppermute | solution.py:54
  41.4 6.7 %collective-permute-start.7 = (bf16[64,512]{1,0:T(8,128)(2,1)S(1)}, bf16[64,512]{1,0:T(8,128)(2,1)S(1)}, u32[]{:S(2)}, u32[]{:S(2)}) collective-permute-start(bf16[64,512]{1,0:T(8,128)(2,1)S(1)} %get-tuple-element.139), channel_id=1, source_target_pairs={{0,40},{4,44},{8,48},{12,52},{16,56},{20,60},{24,0},{28,4},{32,8},... | collective-permute-start | bytes 196616 | tf_op jit(solution)/shard_map/ppermute | solution.py:54
  42.9 7.5 %collective-permute-start.6 = (bf16[64,512]{1,0:T(8,128)(2,1)S(1)}, bf16[64,512]{1,0:T(8,128)(2,1)S(1)}, u32[]{:S(2)}, u32[]{:S(2)}) collective-permute-start(bf16[64,512]{1,0:T(8,128)(2,1)S(1)} %get-tuple-element.138.mine), channel_id=1, source_target_pairs={{0,24},{4,28},{8,32},{12,36},{16,40},{20,44},{24,48},{28,52},{32,5... | collective-permute-start | bytes 196616 | tf_op jit(solution)/shard_map/ppermute | solution.py:54
  50.3 17.0 %collective-permute-start.8 = (bf16[128,2048]{1,0:T(8,128)(2,1)S(1)}, bf16[128,2048]{1,0:T(8,128)(2,1)S(1)}, u32[]{:S(2)}, u32[]{:S(2)}) collective-permute-start(bf16[128,2048]{1,0:T(8,128)(2,1)S(1)} %collective-permute-done.1.refs_2_.refs_6_), channel_id=1, source_target_pairs={{0,1},{1,0},{2,3},{3,2},{4,5},{5,4},{6,7},{7,6},{8,9},{9,8},{10,11... | collective-permute-start | bytes 1572872 | tf_op jit(solution)/shard_map/ppermute | solution.py:58
  50.4 32.5 %collective-permute-start.9 = (bf16[2,2,64,1024]{3,2,1,0:T(8,128)(2,1)}, bf16[2,2,64,1024]{3,2,1,0:T(8,128)(2,1)S(1)}, u32[]{:S(2)}, u32[]{:S(2)}) collective-permute-start(bf16[2,2,64,1024]{3,2,1,0:T(8,128)(2,1)} %get-tuple-element.158), channel_id=1, source_target_pairs={{0,4},{4,0},{8,12},{12,8},{16,20},{20,16},{24,28},{28,24},{32,36},... | collective-permute-start | bytes 1572872 | tf_op jit(solution)/shard_map/ppermute | solution.py:49
  54.8 28.3 %copy-start.5 = (s32[1,1,6]{2,1,0:T(1,128)S(1)}, s32[1,1,6]{2,1,0:T(1,128)}, u32[]{:S(2)}) copy-start(s32[1,1,6]{2,1,0:T(1,128)} %param.12) | copy-start | bytes 76
  54.8 28.1 %all-to-all-start.1 = ((bf16[8,64,512]{2,1,0:T(8,128)(2,1)}), bf16[8,64,512]{2,1,0:T(8,128)(2,1)S(1)}, u32[]{:S(2)}, u32[]{:S(2)}) async-start(bf16[8,64,512]{2,1,0:T(8,128)(2,1)} %relay.1), calls=%async_computation.1 | async-start | bytes 1048576 | tf_op jit(solution)/shard_map/all_to_all | solution.py:45
  59.7 13.2 %collective-permute-start.10 = (bf16[2,64,1024]{2,1,0:T(8,128)(2,1)}, bf16[2,64,1024]{2,1,0:T(8,128)(2,1)S(1)}, u32[]{:S(2)}, u32[]{:S(2)}) collective-permute-start(bf16[2,64,1024]{2,1,0:T(8,128)(2,1)} %get-tuple-element.159), channel_id=1, source_target_pairs={{0,252},{4,8},{8,4},{12,16},{16,12},{20,24},{24,20},{28,32},{32,28... | collective-permute-start | bytes 786440 | tf_op jit(solution)/shard_map/ppermute | solution.py:98
  63.4 18.1 %collective-permute-start.11 = (bf16[2,64,1024]{2,1,0:T(8,128)(2,1)}, bf16[2,64,1024]{2,1,0:T(8,128)(2,1)S(1)}, u32[]{:S(2)}, u32[]{:S(2)}) collective-permute-start(bf16[2,64,1024]{2,1,0:T(8,128)(2,1)} %get-tuple-element.160), channel_id=1, source_target_pairs={{0,8},{4,12},{8,0},{12,4},{16,24},{20,28},{24,16},{28,20},{32,40},... | collective-permute-start | bytes 786440 | tf_op jit(solution)/shard_map/ppermute | solution.py:49
  64.1 17.4 %collective-permute-start.12 = (bf16[2,64,1024]{2,1,0:T(8,128)(2,1)}, bf16[2,64,1024]{2,1,0:T(8,128)(2,1)S(1)}, u32[]{:S(2)}, u32[]{:S(2)}) collective-permute-start(bf16[2,64,1024]{2,1,0:T(8,128)(2,1)} %get-tuple-element.161), channel_id=1, source_target_pairs={{0,16},{4,20},{8,24},{12,28},{16,0},{20,4},{24,8},{28,12},{32,48},... | collective-permute-start | bytes 786440 | tf_op jit(solution)/shard_map/ppermute | solution.py:49
  67.4 2.1 %copy-start.10 = (bf16[128,2048]{1,0:T(8,128)(2,1)}, bf16[128,2048]{1,0:T(8,128)(2,1)S(1)}, u32[]{:S(2)}) copy-start(bf16[128,2048]{1,0:T(8,128)(2,1)S(1)} %collective-permute-done.8.refs_3_.refs_7_) | copy-start | bytes 1572868
  67.4 15.5 %collective-permute-start.13 = (bf16[2,64,1024]{2,1,0:T(8,128)(2,1)}, bf16[2,64,1024]{2,1,0:T(8,128)(2,1)}, u32[]{:S(2)}, u32[]{:S(2)}) collective-permute-start(bf16[2,64,1024]{2,1,0:T(8,128)(2,1)} %get-tuple-element.164), channel_id=1, source_target_pairs={{0,128},{4,132},{8,136},{12,140},{16,144},{20,148},{24,152},{28,15... | collective-permute-start | bytes 786440 | tf_op jit(solution)/shard_map/ppermute | solution.py:49
  72.9 8.6 %copy-start.14 = (bf16[2,64,1024]{2,1,0:T(8,128)(2,1)}, bf16[2,64,1024]{2,1,0:T(8,128)(2,1)S(1)}, u32[]{:S(2)}) copy-start(bf16[2,64,1024]{2,1,0:T(8,128)(2,1)S(1)} %collective-permute-done.10.outer) | copy-start | bytes 786436
  81.5 0.7 copy-start.15
  82.2 0.7 copy-start.16
  82.9 8.1 %copy-start = (bf16[8,64,512]{2,1,0:T(8,128)(2,1)}, bf16[8,64,512]{2,1,0:T(8,128)(2,1)S(1)}, u32[]{:S(2)}) copy-start(bf16[8,64,512]{2,1,0:T(8,128)(2,1)S(1)} %all-to-all-done.1) | copy-start | bytes 1572868
  82.9 2.1 %copy-start.11 = (bf16[2,2,64,1024]{3,2,1,0:T(8,128)(2,1)}, bf16[2,2,64,1024]{3,2,1,0:T(8,128)(2,1)S(1)}, u32[]{:S(2)}) copy-start(bf16[2,2,64,1024]{3,2,1,0:T(8,128)(2,1)S(1)} %collective-permute-done.9.pair) | copy-start | bytes 1572868
  82.9 9.4 %collective-permute-start.17 = (bf16[128,256]{1,0:T(8,128)(2,1)S(1)}, bf16[128,256]{1,0:T(8,128)(2,1)S(1)}, u32[]{:S(2)}, u32[]{:S(2)}) collective-permute-start(bf16[128,256]{1,0:T(8,128)(2,1)S(1)} %get-tuple-element.180), channel_id=1, source_target_pairs={{0,1},{1,0},{2,3},{3,2},{4,5},{5,4},{6,7},{7,6},{8,9},{9,8},{10,11... | collective-permute-start | bytes 196616 | tf_op jit(solution)/shard_map/ppermute | solution.py:58
  83.1 9.8 %collective-permute-start.18 = (bf16[128,256]{1,0:T(8,128)(2,1)S(1)}, bf16[128,256]{1,0:T(8,128)(2,1)S(1)}, u32[]{:S(2)}, u32[]{:S(2)}) collective-permute-start(bf16[128,256]{1,0:T(8,128)(2,1)S(1)} %get-tuple-element.181), channel_id=1, source_target_pairs={{0,2},{1,3},{2,0},{3,1},{4,6},{5,7},{6,4},{7,5},{8,10},{9,11},{10,... | collective-permute-start | bytes 196616 | tf_op jit(solution)/shard_map/ppermute | solution.py:58
  84.0 9.0 %collective-permute-start.19 = (bf16[128,256]{1,0:T(8,128)(2,1)S(1)}, bf16[128,256]{1,0:T(8,128)(2,1)S(1)}, u32[]{:S(2)}, u32[]{:S(2)}) collective-permute-start(bf16[128,256]{1,0:T(8,128)(2,1)S(1)} %get-tuple-element.182), channel_id=1, source_target_pairs={{0,3},{1,2},{2,1},{3,0},{4,7},{5,6},{6,5},{7,4},{8,11},{9,10},{10,... | collective-permute-start | bytes 196616 | tf_op jit(solution)/shard_map/ppermute | solution.py:58
  91.0 9.1 %collective-permute-start.14 = (bf16[128,256]{1,0:T(8,128)(2,1)S(1)}, bf16[128,256]{1,0:T(8,128)(2,1)S(1)}, u32[]{:S(2)}, u32[]{:S(2)}) collective-permute-start(bf16[128,256]{1,0:T(8,128)(2,1)S(1)} %get-tuple-element.175), channel_id=1, source_target_pairs={{0,1},{1,0},{2,3},{3,2},{4,5},{5,4},{6,7},{7,6},{8,9},{9,8},{10,11... | collective-permute-start | bytes 196616 | tf_op jit(solution)/shard_map/ppermute | solution.py:58
  91.4 8.7 %collective-permute-start.15 = (bf16[128,256]{1,0:T(8,128)(2,1)S(1)}, bf16[128,256]{1,0:T(8,128)(2,1)S(1)}, u32[]{:S(2)}, u32[]{:S(2)}) collective-permute-start(bf16[128,256]{1,0:T(8,128)(2,1)S(1)} %get-tuple-element.176), channel_id=1, source_target_pairs={{0,2},{1,3},{2,0},{3,1},{4,6},{5,7},{6,4},{7,5},{8,10},{9,11},{10,... | collective-permute-start | bytes 196616 | tf_op jit(solution)/shard_map/ppermute | solution.py:58
  92.3 7.9 %collective-permute-start.16 = (bf16[128,256]{1,0:T(8,128)(2,1)S(1)}, bf16[128,256]{1,0:T(8,128)(2,1)S(1)}, u32[]{:S(2)}, u32[]{:S(2)}) collective-permute-start(bf16[128,256]{1,0:T(8,128)(2,1)S(1)} %get-tuple-element.177), channel_id=1, source_target_pairs={{0,3},{1,2},{2,1},{3,0},{4,7},{5,6},{6,5},{7,4},{8,11},{9,10},{10,... | collective-permute-start | bytes 196616 | tf_op jit(solution)/shard_map/ppermute | solution.py:58
  104.2 5.0 %copy-start.7 = (bf16[256,2048]{1,0:T(8,128)(2,1)S(1)}, bf16[256,2048]{1,0:T(8,128)(2,1)}, u32[]{:S(2)}) copy-start(bf16[256,2048]{1,0:T(8,128)(2,1)} %refs_0_) | copy-start | bytes 3145732
  104.2 27.7 %copy-start.21 = (bf16[128,2048]{1,0:T(8,128)(2,1)S(1)}, bf16[128,2048]{1,0:T(8,128)(2,1)}, u32[]{:S(2)}) copy-start(bf16[128,2048]{1,0:T(8,128)(2,1)} %get-tuple-element.219) | copy-start | bytes 1572868
  104.2 26.8 %all-to-all-start.2 = ((bf16[8,192,512]{2,1,0:T(8,128)(2,1)}), bf16[8,192,512]{2,1,0:T(8,128)(2,1)S(1)}, u32[]{:S(2)}, u32[]{:S(2)}) async-start(bf16[8,192,512]{2,1,0:T(8,128)(2,1)} %weight.1), calls=%async_computation.2 | async-start | bytes 3145728 | tf_op jit(solution)/shard_map/all_to_all | solution.py:45
  109.2 64.9 %copy-start.1 = (bf16[128,1024]{1,0:T(8,128)(2,1)S(1)}, bf16[128,1024]{1,0:T(8,128)(2,1)}, u32[]{:S(2)}) copy-start(bf16[128,1024]{1,0:T(8,128)(2,1)} %get-tuple-element.226.refs_6_) | copy-start | bytes 786436
  109.2 16.4 %collective-permute-start.21 = (bf16[256,2048]{1,0:T(8,128)(2,1)S(1)}, bf16[256,2048]{1,0:T(8,128)(2,1)}, u32[]{:S(2)}, u32[]{:S(2)}) collective-permute-start(bf16[256,2048]{1,0:T(8,128)(2,1)S(1)} %copy-done.7), channel_id=1, source_target_pairs={{0,1},{1,0},{2,3},{3,2},{4,5},{5,4},{6,7},{7,6},{8,9},{9,8},{10,11... | collective-permute-start | bytes 3145736 | tf_op jit(solution)/shard_map/ppermute | solution.py:58
  109.3 15.6 %collective-permute-start.20 = (bf16[2,64,1024]{2,1,0:T(8,128)(2,1)}, bf16[2,64,1024]{2,1,0:T(8,128)(2,1)S(1)}, u32[]{:S(2)}, u32[]{:S(2)}) collective-permute-start(bf16[2,64,1024]{2,1,0:T(8,128)(2,1)} %get-tuple-element.194), channel_id=1, source_target_pairs={{0,32},{4,36},{8,40},{12,44},{16,48},{20,52},{24,56},{28,60},{32,0... | collective-permute-start | bytes 786440 | tf_op jit(solution)/shard_map/ppermute | solution.py:49
  124.9 0.7 copy-start.23
  131.0 28.0 %collective-permute-start.27 = (bf16[128,2048]{1,0:T(8,128)(2,1)}, bf16[128,2048]{1,0:T(8,128)(2,1)S(1)}, u32[]{:S(2)}, u32[]{:S(2)}) collective-permute-start(bf16[128,2048]{1,0:T(8,128)(2,1)} %get-tuple-element.218), channel_id=1, source_target_pairs={{0,2},{1,3},{2,0},{3,1},{4,6},{5,7},{6,4},{7,5},{8,10},{9,11},{10,... | collective-permute-start | bytes 1572872 | tf_op jit(solution)/shard_map/ppermute | solution.py:58
  131.9 27.2 %collective-permute-start.28 = (bf16[128,2048]{1,0:T(8,128)(2,1)S(1)}, bf16[128,2048]{1,0:T(8,128)(2,1)S(1)}, u32[]{:S(2)}, u32[]{:S(2)}) collective-permute-start(bf16[128,2048]{1,0:T(8,128)(2,1)S(1)} %copy-done.21), channel_id=1, source_target_pairs={{0,6},{1,7},{2,4},{3,5},{4,2},{5,3},{6,0},{7,1},{8,14},{9,15},{10,... | collective-permute-start | bytes 1572872 | tf_op jit(solution)/shard_map/ppermute | solution.py:63
  133.5 5.9 %collective-permute-start.22 = (bf16[128,512]{1,0:T(8,128)(2,1)S(1)}, bf16[128,512]{1,0:T(8,128)(2,1)S(1)}, u32[]{:S(2)}, u32[]{:S(2)}) collective-permute-start(bf16[128,512]{1,0:T(8,128)(2,1)S(1)} %get-tuple-element.203), channel_id=1, source_target_pairs={{0,8},{4,12},{8,0},{12,4},{16,24},{20,28},{24,16},{28,20},{32,40},... | collective-permute-start | bytes 393224 | tf_op jit(solution)/shard_map/ppermute | solution.py:49
  136.2 14.6 %collective-permute-start.25 = (bf16[2,64,1024]{2,1,0:T(8,128)(2,1)}, bf16[2,64,1024]{2,1,0:T(8,128)(2,1)S(1)}, u32[]{:S(2)}, u32[]{:S(2)}) collective-permute-start(bf16[2,64,1024]{2,1,0:T(8,128)(2,1)} %get-tuple-element.211), channel_id=1, source_target_pairs={{0,252},{4,8},{8,4},{12,16},{16,12},{20,24},{24,20},{28,32},{32,28... | collective-permute-start | bytes 786440 | tf_op jit(solution)/shard_map/ppermute | solution.py:98
  137.9 12.8 %collective-permute-start.26 = (bf16[2,64,1024]{2,1,0:T(8,128)(2,1)}, bf16[2,64,1024]{2,1,0:T(8,128)(2,1)S(1)}, u32[]{:S(2)}, u32[]{:S(2)}) collective-permute-start(bf16[2,64,1024]{2,1,0:T(8,128)(2,1)} %get-tuple-element.215), channel_id=1, source_target_pairs={{0,64},{4,68},{8,72},{12,76},{16,80},{20,84},{24,88},{28,92},{32,9... | collective-permute-start | bytes 786440 | tf_op jit(solution)/shard_map/ppermute | solution.py:49
  140.0 10.1 %collective-permute-start.23 = (bf16[96,512]{1,0:T(8,128)(2,1)S(1)}, bf16[96,512]{1,0:T(8,128)(2,1)S(1)}, u32[]{:S(2)}, u32[]{:S(2)}) collective-permute-start(bf16[96,512]{1,0:T(8,128)(2,1)S(1)} %get-tuple-element.206), channel_id=1, source_target_pairs={{0,16},{4,20},{8,24},{12,28},{16,0},{20,4},{24,8},{28,12},{32,48},... | collective-permute-start | bytes 294920 | tf_op jit(solution)/shard_map/ppermute | solution.py:49
  150.6 8.4 %collective-permute-start.24 = (bf16[80,512]{1,0:T(8,128)(2,1)S(1)}, bf16[80,512]{1,0:T(8,128)(2,1)S(1)}, u32[]{:S(2)}, u32[]{:S(2)}) collective-permute-start(bf16[80,512]{1,0:T(8,128)(2,1)S(1)} %get-tuple-element.209), channel_id=1, source_target_pairs={{0,32},{4,36},{8,40},{12,44},{16,48},{20,52},{24,56},{28,60},{32,0... | collective-permute-start | bytes 245768 | tf_op jit(solution)/shard_map/ppermute | solution.py:49
  150.7 10.6 %copy-start.24 = (bf16[2,64,1024]{2,1,0:T(8,128)(2,1)}, bf16[2,64,1024]{2,1,0:T(8,128)(2,1)S(1)}, u32[]{:S(2)}) copy-start(bf16[2,64,1024]{2,1,0:T(8,128)(2,1)S(1)} %collective-permute-done.25.outer) | copy-start | bytes 786436
  150.7 8.3 %copy-start.25 = (bf16[2,64,1024]{2,1,0:T(8,128)(2,1)}, bf16[2,64,1024]{2,1,0:T(8,128)(2,1)S(1)}, u32[]{:S(2)}) copy-start(bf16[2,64,1024]{2,1,0:T(8,128)(2,1)S(1)} %collective-permute-done.26.rest_3_) | copy-start | bytes 786436
  159.1 14.2 %copy-start.17 = (bf16[128,2048]{1,0:T(8,128)(2,1)}, bf16[128,2048]{1,0:T(8,128)(2,1)S(1)}, u32[]{:S(2)}) copy-start(bf16[128,2048]{1,0:T(8,128)(2,1)S(1)} %collective-permute-done.27.refs_2_) | copy-start | bytes 1572868
  159.1 14.2 %copy-start.18 = (bf16[128,2048]{1,0:T(8,128)(2,1)}, bf16[128,2048]{1,0:T(8,128)(2,1)S(1)}, u32[]{:S(2)}) copy-start(bf16[128,2048]{1,0:T(8,128)(2,1)S(1)} %collective-permute-done.28.refs_3_) | copy-start | bytes 1572868
  159.1 12.1 %collective-permute-start.29 = (bf16[128,2048]{1,0:T(8,128)(2,1)S(1)}, bf16[128,2048]{1,0:T(8,128)(2,1)S(1)}, u32[]{:S(2)}, u32[]{:S(2)}) collective-permute-start(bf16[128,2048]{1,0:T(8,128)(2,1)S(1)} %collective-permute-done.27.refs_2_), channel_id=1, source_target_pairs={{0,1},{1,0},{2,3},{3,2},{4,5},{5,4},{6,7},{7,6},{8,9},{9,8},{10,11... | collective-permute-start | bytes 1572872 | tf_op jit(solution)/shard_map/ppermute | solution.py:58
  159.4 13.9 %collective-permute-start.30 = (bf16[128,2048]{1,0:T(8,128)(2,1)S(1)}, bf16[128,2048]{1,0:T(8,128)(2,1)S(1)}, u32[]{:S(2)}, u32[]{:S(2)}) collective-permute-start(bf16[128,2048]{1,0:T(8,128)(2,1)S(1)} %collective-permute-done.28.refs_3_), channel_id=1, source_target_pairs={{0,1},{1,0},{2,3},{3,2},{4,5},{5,4},{6,7},{7,6},{8,9},{9,8},{10,11... | collective-permute-start | bytes 1572872 | tf_op jit(solution)/shard_map/ppermute | solution.py:58
  159.9 23.3 %collective-permute-start.31 = (bf16[2,2,64,1024]{3,2,1,0:T(8,128)(2,1)}, bf16[2,2,64,1024]{3,2,1,0:T(8,128)(2,1)S(1)}, u32[]{:S(2)}, u32[]{:S(2)}) collective-permute-start(bf16[2,2,64,1024]{3,2,1,0:T(8,128)(2,1)} %get-tuple-element.230), channel_id=1, source_target_pairs={{0,4},{4,0},{8,12},{12,8},{16,20},{20,16},{24,28},{28,24},{32,36},... | collective-permute-start | bytes 1572872 | tf_op jit(solution)/shard_map/ppermute | solution.py:49
  161.3 21.1 %all-to-all-start.3 = ((bf16[8,64,512]{2,1,0:T(8,128)(2,1)}), bf16[8,64,512]{2,1,0:T(8,128)(2,1)S(1)}, u32[]{:S(2)}, u32[]{:S(2)}) async-start(bf16[8,64,512]{2,1,0:T(8,128)(2,1)} %get-tuple-element.221), calls=%async_computation.3 | async-start | bytes 1048576 | tf_op jit(solution)/shard_map/all_to_all | solution.py:45
  168.8 13.6 %collective-permute-start.32 = (bf16[2,64,1024]{2,1,0:T(8,128)(2,1)}, bf16[2,64,1024]{2,1,0:T(8,128)(2,1)}, u32[]{:S(2)}, u32[]{:S(2)}) collective-permute-start(bf16[2,64,1024]{2,1,0:T(8,128)(2,1)} %get-tuple-element.232), channel_id=1, source_target_pairs={{0,8},{4,12},{8,0},{12,4},{16,24},{20,28},{24,16},{28,20},{32,40},... | collective-permute-start | bytes 786440 | tf_op jit(solution)/shard_map/ppermute | solution.py:49
  168.8 14.3 %collective-permute-start.33 = (bf16[2,64,1024]{2,1,0:T(8,128)(2,1)}, bf16[2,64,1024]{2,1,0:T(8,128)(2,1)}, u32[]{:S(2)}, u32[]{:S(2)}) collective-permute-start(bf16[2,64,1024]{2,1,0:T(8,128)(2,1)} %get-tuple-element.233), channel_id=1, source_target_pairs={{0,16},{4,20},{8,24},{12,28},{16,0},{20,4},{24,8},{28,12},{32,48},... | collective-permute-start | bytes 786440 | tf_op jit(solution)/shard_map/ppermute | solution.py:49
  171.2 2.1 %copy-start.19 = (bf16[128,2048]{1,0:T(8,128)(2,1)}, bf16[128,2048]{1,0:T(8,128)(2,1)S(1)}, u32[]{:S(2)}) copy-start(bf16[128,2048]{1,0:T(8,128)(2,1)S(1)} %collective-permute-done.29.refs_4_) | copy-start | bytes 1572868
  171.2 12.0 %collective-permute-start.34 = (bf16[2,64,1024]{2,1,0:T(8,128)(2,1)}, bf16[2,64,1024]{2,1,0:T(8,128)(2,1)}, u32[]{:S(2)}, u32[]{:S(2)}) collective-permute-start(bf16[2,64,1024]{2,1,0:T(8,128)(2,1)} %get-tuple-element.236), channel_id=1, source_target_pairs={{0,128},{4,132},{8,136},{12,140},{16,144},{20,148},{24,152},{28,15... | collective-permute-start | bytes 786440 | tf_op jit(solution)/shard_map/ppermute | solution.py:49
  173.3 0.8 copy-start.20
  183.2 0.8 copy-start.22
  (1 other events, 0.7 us)

commit v9 on v8

--- a/solution.py
+++ b/solution.py
@@ -34,7 +34,7 @@
 PARTS = 6
 HALF = WIDTH // 2
 Z_BITS = (1, 2, 3)
-FIRST, THIRD = (3, 4), (2, 1, 5)
+FIRST, THIRD = (3, 4, 5), (2, 1)
 
 
 def mm(left, right, dims):
@@ -570,9 +570,11 @@
     order = feature_order(lax.axis_index("rep"))
     for b in FIRST:
         rand[b] = swapped(rand[b], b)
-    spread, order, grads, pair, outer, rand, lower, upper = together(
-        spread, order, grads, pair, outer, rand, w_out[:HEAD_DIM], w_out[HEAD_DIM:]
+    first_done = [rand[b] for b in FIRST]
+    spread, first_done, order, grads, pair, outer, rand, lower, upper = together(
+        spread, first_done, order, grads, pair, outer, rand, w_out[:HEAD_DIM], w_out[HEAD_DIM:]
     )
+    rand.update(zip(FIRST, first_done))
     mine = gathered(spread)
     two, three = near(mine, along_z(mine, 1), along_z(mine, -1))
     two, three, outer = together(two, three, outer)
@@ -585,8 +587,12 @@
     for b in THIRD:
         rand[b] = swapped(rand[b], b)
     pieces = project(w_out, grads)
-    glob, pieces, pair, outer, rand = together(glob, pieces, pair, outer, rand)
     pieces = [pieces[0]] + [across(pieces[a], a) for a in range(1, 4)]
+    third_done = [rand[b] for b in THIRD]
+    glob, third_done, outer, pair, pieces, rand = together(
+        glob, third_done, outer, pair, pieces, rand
+    )
+    rand.update(zip(THIRD, third_done))
     rand = [rand[b] for b in range(1, BITS)]
     pair, outer, *rand = from_hbm(pair, outer, *rand)
     attn, stats, *ordered = forward(
@@ -619,7 +625,7 @@
     routed, weight_grad = last(where, glob_sum, keep, came)
     glob_total = trade(routed).reshape(2, 2, GLOB, BLK, HALF)
     pair = paired(pair)
-    for b in THIRD:
+    for b in THIRD + (5,):
         back[b] = swapped(back[b], b)
     back = [back[b] for b in range(1, BITS)]
     layer = layer_of(where, parts, attn)

time: 189 us -> 185 us (0.979)
    ppermute x15, waiting for transfers between devices: 44.7 us -> 38.3 us  [swapped(): return lax.ppermute(value, 'seq', [(s, s ^ 1 << bit) for s in range(64)])]
    all_to_all x4, waiting for transfers between devices: 9.46 us -> 14.5 us  [trade(): lax.all_to_all(value, 'seq', 0, 0, axis_index_groups=YX_GROUPS, tiled=True)]
    ppermute x4, starting transfers between devices: 9.84 us -> 6.43 us  [along_z(): return lax.ppermute(value, 'seq', pairs)]
    all_to_all x4, starting transfers between devices: 24.8 us -> 26.7 us  [trade(): lax.all_to_all(value, 'seq', 0, 0, axis_index_groups=YX_GROUPS, tiled=True)]
    unnamed x52 -> x48, local copies, waits for them, and re-layouts: 5.11 us -> 4.53 us
  transfers between devices with their start and end apart: 39 -> 39, of which waited for: 14 -> 18; matrix products, arithmetic and copies ran while one was open for 2% -> 2% of each run, Pallas kernels for 13% -> 10%
where the time goes in v9:
time: 185 us; the launch traced here: 183 us
  starting transfers between devices  75 us (41%)
  waiting for transfers between devices  64.5 us (35%)
  Pallas kernels  34.8 us (19%)
  local copies, waits for them, and re-layouts  5.69 us (3%)
  other arithmetic  2.33 us (1%)
    ppermute x15, waiting for transfers between devices, swapped(): return lax.ppermute(value, 'seq', [(s, s ^ 1 << bit) for s in range(64)])  38.3 us
    ppermute x15, starting transfers between devices, swapped(): return lax.ppermute(value, 'seq', [(s, s ^ 1 << bit) for s in range(64)])  29.4 us
    all_to_all x4, starting transfers between devices, trade(): lax.all_to_all(value, 'seq', 0, 0, axis_index_groups=YX_GROUPS, tiled=True)  26.7 us
    all_to_all x4, waiting for transfers between devices, trade(): lax.all_to_all(value, 'seq', 0, 0, axis_index_groups=YX_GROUPS, tiled=True)  14.5 us
    ppermute x4, waiting for transfers between devices, along_z(): return lax.ppermute(value, 'seq', pairs)  9.59 us
    pallas_call x1, Pallas kernels, backward(): pl.pallas_call(backward_kernel, grid=(HEADS // STEP,), in_specs=[smem(),...  7.13 us
    ppermute x4, starting transfers between devices, along_z(): return lax.ppermute(value, 'seq', pairs)  6.43 us
    pallas_call x1, Pallas kernels, forward(): pl.pallas_call(forward_kernel, grid=(HEADS // STEP,), in_specs=[smem(), f...  6.04 us
  transfers between devices with their start and end apart: 39, of which 18 were waited for; matrix products, arithmetic and copies ran while one was open for 2% of the time, Pallas kernels for 10%

profile of v9, /device:TPU:8, one launch (start us, length us, event | category | flops | bytes accessed | tf_op | source)
XLA Modules:
  0.0 183.4 jit_solution(5395715118197610334)
XLA Ops:
  0.6 0.6 copy-done.2
  1.3 0.7 copy-done.4
  2.0 2.8 %pick.1 = (bf16[2,2,64,1024]{3,2,1,0:T(8,128)(2,1)}, bf16[2,64,1024]{2,1,0:T(8,128)(2,1)}, bf16[2,64,1024]{2,1,0:T(8,128)(2,1)}, bf16[2,64,1024]{2,1,0:T(8,128)(...) custom-call(s32[1]{0:T(128)} %bitcast.me_ref, ...), custom_call_target="tpu_custom_call" | custom-call | tf_op jit(solution)/shard_map/pick/pallas_call | solution.py:131
  4.8 7.4 %all-to-all-start = ((bf16[8,64,512]{2,1,0:T(8,128)(2,1)}), bf16[8,64,512]{2,1,0:T(8,128)(2,1)S(1)}, u32[]{:S(2)}, u32[]{:S(2)}) async-start(bf16[8,64,512]{2,1,0:T(8,128)(2,1)} %get-tuple-element.123), calls=%async_computation | async-start | bytes 1048576 | tf_op jit(solution)/shard_map/all_to_all | solution.py:45
  12.2 0.6 collective-permute-start.4
  12.8 7.2 %collective-permute-start = (bf16[2,64,1024]{2,1,0:T(8,128)(2,1)}, bf16[2,64,1024]{2,1,0:T(8,128)(2,1)S(1)}, u32[]{:S(2)}, u32[]{:S(2)}) collective-permute-start(bf16[2,64,1024]{2,1,0:T(8,128)(2,1)} %get-tuple-element.126), channel_id=1, source_target_pairs={{0,32},{4,36},{8,40},{12,44},{16,48},{20,52},{24,56},{28,60},{32,0... | collective-permute-start | bytes 786440 | tf_op jit(solution)/shard_map/ppermute | solution.py:49
  19.9 2.9 %collective-permute-start.2 = (bf16[2,64,1024]{2,1,0:T(8,128)(2,1)}, bf16[2,64,1024]{2,1,0:T(8,128)(2,1)S(1)}, u32[]{:S(2)}, u32[]{:S(2)}) collective-permute-start(bf16[2,64,1024]{2,1,0:T(8,128)(2,1)} %get-tuple-element.128), channel_id=1, source_target_pairs={{0,128},{4,132},{8,136},{12,140},{16,144},{20,148},{24,152},{28,15... | collective-permute-start | bytes 786440 | tf_op jit(solution)/shard_map/ppermute | solution.py:49
  22.9 1.1 fusion.37
  24.0 2.3 %fusion.rest_6_ = bf16[1024,1024]{1,0:T(8,128)(2,1)} fusion(s32[1024]{0:T(1024)S(1)} %fusion.15), kind=kLoop, calls=%fused_computation.1 | loop fusion | flops 2097152 | bytes 2101248 | tf_op jit(solution)/shard_map/convert_element_type | solution.py:554
  26.3 2.0 %collective-permute-done.rest_2_ = bf16[2,64,1024]{2,1,0:T(8,128)(2,1)S(1)} collective-permute-done((bf16[2,64,1024]{2,1,0:T(8,128)(2,1)}, bf16[2,64,1024]{2,1,0:T(8,128)(2,1)S(1)}, u32[]{:S(2)}, u32[]{:S(2)}) %collective-permute-start) | collective-permute-done | bytes 262176 | tf_op jit(solution)/shard_map/ppermute | solution.py:49
  28.3 1.0 collective-permute-done.1.rest_3_
  29.3 5.8 %collective-permute-done.2.rest_4_ = bf16[2,64,1024]{2,1,0:T(8,128)(2,1)S(1)} collective-permute-done((bf16[2,64,1024]{2,1,0:T(8,128)(2,1)}, bf16[2,64,1024]{2,1,0:T(8,128)(2,1)S(1)}, u32[]{:S(2)}, u32[]{:S(2)}) %collective-permute-start.2) | collective-permute-done | bytes 262176 | tf_op jit(solution)/shard_map/ppermute | solution.py:49
  35.2 2.5 %collective-permute-start.6 = (bf16[64,512]{1,0:T(8,128)(2,1)S(1)}, bf16[64,512]{1,0:T(8,128)(2,1)S(1)}, u32[]{:S(2)}, u32[]{:S(2)}) collective-permute-start(bf16[64,512]{1,0:T(8,128)(2,1)S(1)} %gathered.1.mine), channel_id=1, source_target_pairs={{0,56},{4,60},{8,0},{12,4},{16,8},{20,12},{24,16},{28,20},{32,24},... | collective-permute-start | bytes 196616 | tf_op jit(solution)/shard_map/ppermute | solution.py:54
  37.8 1.9 %collective-permute-done.6.above = bf16[64,512]{1,0:T(8,128)(2,1)S(1)} collective-permute-done((bf16[64,512]{1,0:T(8,128)(2,1)S(1)}, bf16[64,512]{1,0:T(8,128)(2,1)S(1)}, u32[]{:S(2)}, u32[]{:S(2)}) %collective-permute-start.6) | collective-permute-done | bytes 65568 | tf_op jit(solution)/shard_map/ppermute | solution.py:54
  39.7 3.6 %collective-permute-done.5.below = bf16[64,512]{1,0:T(8,128)(2,1)S(1)} collective-permute-done((bf16[64,512]{1,0:T(8,128)(2,1)S(1)}, bf16[64,512]{1,0:T(8,128)(2,1)S(1)}, u32[]{:S(2)}, u32[]{:S(2)}) %collective-permute-start.5) | collective-permute-done | bytes 65568 | tf_op jit(solution)/shard_map/ppermute | solution.py:54
  43.3 0.5 collective-permute-start.8
  43.7 3.4 %collective-permute-start.7 = (bf16[64,512]{1,0:T(8,128)(2,1)S(1)}, bf16[64,512]{1,0:T(8,128)(2,1)S(1)}, u32[]{:S(2)}, u32[]{:S(2)}) collective-permute-start(bf16[64,512]{1,0:T(8,128)(2,1)S(1)} %get-tuple-element.138.mine), channel_id=1, source_target_pairs={{0,24},{4,28},{8,32},{12,36},{16,40},{20,44},{24,48},{28,52},{32,5... | collective-permute-start | bytes 196616 | tf_op jit(solution)/shard_map/ppermute | solution.py:54
  47.2 3.1 %collective-permute-done.8.above = bf16[64,512]{1,0:T(8,128)(2,1)S(1)} collective-permute-done((bf16[64,512]{1,0:T(8,128)(2,1)S(1)}, bf16[64,512]{1,0:T(8,128)(2,1)S(1)}, u32[]{:S(2)}, u32[]{:S(2)}) %collective-permute-start.8) | collective-permute-done | bytes 65568 | tf_op jit(solution)/shard_map/ppermute | solution.py:54
  50.3 1.0 collective-permute-done.7.below
  51.3 4.3 %collective-permute-start.12 = (bf16[2,2,64,1024]{3,2,1,0:T(8,128)(2,1)}, bf16[2,2,64,1024]{3,2,1,0:T(8,128)(2,1)S(1)}, u32[]{:S(2)}, u32[]{:S(2)}) collective-permute-start(bf16[2,2,64,1024]{3,2,1,0:T(8,128)(2,1)} %get-tuple-element.154), channel_id=1, source_target_pairs={{0,4},{4,0},{8,12},{12,8},{16,20},{20,16},{24,28},{28,24},{32,36},... | collective-permute-start | bytes 1572872 | tf_op jit(solution)/shard_map/ppermute | solution.py:49
  55.6 1.7 collective-permute-start.11
  57.4 0.8 relay.1
  58.3 6.6 %all-to-all-start.1 = ((bf16[8,64,512]{2,1,0:T(8,128)(2,1)}), bf16[8,64,512]{2,1,0:T(8,128)(2,1)S(1)}, u32[]{:S(2)}, u32[]{:S(2)}) async-start(bf16[8,64,512]{2,1,0:T(8,128)(2,1)} %relay.1), calls=%async_computation.1 | async-start | bytes 1048576 | tf_op jit(solution)/shard_map/all_to_all | solution.py:45
  64.9 1.8 collective-permute-start.10
  66.7 0.8 copy-done.10
  67.5 3.3 %project.1 = (bf16[128,256]{1,0:T(8,128)(2,1)S(1)}, bf16[128,256]{1,0:T(8,128)(2,1)S(1)}, bf16[128,256]{1,0:T(8,128)(2,1)S(1)}, bf16[128,256]{1,0:T(8,128)(2,1)S(1)}) custom-call(bf16[256,2048]{1,0:T(8,128)(2,1)} %refs_0_, bf16[128,2048]{1,0:T(8,128)(2,1)} %bitcast.32, bf16[128,2048]{1,0:T(8,128)(2,1)} %copy-done.9, bf16[128,2048]{1,0:T(8,128)(2,1)} %copy-done.8, ...), custom_call_target="tpu_custom_call" | custom-call | tf_op jit(solution)/shard_map/project/pallas_call | solution.py:362
  71.0 0.5 collective-permute-start.15
  71.4 4.1 %collective-permute-done.9.rest_1_ = bf16[2,64,1024]{2,1,0:T(8,128)(2,1)} collective-permute-done((bf16[2,64,1024]{2,1,0:T(8,128)(2,1)}, bf16[2,64,1024]{2,1,0:T(8,128)(2,1)}, u32[]{:S(2)}, u32[]{:S(2)}) %collective-permute-start.9) | collective-permute-done | bytes 262176 | tf_op jit(solution)/shard_map/ppermute | solution.py:49
  75.6 1.0 collective-permute-start.16
  76.6 0.3 collective-permute-done.10.rest_0_
  77.0 3.3 %all-to-all-done.1 = bf16[8,64,512]{2,1,0:T(8,128)(2,1)S(1)} async-done(((bf16[8,64,512]{2,1,0:T(8,128)(2,1)}), bf16[8,64,512]{2,1,0:T(8,128)(2,1)S(1)}, u32[]{:S(2)}, u32[]{:S(2)}) %all-to-all-start.1) | async-done | bytes 524320 | tf_op jit(solution)/shard_map/all_to_all | solution.py:45
  80.3 1.4 collective-permute-done.15.rest_9_
  81.7 0.6 collective-permute-done.16.rest_10_
  82.3 6.0 %forward.1 = (bf16[128,1024]{1,0:T(8,128)(2,1)}, f32[8,8,128]{2,1,0:T(8,128)}, bf16[128,256]{1,0:T(8,128)(2,1)S(1)}, bf16[128,256]{1,0:T(8,128)(2,1)S(1)}, bf16[...) custom-call(s32[14]{0:T(128)S(1)} %concatenate.3.where.refs_0_, bf16[128,1024]{1,0:T(8,128)(2,1)} %bitcast.34, ...), custom_call_target="tpu_custom_call" | custom-call | tf_op jit(solution)/shard_map/forward/pallas_call | solution.py:253
  88.6 1.5 collective-permute-start.18
  90.3 7.1 %backward.1 = (bf16[128,1024]{1,0:T(8,128)(2,1)}, f32[2,128,1024]{2,1,0:T(8,128)}, bf16[2,2,64,1024]{3,2,1,0:T(8,128)(2,1)}, bf16[2,64,1024]{2,1,0:T(8,128)(2,1)...) custom-call(s32[14]{0:T(128)S(1)} %concatenate.3.where.refs_0_, ...), custom_call_target="tpu_custom_call" | custom-call | tf_op jit(solution)/shard_map/backward/pallas_call | solution.py:321
  97.5 4.1 %weight.1 = bf16[8,192,512]{2,1,0:T(8,128)(2,1)} custom-call(bf16[128,256]{1,0:T(8,128)(2,1)S(1)} %get-tuple-element.184.refs_0_, bf16[128,256]{1,0:T(8,128)(2,1)S(1)} %collective-permute-done.17.refs_1_, bf16[128,256]{1,0:T(8,128)(2,1)S(1)} %collective-permute-done.18.refs_2_, bf16[128,256]{1,0:T(8,128)(2,1)S(1)} %collective-permute-done.19.refs_3_, ...), custom_call_target="tpu_custom_call" | custom-call | tf_op jit(solution)/shard_map/weight/pallas_call | solution.py:413
  101.6 5.4 %all-to-all-start.2 = ((bf16[8,192,512]{2,1,0:T(8,128)(2,1)}), bf16[8,192,512]{2,1,0:T(8,128)(2,1)S(1)}, u32[]{:S(2)}, u32[]{:S(2)}) async-start(bf16[8,192,512]{2,1,0:T(8,128)(2,1)} %weight.1), calls=%async_computation.2 | async-start | bytes 3145728 | tf_op jit(solution)/shard_map/all_to_all | solution.py:45
  107.1 3.4 %collective-permute-start.20 = (bf16[2,64,1024]{2,1,0:T(8,128)(2,1)}, bf16[2,64,1024]{2,1,0:T(8,128)(2,1)S(1)}, u32[]{:S(2)}, u32[]{:S(2)}) collective-permute-start(bf16[2,64,1024]{2,1,0:T(8,128)(2,1)} %get-tuple-element.194), channel_id=1, source_target_pairs={{0,32},{4,36},{8,40},{12,44},{16,48},{20,52},{24,56},{28,60},{32,0... | collective-permute-start | bytes 786440 | tf_op jit(solution)/shard_map/ppermute | solution.py:49
  110.5 12.5 %collective-permute-done.20.rest_2_ = bf16[2,64,1024]{2,1,0:T(8,128)(2,1)S(1)} collective-permute-done((bf16[2,64,1024]{2,1,0:T(8,128)(2,1)}, bf16[2,64,1024]{2,1,0:T(8,128)(2,1)S(1)}, u32[]{:S(2)}, u32[]{:S(2)}) %collective-permute-start.20) | collective-permute-done | bytes 262176 | tf_op jit(solution)/shard_map/ppermute | solution.py:49
  123.0 0.7 copy-done.21
  123.7 5.0 %all-to-all-done.2.refs_1_ = bf16[8,192,512]{2,1,0:T(8,128)(2,1)S(1)} async-done(((bf16[8,192,512]{2,1,0:T(8,128)(2,1)}), bf16[8,192,512]{2,1,0:T(8,128)(2,1)S(1)}, u32[]{:S(2)}, u32[]{:S(2)}) %all-to-all-start.2) | async-done | bytes 1572896 | tf_op jit(solution)/shard_map/all_to_all | solution.py:45
  128.7 0.9 collective-permute-start.27
  129.5 1.0 collective-permute-start.28
  130.5 0.7 first.1
  131.3 1.7 collective-permute-start.22
  133.0 4.2 %collective-permute-start.25 = (bf16[2,64,1024]{2,1,0:T(8,128)(2,1)}, bf16[2,64,1024]{2,1,0:T(8,128)(2,1)S(1)}, u32[]{:S(2)}, u32[]{:S(2)}) collective-permute-start(bf16[2,64,1024]{2,1,0:T(8,128)(2,1)} %get-tuple-element.211), channel_id=1, source_target_pairs={{0,252},{4,8},{8,4},{12,16},{16,12},{20,24},{24,20},{28,32},{32,28... | collective-permute-start | bytes 786440 | tf_op jit(solution)/shard_map/ppermute | solution.py:98
  137.2 1.3 collective-permute-start.26
  138.5 0.6 fold.2
  139.1 1.0 collective-permute-start.23
  140.1 5.7 %collective-permute-done.23.refs_3_ = bf16[96,512]{1,0:T(8,128)(2,1)S(1)} collective-permute-done((bf16[96,512]{1,0:T(8,128)(2,1)S(1)}, bf16[96,512]{1,0:T(8,128)(2,1)S(1)}, u32[]{:S(2)}, u32[]{:S(2)}) %collective-permute-start.23) | collective-permute-done | bytes 98336 | tf_op jit(solution)/shard_map/ppermute | solution.py:49
  145.8 0.6 fold.3
  146.4 3.2 %collective-permute-start.24 = (bf16[80,512]{1,0:T(8,128)(2,1)S(1)}, bf16[80,512]{1,0:T(8,128)(2,1)S(1)}, u32[]{:S(2)}, u32[]{:S(2)}) collective-permute-start(bf16[80,512]{1,0:T(8,128)(2,1)S(1)} %get-tuple-element.209), channel_id=1, source_target_pairs={{0,32},{4,36},{8,40},{12,44},{16,48},{20,52},{24,56},{28,60},{32,0... | collective-permute-start | bytes 245768 | tf_op jit(solution)/shard_map/ppermute | solution.py:49
  149.6 5.9 %collective-permute-done.24.came = bf16[80,512]{1,0:T(8,128)(2,1)S(1)} collective-permute-done((bf16[80,512]{1,0:T(8,128)(2,1)S(1)}, bf16[80,512]{1,0:T(8,128)(2,1)S(1)}, u32[]{:S(2)}, u32[]{:S(2)}) %collective-permute-start.24) | collective-permute-done | bytes 81952 | tf_op jit(solution)/shard_map/ppermute | solution.py:49
  155.7 0.5 collective-permute-start.30
  156.2 1.4 last.1
  157.6 7.3 %all-to-all-start.3 = ((bf16[8,64,512]{2,1,0:T(8,128)(2,1)}), bf16[8,64,512]{2,1,0:T(8,128)(2,1)S(1)}, u32[]{:S(2)}, u32[]{:S(2)}) async-start(bf16[8,64,512]{2,1,0:T(8,128)(2,1)} %get-tuple-element.221), calls=%async_computation.3 | async-start | bytes 1048576 | tf_op jit(solution)/shard_map/all_to_all | solution.py:45
  165.2 2.1 %collective-permute-start.34 = (bf16[2,64,1024]{2,1,0:T(8,128)(2,1)}, bf16[2,64,1024]{2,1,0:T(8,128)(2,1)}, u32[]{:S(2)}, u32[]{:S(2)}) collective-permute-start(bf16[2,64,1024]{2,1,0:T(8,128)(2,1)} %get-tuple-element.236), channel_id=1, source_target_pairs={{0,128},{4,132},{8,136},{12,140},{16,144},{20,148},{24,152},{28,15... | collective-permute-start | bytes 786440 | tf_op jit(solution)/shard_map/ppermute | solution.py:49
  167.3 0.8 copy-done.18
  168.2 4.3 %layer.1 = bf16[128,2048]{1,0:T(8,128)(2,1)} custom-call(s32[14]{0:T(128)S(1)} %concatenate.3.where.refs_0_, bf16[256,2048]{1,0:T(8,128)(2,1)} %refs_0_, bf16[256,2048]{1,0:T(8,128)(2,1)} %collective-permute-done.21.refs_1_, bf16[128,2048]{1,0:T(8,128)(2,1)} %copy-done.15, bf16[128,2048]{1,0:T(8,128)(2,1)} %copy-done.16, bf16[128,2048]{1,0:T(8,128)(2,1)} %copy-done.17, ...), custom_call_target="tpu_custom_call" | custom-call | tf_op jit(solution)/shard_map/layer/pallas_call | solution.py:378
  172.4 6.2 %all-to-all-done.3 = bf16[8,64,512]{2,1,0:T(8,128)(2,1)S(1)} async-done(((bf16[8,64,512]{2,1,0:T(8,128)(2,1)}), bf16[8,64,512]{2,1,0:T(8,128)(2,1)S(1)}, u32[]{:S(2)}, u32[]{:S(2)}) %all-to-all-start.3) | async-done | bytes 524320 | tf_op jit(solution)/shard_map/all_to_all | solution.py:45
  178.7 0.9 collective-permute-done.33.rest_1_
  179.6 0.8 copy-done.20
  180.4 2.9 %finish.1 = (bf16[128,1024]{1,0:T(8,128)(2,1)}, bf16[128,1024]{1,0:T(8,128)(2,1)}) custom-call(s32[14]{0:T(128)S(1)} %concatenate.3.where.refs_0_, f32[2,128,1024]{2,1,0:T(8,128)} %get-tuple-element.229.own, bf16[2,2,64,1024]{3,2,1,0:T(8,128)(2,1)} %copy-done.20, bf16[2,64,1024]{2,1,0:T(8,128)(2,1)} %copy-done.22, ...), custom_call_target="tpu_custom_call" | custom-call | tf_op jit(solution)/shard_map/finish/pallas_call | solution.py:534
  (82 shorter events, 1.5 us)
Async XLA Ops:
  0.6 0.7 copy-start.2
  1.3 0.7 copy-start.4
  2.0 20.9 %copy-start.6 = (bf16[256,2048]{1,0:T(8,128)(2,1)S(1)}, bf16[256,2048]{1,0:T(8,128)(2,1)}, u32[]{:S(2)}) copy-start(bf16[256,2048]{1,0:T(8,128)(2,1)} %refs_0_) | copy-start | bytes 3145732
  4.8 30.3 %all-to-all-start = ((bf16[8,64,512]{2,1,0:T(8,128)(2,1)}), bf16[8,64,512]{2,1,0:T(8,128)(2,1)S(1)}, u32[]{:S(2)}, u32[]{:S(2)}) async-start(bf16[8,64,512]{2,1,0:T(8,128)(2,1)} %get-tuple-element.123), calls=%async_computation | async-start | bytes 1048576 | tf_op jit(solution)/shard_map/all_to_all | solution.py:45
  12.2 23.0 %collective-permute-start.4 = (bf16[128,2048]{1,0:T(8,128)(2,1)}, bf16[128,2048]{1,0:T(8,128)(2,1)S(1)}, u32[]{:S(2)}, u32[]{:S(2)}) collective-permute-start(bf16[128,2048]{1,0:T(8,128)(2,1)} %bitcast.30), channel_id=1, source_target_pairs={{0,2},{1,3},{2,0},{3,1},{4,6},{5,7},{6,4},{7,5},{8,10},{9,11},{10,... | collective-permute-start | bytes 1572872 | tf_op jit(solution)/shard_map/ppermute | solution.py:58
  12.7 22.4 %collective-permute-start.3 = (bf16[128,2048]{1,0:T(8,128)(2,1)}, bf16[128,2048]{1,0:T(8,128)(2,1)S(1)}, u32[]{:S(2)}, u32[]{:S(2)}) collective-permute-start(bf16[128,2048]{1,0:T(8,128)(2,1)} %bitcast.31), channel_id=1, source_target_pairs={{0,1},{1,0},{2,3},{3,2},{4,5},{5,4},{6,7},{7,6},{8,9},{9,8},{10,11... | collective-permute-start | bytes 1572872 | tf_op jit(solution)/shard_map/ppermute | solution.py:58
  12.8 15.5 %collective-permute-start = (bf16[2,64,1024]{2,1,0:T(8,128)(2,1)}, bf16[2,64,1024]{2,1,0:T(8,128)(2,1)S(1)}, u32[]{:S(2)}, u32[]{:S(2)}) collective-permute-start(bf16[2,64,1024]{2,1,0:T(8,128)(2,1)} %get-tuple-element.126), channel_id=1, source_target_pairs={{0,32},{4,36},{8,40},{12,44},{16,48},{20,52},{24,56},{28,60},{32,0... | collective-permute-start | bytes 786440 | tf_op jit(solution)/shard_map/ppermute | solution.py:49
  19.9 9.4 %collective-permute-start.1 = (bf16[2,64,1024]{2,1,0:T(8,128)(2,1)}, bf16[2,64,1024]{2,1,0:T(8,128)(2,1)S(1)}, u32[]{:S(2)}, u32[]{:S(2)}) collective-permute-start(bf16[2,64,1024]{2,1,0:T(8,128)(2,1)} %get-tuple-element.127), channel_id=1, source_target_pairs={{0,64},{4,68},{8,72},{12,76},{16,80},{20,84},{24,88},{28,92},{32,9... | collective-permute-start | bytes 786440 | tf_op jit(solution)/shard_map/ppermute | solution.py:49
  19.9 15.2 %collective-permute-start.2 = (bf16[2,64,1024]{2,1,0:T(8,128)(2,1)}, bf16[2,64,1024]{2,1,0:T(8,128)(2,1)S(1)}, u32[]{:S(2)}, u32[]{:S(2)}) collective-permute-start(bf16[2,64,1024]{2,1,0:T(8,128)(2,1)} %get-tuple-element.128), channel_id=1, source_target_pairs={{0,128},{4,132},{8,136},{12,140},{16,144},{20,148},{24,152},{28,15... | collective-permute-start | bytes 786440 | tf_op jit(solution)/shard_map/ppermute | solution.py:49
  24.0 42.7 %copy-start.3 = (s32[1,2]{1,0:T(1,128)S(1)}, s32[1,2]{1,0:T(1,128)}, u32[]{:S(2)}) copy-start(s32[1,2]{1,0:T(1,128)} %param.13) | copy-start | bytes 28
  28.3 42.6 %copy-start.12 = (bf16[2,64,1024]{2,1,0:T(8,128)(2,1)}, bf16[2,64,1024]{2,1,0:T(8,128)(2,1)S(1)}, u32[]{:S(2)}) copy-start(bf16[2,64,1024]{2,1,0:T(8,128)(2,1)S(1)} %collective-permute-done.rest_2_) | copy-start | bytes 786436
  29.3 41.6 %copy-start.13 = (bf16[2,64,1024]{2,1,0:T(8,128)(2,1)}, bf16[2,64,1024]{2,1,0:T(8,128)(2,1)S(1)}, u32[]{:S(2)}) copy-start(bf16[2,64,1024]{2,1,0:T(8,128)(2,1)S(1)} %collective-permute-done.1.rest_3_) | copy-start | bytes 786436
  35.1 16.2 %copy-start.14 = (bf16[2,64,1024]{2,1,0:T(8,128)(2,1)}, bf16[2,64,1024]{2,1,0:T(8,128)(2,1)S(1)}, u32[]{:S(2)}) copy-start(bf16[2,64,1024]{2,1,0:T(8,128)(2,1)S(1)} %collective-permute-done.2.rest_4_) | copy-start | bytes 786436
  35.1 31.6 %copy-start.8 = (bf16[128,2048]{1,0:T(8,128)(2,1)}, bf16[128,2048]{1,0:T(8,128)(2,1)S(1)}, u32[]{:S(2)}) copy-start(bf16[128,2048]{1,0:T(8,128)(2,1)S(1)} %collective-permute-done.4.refs_2_.refs_6_) | copy-start | bytes 1572868
  35.1 31.6 %copy-start.9 = (bf16[128,2048]{1,0:T(8,128)(2,1)}, bf16[128,2048]{1,0:T(8,128)(2,1)S(1)}, u32[]{:S(2)}) copy-start(bf16[128,2048]{1,0:T(8,128)(2,1)S(1)} %collective-permute-done.3.refs_1_.refs_5_) | copy-start | bytes 1572868
  35.2 4.4 %collective-permute-start.6 = (bf16[64,512]{1,0:T(8,128)(2,1)S(1)}, bf16[64,512]{1,0:T(8,128)(2,1)S(1)}, u32[]{:S(2)}, u32[]{:S(2)}) collective-permute-start(bf16[64,512]{1,0:T(8,128)(2,1)S(1)} %gathered.1.mine), channel_id=1, source_target_pairs={{0,56},{4,60},{8,0},{12,4},{16,8},{20,12},{24,16},{28,20},{32,24},... | collective-permute-start | bytes 196616 | tf_op jit(solution)/shard_map/ppermute | solution.py:54
  37.8 5.5 %collective-permute-start.5 = (bf16[64,512]{1,0:T(8,128)(2,1)S(1)}, bf16[64,512]{1,0:T(8,128)(2,1)S(1)}, u32[]{:S(2)}, u32[]{:S(2)}) collective-permute-start(bf16[64,512]{1,0:T(8,128)(2,1)S(1)} %gathered.1.mine), channel_id=1, source_target_pairs={{0,8},{4,12},{8,16},{12,20},{16,24},{20,28},{24,32},{28,36},{32,40... | collective-permute-start | bytes 196616 | tf_op jit(solution)/shard_map/ppermute | solution.py:54
  43.3 7.0 %collective-permute-start.8 = (bf16[64,512]{1,0:T(8,128)(2,1)S(1)}, bf16[64,512]{1,0:T(8,128)(2,1)S(1)}, u32[]{:S(2)}, u32[]{:S(2)}) collective-permute-start(bf16[64,512]{1,0:T(8,128)(2,1)S(1)} %get-tuple-element.139), channel_id=1, source_target_pairs={{0,40},{4,44},{8,48},{12,52},{16,56},{20,60},{24,0},{28,4},{32,8},... | collective-permute-start | bytes 196616 | tf_op jit(solution)/shard_map/ppermute | solution.py:54
  43.7 7.5 %collective-permute-start.7 = (bf16[64,512]{1,0:T(8,128)(2,1)S(1)}, bf16[64,512]{1,0:T(8,128)(2,1)S(1)}, u32[]{:S(2)}, u32[]{:S(2)}) collective-permute-start(bf16[64,512]{1,0:T(8,128)(2,1)S(1)} %get-tuple-element.138.mine), channel_id=1, source_target_pairs={{0,24},{4,28},{8,32},{12,36},{16,40},{20,44},{24,48},{28,52},{32,5... | collective-permute-start | bytes 196616 | tf_op jit(solution)/shard_map/ppermute | solution.py:54
  51.3 15.4 %collective-permute-start.13 = (bf16[128,2048]{1,0:T(8,128)(2,1)S(1)}, bf16[128,2048]{1,0:T(8,128)(2,1)S(1)}, u32[]{:S(2)}, u32[]{:S(2)}) collective-permute-start(bf16[128,2048]{1,0:T(8,128)(2,1)S(1)} %collective-permute-done.4.refs_2_.refs_6_), channel_id=1, source_target_pairs={{0,1},{1,0},{2,3},{3,2},{4,5},{5,4},{6,7},{7,6},{8,9},{9,8},{10,11... | collective-permute-start | bytes 1572872 | tf_op jit(solution)/shard_map/ppermute | solution.py:58
  51.3 29.0 %collective-permute-start.12 = (bf16[2,2,64,1024]{3,2,1,0:T(8,128)(2,1)}, bf16[2,2,64,1024]{3,2,1,0:T(8,128)(2,1)S(1)}, u32[]{:S(2)}, u32[]{:S(2)}) collective-permute-start(bf16[2,2,64,1024]{3,2,1,0:T(8,128)(2,1)} %get-tuple-element.154), channel_id=1, source_target_pairs={{0,4},{4,0},{8,12},{12,8},{16,20},{20,16},{24,28},{28,24},{32,36},... | collective-permute-start | bytes 1572872 | tf_op jit(solution)/shard_map/ppermute | solution.py:49
  55.6 15.3 %collective-permute-start.11 = (bf16[2,64,1024]{2,1,0:T(8,128)(2,1)}, bf16[2,64,1024]{2,1,0:T(8,128)(2,1)}, u32[]{:S(2)}, u32[]{:S(2)}) collective-permute-start(bf16[2,64,1024]{2,1,0:T(8,128)(2,1)} %get-tuple-element.153), channel_id=1, source_target_pairs={{0,252},{4,8},{8,4},{12,16},{16,12},{20,24},{24,20},{28,32},{32,28... | collective-permute-start | bytes 786440 | tf_op jit(solution)/shard_map/ppermute | solution.py:98
  57.4 18.2 %collective-permute-start.9 = (bf16[2,64,1024]{2,1,0:T(8,128)(2,1)}, bf16[2,64,1024]{2,1,0:T(8,128)(2,1)}, u32[]{:S(2)}, u32[]{:S(2)}) collective-permute-start(bf16[2,64,1024]{2,1,0:T(8,128)(2,1)} %get-tuple-element.151), channel_id=1, source_target_pairs={{0,16},{4,20},{8,24},{12,28},{16,0},{20,4},{24,8},{28,12},{32,48},... | collective-permute-start | bytes 786440 | tf_op jit(solution)/shard_map/ppermute | solution.py:49
  58.3 18.2 %copy-start.5 = (s32[1,1,6]{2,1,0:T(1,128)S(1)}, s32[1,1,6]{2,1,0:T(1,128)}, u32[]{:S(2)}) copy-start(s32[1,1,6]{2,1,0:T(1,128)} %param.12) | copy-start | bytes 76
  58.3 22.0 %all-to-all-start.1 = ((bf16[8,64,512]{2,1,0:T(8,128)(2,1)}), bf16[8,64,512]{2,1,0:T(8,128)(2,1)S(1)}, u32[]{:S(2)}, u32[]{:S(2)}) async-start(bf16[8,64,512]{2,1,0:T(8,128)(2,1)} %relay.1), calls=%async_computation.1 | async-start | bytes 1048576 | tf_op jit(solution)/shard_map/all_to_all | solution.py:45
  64.9 12.1 %collective-permute-start.10 = (bf16[2,64,1024]{2,1,0:T(8,128)(2,1)}, bf16[2,64,1024]{2,1,0:T(8,128)(2,1)}, u32[]{:S(2)}, u32[]{:S(2)}) collective-permute-start(bf16[2,64,1024]{2,1,0:T(8,128)(2,1)} %get-tuple-element.152), channel_id=1, source_target_pairs={{0,8},{4,12},{8,0},{12,4},{16,24},{20,28},{24,16},{28,20},{32,40},... | collective-permute-start | bytes 786440 | tf_op jit(solution)/shard_map/ppermute | solution.py:49
  66.7 0.8 copy-start.10
  70.9 9.4 %collective-permute-start.14 = (bf16[128,256]{1,0:T(8,128)(2,1)S(1)}, bf16[128,256]{1,0:T(8,128)(2,1)S(1)}, u32[]{:S(2)}, u32[]{:S(2)}) collective-permute-start(bf16[128,256]{1,0:T(8,128)(2,1)S(1)} %get-tuple-element.159), channel_id=1, source_target_pairs={{0,1},{1,0},{2,3},{3,2},{4,5},{5,4},{6,7},{7,6},{8,9},{9,8},{10,11... | collective-permute-start | bytes 196616 | tf_op jit(solution)/shard_map/ppermute | solution.py:58
  71.0 10.7 %collective-permute-start.15 = (bf16[128,256]{1,0:T(8,128)(2,1)S(1)}, bf16[128,256]{1,0:T(8,128)(2,1)S(1)}, u32[]{:S(2)}, u32[]{:S(2)}) collective-permute-start(bf16[128,256]{1,0:T(8,128)(2,1)S(1)} %get-tuple-element.160), channel_id=1, source_target_pairs={{0,2},{1,3},{2,0},{3,1},{4,6},{5,7},{6,4},{7,5},{8,10},{9,11},{10,... | collective-permute-start | bytes 196616 | tf_op jit(solution)/shard_map/ppermute | solution.py:58
  75.6 6.7 %collective-permute-start.16 = (bf16[128,256]{1,0:T(8,128)(2,1)S(1)}, bf16[128,256]{1,0:T(8,128)(2,1)S(1)}, u32[]{:S(2)}, u32[]{:S(2)}) collective-permute-start(bf16[128,256]{1,0:T(8,128)(2,1)S(1)} %get-tuple-element.161), channel_id=1, source_target_pairs={{0,3},{1,2},{2,1},{3,0},{4,7},{5,6},{6,5},{7,4},{8,11},{9,10},{10,... | collective-permute-start | bytes 196616 | tf_op jit(solution)/shard_map/ppermute | solution.py:58
  80.3 8.1 %copy-start = (bf16[8,64,512]{2,1,0:T(8,128)(2,1)}, bf16[8,64,512]{2,1,0:T(8,128)(2,1)S(1)}, u32[]{:S(2)}) copy-start(bf16[8,64,512]{2,1,0:T(8,128)(2,1)S(1)} %all-to-all-done.1) | copy-start | bytes 1572868
  80.3 2.0 %copy-start.11 = (bf16[2,2,64,1024]{3,2,1,0:T(8,128)(2,1)}, bf16[2,2,64,1024]{3,2,1,0:T(8,128)(2,1)S(1)}, u32[]{:S(2)}) copy-start(bf16[2,2,64,1024]{3,2,1,0:T(8,128)(2,1)S(1)} %collective-permute-done.12.pair) | copy-start | bytes 1572868
  88.4 9.1 %collective-permute-start.17 = (bf16[128,256]{1,0:T(8,128)(2,1)S(1)}, bf16[128,256]{1,0:T(8,128)(2,1)S(1)}, u32[]{:S(2)}, u32[]{:S(2)}) collective-permute-start(bf16[128,256]{1,0:T(8,128)(2,1)S(1)} %get-tuple-element.175), channel_id=1, source_target_pairs={{0,1},{1,0},{2,3},{3,2},{4,5},{5,4},{6,7},{7,6},{8,9},{9,8},{10,11... | collective-permute-start | bytes 196616 | tf_op jit(solution)/shard_map/ppermute | solution.py:58
  88.6 8.8 %collective-permute-start.18 = (bf16[128,256]{1,0:T(8,128)(2,1)S(1)}, bf16[128,256]{1,0:T(8,128)(2,1)S(1)}, u32[]{:S(2)}, u32[]{:S(2)}) collective-permute-start(bf16[128,256]{1,0:T(8,128)(2,1)S(1)} %get-tuple-element.176), channel_id=1, source_target_pairs={{0,2},{1,3},{2,0},{3,1},{4,6},{5,7},{6,4},{7,5},{8,10},{9,11},{10,... | collective-permute-start | bytes 196616 | tf_op jit(solution)/shard_map/ppermute | solution.py:58
  90.2 7.3 %collective-permute-start.19 = (bf16[128,256]{1,0:T(8,128)(2,1)S(1)}, bf16[128,256]{1,0:T(8,128)(2,1)S(1)}, u32[]{:S(2)}, u32[]{:S(2)}) collective-permute-start(bf16[128,256]{1,0:T(8,128)(2,1)S(1)} %get-tuple-element.177), channel_id=1, source_target_pairs={{0,3},{1,2},{2,1},{3,0},{4,7},{5,6},{6,5},{7,4},{8,11},{9,10},{10,... | collective-permute-start | bytes 196616 | tf_op jit(solution)/shard_map/ppermute | solution.py:58
  101.6 5.5 %copy-start.7 = (bf16[256,2048]{1,0:T(8,128)(2,1)S(1)}, bf16[256,2048]{1,0:T(8,128)(2,1)}, u32[]{:S(2)}) copy-start(bf16[256,2048]{1,0:T(8,128)(2,1)} %refs_0_) | copy-start | bytes 3145732
  101.6 27.9 %copy-start.19 = (bf16[128,2048]{1,0:T(8,128)(2,1)S(1)}, bf16[128,2048]{1,0:T(8,128)(2,1)}, u32[]{:S(2)}) copy-start(bf16[128,2048]{1,0:T(8,128)(2,1)} %get-tuple-element.219) | copy-start | bytes 1572868
  101.6 27.1 %all-to-all-start.2 = ((bf16[8,192,512]{2,1,0:T(8,128)(2,1)}), bf16[8,192,512]{2,1,0:T(8,128)(2,1)S(1)}, u32[]{:S(2)}, u32[]{:S(2)}) async-start(bf16[8,192,512]{2,1,0:T(8,128)(2,1)} %weight.1), calls=%async_computation.2 | async-start | bytes 3145728 | tf_op jit(solution)/shard_map/all_to_all | solution.py:45
  107.0 61.1 %copy-start.1 = (bf16[128,1024]{1,0:T(8,128)(2,1)S(1)}, bf16[128,1024]{1,0:T(8,128)(2,1)}, u32[]{:S(2)}) copy-start(bf16[128,1024]{1,0:T(8,128)(2,1)} %get-tuple-element.226.refs_6_) | copy-start | bytes 786436
  107.1 16.6 %collective-permute-start.21 = (bf16[256,2048]{1,0:T(8,128)(2,1)S(1)}, bf16[256,2048]{1,0:T(8,128)(2,1)}, u32[]{:S(2)}, u32[]{:S(2)}) collective-permute-start(bf16[256,2048]{1,0:T(8,128)(2,1)S(1)} %copy-done.7), channel_id=1, source_target_pairs={{0,1},{1,0},{2,3},{3,2},{4,5},{5,4},{6,7},{7,6},{8,9},{9,8},{10,11... | collective-permute-start | bytes 3145736 | tf_op jit(solution)/shard_map/ppermute | solution.py:58
  107.1 15.8 %collective-permute-start.20 = (bf16[2,64,1024]{2,1,0:T(8,128)(2,1)}, bf16[2,64,1024]{2,1,0:T(8,128)(2,1)S(1)}, u32[]{:S(2)}, u32[]{:S(2)}) collective-permute-start(bf16[2,64,1024]{2,1,0:T(8,128)(2,1)} %get-tuple-element.194), channel_id=1, source_target_pairs={{0,32},{4,36},{8,40},{12,44},{16,48},{20,52},{24,56},{28,60},{32,0... | collective-permute-start | bytes 786440 | tf_op jit(solution)/shard_map/ppermute | solution.py:49
  123.0 0.7 copy-start.21
  128.7 26.9 %collective-permute-start.27 = (bf16[128,2048]{1,0:T(8,128)(2,1)}, bf16[128,2048]{1,0:T(8,128)(2,1)S(1)}, u32[]{:S(2)}, u32[]{:S(2)}) collective-permute-start(bf16[128,2048]{1,0:T(8,128)(2,1)} %get-tuple-element.218), channel_id=1, source_target_pairs={{0,2},{1,3},{2,0},{3,1},{4,6},{5,7},{6,4},{7,5},{8,10},{9,11},{10,... | collective-permute-start | bytes 1572872 | tf_op jit(solution)/shard_map/ppermute | solution.py:58
  129.5 26.0 %collective-permute-start.28 = (bf16[128,2048]{1,0:T(8,128)(2,1)S(1)}, bf16[128,2048]{1,0:T(8,128)(2,1)S(1)}, u32[]{:S(2)}, u32[]{:S(2)}) collective-permute-start(bf16[128,2048]{1,0:T(8,128)(2,1)S(1)} %copy-done.19), channel_id=1, source_target_pairs={{0,6},{1,7},{2,4},{3,5},{4,2},{5,3},{6,0},{7,1},{8,14},{9,15},{10,... | collective-permute-start | bytes 1572872 | tf_op jit(solution)/shard_map/ppermute | solution.py:63
  131.3 7.2 %collective-permute-start.22 = (bf16[128,512]{1,0:T(8,128)(2,1)S(1)}, bf16[128,512]{1,0:T(8,128)(2,1)S(1)}, u32[]{:S(2)}, u32[]{:S(2)}) collective-permute-start(bf16[128,512]{1,0:T(8,128)(2,1)S(1)} %get-tuple-element.203), channel_id=1, source_target_pairs={{0,8},{4,12},{8,0},{12,4},{16,24},{20,28},{24,16},{28,20},{32,40},... | collective-permute-start | bytes 393224 | tf_op jit(solution)/shard_map/ppermute | solution.py:49
  133.0 16.6 %collective-permute-start.25 = (bf16[2,64,1024]{2,1,0:T(8,128)(2,1)}, bf16[2,64,1024]{2,1,0:T(8,128)(2,1)S(1)}, u32[]{:S(2)}, u32[]{:S(2)}) collective-permute-start(bf16[2,64,1024]{2,1,0:T(8,128)(2,1)} %get-tuple-element.211), channel_id=1, source_target_pairs={{0,252},{4,8},{8,4},{12,16},{16,12},{20,24},{24,20},{28,32},{32,28... | collective-permute-start | bytes 786440 | tf_op jit(solution)/shard_map/ppermute | solution.py:98
  137.2 12.4 %collective-permute-start.26 = (bf16[2,64,1024]{2,1,0:T(8,128)(2,1)}, bf16[2,64,1024]{2,1,0:T(8,128)(2,1)S(1)}, u32[]{:S(2)}, u32[]{:S(2)}) collective-permute-start(bf16[2,64,1024]{2,1,0:T(8,128)(2,1)} %get-tuple-element.215), channel_id=1, source_target_pairs={{0,64},{4,68},{8,72},{12,76},{16,80},{20,84},{24,88},{28,92},{32,9... | collective-permute-start | bytes 786440 | tf_op jit(solution)/shard_map/ppermute | solution.py:49
  139.1 6.7 %collective-permute-start.23 = (bf16[96,512]{1,0:T(8,128)(2,1)S(1)}, bf16[96,512]{1,0:T(8,128)(2,1)S(1)}, u32[]{:S(2)}, u32[]{:S(2)}) collective-permute-start(bf16[96,512]{1,0:T(8,128)(2,1)S(1)} %get-tuple-element.206), channel_id=1, source_target_pairs={{0,16},{4,20},{8,24},{12,28},{16,0},{20,4},{24,8},{28,12},{32,48},... | collective-permute-start | bytes 294920 | tf_op jit(solution)/shard_map/ppermute | solution.py:49
  146.4 9.2 %collective-permute-start.24 = (bf16[80,512]{1,0:T(8,128)(2,1)S(1)}, bf16[80,512]{1,0:T(8,128)(2,1)S(1)}, u32[]{:S(2)}, u32[]{:S(2)}) collective-permute-start(bf16[80,512]{1,0:T(8,128)(2,1)S(1)} %get-tuple-element.209), channel_id=1, source_target_pairs={{0,32},{4,36},{8,40},{12,44},{16,48},{20,52},{24,56},{28,60},{32,0... | collective-permute-start | bytes 245768 | tf_op jit(solution)/shard_map/ppermute | solution.py:49
  149.6 8.0 %copy-start.22 = (bf16[2,64,1024]{2,1,0:T(8,128)(2,1)}, bf16[2,64,1024]{2,1,0:T(8,128)(2,1)S(1)}, u32[]{:S(2)}) copy-start(bf16[2,64,1024]{2,1,0:T(8,128)(2,1)S(1)} %collective-permute-done.25.outer) | copy-start | bytes 786436
  149.6 8.0 %copy-start.23 = (bf16[2,64,1024]{2,1,0:T(8,128)(2,1)}, bf16[2,64,1024]{2,1,0:T(8,128)(2,1)S(1)}, u32[]{:S(2)}) copy-start(bf16[2,64,1024]{2,1,0:T(8,128)(2,1)S(1)} %collective-permute-done.26.rest_3_) | copy-start | bytes 786436
  155.6 11.8 %copy-start.15 = (bf16[128,2048]{1,0:T(8,128)(2,1)}, bf16[128,2048]{1,0:T(8,128)(2,1)S(1)}, u32[]{:S(2)}) copy-start(bf16[128,2048]{1,0:T(8,128)(2,1)S(1)} %collective-permute-done.27.refs_2_) | copy-start | bytes 1572868
  155.6 11.8 %copy-start.16 = (bf16[128,2048]{1,0:T(8,128)(2,1)}, bf16[128,2048]{1,0:T(8,128)(2,1)S(1)}, u32[]{:S(2)}) copy-start(bf16[128,2048]{1,0:T(8,128)(2,1)S(1)} %collective-permute-done.28.refs_3_) | copy-start | bytes 1572868
  155.6 9.6 %collective-permute-start.29 = (bf16[128,2048]{1,0:T(8,128)(2,1)S(1)}, bf16[128,2048]{1,0:T(8,128)(2,1)S(1)}, u32[]{:S(2)}, u32[]{:S(2)}) collective-permute-start(bf16[128,2048]{1,0:T(8,128)(2,1)S(1)} %collective-permute-done.27.refs_2_), channel_id=1, source_target_pairs={{0,1},{1,0},{2,3},{3,2},{4,5},{5,4},{6,7},{7,6},{8,9},{9,8},{10,11... | collective-permute-start | bytes 1572872 | tf_op jit(solution)/shard_map/ppermute | solution.py:58
  155.7 11.6 %collective-permute-start.30 = (bf16[128,2048]{1,0:T(8,128)(2,1)S(1)}, bf16[128,2048]{1,0:T(8,128)(2,1)S(1)}, u32[]{:S(2)}, u32[]{:S(2)}) collective-permute-start(bf16[128,2048]{1,0:T(8,128)(2,1)S(1)} %collective-permute-done.28.refs_3_), channel_id=1, source_target_pairs={{0,1},{1,0},{2,3},{3,2},{4,5},{5,4},{6,7},{7,6},{8,9},{9,8},{10,11... | collective-permute-start | bytes 1572872 | tf_op jit(solution)/shard_map/ppermute | solution.py:58
  156.2 23.4 %collective-permute-start.31 = (bf16[2,2,64,1024]{3,2,1,0:T(8,128)(2,1)}, bf16[2,2,64,1024]{3,2,1,0:T(8,128)(2,1)S(1)}, u32[]{:S(2)}, u32[]{:S(2)}) collective-permute-start(bf16[2,2,64,1024]{3,2,1,0:T(8,128)(2,1)} %get-tuple-element.230), channel_id=1, source_target_pairs={{0,4},{4,0},{8,12},{12,8},{16,20},{20,16},{24,28},{28,24},{32,36},... | collective-permute-start | bytes 1572872 | tf_op jit(solution)/shard_map/ppermute | solution.py:49
  157.6 21.1 %all-to-all-start.3 = ((bf16[8,64,512]{2,1,0:T(8,128)(2,1)}), bf16[8,64,512]{2,1,0:T(8,128)(2,1)S(1)}, u32[]{:S(2)}, u32[]{:S(2)}) async-start(bf16[8,64,512]{2,1,0:T(8,128)(2,1)} %get-tuple-element.221), calls=%async_computation.3 | async-start | bytes 1048576 | tf_op jit(solution)/shard_map/all_to_all | solution.py:45
  164.9 13.8 %collective-permute-start.32 = (bf16[2,64,1024]{2,1,0:T(8,128)(2,1)}, bf16[2,64,1024]{2,1,0:T(8,128)(2,1)}, u32[]{:S(2)}, u32[]{:S(2)}) collective-permute-start(bf16[2,64,1024]{2,1,0:T(8,128)(2,1)} %get-tuple-element.232), channel_id=1, source_target_pairs={{0,8},{4,12},{8,0},{12,4},{16,24},{20,28},{24,16},{28,20},{32,40},... | collective-permute-start | bytes 786440 | tf_op jit(solution)/shard_map/ppermute | solution.py:49
  165.0 14.6 %collective-permute-start.33 = (bf16[2,64,1024]{2,1,0:T(8,128)(2,1)}, bf16[2,64,1024]{2,1,0:T(8,128)(2,1)}, u32[]{:S(2)}, u32[]{:S(2)}) collective-permute-start(bf16[2,64,1024]{2,1,0:T(8,128)(2,1)} %get-tuple-element.233), channel_id=1, source_target_pairs={{0,16},{4,20},{8,24},{12,28},{16,0},{20,4},{24,8},{28,12},{32,48},... | collective-permute-start | bytes 786440 | tf_op jit(solution)/shard_map/ppermute | solution.py:49
  165.2 2.1 %copy-start.17 = (bf16[128,2048]{1,0:T(8,128)(2,1)}, bf16[128,2048]{1,0:T(8,128)(2,1)S(1)}, u32[]{:S(2)}) copy-start(bf16[128,2048]{1,0:T(8,128)(2,1)S(1)} %collective-permute-done.29.refs_4_) | copy-start | bytes 1572868
  165.2 14.4 %collective-permute-start.34 = (bf16[2,64,1024]{2,1,0:T(8,128)(2,1)}, bf16[2,64,1024]{2,1,0:T(8,128)(2,1)}, u32[]{:S(2)}, u32[]{:S(2)}) collective-permute-start(bf16[2,64,1024]{2,1,0:T(8,128)(2,1)} %get-tuple-element.236), channel_id=1, source_target_pairs={{0,128},{4,132},{8,136},{12,140},{16,144},{20,148},{24,152},{28,15... | collective-permute-start | bytes 786440 | tf_op jit(solution)/shard_map/ppermute | solution.py:49
  167.3 0.9 copy-start.18
  179.6 0.8 copy-start.20
